TPU v7x, 32 devices: a whole 2x2x4 slice. The times are simulated.
32 devices in a mesh: dp: 8 (over z, x), ctx: 4 (over y, core).
Axes of the slice: x: 2, y: 2, z: 4, core: 2. Of those that a mesh axis runs over, the one named last changes fastest.
Arguments:
- tokens: bfloat16 [8, 2048, 768], P('dp', 'ctx'), may hold values from -6 to 6
- lengths: int32 [8], P('dp'), may hold values from 513 to 2048, as said below
- thought_pos: int32 [8, 6], P('dp'), may hold values from 1 to 2047, as said below
- cotangent: bfloat16 [8, 2048, 768], P('dp', 'ctx'), may hold values from -6 to 6
- qkv_weight: bfloat16 [768, 2304], P(('dp', 'ctx')), may hold values from -0.21875 to 0.21875
- out_weight: bfloat16 [768, 768], P(('dp', 'ctx')), may hold values from -2.5 to 2.5
- fc_weight: bfloat16 [768, 3072], P(('dp', 'ctx')), may hold values from -0.21875 to 0.21875
- proj_weight: bfloat16 [3072, 768], P(('dp', 'ctx')), may hold values from -0.109375 to 0.109375
- qv_bias: bfloat16 [1536], P(('dp', 'ctx')), may hold values from -1.5 to 1.5
- out_bias: bfloat16 [768], P(('dp', 'ctx')), may hold values from -1.5 to 1.5
- fc_bias: bfloat16 [3072], P(('dp', 'ctx')), may hold values from -1.5 to 1.5
- proj_bias: bfloat16 [768], P(('dp', 'ctx')), may hold values from -1.5 to 1.5
- first_gain: bfloat16 [768], P(('dp', 'ctx')), may hold values from 0.5 to 1.5
- first_shift: bfloat16 [768], P(('dp', 'ctx')), may hold values from -1 to 1
- second_gain: bfloat16 [768], P(('dp', 'ctx')), may hold values from 0.5 to 1.5
- second_shift: bfloat16 [768], P(('dp', 'ctx')), may hold values from -1 to 1
Outputs:
- mixed: bfloat16 [8, 2048, 768], P('dp', 'ctx')
- tokens_grad: float32 [8, 2048, 768], P('dp', 'ctx')
- qkv_weight_grad: float32 [768, 2304], P(('dp', 'ctx'))
- out_weight_grad: float32 [768, 768], P(('dp', 'ctx'))
- fc_weight_grad: float32 [768, 3072], P(('dp', 'ctx'))
- proj_weight_grad: float32 [3072, 768], P(('dp', 'ctx'))
- qv_bias_grad: float32 [1536], P(('dp', 'ctx'))
- out_bias_grad: float32 [768], P(('dp', 'ctx'))
- fc_bias_grad: float32 [3072], P(('dp', 'ctx'))
- proj_bias_grad: float32 [768], P(('dp', 'ctx'))
- first_gain_grad: float32 [768], P(('dp', 'ctx'))
- first_shift_grad: float32 [768], P(('dp', 'ctx'))
- second_gain_grad: float32 [768], P(('dp', 'ctx'))
- second_shift_grad: float32 [768], P(('dp', 'ctx'))
Inputs may be any that keep to these rules, and one draw needn't show every extreme that they name: `lengths`: every draw holds a sequence of length 2048 and one of length 513. `thought_pos`: each entry lies from 1 to its sequence's length minus one; entries may repeat; the first entry of each sequence is a positive multiple of 512; every draw holds an entry 1 and an entry 2047.
All inputs are finite; a program needn't handle non-finite values.
Results may differ from a plain program's by a relative error of at most 0.011.
Values may be sent and summed in bfloat16 or wider, within the bound.
No kernel may reach another device: no remote copies, remote signals or barrier semaphores. Data moves between devices by JAX's collectives and lax.ppermute only.
A program may use at most 256 MiB of HBM per device.

v0:
```python
import jax
import jax.numpy as jnp
from jax import lax
from jax.sharding import PartitionSpec as P

HEADS = 12


def from_behind(value, axis, steps):
    count = lax.axis_size(axis)
    first, last = (max(0, -steps), min(count, count - steps))
    return lax.ppermute(value, axis, [(source, source + steps) for source in range(first, last)])


def layer_norm(values, gain, shift):
    center = values - jnp.mean(values, -1, keepdims=True)
    spread = jnp.mean(center * center, -1, keepdims=True)
    return center * lax.rsqrt(spread + 1e-05) * gain + shift


def gelu_tanh(values):
    return jax.nn.gelu(values, approximate=True)


def shards(
    tokens,
    lengths,
    thought_pos,
    cotangent,
    qkv_weight,
    out_weight,
    fc_weight,
    proj_weight,
    qv_bias,
    out_bias,
    fc_bias,
    proj_bias,
    first_gain,
    first_shift,
    second_gain,
    second_shift,
):
    seq_count, quarter, width = tokens.shape
    rows = seq_count * quarter
    head_dim = width // HEADS
    scale = head_dim ** (-0.5)
    slots = lax.axis_index("ctx") * quarter + jnp.arange(quarter, dtype=jnp.int32)
    thought = jnp.any(thought_pos[:, :, None] == slots[None, None, :], axis=1)
    valid = slots[None, :] < lengths[:, None]
    last_rows = from_behind(tokens[:, quarter - 1 :, :], "ctx", 1)
    earlier = jnp.concatenate([last_rows, tokens[:, :-1, :]], axis=1)
    inputs = (
        jnp.where(thought[:, :, None], earlier, tokens).astype(jnp.float32).reshape(rows, width)
    )
    gathered = (
        lax.all_gather(qkv_weight, ("dp", "ctx"), axis=0, tiled=True),
        lax.all_gather(out_weight, ("dp", "ctx"), axis=0, tiled=True),
        lax.all_gather(fc_weight, ("dp", "ctx"), axis=0, tiled=True),
        lax.all_gather(proj_weight, ("dp", "ctx"), axis=0, tiled=True),
        lax.all_gather(qv_bias, ("dp", "ctx"), axis=0, tiled=True),
        lax.all_gather(out_bias, ("dp", "ctx"), axis=0, tiled=True),
        lax.all_gather(fc_bias, ("dp", "ctx"), axis=0, tiled=True),
        lax.all_gather(proj_bias, ("dp", "ctx"), axis=0, tiled=True),
        lax.all_gather(first_gain, ("dp", "ctx"), axis=0, tiled=True),
        lax.all_gather(first_shift, ("dp", "ctx"), axis=0, tiled=True),
        lax.all_gather(second_gain, ("dp", "ctx"), axis=0, tiled=True),
        lax.all_gather(second_shift, ("dp", "ctx"), axis=0, tiled=True),
    )
    qkv_full, out_full, fc_full, proj_full = (gathered[0], gathered[1], gathered[2], gathered[3])
    small = [piece.astype(jnp.float32) for piece in gathered[4:]]
    (
        qv_full,
        out_bias_full,
        fc_bias_full,
        proj_bias_full,
        gain_one,
        shift_one,
        gain_two,
        shift_two,
    ) = small
    normed = layer_norm(inputs, gain_one, shift_one).astype(jnp.bfloat16)
    bias_full = jnp.concatenate(
        [qv_full[:width], jnp.zeros((width,), jnp.float32), qv_full[width:]]
    )
    projected = (jnp.dot(normed, qkv_full, preferred_element_type=jnp.float32) + bias_full).astype(
        jnp.bfloat16
    )
    projected = projected.reshape(seq_count, quarter, 3 * width)
    queries = projected[:, :, :width]
    keyval = projected[:, :, width:]
    keyval_all = lax.all_gather(keyval, "ctx", axis=1, tiled=True)

    def score_block(query_rows, keyval_rows, limit):
        total = keyval_rows.shape[0]
        key_heads = keyval_rows[:, :width].reshape(total, HEADS, head_dim)
        value_heads = keyval_rows[:, width:].reshape(total, HEADS, head_dim)
        query_heads = query_rows.reshape(quarter, HEADS, head_dim)
        key_slots = jnp.arange(total, dtype=jnp.int32)
        allowed = (key_slots[None, :] <= slots[:, None]) & (key_slots[None, :] < limit)
        scores = (
            jnp.einsum("qhd,khd->hqk", query_heads, key_heads, preferred_element_type=jnp.float32)
            * scale
        )
        scores = jnp.where(allowed[None], scores, -1000000000.0)
        return (scores, query_heads, key_heads, value_heads)

    def attend(packed):
        query_rows, keyval_rows, limit = packed
        scores, query_heads, key_heads, value_heads = score_block(query_rows, keyval_rows, limit)
        top = jnp.max(scores, -1, keepdims=True)
        expo = jnp.exp(scores - top)
        denom = jnp.sum(expo, -1, keepdims=True)
        probs_low = (expo / denom).astype(jnp.bfloat16)
        result = jnp.einsum(
            "hqk,khd->qhd", probs_low, value_heads, preferred_element_type=jnp.float32
        )
        return (result.reshape(quarter, width), top + jnp.log(denom))

    attended, logsum = lax.map(attend, (queries, keyval_all, lengths))
    attended = attended.reshape(rows, width).astype(jnp.bfloat16)
    middle = (
        inputs + jnp.dot(attended, out_full, preferred_element_type=jnp.float32) + out_bias_full
    )
    normed_two = layer_norm(middle, gain_two, shift_two).astype(jnp.bfloat16)
    hidden = jnp.dot(normed_two, fc_full, preferred_element_type=jnp.float32) + fc_bias_full
    active = gelu_tanh(hidden).astype(jnp.bfloat16)
    output = (
        middle + jnp.dot(active, proj_full, preferred_element_type=jnp.float32) + proj_bias_full
    )
    valid_rows = valid.reshape(rows, 1)
    mixed = (
        jnp.where(valid_rows, output, 0.0).astype(jnp.bfloat16).reshape(seq_count, quarter, width)
    )
    regathered = (
        lax.all_gather(qkv_weight, ("dp", "ctx"), axis=0, tiled=True),
        lax.all_gather(out_weight, ("dp", "ctx"), axis=0, tiled=True),
        lax.all_gather(fc_weight, ("dp", "ctx"), axis=0, tiled=True),
        lax.all_gather(proj_weight, ("dp", "ctx"), axis=0, tiled=True),
        lax.all_gather(qv_bias, ("dp", "ctx"), axis=0, tiled=True),
        lax.all_gather(out_bias, ("dp", "ctx"), axis=0, tiled=True),
        lax.all_gather(fc_bias, ("dp", "ctx"), axis=0, tiled=True),
        lax.all_gather(proj_bias, ("dp", "ctx"), axis=0, tiled=True),
        lax.all_gather(first_gain, ("dp", "ctx"), axis=0, tiled=True),
        lax.all_gather(first_shift, ("dp", "ctx"), axis=0, tiled=True),
        lax.all_gather(second_gain, ("dp", "ctx"), axis=0, tiled=True),
        lax.all_gather(second_shift, ("dp", "ctx"), axis=0, tiled=True),
    )
    keyval_back = lax.all_gather(keyval, "ctx", axis=1, tiled=True)
    qkv_back, out_back, fc_back, proj_back = (
        regathered[0],
        regathered[1],
        regathered[2],
        regathered[3],
    )
    grad_valid = jnp.where(valid_rows, cotangent.reshape(rows, width).astype(jnp.float32), 0.0)
    grad_branch = grad_valid.astype(jnp.bfloat16)
    proj_weight_grad = jnp.einsum(
        "rf,rd->fd", active, grad_branch, preferred_element_type=jnp.float32
    )
    proj_bias_grad = jnp.sum(grad_branch.astype(jnp.float32), 0)
    grad_active = jnp.einsum(
        "rd,fd->rf", grad_branch, proj_back, preferred_element_type=jnp.float32
    )
    unused_value, gelu_back = jax.vjp(gelu_tanh, hidden)
    grad_hidden = gelu_back(grad_active)[0].astype(jnp.bfloat16)
    fc_weight_grad = jnp.einsum(
        "rd,rf->df", normed_two, grad_hidden, preferred_element_type=jnp.float32
    )
    fc_bias_grad = jnp.sum(grad_hidden.astype(jnp.float32), 0)
    grad_normed_two = jnp.einsum(
        "rf,df->rd", grad_hidden, fc_back, preferred_element_type=jnp.float32
    )
    unused_norm, norm_back_two = jax.vjp(layer_norm, middle, gain_two, shift_two)
    middle_part, second_gain_grad, second_shift_grad = norm_back_two(grad_normed_two)
    grad_middle = grad_valid + middle_part
    grad_attn = grad_middle.astype(jnp.bfloat16)
    out_weight_grad = jnp.einsum(
        "rd,re->de", attended, grad_attn, preferred_element_type=jnp.float32
    )
    out_bias_grad = jnp.sum(grad_attn.astype(jnp.float32), 0)
    grad_attended = jnp.einsum(
        "re,de->rd", grad_attn, out_back, preferred_element_type=jnp.float32
    ).astype(jnp.bfloat16)
    grad_attended = grad_attended.reshape(seq_count, quarter, width)

    def query_side(query_rows, keyval_rows, limit, grad_rows, logsum_rows):
        scores, query_heads, key_heads, value_heads = score_block(query_rows, keyval_rows, limit)
        probs = jnp.exp(scores - logsum_rows)
        grad_heads = grad_rows.reshape(quarter, HEADS, head_dim)
        grad_probs = jnp.einsum(
            "qhd,khd->hqk", grad_heads, value_heads, preferred_element_type=jnp.float32
        )
        delta = jnp.sum(probs * grad_probs, -1, keepdims=True)
        grad_scores = (probs * (grad_probs - delta)).astype(jnp.bfloat16)
        grad_query = (
            jnp.einsum("hqk,khd->qhd", grad_scores, key_heads, preferred_element_type=jnp.float32)
            * scale
        )
        return (
            grad_query.reshape(quarter, width),
            delta,
            grad_scores,
            probs,
            query_heads,
            grad_heads,
        )

    def attend_back(packed):
        query_rows, keyval_rows, limit, grad_rows, logsum_rows = packed
        total = keyval_rows.shape[0]
        grad_query, delta, grad_scores, probs, query_heads, grad_heads = query_side(
            query_rows, keyval_rows, limit, grad_rows, logsum_rows
        )
        probs_low = probs.astype(jnp.bfloat16)
        grad_keys = (
            jnp.einsum("hqk,qhd->khd", grad_scores, query_heads, preferred_element_type=jnp.float32)
            * scale
        )
        grad_values = jnp.einsum(
            "hqk,qhd->khd", probs_low, grad_heads, preferred_element_type=jnp.float32
        )
        grad_keyval = jnp.concatenate(
            [grad_keys.reshape(total, width), grad_values.reshape(total, width)], -1
        )
        return (grad_query, grad_keyval)

    grad_queries, grad_keyval_all = lax.map(
        attend_back, (queries, keyval_back, lengths, grad_attended, logsum)
    )
    grad_keyval = lax.psum_scatter(
        grad_keyval_all.astype(jnp.bfloat16), "ctx", scatter_dimension=1, tiled=True
    ).astype(jnp.float32)
    grad_qkv = (
        jnp.concatenate([grad_queries, grad_keyval], -1)
        .astype(jnp.bfloat16)
        .reshape(rows, 3 * width)
    )
    qkv_weight_grad = jnp.einsum("rd,re->de", normed, grad_qkv, preferred_element_type=jnp.float32)
    column_sums = jnp.sum(grad_qkv.astype(jnp.float32), 0)
    qv_bias_grad = jnp.concatenate([column_sums[:width], column_sums[2 * width :]])
    grad_normed = jnp.einsum("re,de->rd", grad_qkv, qkv_back, preferred_element_type=jnp.float32)
    unused_first, norm_back_one = jax.vjp(layer_norm, inputs, gain_one, shift_one)
    inputs_part, first_gain_grad, first_shift_grad = norm_back_one(grad_normed)
    grad_inputs = (grad_middle + inputs_part).reshape(seq_count, quarter, width)
    thought_col = thought[:, :, None]
    kept_grad = jnp.where(thought_col, 0.0, grad_inputs)
    moved_grad = jnp.where(thought_col, grad_inputs, 0.0)
    following = from_behind(moved_grad[:, :1, :], "ctx", -1)
    shifted = jnp.concatenate([moved_grad[:, 1:, :], following], axis=1)
    tokens_grad = kept_grad + shifted
    grads = (
        qkv_weight_grad,
        out_weight_grad,
        fc_weight_grad,
        proj_weight_grad,
        qv_bias_grad,
        out_bias_grad,
        fc_bias_grad,
        proj_bias_grad,
        first_gain_grad,
        first_shift_grad,
        second_gain_grad,
        second_shift_grad,
    )
    shares = (
        lax.psum_scatter(grads[0], ("dp", "ctx"), scatter_dimension=0, tiled=True),
        lax.psum_scatter(grads[1], ("dp", "ctx"), scatter_dimension=0, tiled=True),
        lax.psum_scatter(grads[2], ("dp", "ctx"), scatter_dimension=0, tiled=True),
        lax.psum_scatter(grads[3], ("dp", "ctx"), scatter_dimension=0, tiled=True),
        lax.psum_scatter(grads[4], ("dp", "ctx"), scatter_dimension=0, tiled=True),
        lax.psum_scatter(grads[5], ("dp", "ctx"), scatter_dimension=0, tiled=True),
        lax.psum_scatter(grads[6], ("dp", "ctx"), scatter_dimension=0, tiled=True),
        lax.psum_scatter(grads[7], ("dp", "ctx"), scatter_dimension=0, tiled=True),
        lax.psum_scatter(grads[8], ("dp", "ctx"), scatter_dimension=0, tiled=True),
        lax.psum_scatter(grads[9], ("dp", "ctx"), scatter_dimension=0, tiled=True),
        lax.psum_scatter(grads[10], ("dp", "ctx"), scatter_dimension=0, tiled=True),
        lax.psum_scatter(grads[11], ("dp", "ctx"), scatter_dimension=0, tiled=True),
    )
    return (
        mixed,
        tokens_grad,
        shares[0],
        shares[1],
        shares[2],
        shares[3],
        shares[4],
        shares[5],
        shares[6],
        shares[7],
        shares[8],
        shares[9],
        shares[10],
        shares[11],
    )


def solution(mesh):
    placed = (
        P("dp", "ctx", None),
        P("dp"),
        P("dp", None),
        P("dp", "ctx", None),
        P(("dp", "ctx"), None),
        P(("dp", "ctx"), None),
        P(("dp", "ctx"), None),
        P(("dp", "ctx"), None),
        P(("dp", "ctx")),
        P(("dp", "ctx")),
        P(("dp", "ctx")),
        P(("dp", "ctx")),
        P(("dp", "ctx")),
        P(("dp", "ctx")),
        P(("dp", "ctx")),
        P(("dp", "ctx")),
    )
    return jax.shard_map(
        shards,
        mesh=mesh,
        in_specs=placed,
        out_specs=(
            P("dp", "ctx", None),
            P("dp", "ctx", None),
            P(("dp", "ctx"), None),
            P(("dp", "ctx"), None),
            P(("dp", "ctx"), None),
            P(("dp", "ctx"), None),
            P(("dp", "ctx")),
            P(("dp", "ctx")),
            P(("dp", "ctx")),
            P(("dp", "ctx")),
            P(("dp", "ctx")),
            P(("dp", "ctx")),
            P(("dp", "ctx")),
            P(("dp", "ctx")),
        ),
        check_vma=False,
    )
```

profile of v0, /device:TPU:1, one launch (start us, length us, event | category | flops | bytes accessed | tf_op | source)
XLA Modules:
  0.0 1026.9 jit_solution(12014408498325250842)
XLA Ops:
  8.7 4.5 collective-permute-start
  19.9 38.6 %all-reduce.17 = (bf16[1536]{0:T(1024)(128)(2,1)S(1)}, bf16[768]{0:T(1024)(128)(2,1)S(1)}, bf16[768]{0:T(1024)(128)(2,1)S(1)}, bf16[768]{0:T(1024)(128)(2,1)S(1)...) all-reduce(bf16[1536]{0:T(1024)(128)(2,1)S(1)} %dynamic-update-slic, ...), channel_id=1, replica_groups=mesh['dp'=8,'ctx'=4] {'dp','ctx'}, use_global_device_ids=true, to_apply=%add.2 | all-reduce | flops 9216 | bytes 36864
  61.8 12.0 %all-gather.6.cloned.1.call-done = bf16[768,2304]{1,0:T(8,128)(2,1)} async-done(((bf16[24,2304]{1,0:T(8,128)(2,1)}), bf16[768,2304]{1,0:T(8,128)(2,1)}) %all-gather.6.cloned.1.call-update) | async-done | bytes 3538960 | tf_op jit(solution)/shard_map/all_gather | solution.py:56
  73.8 4.2 fusion.16
  84.5 41.8 %all-gather.8.cloned.1.call-done = bf16[1,2048,1536]{2,1,0:T(8,128)(2,1)} async-done(((bf16[1,512,1536]{2,1,0:T(8,128)(2,1)}), bf16[1,2048,1536]{2,1,0:T(8,128)(2,1)}) %all-gather.8.cloned.1.call-update) | async-done | bytes 6291472 | tf_op jit(solution)/shard_map/all_gather | solution.py:91
  126.3 5.9 fusion.64
  132.2 5.0 copy.48
  137.2 4.7 copy.46
  141.9 22.3 %fusion.6 = (f32[12,512]{1,0:T(8,128)S(1)}, f32[12,512,2048]{2,1,0:T(8,128)}) fusion(pred[512,2048]{1,0:T(8,128)(4,1)S(1)} %fusion.15, bf16[512,12,64]{0,2,1:T(8,128)(2,1)S(1)} %bitcast.117, bf16[2048,12,64]{0,2,1:T(8,128)(2,1)} %bitcast.112), kind=kOutput, calls=%fused_computation.11 | convolution fusion | flops 1648355328 | bytes 55336960 | tf_op jit(solution)/shard_map/while/body/eval_jaxpr/qhd,khd->hqk/dot_general | solution.py:101
  164.2 22.0 %fusion = f32[12,512]{1,0:T(8,128)S(1)} fusion(f32[12,512]{1,0:T(8,128)S(1)} %get-tuple-element.100, f32[12,512,2048]{2,1,0:T(8,128)} %get-tuple-element.101, pred[512,2048]{1,0:T(8,128)(4,1)S(1)} %fusion.15), kind=kLoop, calls=%fused_computation.6 | loop fusion | flops 50325504 | bytes 51429376 | tf_op jit(solution)/shard_map/while/body/eval_jaxpr/reduce_sum | solution.py:112
  186.2 21.8 %fusion.37 = bf16[12,64,512]{2,1,0:T(8,128)(2,1)} fusion(bf16[2048,12,64]{0,2,1:T(8,128)(2,1)} %bitcast.114, f32[12,512]{1,0:T(8,128)S(1)} %fusion, f32[12,512]{1,0:T(8,128)S(1)} %get-tuple-element.100, f32[12,512,2048]{2,1,0:T(8,128)} %get-tuple-element.101, pred[512,2048]{1,0:T(8,128)(4,1)S(1)} %fusion.15), kind=kOutput, calls=%fused_computation.68 | convolution fusion | flops 1673920512 | bytes 55361536 | tf_op jit(solution)/shard_map/while/body/eval_jaxpr/hqk,khd->qhd/dot_general | solution.py:114
  210.8 37.8 %all-gather.12.cloned.1.call-done = bf16[768,3072]{1,0:T(8,128)(2,1)} async-done(((bf16[24,3072]{1,0:T(8,128)(2,1)}), bf16[768,3072]{1,0:T(8,128)(2,1)}) %all-gather.12.cloned.1.call-update) | async-done | bytes 4718608 | tf_op jit(solution)/shard_map/all_gather | solution.py:58
  248.7 7.1 fusion.60
  255.8 58.1 %all-gather.14.cloned.1.call-done = bf16[3072,768]{1,0:T(8,128)(2,1)} async-done(((bf16[96,768]{1,0:T(8,128)(2,1)}), bf16[3072,768]{1,0:T(8,128)(2,1)}) %all-gather.14.cloned.1.call-update) | async-done | bytes 4718608 | tf_op jit(solution)/shard_map/all_gather | solution.py:59
  313.9 10.4 %convert_reduce_fusion = (f32[3072]{0:T(1024)}, bf16[512,3072]{1,0:T(8,128)(2,1)S(1)}) fusion(f32[512,3072]{1,0:T(8,128)} %fusion.60, f32[3072]{0:T(1024)S(1)} %convert_element_type.121, bf16[3072,768]{1,0:T(8,128)(2,1)} %all-gather.14.cloned.1.call-done, bf16[1,512,768]{2,1,0:T(8,128)(2,1)S(1)} %copy-done.10, pred[512]{0:T(512)(128)(4,1)S(1)} %broadcast_compare_fusion), kind=kOutput, calls=%fused_computation.22 | convolution fusion | flops 2453271552 | bytes 14967296 | tf_op jit(solution)/shard_map/rd,fd->rf/dot_general | solution.py:161
  324.3 3.5 multiply_reduce_fusion.1
  334.6 22.3 %fusion.17 = bf16[12,64,2048]{2,1,0:T(8,128)(2,1)} fusion(bf16[512,12,64]{0,2,1:T(8,128)(2,1)S(1)} %bitcast.124, f32[12,512]{1,0:T(8,128)S(1)} %log_add_fusion, f32[12,512,2048]{2,1,0:T(8,128)} %get-tuple-element.101, pred[512,2048]{1,0:T(8,128)(4,1)S(1)} %fusion.15), kind=kOutput, calls=%fused_computation.31 | convolution fusion | flops 1662517248 | bytes 55336960 | tf_op jit(solution)/shard_map/while/body/eval_jaxpr/hqk,qhd->khd/dot_general | solution.py:219
  356.9 37.2 %multiply_reduce_fusion = (f32[12,512]{1,0:T(8,128)S(1)}, f32[12,512,2048]{2,1,0:T(8,128)}) fusion(f32[12,512]{1,0:T(8,128)S(1)} %log_add_fusion, f32[12,512,2048]{2,1,0:T(8,128)} %get-tuple-element.101, pred[512,2048]{1,0:T(8,128)(4,1)S(1)} %fusion.15, bf16[512,12,64]{0,2,1:T(8,128)(2,1)S(1)} %bitcast.125, bf16[2048,12,64]{0,2,1:T(8,128)(2,1)} %bitcast.115), kind=kOutput, calls=%fused_computation.1 | convolution fusion | flops 1673521152 | bytes 105693184 | tf_op jit(solution)/shard_map/while/body/eval_jaxpr/qhd,khd->hqk/dot_general | solution.py:190
  394.1 40.4 %multiply_convert_fusion = bf16[12,512,2048]{2,1,0:T(8,128)(2,1)} fusion(f32[12,512,2048]{2,1,0:T(8,128)} %get-tuple-element.106, f32[12,512]{1,0:T(8,128)S(1)} %get-tuple-element.105, f32[12,512]{1,0:T(8,128)S(1)} %log_add_fusion, f32[12,512,2048]{2,1,0:T(8,128)} %get-tuple-element.101, pred[512,2048]{1,0:T(8,128)(4,1)S(1)} %fusion.15), kind=kLoop, calls=%fused_computation | loop fusion | flops 75497472 | bytes 126926848 | tf_op jit(solution)/shard_map/while/body/eval_jaxpr/convert_element_type | solution.py:194
  434.6 12.8 %multiply_convert_fusion.1 = bf16[12,64,2048]{2,1,0:T(8,128)(2,1)S(1)} fusion(bf16[512,12,64]{0,2,1:T(8,128)(2,1)S(1)} %bitcast.118, bf16[12,512,2048]{2,1,0:T(8,128)(2,1)} %multiply_convert_fusion), kind=kOutput, calls=%fused_computation.23 | convolution fusion | flops 1613758464 | bytes 29097984 | tf_op jit(solution)/shard_map/while/body/eval_jaxpr/hqk,qhd->khd/dot_general | solution.py:216
  447.3 3.7 pad_maximum_fusion
  455.6 10.8 %fusion.50 = f32[3072,768]{1,0:T(8,128)} fusion(bf16[1,512,768]{2,1,0:T(8,128)(2,1)S(1)} %copy-done.11, pred[512]{0:T(512)(128)(4,1)S(1)} %broadcast_compare_fusion, f32[512,3072]{1,0:T(8,128)} %fusion.60, f32[3072]{0:T(1024)S(1)} %convert_element_type.121), kind=kOutput, calls=%fused_computation.97 | convolution fusion | flops 2432827392 | bytes 16527872 | tf_op jit(solution)/shard_map/rf,rd->fd/dot_general | solution.py:157
  466.5 7.5 fusion.59
  475.9 13.4 %multiply_convert_fusion.3 = bf16[12,64,512]{2,1,0:T(8,128)(2,1)} fusion(bf16[2048,12,64]{0,2,1:T(8,128)(2,1)S(1)} %bitcast.113, bf16[12,512,2048]{2,1,0:T(8,128)(2,1)} %multiply_convert_fusion), kind=kOutput, calls=%fused_computation.62 | convolution fusion | flops 1611399168 | bytes 29097984 | tf_op jit(solution)/shard_map/while/body/eval_jaxpr/hqk,khd->qhd/dot_general | solution.py:196
  489.3 18.7 %reduce-scatter.6.cloned.1.call-done = bf16[1,512,1536]{1,2,0:T(8,128)(2,1)} async-done(((bf16[1,2048,1536]{1,2,0:T(8,128)(2,1)}), bf16[1,512,1536]{1,2,0:T(8,128)(2,1)}) %reduce-scatter.6.cloned.1.call-update) | async-done | bytes 1572880 | tf_op jit(solution)/shard_map/reduce_scatter | solution.py:230
  508.0 7.1 fusion.40
  516.5 9.1 fusion.38
  534.0 40.6 %all-reduce.16 = (f32[1536]{0:T(1024)S(1)}, f32[768]{0:T(1024)S(1)}, f32[3072]{0:T(1024)S(1)}, f32[768]{0:T(1024)S(1)}, f32[768]{0:T(1024)S(1)}, /*index=5*/f32[...) all-reduce(f32[1536]{0:T(1024)S(1)} %pad_maximum_fusion.5, ...), channel_id=7, replica_groups=mesh['dp'=8,'ctx'=4] {'dp','ctx'}, use_global_device_ids=true, to_apply=%region_18.19.clone | all-reduce | flops 9216 | bytes 73728
  580.6 31.7 %reduce-scatter.10.cloned.1.call-done = f32[24,768]{1,0:T(8,128)} async-done(((f32[768,768]{1,0:T(8,128)}), f32[24,768]{1,0:T(8,128)}) %reduce-scatter.10.cloned.1.call-update) | async-done | bytes 73744 | tf_op jit(solution)/shard_map/reduce_scatter | solution.py:267
  612.2 140.8 %reduce-scatter.14.cloned.1.call-done = f32[96,768]{1,0:T(8,128)} async-done(((f32[3072,768]{1,0:T(8,128)}), f32[96,768]{1,0:T(8,128)}) %reduce-scatter.14.cloned.1.call-update) | async-done | bytes 294928 | tf_op jit(solution)/shard_map/reduce_scatter | solution.py:269
  753.1 142.1 %reduce-scatter.12.cloned.1.call-done = f32[24,3072]{1,0:T(8,128)} async-done(((f32[768,3072]{1,0:T(8,128)}), f32[24,3072]{1,0:T(8,128)}) %reduce-scatter.12.cloned.1.call-update) | async-done | bytes 294928 | tf_op jit(solution)/shard_map/reduce_scatter | solution.py:268
  895.2 124.5 %reduce-scatter.8.cloned.1.call-done = f32[24,2304]{1,0:T(8,128)} async-done(((f32[768,2304]{1,0:T(8,128)}), f32[24,2304]{1,0:T(8,128)}) %reduce-scatter.8.cloned.1.call-update) | async-done | bytes 221200 | tf_op jit(solution)/shard_map/reduce_scatter | solution.py:266
  (179 shorter events, 48.6 us)
Async XLA Ops:
  7.2 66.6 %all-gather.6.cloned.1.call-start = ((), (), s32[]{:S(2)}) async-start(), calls=%async_computation.5 | async-start | bytes 3649536 | tf_op jit(solution)/shard_map/all_gather | solution.py:56
  7.9 118.4 %all-gather.8.cloned.1.call-start = ((), (), s32[]{:S(2)}) async-start(), calls=%async_computation.6 | async-start | bytes 7864320 | tf_op jit(solution)/shard_map/all_gather | solution.py:91
  8.7 50.7 %collective-permute-start = (bf16[1,1,768]{2,1,0:T(2,128)(2,1)S(1)}, bf16[1,1,768]{2,1,0:T(2,128)(2,1)S(1)}, u32[]{:S(2)}, u32[]{:S(2)}) collective-permute-start(bf16[1,1,768]{2,1,0:T(2,128)(2,1)S(1)} %slice.42), channel_id=1, source_target_pairs={{0,1},{1,2},{2,3},{4,5},{5,6},{6,7},{8,9},{9,10},{10,11},{12,13},{... | collective-permute-start | bytes 4616 | tf_op jit(solution)/shard_map/ppermute | solution.py:12
  59.3 18.6 %copy-start.18 = (f32[768]{0:T(1024)}, f32[768]{0:T(1024)S(1)}, u32[]{:S(2)}) copy-start(f32[768]{0:T(1024)S(1)} %convert_element_type.108) | copy-start | bytes 9220
  59.4 18.6 %copy-start.33 = (f32[768]{0:T(1024)}, f32[768]{0:T(1024)S(1)}, u32[]{:S(2)}) copy-start(f32[768]{0:T(1024)S(1)} %convert_element_type.109) | copy-start | bytes 9220
  61.4 146.6 %copy-start.3 = (bf16[1,512,768]{2,1,0:T(8,128)(2,1)}, bf16[1,512,768]{2,1,0:T(8,128)(2,1)S(1)}, u32[]{:S(2)}) copy-start(bf16[1,512,768]{2,1,0:T(8,128)(2,1)S(1)} %get-tuple-element.92) | copy-start | bytes 2359300
  61.4 16.6 %copy-start.20 = (f32[512]{0:T(512)}, f32[512]{0:T(512)S(1)}, u32[]{:S(2)}) copy-start(f32[512]{0:T(512)S(1)} %broadcast_multiply_fusion.1) | copy-start | bytes 6148
  61.8 16.2 %copy-start.26 = (f32[512]{0:T(512)}, f32[512]{0:T(512)S(1)}, u32[]{:S(2)}) copy-start(f32[512]{0:T(512)S(1)} %fusion.31) | copy-start | bytes 6148
  61.8 16.2 %copy-start.22 = (f32[512]{0:T(512)}, f32[512]{0:T(512)S(1)}, u32[]{:S(2)}) copy-start(f32[512]{0:T(512)S(1)} %fusion.42) | copy-start | bytes 6148
  80.8 127.3 %all-gather.10.cloned.1.call-start = ((), (), s32[]{:S(2)}) async-start(), calls=%async_computation.7 | async-start | bytes 1216512 | tf_op jit(solution)/shard_map/all_gather | solution.py:57
  81.5 167.2 %all-gather.12.cloned.1.call-start = ((), (), s32[]{:S(2)}) async-start(), calls=%async_computation.8 | async-start | bytes 4866048 | tf_op jit(solution)/shard_map/all_gather | solution.py:58
  82.1 231.8 %all-gather.14.cloned.1.call-start = ((), (), s32[]{:S(2)}) async-start(), calls=%async_computation.9 | async-start | bytes 4866048 | tf_op jit(solution)/shard_map/all_gather | solution.py:59
  82.7 425.3 %reduce-scatter.6.cloned.1.call-start = ((), (), s32[]{:S(2)}) async-start(), calls=%async_computation.10 | async-start | bytes 7864320 | tf_op jit(solution)/shard_map/reduce_scatter | solution.py:230
  84.5 57.4 %copy-start.5 = (bf16[1,512,768]{1,2,0:T(8,128)(2,1)}, bf16[1,512,768]{1,2,0:T(8,128)(2,1)S(1)}, u32[]{:S(2)}) copy-start(bf16[1,512,768]{1,2,0:T(8,128)(2,1)S(1)} %copy.47) | copy-start | bytes 2359300
  210.5 256.0 %copy-start.7 = (f32[512,768]{1,0:T(8,128)}, f32[512,768]{1,0:T(8,128)S(1)}, u32[]{:S(2)}) copy-start(f32[512,768]{1,0:T(8,128)S(1)} %get-tuple-element.103) | copy-start | bytes 4718596
  210.8 103.0 %copy-start.10 = (bf16[1,512,768]{2,1,0:T(8,128)(2,1)S(1)}, bf16[1,512,768]{2,1,0:T(8,128)(2,1)}, u32[]{:S(2)}) copy-start(bf16[1,512,768]{2,1,0:T(8,128)(2,1)} %param.19) | copy-start | bytes 2359300
  313.9 10.4 %copy-start.38 = (bf16[768,3072]{1,0:T(8,128)(2,1)S(1)}, bf16[768,3072]{1,0:T(8,128)(2,1)}, u32[]{:S(2)}) copy-start(bf16[768,3072]{1,0:T(8,128)(2,1)} %all-gather.12.cloned.1.call-done) | copy-start | bytes 14155780
  394.1 40.4 %copy-start.6 = (bf16[1,512,768]{1,2,0:T(8,128)(2,1)S(1)}, bf16[1,512,768]{1,2,0:T(8,128)(2,1)}, u32[]{:S(2)}) copy-start(bf16[1,512,768]{1,2,0:T(8,128)(2,1)} %copy-done.5) | copy-start | bytes 2359300
  434.5 12.8 %copy-start.14 = (bf16[12,64,2048]{2,1,0:T(8,128)(2,1)S(1)}, bf16[12,64,2048]{2,1,0:T(8,128)(2,1)}, u32[]{:S(2)}) copy-start(bf16[12,64,2048]{2,1,0:T(8,128)(2,1)} %fusion.17) | copy-start | bytes 9437188
  451.1 161.1 %reduce-scatter.10.cloned.1.call-start = ((), (), s32[]{:S(2)}) async-start(), calls=%async_computation.12 | async-start | bytes 2433024 | tf_op jit(solution)/shard_map/reduce_scatter | solution.py:267
  455.5 297.6 %reduce-scatter.14.cloned.1.call-start = ((), (), s32[]{:S(2)}) async-start(), calls=%async_computation.14 | async-start | bytes 9732096 | tf_op jit(solution)/shard_map/reduce_scatter | solution.py:269
  466.4 428.7 %reduce-scatter.12.cloned.1.call-start = ((), (), s32[]{:S(2)}) async-start(), calls=%async_computation.13 | async-start | bytes 9732096 | tf_op jit(solution)/shard_map/reduce_scatter | solution.py:268
  474.0 34.0 %copy-start.19 = (f32[768]{0:T(1024)S(1)}, f32[768]{0:T(1024)}, u32[]{:S(2)}) copy-start(f32[768]{0:T(1024)} %copy-done.18) | copy-start | bytes 9220
  474.0 33.9 %copy-start.21 = (f32[512]{0:T(512)S(1)}, f32[512]{0:T(512)}, u32[]{:S(2)}) copy-start(f32[512]{0:T(512)} %copy-done.20) | copy-start | bytes 6148
  474.1 33.9 %copy-start.23 = (f32[512]{0:T(512)S(1)}, f32[512]{0:T(512)}, u32[]{:S(2)}) copy-start(f32[512]{0:T(512)} %copy-done.22) | copy-start | bytes 6148
  474.1 33.9 %copy-start.34 = (f32[768]{0:T(1024)S(1)}, f32[768]{0:T(1024)}, u32[]{:S(2)}) copy-start(f32[768]{0:T(1024)} %copy-done.33) | copy-start | bytes 9220
  474.1 545.6 %reduce-scatter.8.cloned.1.call-start = ((), (), s32[]{:S(2)}) async-start(), calls=%async_computation.11 | async-start | bytes 7299072 | tf_op jit(solution)/shard_map/reduce_scatter | solution.py:266
  516.5 9.2 copy-start.4
  516.5 9.2 copy-start.9
  516.5 9.2 copy-start.17
  516.5 9.2 copy-start.39
  530.8 48.4 %collective-permute-start.1 = (f32[1,1,768]{2,1,0:T(1,128)S(1)}, f32[1,1,768]{2,1,0:T(1,128)S(1)}, u32[]{:S(2)}, u32[]{:S(2)}) collective-permute-start(f32[1,1,768]{2,1,0:T(1,128)S(1)} %slice.61), channel_id=1, source_target_pairs={{1,0},{2,1},{3,2},{5,4},{6,5},{7,6},{9,8},{10,9},{11,10},{13,12},{... | collective-permute-start | bytes 9224 | tf_op jit(solution)/shard_map/ppermute | solution.py:12
  (23 other events, 57.4 us)
Sparse Core Ops, SparseCore 0:
  10.9 62.8 all-gather.5
  80.9 45.3 all-gather.7
  129.2 54.0 all-gather.9
  186.1 62.5 all-gather.11
  251.4 62.3 all-gather.13
  451.2 56.7 reduce-scatter.5
  514.7 97.5 reduce-scatter.9
  618.7 134.3 reduce-scatter.13
  760.6 134.5 reduce-scatter.11
  901.3 118.3 reduce-scatter.7
where the time goes:
time: 1040 us; the launch traced here: 1030 us
  waiting for transfers between devices  610 us (59%)
  matrix products  199 us (19%)
  blocking collectives  79.2 us (8%)
  other arithmetic  76 us (7%)
  local copies, waits for them, and re-layouts  38.9 us (4%)
  between operations  16 us (2%)
    reduce_scatter x1, waiting for transfers between devices, shards(): lax.psum_scatter(grads[2], ('dp', 'ctx'), scatter_dimension=0, tiled=True)  142 us
    reduce_scatter x1, waiting for transfers between devices, shards(): lax.psum_scatter(grads[3], ('dp', 'ctx'), scatter_dimension=0, tiled=True)  141 us
    reduce_scatter x1, waiting for transfers between devices, shards(): lax.psum_scatter(grads[0], ('dp', 'ctx'), scatter_dimension=0, tiled=True)  124 us
    unnamed x2, blocking collectives  79.2 us
    all_gather x1, waiting for transfers between devices, shards(): lax.all_gather(proj_weight, ('dp', 'ctx'), axis=0, tiled=True)  58.1 us
    all_gather x1, waiting for transfers between devices, shards(): keyval_all = lax.all_gather(keyval, 'ctx', axis=1, tiled=True)  41.8 us
    convert_element_type x1, other arithmetic, query_side(): grad_scores = (probs * (grad_probs - delta)).astype(jnp.bfloat16)  40.4 us
    all_gather x1, waiting for transfers between devices, shards(): lax.all_gather(fc_weight, ('dp', 'ctx'), axis=0, tiled=True)  37.8 us
  transfers between devices with their start and end apart: 12, of which 9 were waited for; matrix products, arithmetic and copies ran while one was open for 16% of the time, Pallas kernels for 0%

commit v1 on v0

v1 whole, which is shorter than its diff:
```python
import jax
import jax.numpy as jnp
from jax import lax
from jax.experimental import pallas as pl
from jax.experimental.pallas import tpu as pltpu
from jax.sharding import PartitionSpec as P

ALL = ("dp", "ctx")
LOW = jnp.bfloat16
FULL = jnp.float32
HEAD = 64
LANES = 128
SCALE = 0.125
VMEM = 48 << 20


def flat_bits():
    return (lax.axis_size("dp") * lax.axis_size("ctx")).bit_length() - 1


def flat_index():
    return lax.axis_index("dp") * lax.axis_size("ctx") + lax.axis_index("ctx")


def bit_of(bit):
    return (flat_index() >> bit) & 1


def swap(value, bit):
    count = 1 << flat_bits()
    return lax.ppermute(value, ALL, [(i, i ^ (1 << bit)) for i in range(count)])


def pair(mine, other, place, axis):
    shape = mine.shape[:axis] + (2,) + mine.shape[axis:]
    mine, other = jnp.expand_dims(mine, axis), jnp.expand_dims(other, axis)
    whole = jnp.zeros(shape, mine.dtype)
    whole = lax.dynamic_update_slice_in_dim(whole, mine, place, axis)
    return lax.dynamic_update_slice_in_dim(whole, other, 1 - place, axis)


def orders():
    top = flat_bits()
    rest = list(range(4, top))
    return ([1, 2, 3] + rest, [2, 3, 1] + rest, [3, 1, 2] + rest)


def grow(block, done, bit):
    other = swap(block, bit)
    rows, cols = block.shape[1:]
    high = 1 << len([b for b in done if b > bit])
    low = 1 << len([b for b in done if b < bit])
    whole = pair(
        block.reshape(high, low, rows, cols), other.reshape(high, low, rows, cols), bit_of(bit), 1
    )
    return whole.reshape(high * 2 * low, rows, cols)


def gather_links(block, cuts):
    plans = [list(reversed(order)) for order in orders()]
    block = block[None]
    done = []
    common = flat_bits() - 4
    for bit in plans[0][:common]:
        block = grow(block, done, bit)
        done = done + [bit]
    parts, at = [], 0
    for cut in cuts:
        parts.append(block[:, :, at : at + cut])
        at += cut
    known = [list(done) for _ in cuts]
    for step in range(common, flat_bits() - 1):
        for which in range(len(cuts)):
            bit = plans[which][step]
            parts[which] = grow(parts[which], known[which], bit)
            known[which].append(bit)
    return parts


class Sum:
    def __init__(self, addends, left):
        self.addends = addends
        self.left = left

    def half(self, bit, place):
        low = 1 << len([b for b in self.left if b < bit])
        high = 1 << len([b for b in self.left if b > bit])
        out = []
        for value in self.addends:
            rows, cols = value.shape[1:]
            view = value.reshape(high, 2, low, rows, cols)
            out.append(
                lax.dynamic_index_in_dim(view, place, 1, keepdims=False).reshape(
                    high * low, rows, cols
                )
            )
        return out

    def total(self):
        result = self.addends[0].astype(FULL)
        for value in self.addends[1:]:
            result = result + value.astype(FULL)
        return result

    def step(self, bit):
        place = bit_of(bit)
        left = [b for b in self.left if b != bit]
        send = Sum(self.half(bit, 1 - place), left).total().astype(LOW)
        return Sum(self.half(bit, place) + [swap(send, bit)], left)


def scatter_links(parts, plans):
    links = list(range(1, flat_bits()))
    sums = [Sum(addends, links) for addends in parts]
    for step in range(len(links)):
        sums = [value.step(plan[step]) for value, plan in zip(sums, plans)]
    return [value.total()[0] for value in sums]


def finish(total, rows, cols):
    core = bit_of(0)
    mine = lax.dynamic_slice_in_dim(total, core * rows, rows, 0)
    other = swap(lax.dynamic_slice_in_dim(total, (1 - core) * rows, rows, 0), 0)
    first = jnp.where(core == 0, mine, other)
    second = jnp.where(core == 0, other, mine)
    return first, second


def weight_grad(left, right, plan):
    core = bit_of(0)
    height, cols = left.shape[1], right.shape[1]
    half = cols // 2
    rows = height >> flat_bits()
    kept = dot_tn(left, lax.dynamic_slice_in_dim(right, core * half, half, 1))
    send = dot_tn(left, lax.dynamic_slice_in_dim(right, (1 - core) * half, half, 1)).astype(LOW)
    shape = (height // (2 * rows), 2 * rows, half)
    (total,) = scatter_links([[kept.reshape(shape), swap(send, 0).reshape(shape)]], [plan])
    return jnp.concatenate(finish(total, rows, cols), 1)


def dot(a, b):
    return lax.dot_general(a, b, (((1,), (0,)), ((), ())), preferred_element_type=FULL)


def dot_nt(a, b):
    return lax.dot_general(a, b, (((1,), (1,)), ((), ())), preferred_element_type=FULL)


def dot_tn(a, b):
    return lax.dot_general(a, b, (((0,), (0,)), ((), ())), preferred_element_type=FULL)


def head_lanes(value, head):
    lane = lax.broadcasted_iota(jnp.int32, (1, LANES), 1)
    return jnp.where(lane // HEAD == head, value, jnp.zeros_like(value))


def causal(size):
    shape = (size, size)
    return lax.broadcasted_iota(jnp.int32, shape, 0) <= lax.broadcasted_iota(jnp.int32, shape, 1)


def attend_kernel(far_ref, q_ref, k_ref, v_ref, out_ref, lse_ref, top_ref, acc_ref):
    size = q_ref.shape[0]
    mine = pl.program_id(1)
    query = q_ref[...] * jnp.asarray(SCALE, LOW)

    def step(block, first):
        at = pl.ds(pl.multiple_of(block * size, size), size)
        key = k_ref[at, :]
        value = jnp.transpose(v_ref[at, :])
        for head in range(2):
            ones = jnp.ones((16, size), LOW)
            wide = jnp.concatenate([value[head * HEAD : (head + 1) * HEAD], ones], 0)
            scores = dot_nt(key, head_lanes(query, head))
            row = slice(head, head + 1)
            if first:
                scores = jnp.where(causal(size), scores, -1e9)
                top = jnp.max(scores, 0, keepdims=True)
                acc_ref[head] = dot(wide, jnp.exp(scores - top).astype(LOW))
            else:
                old = top_ref[row, :]
                top = jnp.maximum(old, jnp.max(scores, 0, keepdims=True))
                acc_ref[head] = acc_ref[head] * jnp.exp(old - top) + dot(
                    wide, jnp.exp(scores - top).astype(LOW)
                )
            top_ref[row, :] = top

    step(mine, True)

    @pl.loop(0, mine + far_ref[0])
    def _(i):
        step(jnp.where(i < mine, 0, 2 + i - mine), False)

    outs = []
    for head in range(2):
        total = acc_ref[head, HEAD : HEAD + 1, :]
        outs.append(acc_ref[head, :HEAD, :] / total)
        lse_ref[0, head : head + 1, :] = top_ref[head : head + 1, :] + jnp.log(total)
    out_ref[...] = jnp.transpose(jnp.concatenate(outs, 0)).astype(LOW)


def attend(far, query, key, value, quarter):
    near, width = query.shape
    pairs = width // LANES
    total = key.shape[0]
    rows = pl.BlockSpec((quarter, LANES), lambda p, i, s: (i, p))
    every = pl.BlockSpec((total, LANES), lambda p, i, s: (0, p))
    return pl.pallas_call(
        attend_kernel,
        out_shape=(
            jax.ShapeDtypeStruct((near, width), LOW),
            jax.ShapeDtypeStruct((pairs, 8, near), FULL),
        ),
        grid_spec=pltpu.PrefetchScalarGridSpec(
            num_scalar_prefetch=1,
            grid=(pairs, near // quarter),
            in_specs=[rows, every, every],
            out_specs=(rows, pl.BlockSpec((1, 8, quarter), lambda p, i, s: (p, 0, i))),
            scratch_shapes=[
                pltpu.VMEM((8, quarter), FULL),
                pltpu.VMEM((2, HEAD + 16, quarter), FULL),
            ],
        ),
        compiler_params=pltpu.CompilerParams(vmem_limit_bytes=VMEM),
        cost_estimate=pl.CostEstimate(
            flops=6 * 4 * quarter * quarter * LANES * 2 * pairs,
            bytes_accessed=8 << 20,
            transcendentals=6 * quarter * quarter * 2 * pairs,
        ),
        name="attend",
    )(far, query, key, value)


def attend_back_kernel(
    far_ref, q_ref, k_ref, v_ref, grad_ref, out_ref, lse_ref, dq_ref, dk_ref, dv_ref, acc_ref
):
    near = q_ref.shape[0]
    size = near // 2
    spans = (slice(0, size), slice(size, near))
    query = q_ref[...] * jnp.asarray(SCALE, LOW)
    grad = grad_ref[...]
    product = jnp.transpose(grad.astype(FULL) * out_ref[...].astype(FULL))
    delta = [
        jnp.sum(product[head * HEAD : (head + 1) * HEAD], 0, keepdims=True) for head in range(2)
    ]

    def block(at, work):
        key, value = k_ref[at, :], v_ref[at, :]
        turned = jnp.transpose(key)
        dk = dv = None
        for which, masked, first in work:
            span = spans[which]
            for head in range(2):
                part = slice(head * HEAD, (head + 1) * HEAD)
                q_head = head_lanes(query[span], head)
                g_head = head_lanes(grad[span], head)
                probs = jnp.exp(dot_nt(key, q_head) - lse_ref[0, head : head + 1, span])
                if masked:
                    probs = jnp.where(causal(size), probs, 0.0)
                moved = probs * (dot_nt(value, g_head) - delta[head][:, span])
                moved, probs = moved.astype(LOW), probs.astype(LOW)
                new_k, new_v = dot(moved, q_head), dot(probs, g_head)
                dk = new_k if dk is None else dk + new_k
                dv = new_v if dv is None else dv + new_v
                new_q = dot(turned[part], moved)
                if first:
                    acc_ref[which, part, :] = new_q
                else:
                    acc_ref[which, part, :] += new_q
        dk_ref[at, :] = dk.astype(LOW)
        dv_ref[at, :] = dv.astype(LOW)

    block(spans[0], [(0, True, True), (1, False, True)])
    block(spans[1], [(1, True, False)])

    @pl.loop(0, far_ref[0])
    def _(i):
        at = pl.ds(pl.multiple_of(near + i * size, size), size)
        block(at, [(0, False, False), (1, False, False)])

    @pl.loop(far_ref[0], 2)
    def _(i):
        at = pl.ds(pl.multiple_of(near + i * size, size), size)
        dk_ref[at, :] = jnp.zeros((size, LANES), LOW)
        dv_ref[at, :] = jnp.zeros((size, LANES), LOW)

    for which in range(2):
        dq_ref[spans[which], :] = (jnp.transpose(acc_ref[which]) * SCALE).astype(LOW)


def attend_back(far, query, key, value, grad, out, lse):
    near, width = query.shape
    pairs = width // LANES
    total = key.shape[0]
    rows = pl.BlockSpec((near, LANES), lambda p, s: (0, p))
    every = pl.BlockSpec((total, LANES), lambda p, s: (0, p))
    return pl.pallas_call(
        attend_back_kernel,
        out_shape=(
            jax.ShapeDtypeStruct((near, width), LOW),
            jax.ShapeDtypeStruct((total, width), LOW),
            jax.ShapeDtypeStruct((total, width), LOW),
        ),
        grid_spec=pltpu.PrefetchScalarGridSpec(
            num_scalar_prefetch=1,
            grid=(pairs,),
            in_specs=[rows, every, every, rows, rows, pl.BlockSpec((1, 8, near), lambda p, s: (p, 0, 0))],
            out_specs=(rows, every, every),
            scratch_shapes=[pltpu.VMEM((2, LANES, near // 2), FULL)],
        ),
        compiler_params=pltpu.CompilerParams(vmem_limit_bytes=VMEM),
        cost_estimate=pl.CostEstimate(
            flops=6 * 10 * near * near // 4 * LANES * 2 * pairs,
            bytes_accessed=16 << 20,
            transcendentals=6 * near * near // 4 * 2 * pairs,
        ),
        name="attend_back",
    )(far, query, key, value, grad, out, lse)


def normalize(values):
    center = values - jnp.mean(values, -1, keepdims=True)
    spread = jnp.mean(center * center, -1, keepdims=True)
    root = lax.rsqrt(spread + 1e-05)
    return center * root, root


def normalize_back(grad, gain, hat, root):
    scaled = grad * gain
    return root * (
        scaled
        - jnp.mean(scaled, -1, keepdims=True)
        - hat * jnp.mean(scaled * hat, -1, keepdims=True)
    )


def gelu_tanh(values):
    return jax.nn.gelu(values, approximate=True)


def shards(
    tokens,
    lengths,
    thought_pos,
    cotangent,
    qkv_weight,
    out_weight,
    fc_weight,
    proj_weight,
    qv_bias,
    out_bias,
    fc_bias,
    proj_bias,
    first_gain,
    first_shift,
    second_gain,
    second_shift,
):
    _, quarter, width = tokens.shape
    half = width // 2
    near = 2 * quarter
    slice_rows = qkv_weight.shape[0]
    count = 1 << flat_bits()
    plans = orders()
    core, second = bit_of(0), bit_of(1)
    far = (2 * second).astype(jnp.int32).reshape(1)

    late = lax.all_gather(
        jnp.concatenate([fc_weight, out_weight], 1), ALL, axis=0, tiled=True
    )
    hidden_width = fc_weight.shape[1]
    fc_full, out_full = late[:, :hidden_width], late[:, hidden_width:]

    mine = tokens[0]
    flips = [(i, i ^ 2) for i in range(count) if not i & 2]
    before = lax.ppermute(mine, ALL, flips)
    partner = swap(mine, 0)
    near_tokens = pair(mine, partner, core, 0).reshape(near, width)
    before_partner = swap(before, 0)
    far_tokens = pair(before, before_partner, core, 0).reshape(near, width)

    third = slice_rows * 4
    small = jnp.zeros((slice_rows, LANES), LOW)
    rows_of = (
        jnp.concatenate([qv_bias, out_bias, first_gain]),
        fc_bias,
        jnp.concatenate([proj_bias, first_shift, second_gain, second_shift]),
    )
    small = small.at[:3, :third].set(jnp.stack(rows_of))
    split = qkv_weight.reshape(slice_rows, 3, 2, half)
    keep = lax.dynamic_index_in_dim(split, core, 2, keepdims=False).reshape(slice_rows, 3 * half)
    send = lax.dynamic_index_in_dim(split, 1 - core, 2, keepdims=False).reshape(
        slice_rows, 3 * half
    )
    keep, send = jnp.concatenate([keep, small], 1), jnp.concatenate([send, small], 1)
    chip = pair(keep, swap(send, 0), core, 0).reshape(2 * slice_rows, 3 * half + LANES)
    q_weight, k_weight, v_small = gather_links(chip, (half, half, half + LANES))
    q_weight = q_weight.reshape(width, half)
    k_weight = k_weight.reshape(width, half)
    v_weight = v_small[:, :, :half].reshape(width, half)
    small = v_small.reshape(count, slice_rows, half + LANES)[:, :3, half : half + third]
    small = small.astype(FULL)
    at = slice_rows

    def vector(row, first, size):
        return small[:, row, first : first + size].reshape(1, count * size)

    qv_full = vector(0, 0, 2 * at)
    out_bias_full, gain_one = vector(0, 2 * at, at), vector(0, 3 * at, at)
    fc_bias_full = vector(1, 0, 4 * at)
    proj_bias_full, shift_one = vector(2, 0, at), vector(2, at, at)
    gain_two, shift_two = vector(2, 2 * at, at), vector(2, 3 * at, at)

    high = proj_weight.shape[0]
    split = proj_weight.reshape(high, 2, half)
    keep = lax.dynamic_index_in_dim(split, core, 1, keepdims=False)
    send = lax.dynamic_index_in_dim(split, 1 - core, 1, keepdims=False)
    chip = pair(keep, swap(send, 0), core, 0).reshape(2 * high, half)
    proj_parts = gather_links(chip, (half // 3,) * 3)
    proj_half = jnp.concatenate(proj_parts, 2).reshape(count * high, half)
    proj_full = pair(proj_half, swap(proj_half, 0), core, 1).reshape(count * high, width)

    slots = jnp.arange(near, dtype=jnp.int32)
    thoughts = thought_pos[0]

    def is_thought(at_slots):
        return jnp.any(thoughts[None, :] == at_slots[:, None], 1, keepdims=True)

    thought_near = is_thought(second * near + slots)
    thought_far = is_thought(slots)
    shifted_near = jnp.concatenate([far_tokens[-1:], near_tokens[:-1]], 0)
    shifted_far = jnp.concatenate([far_tokens[:1], far_tokens[:-1]], 0)
    inputs_near = jnp.where(thought_near, shifted_near, near_tokens)
    inputs_far = jnp.where(thought_far, shifted_far, far_tokens)
    inputs_all = jnp.concatenate([inputs_near, inputs_far], 0)
    hat_all, root_all = normalize(inputs_all.astype(FULL))
    normed = (hat_all * gain_one + shift_one).astype(LOW)
    own = core * quarter
    inputs = lax.dynamic_slice_in_dim(inputs_near, own, quarter, 0).astype(FULL)

    own_half = core * half
    q_bias = lax.dynamic_slice_in_dim(qv_full[:, :width], own_half, half, 1)
    v_bias = lax.dynamic_slice_in_dim(qv_full[:, width:], own_half, half, 1)
    query = (dot(normed[:near], q_weight) + q_bias).astype(LOW)
    key = dot(normed, k_weight).astype(LOW)
    value = (dot(normed, v_weight) + v_bias).astype(LOW)

    attended_heads, logsum = attend(far, query, key, value, quarter)

    def rows_to_core(array):
        return (
            lax.dynamic_slice_in_dim(array, own, quarter, 0),
            lax.dynamic_slice_in_dim(array, quarter - own, quarter, 0),
        )

    keep, send = rows_to_core(attended_heads)
    attended = pair(keep, swap(send, 0), core, 1).reshape(quarter, width)

    middle = inputs + dot(attended, out_full) + out_bias_full
    hat_two, root_two = normalize(middle)
    normed_two = (hat_two * gain_two + shift_two).astype(LOW)
    hidden = dot(normed_two, fc_full) + fc_bias_full
    active = gelu_tanh(hidden).astype(LOW)
    my_slots = (2 * second + core) * quarter + jnp.arange(quarter, dtype=jnp.int32)
    valid = (my_slots < lengths[0])[:, None]
    grad_valid = jnp.where(valid, cotangent[0], jnp.zeros_like(cotangent[0]))
    proj_weight_grad = weight_grad(active, grad_valid, plans[1])
    output = middle + dot(active, proj_full) + proj_bias_full
    mixed = jnp.where(valid, output, 0.0).astype(LOW)[None]

    proj_bias_grad = jnp.sum(grad_valid.astype(FULL), 0)
    grad_active = dot_nt(grad_valid, proj_full)
    _, gelu_back = jax.vjp(gelu_tanh, hidden)
    grad_hidden = gelu_back(grad_active)[0].astype(LOW)
    fc_weight_grad = weight_grad(normed_two, grad_hidden, plans[0])
    fc_bias_grad = jnp.sum(grad_hidden.astype(FULL), 0)
    grad_normed_two = dot_nt(grad_hidden, fc_full)
    second_gain_grad = jnp.sum(grad_normed_two * hat_two, 0)
    second_shift_grad = jnp.sum(grad_normed_two, 0)
    grad_middle = grad_valid.astype(FULL) + normalize_back(
        grad_normed_two, gain_two, hat_two, root_two
    )
    grad_attn = grad_middle.astype(LOW)
    out_weight_grad = weight_grad(attended, grad_attn, plans[2])
    out_bias_grad = jnp.sum(grad_attn.astype(FULL), 0)
    grad_attended = dot_nt(grad_attn, out_full).astype(LOW)

    keep = lax.dynamic_slice_in_dim(grad_attended, own_half, half, 1)
    send = lax.dynamic_slice_in_dim(grad_attended, half - own_half, half, 1)
    grad_heads = pair(keep, swap(send, 0), core, 0).reshape(near, half)

    grad_query, grad_key, grad_value = attend_back(
        far, query, key, value, grad_heads, attended_heads, logsum
    )

    shape = (count // 2, 2 * slice_rows, half)
    q_grad = dot_tn(normed[:near], grad_query).reshape(shape)
    k_grad = dot_tn(normed, grad_key).reshape(shape)
    v_grad = dot_tn(normed, grad_value).reshape(shape)
    totals = scatter_links([[q_grad], [k_grad], [v_grad]], plans)
    first, last = finish(jnp.concatenate(totals, 1), slice_rows, 3 * width)
    qkv_weight_grad = jnp.stack(
        [first.reshape(slice_rows, 3, half), last.reshape(slice_rows, 3, half)], 2
    ).reshape(slice_rows, 3 * width)
    zero = jnp.zeros((half,), FULL)
    q_sum = jnp.sum(grad_query.astype(FULL), 0)
    v_sum = jnp.sum(grad_value.astype(FULL), 0)
    low_core = core == 0
    qv_bias_grad = jnp.concatenate(
        [
            jnp.where(low_core, q_sum, zero),
            jnp.where(low_core, zero, q_sum),
            jnp.where(low_core, v_sum, zero),
            jnp.where(low_core, zero, v_sum),
        ]
    )

    part = dot_nt(grad_key, k_weight) + dot_nt(grad_value, v_weight)
    part_near = part[:near] + dot_nt(grad_query, q_weight)
    part_far = part[near:]
    first_gain_grad = jnp.sum(part_near * hat_all[:near], 0) + jnp.sum(
        part_far * hat_all[near:], 0
    )
    first_shift_grad = jnp.sum(part_near, 0) + jnp.sum(part_far, 0)
    keep_near, send_near = rows_to_core(part_near)
    keep_far, send_far = rows_to_core(part_far)
    got = swap(jnp.stack([send_near, send_far]).astype(LOW), 0).astype(FULL)
    back = lax.ppermute(
        (keep_far + got[1]).astype(LOW), ALL, [(b, a) for a, b in flips]
    ).astype(FULL)
    grad_normed = keep_near + got[0] + back
    hat = lax.dynamic_slice_in_dim(hat_all, own, quarter, 0)
    root = lax.dynamic_slice_in_dim(root_all, own, quarter, 0)
    grad_inputs = grad_middle + normalize_back(grad_normed, gain_one, hat, root)
    thought = lax.dynamic_slice_in_dim(thought_near, own, quarter, 0)
    kept = jnp.where(thought, 0.0, grad_inputs)
    moved = jnp.where(thought, grad_inputs, 0.0)
    parts = lax.axis_size("ctx")
    following = lax.ppermute(moved[:1], "ctx", [(i, i - 1) for i in range(1, parts)])
    tokens_grad = (kept + jnp.concatenate([moved[1:], following], 0))[None]

    grads = (
        qv_bias_grad,
        out_bias_grad,
        fc_bias_grad,
        proj_bias_grad,
        first_gain_grad,
        first_shift_grad,
        second_gain_grad,
        second_shift_grad,
    )
    sizes = [grad.shape[0] // count for grad in grads]
    packed = jnp.concatenate([g.reshape(count, s) for g, s in zip(grads, sizes)], 1)
    left = packed
    for bit in reversed(range(flat_bits())):
        place = bit_of(bit)
        size = left.shape[0] // 2
        there = lax.dynamic_slice_in_dim(left, (1 - place) * size, size, 0)
        left = lax.dynamic_slice_in_dim(left, place * size, size, 0) + swap(there, bit)
    shares, at = [], 0
    for size in sizes:
        shares.append(left[0, at : at + size])
        at += size
    return (
        mixed,
        tokens_grad,
        qkv_weight_grad,
        out_weight_grad,
        fc_weight_grad,
        proj_weight_grad,
        *shares,
    )


def solution(mesh):
    rows, matrix, vector = P("dp", "ctx", None), P(ALL, None), P(ALL)
    return jax.shard_map(
        shards,
        mesh=mesh,
        in_specs=(rows, P("dp"), P("dp", None), rows) + (matrix,) * 4 + (vector,) * 8,
        out_specs=(rows, rows) + (matrix,) * 4 + (vector,) * 8,
        check_vma=False,
    )
```

time: 1040 us -> 470 us (0.45)
  waiting for transfers between devices: 610 us -> 102 us
  starting transfers between devices: 7.74 us -> 140 us
  matrix products: 199 us -> 73.3 us
  blocking collectives: 79.2 us -> 0 us
  other arithmetic: 76 us -> 37.1 us
  Pallas kernels: 0 us -> 28 us
  local copies, waits for them, and re-layouts: 38.9 us -> 65.8 us
    reduce_scatter x5 -> x0, waiting for transfers between devices: 458 us -> none  [the longest x1 142 us: shards(): lax.psum_scatter(grads[2], ('dp', 'ctx'), scatter_dimension=0, tiled=True)]
    all_gather x5 -> x1, waiting for transfers between devices: 150 us -> 0.01 us  [shards(): lax.all_gather(jnp.concatenate([fc_weight, out_weight], 1), ALL, axis=0,...]
    ppermute x2 -> x67, starting transfers between devices: 7.13 us -> 140 us  [the longest x64 128 us: swap(): return lax.ppermute(value, ALL, [(i, i ^ 1 << bit) for i in range(count)])]
    dot_general x18 -> x21, matrix products: 199 us -> 73.3 us  [the longest x9 28.4 us: dot_tn(): lax.dot_general(a, b, (((0,), (0,)), ((), ())), preferred_element_type=FULL)]
    ppermute x2 -> x67, waiting for transfers between devices: 0.01 us -> 102 us  [the longest x64 93.8 us: swap(): return lax.ppermute(value, ALL, [(i, i ^ 1 << bit) for i in range(count)])]
    unnamed x2 -> x0, blocking collectives: 79.2 us -> none
    convert_element_type x8 -> x21, other arithmetic: 40.4 us -> 9.54 us  [the longest x18 7.56 us: step(): send = Sum(self.half(bit, 1 - place), left).total().astype(LOW)]
    pallas_call x0 -> x2, Pallas kernels: none -> 28 us  [the longest x1 16.7 us: attend_back(): pl.pallas_call(attend_back_kernel, out_shape=(jax.ShapeDtypeStruct((near,...]
  transfers between devices with their start and end apart: 12 -> 68, of which waited for: 9 -> 28; matrix products, arithmetic and copies ran while one was open for 16% -> 27% of each run, Pallas kernels for 0% -> 6%
where the time goes in v1:
time: 470 us; the launch traced here: 463 us
  starting transfers between devices  140 us (30%)
  waiting for transfers between devices  102 us (22%)
  matrix products  73.3 us (16%)
  local copies, waits for them, and re-layouts  65.8 us (14%)
  other arithmetic  37.1 us (8%)
  Pallas kernels  28 us (6%)
  between operations  16.9 us (4%)
    ppermute x64, starting transfers between devices, swap(): return lax.ppermute(value, ALL, [(i, i ^ 1 << bit) for i in range(count)])  128 us
    ppermute x64, waiting for transfers between devices, swap(): return lax.ppermute(value, ALL, [(i, i ^ 1 << bit) for i in range(count)])  93.8 us
    dot_general x9, matrix products, dot_tn(): lax.dot_general(a, b, (((0,), (0,)), ((), ())), preferred_element_type=FULL)  28.4 us
    dot_general x6, matrix products, dot_nt(): lax.dot_general(a, b, (((1,), (1,)), ((), ())), preferred_element_type=FULL)  25.5 us
    dot_general x6, matrix products, dot(): lax.dot_general(a, b, (((1,), (0,)), ((), ())), preferred_element_type=FULL)  19.4 us
    pallas_call x1, Pallas kernels, attend_back(): pl.pallas_call(attend_back_kernel, out_shape=(jax.ShapeDtypeStruct((near,...  16.7 us
    dynamic_update_slice x27, local copies, waits for them, and re-layouts, pair(): return lax.dynamic_update_slice_in_dim(whole, other, 1 - place, axis)  12.5 us
    pallas_call x1, Pallas kernels, attend(): pl.pallas_call(attend_kernel, out_shape=(jax.ShapeDtypeStruct((near, widt...  11.3 us
  transfers between devices with their start and end apart: 68, of which 28 were waited for; matrix products, arithmetic and copies ran while one was open for 27% of the time, Pallas kernels for 6%

profile of v1, /device:TPU:1, one launch (start us, length us, event | category | flops | bytes accessed | tf_op | source)
XLA Modules:
  0.0 462.6 jit_solution(15567020461440224380)
XLA Ops:
  7.4 5.5 %collective-permute-start = (bf16[512,768]{1,0:T(8,128)(2,1)}, bf16[512,768]{1,0:T(8,128)(2,1)}, u32[]{:S(2)}, u32[]{:S(2)}) collective-permute-start(bf16[512,768]{1,0:T(8,128)(2,1)} %bitcast.519), channel_id=1, source_target_pairs={{0,2},{1,3},{4,6},{5,7},{8,10},{9,11},{12,14},{13,15},{16,18},{17,... | collective-permute-start | bytes 2359304 | tf_op jit(solution)/shard_map/ppermute | solution.py:377
  24.3 10.0 %collective-permute-done.4 = bf16[1,48,1280]{2,1,0:T(8,128)(2,1)S(1)} collective-permute-done((bf16[1,48,1280]{2,1,0:T(8,128)(2,1)S(1)}, bf16[1,48,1280]{2,1,0:T(8,128)(2,1)S(1)}, u32[]{:S(2)}, u32[]{:S(2)}) %collective-permute-start.4) | collective-permute-done | bytes 122912 | tf_op jit(solution)/shard_map/ppermute | solution.py:31
  56.5 3.4 collective-permute-done.24
  72.4 15.9 %collective-permute-start.1 = (bf16[512,768]{1,0:T(8,128)(2,1)}, bf16[512,768]{1,0:T(8,128)(2,1)}, u32[]{:S(2)}, u32[]{:S(2)}) collective-permute-start(bf16[512,768]{1,0:T(8,128)(2,1)} %collective-permute-done), channel_id=1, source_target_pairs={{0,1},{1,0},{2,3},{3,2},{4,5},{5,4},{6,7},{7,6},{8,9},{9,8},{10,11... | collective-permute-start | bytes 2359304 | tf_op jit(solution)/shard_map/ppermute | solution.py:31
  100.8 4.7 %copy.171 = bf16[3072,1,384]{0,2,1:T(8,128)(2,1)} copy(bf16[3072,1,384]{2,0,1:T(8,128)(2,1)} %pad_maximum_fusion.1) | data formatting | bytes 4718592 | tf_op jit(solution)/shard_map/concatenate | solution.py:421
  108.3 6.5 %collective-permute-start.26 = (bf16[3072,384]{1,0:T(8,128)(2,1)}, bf16[3072,384]{1,0:T(8,128)(2,1)}, u32[]{:S(2)}, u32[]{:S(2)}) collective-permute-start(bf16[3072,384]{1,0:T(8,128)(2,1)} %pad_maximum_fusion.2), channel_id=1, source_target_pairs={{0,1},{1,0},{2,3},{3,2},{4,5},{5,4},{6,7},{7,6},{8,9},{9,8},{10,11... | collective-permute-start | bytes 7077896 | tf_op jit(solution)/shard_map/ppermute | solution.py:31
  120.8 4.0 fusion
  129.9 11.3 %attend.1 = (bf16[1024,384]{1,0:T(8,128)(2,1)S(1)}, f32[3,8,1024]{2,1,0:T(8,128)S(1)}) custom-call(s32[1]{0:T(128)} %bitcast.8.far_ref, bf16[1024,384]{1,0:T(8,128)(2,1)S(1)} %add_convert_fusion.5.q_ref, bf16[2048,384]{1,0:T(8,128)(2,1)S(1)} %convolution_convert_fusion.2.k_ref, bf16[2048,384]{1,0:T(8,128)(2,1)S(1)} %add_convert_fusion.1.v_ref), custom_call_target="tpu_custom_call" | custom-call | flops 4831838208 | bytes 8388608 | tf_op jit(solution)/shard_map/attend/pallas_call | solution.py:209
  146.9 4.3 copy.172
  157.4 5.5 %multiply_convert_fusion = (bf16[512,3072]{1,0:T(8,128)(2,1)}, f32[512,3072]{1,0:T(8,128)S(1)}) fusion(f32[3072]{0:T(1024)S(1)} %add.1464, bf16[768,3840]{1,0:T(8,128)(2,1)S(1)} %copy-done.57, f32[512,768]{1,0:T(8,128)S(1)} %get-tuple-element.113, f32[768]{0:T(1024)S(1)} %add.1461, f32[768]{0:T(1024)S(1)} %mul.139, f32[512]{0:T(512)S(1)} %add_rsqrt_fusion.1, ...), kind=kOutput, calls=%fused_computation.15 | convolution fusion | flops 2433613824 | bytes 15753216 | tf_op jit(solution)/shard_map/dot_general | solution.py:142
  162.9 8.7 %convert_reduce_fusion.1 = (f32[3072]{0:T(1024)S(1)}, bf16[512,3072]{1,0:T(8,128)(2,1)}) fusion(f32[512,3072]{1,0:T(8,128)S(1)} %get-tuple-element.115, f32[3072]{0:T(1024)S(1)} %add.1464, bf16[3072,768]{0,1:T(8,128)(2,1)S(1)} %bitcast.459, bf16[1,512,768]{2,1,0:T(8,128)(2,1)S(1)} %copy-done.52, pred[512]{0:T(512)(128)(4,1)S(1)} %add_compare_fusion), kind=kOutput, calls=%fused_computation.14 | convolution fusion | flops 2452485120 | bytes 14967296 | tf_op jit(solution)/shard_map/dot_general | solution.py:146
  171.7 7.3 %multiply_reduce_fusion = (f32[768]{0:T(1024)S(1)}, f32[512]{0:T(512)S(1)}, f32[512]{0:T(512)S(1)}, f32[768]{0:T(1024)S(1)}, f32[512,768]{1,0:T(8,128)}) fusion(f32[512,768]{1,0:T(8,128)S(1)} %copy-done.28, f32[512]{0:T(512)S(1)} %add_rsqrt_fusion.1, f32[512]{0:T(512)S(1)} %broadcast_multiply_fusion.5, f32[768]{0:T(1024)S(1)} %mul.139, ...), kind=kOutput, calls=%fused_computation.51 | convolution fusion | flops 2419455488 | bytes 11027456 | tf_op jit(solution)/shard_map/dot_general | solution.py:146
  179.2 7.0 %fusion.28 = bf16[1,512,768]{2,1,0:T(8,128)(2,1)} fusion(f32[512,768]{1,0:T(8,128)S(1)} %copy-done.28, bf16[512,3072]{1,0:T(8,128)(2,1)} %get-tuple-element.114, bf16[3072,768]{0,1:T(8,128)(2,1)} %bitcast.456, f32[768]{0:T(1024)S(1)} %add.1470, pred[512]{0:T(512)(128)(4,1)S(1)} %add_compare_fusion), kind=kOutput, calls=%fused_computation.74 | convolution fusion | flops 2417491968 | bytes 10227200 | tf_op jit(solution)/shard_map/dot_general | solution.py:142
  186.2 4.0 fusion.44
  203.0 4.5 convolution_convert_fusion.1
  208.4 3.9 fusion.23
  212.4 16.7 %attend_back.1 = (bf16[1024,384]{1,0:T(8,128)(2,1)S(1)}, bf16[2048,384]{1,0:T(8,128)(2,1)S(1)}, bf16[2048,384]{1,0:T(8,128)(2,1)}) custom-call(s32[1]{0:T(128)} %bitcast.8.far_ref, bf16[1024,384]{1,0:T(8,128)(2,1)S(1)} %copy-done.3, bf16[2048,384]{1,0:T(8,128)(2,1)} %copy-done.4, bf16[2048,384]{1,0:T(8,128)(2,1)} %copy-done.5, ...), custom_call_target="tpu_custom_call" | custom-call | flops 12079595520 | bytes 16777216 | tf_op jit(solution)/shard_map/attend_back/pallas_call | solution.py:298
  236.1 4.6 fusion.111
  241.0 3.9 fusion.112
  254.7 4.0 collective-permute-start.62
  265.5 29.9 %collective-permute-start.65 = (f32[2,288]{1,0:T(2,128)S(1)}, f32[2,288]{1,0:T(2,128)S(1)}, u32[]{:S(2)}, u32[]{:S(2)}) collective-permute-start(f32[2,288]{1,0:T(2,128)S(1)} %constant_dynamic-slice_fusion.35), channel_id=1, source_target_pairs={{0,2},{1,3},{2,0},{3,1},{4,6},{5,7},{6,4},{7,5},{8,10},{9,11},{10,... | collective-permute-start | bytes 6920 | tf_op jit(solution)/shard_map/ppermute | solution.py:31
  296.4 4.4 collective-permute-start.66
  314.4 8.2 %collective-permute-done.36 = bf16[4,48,384]{2,1,0:T(8,128)(2,1)S(1)} collective-permute-done((bf16[4,48,384]{2,1,0:T(8,128)(2,1)S(1)}, bf16[4,48,384]{2,1,0:T(8,128)(2,1)S(1)}, u32[]{:S(2)}, u32[]{:S(2)}) %collective-permute-start.36) | collective-permute-done | bytes 147488 | tf_op jit(solution)/shard_map/ppermute | solution.py:31
  346.9 8.2 %collective-permute-start.43 = (f32[24,1152]{1,0:T(8,128)S(1)}, f32[24,1152]{1,0:T(8,128)S(1)}, u32[]{:S(2)}, u32[]{:S(2)}) collective-permute-start(f32[24,1152]{1,0:T(8,128)S(1)} %constant_dynamic-slice_fusion.30), channel_id=1, source_target_pairs={{0,1},{1,0},{2,3},{3,2},{4,5},{5,4},{6,7},{7,6},{8,9},{9,8},{10,11... | collective-permute-start | bytes 331784 | tf_op jit(solution)/shard_map/ppermute | solution.py:31
  359.2 3.9 collective-permute-start.49
  368.9 3.4 fusion.29
  380.6 7.9 %collective-permute-done.29 = bf16[512,768]{1,0:T(8,128)(2,1)S(1)} collective-permute-done((bf16[512,768]{1,0:T(8,128)(2,1)S(1)}, bf16[512,768]{1,0:T(8,128)(2,1)S(1)}, u32[]{:S(2)}, u32[]{:S(2)}) %collective-permute-start.29) | collective-permute-done | bytes 786464 | tf_op jit(solution)/shard_map/ppermute | solution.py:529
  389.1 24.7 %collective-permute-done.51 = bf16[8,48,1536]{2,1,0:T(8,128)(2,1)S(1)} collective-permute-done((bf16[8,48,1536]{2,1,0:T(8,128)(2,1)S(1)}, bf16[8,48,1536]{2,1,0:T(8,128)(2,1)S(1)}, u32[]{:S(2)}, u32[]{:S(2)}) %collective-permute-start.51) | collective-permute-done | bytes 1179680 | tf_op jit(solution)/shard_map/ppermute | solution.py:31
  415.7 12.3 %collective-permute-done.52 = bf16[4,48,1536]{2,1,0:T(8,128)(2,1)S(1)} collective-permute-done((bf16[4,48,1536]{2,1,0:T(8,128)(2,1)S(1)}, bf16[4,48,1536]{2,1,0:T(8,128)(2,1)S(1)}, u32[]{:S(2)}, u32[]{:S(2)}) %collective-permute-start.52) | collective-permute-done | bytes 589856 | tf_op jit(solution)/shard_map/ppermute | solution.py:31
  430.0 4.1 collective-permute-start.30
  438.9 4.3 collective-permute-done.59
  446.7 6.5 %collective-permute-done.60 = bf16[1,192,384]{2,1,0:T(8,128)(2,1)S(1)} collective-permute-done((bf16[1,192,384]{2,1,0:T(8,128)(2,1)S(1)}, bf16[1,192,384]{2,1,0:T(8,128)(2,1)S(1)}, u32[]{:S(2)}, u32[]{:S(2)}) %collective-permute-start.60) | collective-permute-done | bytes 147488 | tf_op jit(solution)/shard_map/ppermute | solution.py:31
  (508 shorter events, 192.4 us)
Async XLA Ops:
  7.2 147.1 %all-gather.2.cloned.1.call-start = ((), (), s32[]{:S(2)}) async-start(), calls=%async_computation | async-start | bytes 6082560 | tf_op jit(solution)/shard_map/all_gather | solution.py:369
  7.3 65.2 %collective-permute-start.2 = (bf16[512,768]{1,0:T(8,128)(2,1)}, bf16[512,768]{1,0:T(8,128)(2,1)}, u32[]{:S(2)}, u32[]{:S(2)}) collective-permute-start(bf16[512,768]{1,0:T(8,128)(2,1)} %bitcast.518), channel_id=1, source_target_pairs={{0,1},{1,0},{2,3},{3,2},{4,5},{5,4},{6,7},{7,6},{8,9},{9,8},{10,11... | collective-permute-start | bytes 2359304 | tf_op jit(solution)/shard_map/ppermute | solution.py:31
  7.4 62.7 %collective-permute-start = (bf16[512,768]{1,0:T(8,128)(2,1)}, bf16[512,768]{1,0:T(8,128)(2,1)}, u32[]{:S(2)}, u32[]{:S(2)}) collective-permute-start(bf16[512,768]{1,0:T(8,128)(2,1)} %bitcast.519), channel_id=1, source_target_pairs={{0,2},{1,3},{4,6},{5,7},{8,10},{9,11},{12,14},{13,15},{16,18},{17,... | collective-permute-start | bytes 2359304 | tf_op jit(solution)/shard_map/ppermute | solution.py:377
  21.7 12.6 %collective-permute-start.4 = (bf16[1,48,1280]{2,1,0:T(8,128)(2,1)S(1)}, bf16[1,48,1280]{2,1,0:T(8,128)(2,1)S(1)}, u32[]{:S(2)}, u32[]{:S(2)}) collective-permute-start(bf16[1,48,1280]{2,1,0:T(8,128)(2,1)S(1)} %bitcast.553), channel_id=1, source_target_pairs={{0,16},{1,17},{2,18},{3,19},{4,20},{5,21},{6,22},{7,23},{8,24},{9,... | collective-permute-start | bytes 368648 | tf_op jit(solution)/shard_map/ppermute | solution.py:31
  24.1 14.7 %collective-permute-start.16 = (bf16[1,192,384]{2,1,0:T(8,128)(2,1)S(1)}, bf16[1,192,384]{2,1,0:T(8,128)(2,1)S(1)}, u32[]{:S(2)}, u32[]{:S(2)}) collective-permute-start(bf16[1,192,384]{2,1,0:T(8,128)(2,1)S(1)} %bitcast.541), channel_id=1, source_target_pairs={{0,16},{1,17},{2,18},{3,19},{4,20},{5,21},{6,22},{7,23},{8,24},{9,... | collective-permute-start | bytes 442376 | tf_op jit(solution)/shard_map/ppermute | solution.py:31
  44.7 10.2 %collective-permute-start.9 = (bf16[4,48,384]{2,1,0:T(8,128)(2,1)S(1)}, bf16[4,48,384]{2,1,0:T(8,128)(2,1)S(1)}, u32[]{:S(2)}, u32[]{:S(2)}) collective-permute-start(bf16[4,48,384]{2,1,0:T(8,128)(2,1)S(1)} %bitcast.545), channel_id=1, source_target_pairs={{0,4},{1,5},{2,6},{3,7},{4,0},{5,1},{6,2},{7,3},{8,12},{9,13},{10,... | collective-permute-start | bytes 442376 | tf_op jit(solution)/shard_map/ppermute | solution.py:31
  59.9 10.0 %collective-permute-start.10 = (bf16[8,48,384]{2,1,0:T(8,128)(2,1)S(1)}, bf16[8,48,384]{2,1,0:T(8,128)(2,1)S(1)}, u32[]{:S(2)}, u32[]{:S(2)}) collective-permute-start(bf16[8,48,384]{2,1,0:T(8,128)(2,1)S(1)} %bitcast.502), channel_id=1, source_target_pairs={{0,2},{1,3},{2,0},{3,1},{4,6},{5,7},{6,4},{7,5},{8,10},{9,11},{10,... | collective-permute-start | bytes 884744 | tf_op jit(solution)/shard_map/ppermute | solution.py:31
  63.2 26.3 %collective-permute-start.7 = (bf16[8,48,512]{2,1,0:T(8,128)(2,1)S(1)}, bf16[8,48,512]{2,1,0:T(8,128)(2,1)S(1)}, u32[]{:S(2)}, u32[]{:S(2)}) collective-permute-start(bf16[8,48,512]{2,1,0:T(8,128)(2,1)S(1)} %bitcast.495), channel_id=1, source_target_pairs={{0,8},{1,9},{2,10},{3,11},{4,12},{5,13},{6,14},{7,15},{8,0},{9,1},... | collective-permute-start | bytes 1179656 | tf_op jit(solution)/shard_map/ppermute | solution.py:31
  68.4 28.4 %collective-permute-start.19 = (bf16[8,192,128]{2,1,0:T(8,128)(2,1)}, bf16[8,192,128]{2,1,0:T(8,128)(2,1)}, u32[]{:S(2)}, u32[]{:S(2)}) collective-permute-start(bf16[8,192,128]{2,1,0:T(8,128)(2,1)} %bitcast.75), channel_id=1, source_target_pairs={{0,2},{1,3},{2,0},{3,1},{4,6},{5,7},{6,4},{7,5},{8,10},{9,11},{10,... | collective-permute-start | bytes 1179656 | tf_op jit(solution)/shard_map/ppermute | solution.py:31
  69.9 25.7 %collective-permute-start.22 = (bf16[8,192,128]{2,1,0:T(8,128)(2,1)}, bf16[8,192,128]{2,1,0:T(8,128)(2,1)}, u32[]{:S(2)}, u32[]{:S(2)}) collective-permute-start(bf16[8,192,128]{2,1,0:T(8,128)(2,1)} %bitcast.89), channel_id=1, source_target_pairs={{0,4},{1,5},{2,6},{3,7},{4,0},{5,1},{6,2},{7,3},{8,12},{9,13},{10,... | collective-permute-start | bytes 1179656 | tf_op jit(solution)/shard_map/ppermute | solution.py:31
  70.8 23.1 %collective-permute-start.25 = (bf16[8,192,128]{2,1,0:T(8,128)(2,1)}, bf16[8,192,128]{2,1,0:T(8,128)(2,1)}, u32[]{:S(2)}, u32[]{:S(2)}) collective-permute-start(bf16[8,192,128]{2,1,0:T(8,128)(2,1)} %bitcast.103), channel_id=1, source_target_pairs={{0,8},{1,9},{2,10},{3,11},{4,12},{5,13},{6,14},{7,15},{8,0},{9,1},... | collective-permute-start | bytes 1179656 | tf_op jit(solution)/shard_map/ppermute | solution.py:31
  72.4 42.4 %collective-permute-start.1 = (bf16[512,768]{1,0:T(8,128)(2,1)}, bf16[512,768]{1,0:T(8,128)(2,1)}, u32[]{:S(2)}, u32[]{:S(2)}) collective-permute-start(bf16[512,768]{1,0:T(8,128)(2,1)} %collective-permute-done), channel_id=1, source_target_pairs={{0,1},{1,0},{2,3},{3,2},{4,5},{5,4},{6,7},{7,6},{8,9},{9,8},{10,11... | collective-permute-start | bytes 2359304 | tf_op jit(solution)/shard_map/ppermute | solution.py:31
  108.3 38.6 %collective-permute-start.26 = (bf16[3072,384]{1,0:T(8,128)(2,1)}, bf16[3072,384]{1,0:T(8,128)(2,1)}, u32[]{:S(2)}, u32[]{:S(2)}) collective-permute-start(bf16[3072,384]{1,0:T(8,128)(2,1)} %pad_maximum_fusion.2), channel_id=1, source_target_pairs={{0,1},{1,0},{2,3},{3,2},{4,5},{5,4},{6,7},{7,6},{8,9},{9,8},{10,11... | collective-permute-start | bytes 7077896 | tf_op jit(solution)/shard_map/ppermute | solution.py:31
  199.9 12.5 %collective-permute-start.27 = (bf16[512,384]{1,0:T(8,128)(2,1)}, bf16[512,384]{1,0:T(8,128)(2,1)S(1)}, u32[]{:S(2)}, u32[]{:S(2)}) collective-permute-start(bf16[512,384]{1,0:T(8,128)(2,1)} %constant_dynamic-slice_fusion.58), channel_id=1, source_target_pairs={{0,1},{1,0},{2,3},{3,2},{4,5},{5,4},{6,7},{7,6},{8,9},{9,8},{10,11... | collective-permute-start | bytes 1179656 | tf_op jit(solution)/shard_map/ppermute | solution.py:31
  203.0 102.1 %collective-permute-start.44 = (bf16[768,384]{1,0:T(8,128)(2,1)}, bf16[768,384]{1,0:T(8,128)(2,1)}, u32[]{:S(2)}, u32[]{:S(2)}) collective-permute-start(bf16[768,384]{1,0:T(8,128)(2,1)} %convolution_convert_fusion.4), channel_id=1, source_target_pairs={{0,1},{1,0},{2,3},{3,2},{4,5},{5,4},{6,7},{7,6},{8,9},{9,8},{10,11... | collective-permute-start | bytes 1769480 | tf_op jit(solution)/shard_map/ppermute | solution.py:31
  207.6 161.3 %collective-permute-start.50 = (bf16[768,1536]{1,0:T(8,128)(2,1)}, bf16[768,1536]{1,0:T(8,128)(2,1)}, u32[]{:S(2)}, u32[]{:S(2)}) collective-permute-start(bf16[768,1536]{1,0:T(8,128)(2,1)} %convolution_convert_fusion.1), channel_id=1, source_target_pairs={{0,1},{1,0},{2,3},{3,2},{4,5},{5,4},{6,7},{7,6},{8,9},{9,8},{10,11... | collective-permute-start | bytes 7077896 | tf_op jit(solution)/shard_map/ppermute | solution.py:31
  208.4 166.2 %collective-permute-start.56 = (bf16[3072,384]{1,0:T(8,128)(2,1)}, bf16[3072,384]{1,0:T(8,128)(2,1)}, u32[]{:S(2)}, u32[]{:S(2)}) collective-permute-start(bf16[3072,384]{1,0:T(8,128)(2,1)} %convolution_convert_fusion), channel_id=1, source_target_pairs={{0,1},{1,0},{2,3},{3,2},{4,5},{5,4},{6,7},{7,6},{8,9},{9,8},{10,11... | collective-permute-start | bytes 7077896 | tf_op jit(solution)/shard_map/ppermute | solution.py:31
  264.1 44.6 %collective-permute-start.35 = (bf16[8,48,384]{2,1,0:T(8,128)(2,1)S(1)}, bf16[8,48,384]{2,1,0:T(8,128)(2,1)S(1)}, u32[]{:S(2)}, u32[]{:S(2)}) collective-permute-start(bf16[8,48,384]{2,1,0:T(8,128)(2,1)S(1)} %bitcast.564), channel_id=1, source_target_pairs={{0,4},{1,5},{2,6},{3,7},{4,0},{5,1},{6,2},{7,3},{8,12},{9,13},{10,... | collective-permute-start | bytes 884744 | tf_op jit(solution)/shard_map/ppermute | solution.py:31
  265.5 30.9 %collective-permute-start.65 = (f32[2,288]{1,0:T(2,128)S(1)}, f32[2,288]{1,0:T(2,128)S(1)}, u32[]{:S(2)}, u32[]{:S(2)}) collective-permute-start(f32[2,288]{1,0:T(2,128)S(1)} %constant_dynamic-slice_fusion.35), channel_id=1, source_target_pairs={{0,2},{1,3},{2,0},{3,1},{4,6},{5,7},{6,4},{7,5},{8,10},{9,11},{10,... | collective-permute-start | bytes 6920 | tf_op jit(solution)/shard_map/ppermute | solution.py:31
  308.7 18.2 %collective-permute-start.45 = (bf16[8,48,384]{2,1,0:T(8,128)(2,1)S(1)}, bf16[8,48,384]{2,1,0:T(8,128)(2,1)S(1)}, u32[]{:S(2)}, u32[]{:S(2)}) collective-permute-start(bf16[8,48,384]{2,1,0:T(8,128)(2,1)S(1)} %bitcast.572), channel_id=1, source_target_pairs={{0,8},{1,9},{2,10},{3,11},{4,12},{5,13},{6,14},{7,15},{8,0},{9,1},... | collective-permute-start | bytes 884744 | tf_op jit(solution)/shard_map/ppermute | solution.py:31
  310.5 12.1 %collective-permute-start.36 = (bf16[4,48,384]{2,1,0:T(8,128)(2,1)S(1)}, bf16[4,48,384]{2,1,0:T(8,128)(2,1)S(1)}, u32[]{:S(2)}, u32[]{:S(2)}) collective-permute-start(bf16[4,48,384]{2,1,0:T(8,128)(2,1)S(1)} %bitcast.589), channel_id=1, source_target_pairs={{0,8},{1,9},{2,10},{3,11},{4,12},{5,13},{6,14},{7,15},{8,0},{9,1},... | collective-permute-start | bytes 442376 | tf_op jit(solution)/shard_map/ppermute | solution.py:31
  322.9 41.9 %collective-permute-start.28 = (bf16[2,512,768]{2,1,0:T(8,128)(2,1)S(1)}, bf16[2,512,768]{2,1,0:T(8,128)(2,1)}, u32[]{:S(2)}, u32[]{:S(2)}) collective-permute-start(bf16[2,512,768]{2,1,0:T(8,128)(2,1)S(1)} %pad_maximum_fusion.3), channel_id=1, source_target_pairs={{0,1},{1,0},{2,3},{3,2},{4,5},{5,4},{6,7},{7,6},{8,9},{9,8},{10,11... | collective-permute-start | bytes 4718600 | tf_op jit(solution)/shard_map/ppermute | solution.py:31
  331.4 13.6 %collective-permute-start.46 = (bf16[4,48,384]{2,1,0:T(8,128)(2,1)S(1)}, bf16[4,48,384]{2,1,0:T(8,128)(2,1)S(1)}, u32[]{:S(2)}, u32[]{:S(2)}) collective-permute-start(bf16[4,48,384]{2,1,0:T(8,128)(2,1)S(1)} %get-tuple-element.79), channel_id=1, source_target_pairs={{0,2},{1,3},{2,0},{3,1},{4,6},{5,7},{6,4},{7,5},{8,10},{9,11},{10,... | collective-permute-start | bytes 442376 | tf_op jit(solution)/shard_map/ppermute | solution.py:31
  345.1 10.0 %collective-permute-start.47 = (bf16[2,48,384]{2,1,0:T(8,128)(2,1)S(1)}, bf16[2,48,384]{2,1,0:T(8,128)(2,1)S(1)}, u32[]{:S(2)}, u32[]{:S(2)}) collective-permute-start(bf16[2,48,384]{2,1,0:T(8,128)(2,1)S(1)} %fusion.62), channel_id=1, source_target_pairs={{0,4},{1,5},{2,6},{3,7},{4,0},{5,1},{6,2},{7,3},{8,12},{9,13},{10,... | collective-permute-start | bytes 221192 | tf_op jit(solution)/shard_map/ppermute | solution.py:31
  346.9 10.3 %collective-permute-start.43 = (f32[24,1152]{1,0:T(8,128)S(1)}, f32[24,1152]{1,0:T(8,128)S(1)}, u32[]{:S(2)}, u32[]{:S(2)}) collective-permute-start(f32[24,1152]{1,0:T(8,128)S(1)} %constant_dynamic-slice_fusion.30), channel_id=1, source_target_pairs={{0,1},{1,0},{2,3},{3,2},{4,5},{5,4},{6,7},{7,6},{8,9},{9,8},{10,11... | collective-permute-start | bytes 331784 | tf_op jit(solution)/shard_map/ppermute | solution.py:31
  367.3 21.2 %collective-permute-start.29 = (bf16[512,768]{1,0:T(8,128)(2,1)S(1)}, bf16[512,768]{1,0:T(8,128)(2,1)S(1)}, u32[]{:S(2)}, u32[]{:S(2)}) collective-permute-start(bf16[512,768]{1,0:T(8,128)(2,1)S(1)} %fusion.17), channel_id=1, source_target_pairs={{2,0},{3,1},{6,4},{7,5},{10,8},{11,9},{14,12},{15,13},{18,16},{19,... | collective-permute-start | bytes 2359304 | tf_op jit(solution)/shard_map/ppermute | solution.py:529
  372.4 41.4 %collective-permute-start.51 = (bf16[8,48,1536]{2,1,0:T(8,128)(2,1)S(1)}, bf16[8,48,1536]{2,1,0:T(8,128)(2,1)S(1)}, u32[]{:S(2)}, u32[]{:S(2)}) collective-permute-start(bf16[8,48,1536]{2,1,0:T(8,128)(2,1)S(1)} %get-tuple-element.67), channel_id=1, source_target_pairs={{0,2},{1,3},{2,0},{3,1},{4,6},{5,7},{6,4},{7,5},{8,10},{9,11},{10,... | collective-permute-start | bytes 3538952 | tf_op jit(solution)/shard_map/ppermute | solution.py:31
  376.4 38.8 %collective-permute-start.57 = (bf16[8,192,384]{2,1,0:T(8,128)(2,1)S(1)}, bf16[8,192,384]{2,1,0:T(8,128)(2,1)S(1)}, u32[]{:S(2)}, u32[]{:S(2)}) collective-permute-start(bf16[8,192,384]{2,1,0:T(8,128)(2,1)S(1)} %bitcast.496), channel_id=1, source_target_pairs={{0,4},{1,5},{2,6},{3,7},{4,0},{5,1},{6,2},{7,3},{8,12},{9,13},{10,... | collective-permute-start | bytes 3538952 | tf_op jit(solution)/shard_map/ppermute | solution.py:31
  414.1 13.9 %collective-permute-start.52 = (bf16[4,48,1536]{2,1,0:T(8,128)(2,1)S(1)}, bf16[4,48,1536]{2,1,0:T(8,128)(2,1)S(1)}, u32[]{:S(2)}, u32[]{:S(2)}) collective-permute-start(bf16[4,48,1536]{2,1,0:T(8,128)(2,1)S(1)} %get-tuple-element.71), channel_id=1, source_target_pairs={{0,4},{1,5},{2,6},{3,7},{4,0},{5,1},{6,2},{7,3},{8,12},{9,13},{10,... | collective-permute-start | bytes 1769480 | tf_op jit(solution)/shard_map/ppermute | solution.py:31
  415.5 18.6 %collective-permute-start.58 = (bf16[4,192,384]{2,1,0:T(8,128)(2,1)S(1)}, bf16[4,192,384]{2,1,0:T(8,128)(2,1)S(1)}, u32[]{:S(2)}, u32[]{:S(2)}) collective-permute-start(bf16[4,192,384]{2,1,0:T(8,128)(2,1)S(1)} %bitcast.552), channel_id=1, source_target_pairs={{0,8},{1,9},{2,10},{3,11},{4,12},{5,13},{6,14},{7,15},{8,0},{9,1},... | collective-permute-start | bytes 1769480 | tf_op jit(solution)/shard_map/ppermute | solution.py:31
  434.9 11.0 %collective-permute-start.54 = (bf16[1,48,1536]{2,1,0:T(8,128)(2,1)S(1)}, bf16[1,48,1536]{2,1,0:T(8,128)(2,1)S(1)}, u32[]{:S(2)}, u32[]{:S(2)}) collective-permute-start(bf16[1,48,1536]{2,1,0:T(8,128)(2,1)S(1)} %fusion.54), channel_id=1, source_target_pairs={{0,16},{1,17},{2,18},{3,19},{4,20},{5,21},{6,22},{7,23},{8,24},{9,... | collective-permute-start | bytes 442376 | tf_op jit(solution)/shard_map/ppermute | solution.py:31
  443.2 9.9 %collective-permute-start.60 = (bf16[1,192,384]{2,1,0:T(8,128)(2,1)S(1)}, bf16[1,192,384]{2,1,0:T(8,128)(2,1)S(1)}, u32[]{:S(2)}, u32[]{:S(2)}) collective-permute-start(bf16[1,192,384]{2,1,0:T(8,128)(2,1)S(1)} %fusion.52), channel_id=1, source_target_pairs={{0,16},{1,17},{2,18},{3,19},{4,20},{5,21},{6,22},{7,23},{8,24},{9,... | collective-permute-start | bytes 442376 | tf_op jit(solution)/shard_map/ppermute | solution.py:31
  (103 other events, 644.6 us)
Sparse Core Ops, SparseCore 0:
  18.8 81.9 all-gather.1

commit v2 on v1

v2 whole, which is shorter than its diff:
```python
import jax
import jax.numpy as jnp
from jax import lax
from jax.experimental import pallas as pl
from jax.experimental.pallas import tpu as pltpu
from jax.sharding import PartitionSpec as P

ALL = ("dp", "ctx")
LOW = jnp.bfloat16
FULL = jnp.float32
HEAD = 64
LANES = 128
SCALE = 0.125
VMEM = 48 << 20
SHORT = pl.CostEstimate(flops=1 << 29, bytes_accessed=1 << 19, transcendentals=0)


def flat_bits():
    return (lax.axis_size("dp") * lax.axis_size("ctx")).bit_length() - 1


def flat_index():
    return lax.axis_index("dp") * lax.axis_size("ctx") + lax.axis_index("ctx")


def bit_of(bit):
    return (flat_index() >> bit) & 1


def swap(value, bit):
    count = 1 << flat_bits()
    return lax.ppermute(value, ALL, [(i, i ^ (1 << bit)) for i in range(count)])


def after(value, *others):
    return lax.optimization_barrier((value, others))[0]


def pair(mine, other, place, axis):
    shape = mine.shape[:axis] + (2,) + mine.shape[axis:]
    whole = jnp.broadcast_to(jnp.expand_dims(mine, axis), shape)
    return lax.dynamic_update_slice_in_dim(whole, jnp.expand_dims(other, axis), 1 - place, axis)


def beside(mine, other, place):
    low = place == 0
    return jnp.concatenate([jnp.where(low, mine, other), jnp.where(low, other, mine)], -1)


def orders():
    rest = list(range(3, flat_bits()))
    return [1, 2] + rest, [2, 1] + rest


def grow(block, done, bit, wait=()):
    other = after(swap(block, bit), *wait)
    rows, cols = block.shape[1:]
    high = 1 << len([b for b in done if b > bit])
    low = 1 << len([b for b in done if b < bit])
    whole = pair(
        block.reshape(high, low, rows, cols), other.reshape(high, low, rows, cols), bit_of(bit), 1
    )
    return whole.reshape(high * 2 * low, rows, cols)


def gather_common(block):
    block, done = block[None], []
    for bit in reversed(range(3, flat_bits())):
        block = grow(block, done, bit)
        done.append(bit)
    return block


def gather_step(parts, plans, step, wait=()):
    out = []
    for part, order in zip(parts, plans):
        plan = list(reversed(order))
        at = flat_bits() - 3 + step
        out.append(grow(part, plan[:at], plan[at], wait))
    return out


class Sum:
    def __init__(self, addends, left, kind=LOW):
        self.addends = addends
        self.left = left
        self.kind = kind

    def total(self, bit=None, place=None):
        result = None
        for value, bits, (start, size) in self.addends:
            rows = value.shape[1]
            dims, begin, width = [], [], []
            for b in sorted(bits, reverse=True):
                dims.append(2)
                if b == bit:
                    begin.append(place)
                    width.append(1)
                elif b in self.left:
                    begin.append(0)
                    width.append(2)
                else:
                    begin.append(bit_of(b))
                    width.append(1)
            view = value.reshape(*dims, rows, value.shape[2])
            piece = lax.dynamic_slice(view, (*begin, 0, start), (*width, rows, size))
            piece = piece.reshape(-1, rows, size).astype(FULL)
            result = piece if result is None else result + piece
        return result

    def prepare(self, bit):
        send = self.total(bit, 1 - bit_of(bit)).astype(self.kind)
        return send, Sum(self.addends, [b for b in self.left if b != bit], self.kind), bit


def prepare(sums, plans, step):
    return [value.prepare(plan[step]) for value, plan in zip(sums, plans)]


def sends(prepared):
    return [send for send, _, _ in prepared]


def exchange(prepared, wait=()):
    out = []
    for send, keep, bit in prepared:
        got = after(swap(send, bit), *wait)
        out.append(Sum(keep.addends + [(got, keep.left, (0, got.shape[2]))], keep.left, keep.kind))
    return out


def start_sum(arrays, start, size, kind=LOW):
    links = list(range(1, flat_bits()))
    return Sum([(value, links, (start, size)) for value in arrays], links, kind)


def finish(total, rows):
    core = bit_of(0)
    mine = lax.dynamic_slice_in_dim(total, core * rows, rows, 0)
    other = swap(lax.dynamic_slice_in_dim(total, (1 - core) * rows, rows, 0), 0)
    return jnp.where(core == 0, mine, other), jnp.where(core == 0, other, mine)


def dot(a, b):
    return lax.dot_general(a, b, (((1,), (0,)), ((), ())), preferred_element_type=FULL)


def dot_nt(a, b):
    return lax.dot_general(a, b, (((1,), (1,)), ((), ())), preferred_element_type=FULL)


def dot_tn(a, b):
    return lax.dot_general(a, b, (((0,), (0,)), ((), ())), preferred_element_type=FULL)


def head_lanes(value, head):
    lane = lax.broadcasted_iota(jnp.int32, (1, LANES), 1)
    return jnp.where(lane // HEAD == head, value, jnp.zeros_like(value))


def causal(size):
    shape = (size, size)
    return lax.broadcasted_iota(jnp.int32, shape, 0) <= lax.broadcasted_iota(jnp.int32, shape, 1)


def attend_kernel(far_ref, q_ref, k_ref, v_ref, *refs):
    out_ref, lse_ref, top_ref, acc_ref = refs[-4:]
    size = q_ref.shape[0]
    mine = pl.program_id(0)
    query = q_ref[...] * jnp.asarray(SCALE, LOW)

    def step(block, first):
        at = pl.ds(pl.multiple_of(block * size, size), size)
        key = k_ref[at, :]
        value = jnp.transpose(v_ref[at, :])
        for head in range(2):
            ones = jnp.ones((16, size), LOW)
            wide = jnp.concatenate([value[head * HEAD : (head + 1) * HEAD], ones], 0)
            scores = dot_nt(key, head_lanes(query, head))
            row = slice(head, head + 1)
            if first:
                scores = jnp.where(causal(size), scores, -1e9)
                top = jnp.max(scores, 0, keepdims=True)
                acc_ref[head] = dot(wide, jnp.exp(scores - top).astype(LOW))
            else:
                old = top_ref[row, :]
                top = jnp.maximum(old, jnp.max(scores, 0, keepdims=True))
                acc_ref[head] = acc_ref[head] * jnp.exp(old - top) + dot(
                    wide, jnp.exp(scores - top).astype(LOW)
                )
            top_ref[row, :] = top

    step(mine, True)

    @pl.loop(0, mine + far_ref[0])
    def _(i):
        step(jnp.where(i < mine, 0, 2 + i - mine), False)

    outs = []
    for head in range(2):
        total = acc_ref[head, HEAD : HEAD + 1, :]
        outs.append(acc_ref[head, :HEAD, :] / total)
        lse_ref[0, head : head + 1, :] = top_ref[head : head + 1, :] + jnp.log(total)
    out_ref[...] = jnp.transpose(jnp.concatenate(outs, 0)).astype(LOW)


def attend(far, query, keyval, quarter, which, earlier):
    near, width = query.shape
    total = keyval.shape[0]
    pairs = width // LANES
    rows = pl.BlockSpec((quarter, LANES), lambda i, s: (i, which))
    return pl.pallas_call(
        attend_kernel,
        out_shape=(
            jax.ShapeDtypeStruct((near, width), LOW),
            jax.ShapeDtypeStruct((pairs, 8, near), FULL),
        ),
        grid_spec=pltpu.PrefetchScalarGridSpec(
            num_scalar_prefetch=1,
            grid=(near // quarter,),
            in_specs=[
                rows,
                pl.BlockSpec((total, LANES), lambda i, s: (0, which)),
                pl.BlockSpec((total, LANES), lambda i, s: (0, which + pairs)),
            ]
            + [pl.BlockSpec(memory_space=pl.ANY)] * len(earlier),
            out_specs=(rows, pl.BlockSpec((1, 8, quarter), lambda i, s: (which, 0, i))),
            scratch_shapes=[
                pltpu.VMEM((8, quarter), FULL),
                pltpu.VMEM((2, HEAD + 16, quarter), FULL),
            ],
        ),
        input_output_aliases={4 + i: i for i in range(len(earlier))},
        compiler_params=pltpu.CompilerParams(vmem_limit_bytes=VMEM),
        cost_estimate=SHORT,
        name="attend",
    )(far, query, keyval, keyval, *earlier)


def attend_back_kernel(
    far_ref, q_ref, k_ref, v_ref, grad_ref, out_ref, lse_ref, *refs
):
    dq_ref, dk_ref, dv_ref, acc_ref = refs[-4:]
    near = q_ref.shape[0]
    size = near // 2
    spans = (slice(0, size), slice(size, near))
    query = q_ref[...] * jnp.asarray(SCALE, LOW)
    grad = grad_ref[...]
    product = jnp.transpose(grad.astype(FULL) * out_ref[...].astype(FULL))
    delta = [
        jnp.sum(product[head * HEAD : (head + 1) * HEAD], 0, keepdims=True) for head in range(2)
    ]

    def block(at, work):
        key, value = k_ref[at, :], v_ref[at, :]
        turned = jnp.transpose(key)
        dk = dv = None
        for which, masked, first in work:
            span = spans[which]
            for head in range(2):
                part = slice(head * HEAD, (head + 1) * HEAD)
                q_head = head_lanes(query[span], head)
                g_head = head_lanes(grad[span], head)
                probs = jnp.exp(dot_nt(key, q_head) - lse_ref[0, head : head + 1, span])
                if masked:
                    probs = jnp.where(causal(size), probs, 0.0)
                moved = probs * (dot_nt(value, g_head) - delta[head][:, span])
                moved, probs = moved.astype(LOW), probs.astype(LOW)
                new_k, new_v = dot(moved, q_head), dot(probs, g_head)
                dk = new_k if dk is None else dk + new_k
                dv = new_v if dv is None else dv + new_v
                new_q = dot(turned[part], moved)
                if first:
                    acc_ref[which, part, :] = new_q
                else:
                    acc_ref[which, part, :] += new_q
        dk_ref[at, :] = dk.astype(LOW)
        dv_ref[at, :] = dv.astype(LOW)

    block(spans[0], [(0, True, True), (1, False, True)])
    block(spans[1], [(1, True, False)])

    @pl.loop(0, far_ref[0])
    def _(i):
        at = pl.ds(pl.multiple_of(near + i * size, size), size)
        block(at, [(0, False, False), (1, False, False)])

    @pl.loop(far_ref[0], 2)
    def _(i):
        at = pl.ds(pl.multiple_of(near + i * size, size), size)
        dk_ref[at, :] = jnp.zeros((size, LANES), LOW)
        dv_ref[at, :] = jnp.zeros((size, LANES), LOW)

    for which in range(2):
        dq_ref[spans[which], :] = (jnp.transpose(acc_ref[which]) * SCALE).astype(LOW)


def attend_back(far, query, keyval, grad, out, lse, which, earlier):
    near, width = query.shape
    total = keyval.shape[0]
    pairs = width // LANES
    rows = pl.BlockSpec((near, LANES), lambda p, s: (0, which))
    every = pl.BlockSpec((total, LANES), lambda p, s: (0, which))
    return pl.pallas_call(
        attend_back_kernel,
        out_shape=(
            jax.ShapeDtypeStruct((near, width), LOW),
            jax.ShapeDtypeStruct((total, width), LOW),
            jax.ShapeDtypeStruct((total, width), LOW),
        ),
        grid_spec=pltpu.PrefetchScalarGridSpec(
            num_scalar_prefetch=1,
            grid=(1,),
            in_specs=[
                rows,
                every,
                pl.BlockSpec((total, LANES), lambda p, s: (0, which + pairs)),
                rows,
                rows,
                pl.BlockSpec((1, 8, near), lambda p, s: (which, 0, 0)),
            ]
            + [pl.BlockSpec(memory_space=pl.ANY)] * len(earlier),
            out_specs=(rows, every, every),
            scratch_shapes=[pltpu.VMEM((2, LANES, near // 2), FULL)],
        ),
        input_output_aliases={7 + i: i for i in range(len(earlier))},
        compiler_params=pltpu.CompilerParams(vmem_limit_bytes=VMEM),
        cost_estimate=SHORT,
        name="attend_back",
    )(far, query, keyval, keyval, grad, out, lse, *earlier)


def grads_kernel(n_ref, dq_ref, dk_ref, dv_ref, a_ref, b_ref):
    near, width = dq_ref.shape
    turned = jnp.transpose(n_ref[...])
    low = jnp.concatenate(
        [
            dot(turned[:, :near], dq_ref[...]).astype(LOW),
            dot(turned, dk_ref[...]).astype(LOW),
            dot(turned, dv_ref[...]).astype(LOW),
        ],
        1,
    )
    cut = a_ref.shape[1]
    a_ref[...] = low[:, :cut]
    b_ref[...] = low[:, cut:]


def qkv_grads(normed, dq, dk, dv):
    width = normed.shape[1]
    cols = 3 * dq.shape[1]
    cut = (cols // LANES + 1) // 2 * LANES
    return pl.pallas_call(
        grads_kernel,
        out_shape=(
            jax.ShapeDtypeStruct((width, cut), LOW),
            jax.ShapeDtypeStruct((width, cols - cut), LOW),
        ),
        compiler_params=pltpu.CompilerParams(vmem_limit_bytes=VMEM),
        cost_estimate=SHORT,
        name="qkv_grads",
    )(normed, dq, dk, dv)


CURVE = 0.7978845608028654
CUBIC = 0.044715


def feed_kernel(
    core_ref, n_ref, g_ref, fc_ref, fb_ref, pr_ref,
    out_ref, back_ref, fc_grad_ref, pr_grad_ref, fb_grad_ref, turned_ref,
):
    step = pl.program_id(0)
    half = g_ref.shape[1] // 2

    @pl.when(step == 0)
    def _():
        turned_ref[...] = jnp.transpose(n_ref[...])

    proj = pr_ref[...].reshape(fc_ref.shape[1], n_ref.shape[1])
    grad = g_ref[...]
    hidden = dot(n_ref[...], fc_ref[...]) + fb_ref[...]
    square = hidden * hidden
    bend = jnp.tanh(hidden * (CURVE + (CURVE * CUBIC) * square))
    gate = 0.5 * (1.0 + bend)
    active = (hidden * gate).astype(LOW)
    slope = gate + hidden * (0.5 * (1.0 - bend * bend)) * (
        CURVE + (3 * CURVE * CUBIC) * square
    )
    grad_hidden = (dot_nt(grad, proj) * slope).astype(LOW)
    out, back = dot(active, proj), dot_nt(grad_hidden, fc_ref[...])

    @pl.when(step == 0)
    def _():
        out_ref[...] = out
        back_ref[...] = back

    @pl.when(step > 0)
    def _():
        out_ref[...] += out
        back_ref[...] += back

    fb_grad_ref[...] = jnp.sum(grad_hidden.astype(FULL), 0, keepdims=True)
    fc_grad_ref[0] = dot(turned_ref[...], grad_hidden).astype(LOW)
    pr_grad = dot_tn(active, grad)
    low, high = pr_grad[:, :half].astype(LOW), pr_grad[:, half:].astype(LOW)
    first = core_ref[0] == 0
    pr_grad_ref[0] = jnp.where(first, high, low)
    pr_grad_ref[1] = jnp.where(first, low, high)


def feed(core, normed, grad, fc, fc_bias, proj, proj_rows):
    rows, width = normed.shape
    hidden = fc.shape[1]
    chunk = hidden // 4
    group = chunk // proj_rows
    steps = hidden // (2 * chunk)

    def block(i, s):
        return jnp.where(i < steps, (1 - s[0]) * steps + i, s[0] * steps + i - steps)

    whole = pl.BlockSpec((rows, width), lambda i, s: (0, 0))
    return pl.pallas_call(
        feed_kernel,
        out_shape=(
            jax.ShapeDtypeStruct((rows, width), FULL),
            jax.ShapeDtypeStruct((rows, width), FULL),
            jax.ShapeDtypeStruct((2, width, hidden // 2), LOW),
            jax.ShapeDtypeStruct((2, hidden, width // 2), LOW),
            jax.ShapeDtypeStruct((1, hidden), FULL),
        ),
        grid_spec=pltpu.PrefetchScalarGridSpec(
            num_scalar_prefetch=1,
            grid=(2 * steps,),
            in_specs=[
                whole,
                whole,
                pl.BlockSpec((width, chunk), lambda i, s: (0, block(i, s))),
                pl.BlockSpec((1, chunk), lambda i, s: (0, block(i, s))),
                pl.BlockSpec((group, proj_rows, width), lambda i, s: (block(i, s), 0, 0)),
            ],
            out_specs=(
                whole,
                whole,
                pl.BlockSpec(
                    (1, width, chunk), lambda i, s: (jnp.where(i < steps, 0, 1), 0, lax.rem(i, steps))
                ),
                pl.BlockSpec((2, chunk, width // 2), lambda i, s: (0, block(i, s), 0)),
                pl.BlockSpec((1, chunk), lambda i, s: (0, block(i, s))),
            ),
            scratch_shapes=[pltpu.VMEM((width, rows), LOW)],
        ),
        compiler_params=pltpu.CompilerParams(vmem_limit_bytes=VMEM),
        cost_estimate=SHORT,
        name="feed",
    )(core, normed, grad, fc, fc_bias, proj)


def turn_kernel(
    core_ref, n_ref, hat_ref, root_ref, gain_ref, g_ref, att_ref, w_ref,
    middle_ref, keep_ref, send_ref, w_keep_ref, w_send_ref, gain_grad_ref, shift_ref, bias_ref,
):
    half = keep_ref.shape[1]
    grad, hat = n_ref[...], hat_ref[...]
    gain_grad_ref[...] = jnp.sum(grad * hat, 0, keepdims=True)
    shift_ref[...] = jnp.sum(grad, 0, keepdims=True)
    middle = g_ref[...].astype(FULL) + normalize_back(grad, gain_ref[...], hat, root_ref[...])
    middle_ref[...] = middle
    low = middle.astype(LOW)
    bias_ref[...] = jnp.sum(low.astype(FULL), 0, keepdims=True)
    first = core_ref[0] == 0
    for whole, kept, sent in (
        (dot_nt(low, w_ref[...]), keep_ref, send_ref),
        (dot(jnp.transpose(att_ref[...]), low), w_keep_ref, w_send_ref),
    ):
        whole = whole.astype(LOW)
        one, two = whole[:, :half], whole[:, half:]
        kept[...] = jnp.where(first, one, two)
        sent[...] = jnp.where(first, two, one)


def turn(core, grad, hat, root, gain, grad_valid, attended, weight):
    rows, width = grad.shape
    vmem = pl.BlockSpec(memory_space=pltpu.VMEM)
    shape = jax.ShapeDtypeStruct
    return pl.pallas_call(
        turn_kernel,
        in_specs=[pl.BlockSpec(memory_space=pltpu.SMEM)] + [vmem] * 7,
        out_shape=(
            shape((rows, width), FULL),
            shape((rows, width // 2), LOW),
            shape((rows, width // 2), LOW),
            shape((width, width // 2), LOW),
            shape((width, width // 2), LOW),
            shape((1, width), FULL),
            shape((1, width), FULL),
            shape((1, width), FULL),
        ),
        compiler_params=pltpu.CompilerParams(vmem_limit_bytes=VMEM),
        cost_estimate=SHORT,
        name="turn",
    )(core, grad, hat, root, gain, grad_valid, attended, weight)


def norm_back_kernel(
    core_ref, dq_ref, dk_ref, dv_ref, wq_ref, wkv_ref, hat_ref,
    keep_ref, send_ref, gain_ref, shift_ref, q_sum_ref, v_sum_ref, part_ref,
):
    step = pl.program_id(0)
    half = dk_ref.shape[1]
    part_ref[...] = dot_nt(dk_ref[...], wkv_ref[:, :half]) + dot_nt(
        dv_ref[...], wkv_ref[:, half:]
    )

    @pl.when(step == 0)
    def _():
        for ref in (gain_ref, shift_ref, q_sum_ref, v_sum_ref):
            ref[...] = jnp.zeros_like(ref)

    @pl.when(lax.rem(step, 2) == 1)
    def _():
        part_ref[...] += dot_nt(dq_ref[...], wq_ref[...])
        q_sum_ref[...] += jnp.sum(dq_ref[...].astype(FULL), 0, keepdims=True)

    part = part_ref[...]
    v_sum_ref[...] += jnp.sum(dv_ref[...].astype(FULL), 0, keepdims=True)
    gain_ref[...] += jnp.sum(part * hat_ref[...], 0, keepdims=True)
    shift_ref[...] += jnp.sum(part, 0, keepdims=True)

    @pl.when(step < 2)
    def _():
        send_ref[0] = part.astype(LOW)

    @pl.when(step >= 2)
    def _():
        keep_ref[0] = part


def norm_back(core, dq, dk, dv, q_weight, keyval_weight, hat):
    quarter, half, width = dq.shape[0] // 2, dq.shape[1], hat.shape[1]

    def at(i, s):
        return jnp.where(i < 2, 1 - s[0], s[0])

    def block(i, s):
        return (jnp.where(lax.rem(i, 2) == 0, 2, 0) + at(i, s), 0)

    whole = lambda i, s: (0, 0)
    line, short = pl.BlockSpec((1, width), whole), pl.BlockSpec((1, half), whole)
    shape = jax.ShapeDtypeStruct
    return pl.pallas_call(
        norm_back_kernel,
        out_shape=(
            shape((2, quarter, width), FULL),
            shape((2, quarter, width), LOW),
            shape((1, width), FULL),
            shape((1, width), FULL),
            shape((1, half), FULL),
            shape((1, half), FULL),
        ),
        grid_spec=pltpu.PrefetchScalarGridSpec(
            num_scalar_prefetch=1,
            grid=(4,),
            in_specs=[
                pl.BlockSpec((quarter, half), lambda i, s: (at(i, s), 0)),
                pl.BlockSpec((quarter, half), block),
                pl.BlockSpec((quarter, half), block),
                pl.BlockSpec((width, half), whole),
                pl.BlockSpec((width, 2 * half), whole),
                pl.BlockSpec((quarter, width), block),
            ],
            out_specs=(
                pl.BlockSpec((1, quarter, width), lambda i, s: (jnp.maximum(i - 2, 0), 0, 0)),
                pl.BlockSpec((1, quarter, width), lambda i, s: (jnp.minimum(i, 1), 0, 0)),
                line,
                line,
                short,
                short,
            ),
            scratch_shapes=[pltpu.VMEM((quarter, width), FULL)],
        ),
        compiler_params=pltpu.CompilerParams(vmem_limit_bytes=VMEM),
        cost_estimate=SHORT,
        name="norm_back",
    )(core, dq, dk, dv, q_weight, keyval_weight, hat)


def normalize(values):
    center = values - jnp.mean(values, -1, keepdims=True)
    spread = jnp.mean(center * center, -1, keepdims=True)
    root = lax.rsqrt(spread + 1e-05)
    return center * root, root


def normalize_back(grad, gain, hat, root):
    scaled = grad * gain
    return root * (
        scaled
        - jnp.mean(scaled, -1, keepdims=True)
        - hat * jnp.mean(scaled * hat, -1, keepdims=True)
    )


def shards(
    tokens,
    lengths,
    thought_pos,
    cotangent,
    qkv_weight,
    out_weight,
    fc_weight,
    proj_weight,
    qv_bias,
    out_bias,
    fc_bias,
    proj_bias,
    first_gain,
    first_shift,
    second_gain,
    second_shift,
):
    _, quarter, width = tokens.shape
    half = width // 2
    near = 2 * quarter
    slice_rows = qkv_weight.shape[0]
    count = 1 << flat_bits()
    plans = orders()
    core, second = bit_of(0), bit_of(1)
    far = (2 * second).astype(jnp.int32).reshape(1)

    high, hidden_width = proj_weight.shape[0], fc_weight.shape[1]
    blocks = hidden_width // width
    fc_rows = [fc_weight[:, i * width : (i + 1) * width] for i in range(blocks)]
    late = lax.all_gather(
        jnp.concatenate([proj_weight, *fc_rows, out_weight], 0), ALL, axis=0, tiled=True
    ).reshape(count, high + (blocks + 1) * slice_rows, width)

    mine = tokens[0]
    flips = [(i, i ^ 2) for i in range(count) if not i & 2]
    before = lax.ppermute(mine, ALL, flips)
    near_tokens = pair(mine, swap(mine, 0), core, 0).reshape(near, width)

    third = slice_rows * 4
    small = jnp.zeros((slice_rows, LANES), LOW)
    rows_of = (
        jnp.concatenate([qv_bias, out_bias, first_gain]),
        fc_bias,
        jnp.concatenate([proj_bias, first_shift, second_gain, second_shift]),
    )
    small = small.at[:3, :third].set(jnp.stack(rows_of))
    split = qkv_weight.reshape(slice_rows, 3, 2, half)
    keep = lax.dynamic_index_in_dim(split, core, 2, keepdims=False).reshape(slice_rows, 3 * half)
    send = lax.dynamic_index_in_dim(split, 1 - core, 2, keepdims=False).reshape(
        slice_rows, 3 * half
    )
    keep, send = jnp.concatenate([keep, small], 1), jnp.concatenate([send, small], 1)
    chip = pair(keep, swap(send, 0), core, 0).reshape(2 * slice_rows, 3 * half + LANES)
    block = gather_common(chip)
    parts = [
        jnp.concatenate([block[:, :, :half], block[:, :, 3 * half :]], 2),
        block[:, :, half : 3 * half],
    ]
    first_parts = gather_step(parts, plans, 0)

    before = after(before, block)
    far_tokens = pair(before, swap(before, 0), core, 0).reshape(near, width)
    slots = jnp.arange(near, dtype=jnp.int32)
    thoughts = thought_pos[0]

    def is_thought(at_slots):
        return jnp.any(thoughts[None, :] == at_slots[:, None], 1, keepdims=True)

    thought_near = is_thought(second * near + slots)
    thought_far = is_thought(slots)
    shifted_near = jnp.concatenate([far_tokens[-1:], near_tokens[:-1]], 0)
    shifted_far = jnp.concatenate([far_tokens[:1], far_tokens[:-1]], 0)
    inputs_near = jnp.where(thought_near, shifted_near, near_tokens)
    inputs_far = jnp.where(thought_far, shifted_far, far_tokens)
    inputs_all = jnp.concatenate([inputs_near, inputs_far], 0)
    hat_all, root_all = normalize(inputs_all.astype(FULL))
    own = core * quarter
    inputs = lax.dynamic_slice_in_dim(inputs_near, own, quarter, 0).astype(FULL)

    parts = gather_step(first_parts, plans, 1, (hat_all, root_all))
    q_weight = parts[0][:, :, :half].reshape(width, half)
    keyval_weight = parts[1].reshape(width, 2 * half)
    small = parts[0].reshape(count, slice_rows, half + LANES)[:, :3, half : half + third]
    small = small.astype(FULL)
    at = slice_rows

    def vector(row, first, size):
        return small[:, row, first : first + size].reshape(1, count * size)

    qv_full = vector(0, 0, 2 * at)
    out_bias_full, gain_one = vector(0, 2 * at, at), vector(0, 3 * at, at)
    fc_bias_full = vector(1, 0, 4 * at)
    proj_bias_full, shift_one = vector(2, 0, at), vector(2, at, at)
    gain_two, shift_two = vector(2, 2 * at, at), vector(2, 3 * at, at)

    normed = (hat_all * gain_one + shift_one).astype(LOW)
    own_half = core * half
    q_bias = lax.dynamic_slice_in_dim(qv_full[:, :width], own_half, half, 1)
    v_bias = lax.dynamic_slice_in_dim(qv_full[:, width:], own_half, half, 1)
    query = (dot(normed[:near], q_weight) + q_bias).astype(LOW)
    keyval_bias = jnp.concatenate([jnp.zeros((1, half), FULL), v_bias], 1)
    keyval = (dot(normed, keyval_weight) + keyval_bias).astype(LOW)

    def rows_to_core(array):
        return (
            lax.dynamic_slice_in_dim(array, own, quarter, 0),
            lax.dynamic_slice_in_dim(array, quarter - own, quarter, 0),
        )

    pairs = half // LANES
    heads = ()
    for which in range(pairs):
        heads = attend(far, query, keyval, quarter, which, heads)
    heads, logsums = heads
    keep, send = rows_to_core(heads)
    attended = beside(keep, swap(send, 0), core)
    late = after(late, attended)
    fc_full = late[:, high : high + blocks * slice_rows]
    fc_full = fc_full.reshape(count, blocks, slice_rows, width).transpose(0, 2, 1, 3)
    fc_full = fc_full.reshape(width, hidden_width)
    out_full = late[:, high + blocks * slice_rows :].reshape(width, width)

    middle = inputs + dot(attended, out_full) + out_bias_full
    hat_two, root_two = normalize(middle)
    normed_two = (hat_two * gain_two + shift_two).astype(LOW)
    my_slots = (2 * second + core) * quarter + jnp.arange(quarter, dtype=jnp.int32)
    valid = (my_slots < lengths[0])[:, None]
    grad_valid = jnp.where(valid, cotangent[0], jnp.zeros_like(cotangent[0]))
    proj_full, proj_rows = late, high
    if high % 16:
        proj_full, proj_rows = late[:, :high].reshape(1, hidden_width, width), hidden_width // 4
        proj_full = proj_full.reshape(4, proj_rows, width)
    core_at = core.astype(jnp.int32).reshape(1)
    fed, grad_normed_two, fc_grads, proj_grads, fc_bias_grad = feed(
        core_at, normed_two, grad_valid, fc_full, fc_bias_full, proj_full, proj_rows
    )
    fc_bias_grad = fc_bias_grad[0]
    output = middle + fed + proj_bias_full
    mixed = jnp.where(valid, output, 0.0).astype(LOW)[None]
    proj_bias_grad = jnp.sum(grad_valid.astype(FULL), 0)

    chips = count // 2
    fc_shape = (chips, 2 * slice_rows, hidden_width // 2)
    fc_pair = [fc_grads[1].reshape(fc_shape), swap(fc_grads[0], 0).reshape(fc_shape)]

    turned = turn(
        core_at, grad_normed_two, hat_two, root_two, gain_two, grad_valid, attended, out_full
    )
    grad_middle, keep, send, out_kept, out_send = turned[:5]
    second_gain_grad, second_shift_grad, out_bias_grad = (value[0] for value in turned[5:])
    grad_heads = pair(keep, swap(send, 0), core, 0).reshape(near, half)
    out_shape = (chips, 2 * slice_rows, half)
    proj_shape = (chips, 2 * high, half)
    proj_kept, proj_send = (
        jnp.concatenate(
            [grad.reshape(proj_shape), other.reshape(out_shape)], 1
        )
        for grad, other in ((proj_grads[1], out_kept), (proj_grads[0], out_send))
    )
    proj_pair = [proj_kept, swap(proj_send, 0)]
    early = [start_sum(fc_pair, 0, hidden_width // 2), start_sum(proj_pair, 0, half)]
    early_plans = plans
    ready = prepare(early, early_plans, 0)

    grads = ()
    now = after(grad_heads, *sends(ready))
    for which in range(pairs):
        if which == 2:
            ready = prepare(exchange(ready, grads), early_plans, 1)
            now = after(grad_heads, *sends(ready))
        grads = attend_back(
            far, query, keyval, now, heads, logsums, which, grads
        )
    ready = prepare(exchange(ready, grads), early_plans, 2)
    grad_query, grad_key, grad_value = after(grads, *sends(ready))

    last = [
        start_sum([value.reshape(chips, 2 * slice_rows, -1)], 0, value.shape[1])
        for value in qkv_grads(normed, grad_query, grad_key, grad_value)
    ]
    last_ready = prepare(last, plans, 0)

    part, part_send, first_gain_grad, first_shift_grad, q_sum, v_sum = norm_back(
        core_at,
        after(grad_query, *sends(last_ready)),
        grad_key,
        grad_value,
        q_weight,
        keyval_weight,
        hat_all,
    )
    got = swap(part_send, 0)
    ready = prepare(exchange(ready, (part_send,)), early_plans, 3)
    last = exchange(last_ready, (part_send,))
    last_ready = prepare(last, plans, 1)
    got = after(got, *sends(last_ready), *sends(ready))
    far_sum = (part[0] + got[0].astype(FULL)).astype(LOW)
    back = lax.ppermute(far_sum, ALL, [(b, a) for a, b in flips])
    first_gain_grad, first_shift_grad, q_sum, v_sum = (
        value[0] for value in (first_gain_grad, first_shift_grad, q_sum, v_sum)
    )
    zero = jnp.zeros((half,), FULL)
    low_core = core == 0
    qv_bias_grad = jnp.concatenate(
        [
            jnp.where(low_core, q_sum, zero),
            jnp.where(low_core, zero, q_sum),
            jnp.where(low_core, v_sum, zero),
            jnp.where(low_core, zero, v_sum),
        ]
    )
    grads = (
        qv_bias_grad,
        out_bias_grad,
        fc_bias_grad,
        proj_bias_grad,
        first_gain_grad,
        first_shift_grad,
        second_gain_grad,
        second_shift_grad,
    )
    sizes = [grad.shape[0] // count for grad in grads]
    packed = jnp.concatenate([g.reshape(count, s) for g, s in zip(grads, sizes)], 1)
    share = jnp.sum(lax.all_to_all(packed, ALL, 0, 0, tiled=True), 0, keepdims=True)
    for step in range(2, flat_bits() - 1):
        last = exchange(last_ready, (far_sum,))
        last_ready = prepare(last, plans, step)
    last = exchange(last_ready)
    for step in range(4, flat_bits() - 1):
        ready = prepare(exchange(ready), early_plans, step)
    early = exchange(ready, (far_sum,))
    fc_total, proj_total = (value.total()[0] for value in early)
    fc_weight_grad = jnp.concatenate(finish(fc_total, slice_rows), 1)

    def by_core(total):
        mine = lax.dynamic_slice_in_dim(total, core * (total.shape[0] // 2), total.shape[0] // 2, 0)
        return mine

    def by_other(total):
        size = total.shape[0] // 2
        return lax.dynamic_slice_in_dim(total, (1 - core) * size, size, 0)

    proj_part, out_part = proj_total[: 2 * high], proj_total[2 * high :]
    mine = jnp.concatenate([by_core(proj_part), by_core(out_part)], 0)
    other = swap(jnp.concatenate([by_other(proj_part), by_other(out_part)], 0), 0)
    both = beside(mine, other, core)
    proj_weight_grad, out_weight_grad = both[:high], both[high:]
    sides = finish(jnp.concatenate([value.total()[0] for value in last], 1), slice_rows)
    qkv_weight_grad = jnp.concatenate(
        [
            side[:, kind * half : (kind + 1) * half]
            for kind in range(3)
            for side in sides
        ],
        1,
    )

    grad_normed = part[1] + got[1].astype(FULL) + back.astype(FULL)
    hat = lax.dynamic_slice_in_dim(hat_all, own, quarter, 0)
    root = lax.dynamic_slice_in_dim(root_all, own, quarter, 0)
    grad_inputs = grad_middle + normalize_back(grad_normed, gain_one, hat, root)
    thought = lax.dynamic_slice_in_dim(thought_near, own, quarter, 0)
    kept = jnp.where(thought, 0.0, grad_inputs)
    moved = jnp.where(thought, grad_inputs, 0.0)
    ctx = lax.axis_size("ctx")
    following = lax.ppermute(moved[:1], "ctx", [(i, i - 1) for i in range(1, ctx)])
    tokens_grad = (kept + jnp.concatenate([moved[1:], following], 0))[None]

    shares, at = [], 0
    for size in sizes:
        shares.append(share[0, at : at + size])
        at += size
    return (
        mixed,
        tokens_grad,
        qkv_weight_grad,
        out_weight_grad,
        fc_weight_grad,
        proj_weight_grad,
        *shares,
    )


def solution(mesh):
    rows, matrix, vector = P("dp", "ctx", None), P(ALL, None), P(ALL)
    return jax.shard_map(
        shards,
        mesh=mesh,
        in_specs=(rows, P("dp"), P("dp", None), rows) + (matrix,) * 4 + (vector,) * 8,
        out_specs=(rows, rows) + (matrix,) * 4 + (vector,) * 8,
        check_vma=False,
    )
```

time: 470 us -> 342 us (0.73)
  matrix products: 73.3 us -> 4.67 us
  starting transfers between devices: 140 us -> 78.6 us
  Pallas kernels: 28 us -> 72.6 us
  waiting for transfers between devices: 102 us -> 60.2 us
  other arithmetic: 37.1 us -> 50.3 us
  local copies, waits for them, and re-layouts: 65.8 us -> 53.5 us
    ppermute x64 -> x33, starting transfers between devices: 128 us -> 56.8 us  [swap(): return lax.ppermute(value, ALL, [(i, i ^ 1 << bit) for i in range(count)])]
    dot_general x15 -> x0, matrix products: 53.9 us -> none  [the longest x9 28.4 us: dot_tn(): lax.dot_general(a, b, (((0,), (0,)), ((), ())), preferred_element_type=FULL)]
    ppermute x64 -> x33, waiting for transfers between devices: 93.8 us -> 42.2 us  [swap(): return lax.ppermute(value, ALL, [(i, i ^ 1 << bit) for i in range(count)])]
    pallas_call x0 -> x4, Pallas kernels: none -> 41.6 us  [the longest x1 21 us: feed(): pl.pallas_call(feed_kernel, out_shape=(jax.ShapeDtypeStruct((rows, width)...]
    dynamic_update_slice x53 -> x10, local copies, waits for them, and re-layouts: 19.9 us -> 0.37 us  [pair(): lax.dynamic_update_slice_in_dim(whole, jnp.expand_dims(other, axis), 1 -...]
    dot_general x6 -> x3, matrix products: 19.4 us -> 4.67 us  [dot(): lax.dot_general(a, b, (((1,), (0,)), ((), ())), preferred_element_type=FULL)]
    all_to_all x0 -> x1, starting transfers between devices: none -> 13.1 us  [shards(): lax.all_to_all(packed, ALL, 0, 0, tiled=True)]
    convert_element_type x20 -> x17, other arithmetic: 9.53 us -> 21.2 us  [the longest x14 16 us: prepare(): send = self.total(bit, 1 - bit_of(bit)).astype(self.kind)]
  transfers between devices with their start and end apart: 68 -> 38, of which waited for: 28 -> 16; matrix products, arithmetic and copies ran while one was open for 27% -> 20% of each run, Pallas kernels for 6% -> 14%
where the time goes in v2:
time: 342 us; the launch traced here: 337 us
  starting transfers between devices  78.6 us (23%)
  Pallas kernels  72.6 us (21%)
  waiting for transfers between devices  60.2 us (18%)
  local copies, waits for them, and re-layouts  53.5 us (16%)
  other arithmetic  50.3 us (15%)
  between operations  16.6 us (5%)
  matrix products  4.67 us (1%)
    ppermute x33, starting transfers between devices, swap(): return lax.ppermute(value, ALL, [(i, i ^ 1 << bit) for i in range(count)])  56.8 us
    ppermute x33, waiting for transfers between devices, swap(): return lax.ppermute(value, ALL, [(i, i ^ 1 << bit) for i in range(count)])  42.2 us
    pallas_call x1, Pallas kernels, feed(): pl.pallas_call(feed_kernel, out_shape=(jax.ShapeDtypeStruct((rows, width)...  21 us
    pallas_call x3, Pallas kernels, attend_back(): pl.pallas_call(attend_back_kernel, out_shape=(jax.ShapeDtypeStruct((near,...  19.8 us
    unnamed x143, local copies, waits for them, and re-layouts  18.9 us
    convert_element_type x14, other arithmetic, prepare(): send = self.total(bit, 1 - bit_of(bit)).astype(self.kind)  16 us
    all_to_all x1, starting transfers between devices, shards(): lax.all_to_all(packed, ALL, 0, 0, tiled=True)  13.1 us
    pallas_call x3, Pallas kernels, attend(): pl.pallas_call(attend_kernel, out_shape=(jax.ShapeDtypeStruct((near, widt...  11.2 us
  transfers between devices with their start and end apart: 38, of which 16 were waited for; matrix products, arithmetic and copies ran while one was open for 20% of the time, Pallas kernels for 14%

profile of v2, /device:TPU:1, one launch (start us, length us, event | category | flops | bytes accessed | tf_op | source)
XLA Modules:
  0.0 336.5 jit_solution(7522166173995212550)
XLA Ops:
  16.2 3.5 %collective-permute-start.2 = (bf16[1,48,1280]{2,1,0:T(8,128)(2,1)S(1)}, bf16[1,48,1280]{2,1,0:T(8,128)(2,1)S(1)}, u32[]{:S(2)}, u32[]{:S(2)}) collective-permute-start(bf16[1,48,1280]{2,1,0:T(8,128)(2,1)S(1)} %bitcast.364), channel_id=1, source_target_pairs={{0,16},{1,17},{2,18},{3,19},{4,20},{5,21},{6,22},{7,23},{8,24},{9,... | collective-permute-start | bytes 368648 | tf_op jit(solution)/shard_map/ppermute | solution.py:32
  19.7 6.0 %collective-permute-done.2 = bf16[1,48,1280]{2,1,0:T(8,128)(2,1)S(1)} collective-permute-done((bf16[1,48,1280]{2,1,0:T(8,128)(2,1)S(1)}, bf16[1,48,1280]{2,1,0:T(8,128)(2,1)S(1)}, u32[]{:S(2)}, u32[]{:S(2)}) %collective-permute-start.2) | collective-permute-done | bytes 122912 | tf_op jit(solution)/shard_map/ppermute | solution.py:32
  26.9 3.6 %collective-permute-start = (bf16[512,768]{1,0:T(8,128)(2,1)S(1)}, bf16[512,768]{1,0:T(8,128)(2,1)}, u32[]{:S(2)}, u32[]{:S(2)}) collective-permute-start(bf16[512,768]{1,0:T(8,128)(2,1)S(1)} %bitcast.360), channel_id=1, source_target_pairs={{0,2},{1,3},{4,6},{5,7},{8,10},{9,11},{12,14},{13,15},{16,18},{17,... | collective-permute-start | bytes 2359304 | tf_op jit(solution)/shard_map/ppermute | solution.py:640
  32.6 5.7 %collective-permute-done.3 = bf16[2,48,1280]{2,1,0:T(8,128)(2,1)S(1)} collective-permute-done((bf16[2,48,1280]{2,1,0:T(8,128)(2,1)S(1)}, bf16[2,48,1280]{2,1,0:T(8,128)(2,1)S(1)}, u32[]{:S(2)}, u32[]{:S(2)}) %collective-permute-start.3) | collective-permute-done | bytes 245792 | tf_op jit(solution)/shard_map/ppermute | solution.py:32
  41.3 3.5 %collective-permute-done = bf16[512,768]{1,0:T(8,128)(2,1)} collective-permute-done((bf16[512,768]{1,0:T(8,128)(2,1)S(1)}, bf16[512,768]{1,0:T(8,128)(2,1)}, u32[]{:S(2)}, u32[]{:S(2)}) %collective-permute-start) | collective-permute-done | bytes 786464 | tf_op jit(solution)/shard_map/ppermute | solution.py:640
  44.8 8.9 %collective-permute-start.4 = (bf16[512,768]{1,0:T(8,128)(2,1)}, bf16[512,768]{1,0:T(8,128)(2,1)S(1)}, u32[]{:S(2)}, u32[]{:S(2)}) collective-permute-start(bf16[512,768]{1,0:T(8,128)(2,1)} %collective-permute-done), channel_id=1, source_target_pairs={{0,1},{1,0},{2,3},{3,2},{4,5},{5,4},{6,7},{7,6},{8,9},{9,8},{10,11... | collective-permute-start | bytes 2359304 | tf_op jit(solution)/shard_map/ppermute | solution.py:32
  61.6 3.2 fusion.2
  64.7 3.6 %fusion.hat_ref = f32[2048,768]{1,0:T(8,128)} fusion(f32[2048]{0:T(1024)S(1)} %add_rsqrt_fusion, f32[2048]{0:T(1024)S(1)} %broadcast_multiply_fusion, bf16[1024,768]{1,0:T(8,128)(2,1)S(1)} %maximum_select_fusion.1, bf16[1024,768]{1,0:T(8,128)(2,1)S(1)} %maximum_select_fusion), kind=kLoop, calls=%fused_computation.2 | loop fusion | flops 9437184 | bytes 9453568 | tf_op jit(solution)/shard_map/mul | solution.py:592
  77.0 2.8 add_convert_fusion.k_ref.v_ref
  79.9 3.6 %attend.3 = (bf16[1024,384]{1,0:T(8,128)(2,1)S(1)}, f32[3,8,1024]{2,1,0:T(8,128)S(1)}) custom-call(s32[1]{0:T(128)} %bitcast.15.far_ref, bf16[1024,384]{1,0:T(8,128)(2,1)S(1)} %add_convert_fusion.6.q_ref, bf16[2048,768]{1,0:T(8,128)(2,1)S(1)} %add_convert_fusion.k_ref.v_ref, bf16[2048,768]{1,0:T(8,128)(2,1)S(1)} %add_convert_fusion.k_ref.v_ref), custom_call_target="tpu_custom_call" | custom-call | flops 536870912 | bytes 524288 | tf_op jit(solution)/shard_map/attend/pallas_call | solution.py:212
  83.4 3.6 %attend.4 = (bf16[1024,384]{1,0:T(8,128)(2,1)S(1)}, f32[3,8,1024]{2,1,0:T(8,128)S(1)}) custom-call(s32[1]{0:T(128)} %bitcast.15.far_ref, bf16[1024,384]{1,0:T(8,128)(2,1)S(1)} %add_convert_fusion.6.q_ref, bf16[2048,768]{1,0:T(8,128)(2,1)S(1)} %add_convert_fusion.k_ref.v_ref, ...), custom_call_target="tpu_custom_call", output_to_operand_aliasing={{0}: (4, {}), {1}: (5, {})} | custom-call | flops 536870912 | bytes 524288 | tf_op jit(solution)/shard_map/attend/pallas_call | solution.py:212
  87.1 4.0 %attend.5 = (bf16[1024,384]{1,0:T(8,128)(2,1)S(1)}, f32[3,8,1024]{2,1,0:T(8,128)S(1)}) custom-call(s32[1]{0:T(128)} %bitcast.15.far_ref, bf16[1024,384]{1,0:T(8,128)(2,1)S(1)} %add_convert_fusion.6.q_ref, bf16[2048,768]{1,0:T(8,128)(2,1)S(1)} %add_convert_fusion.k_ref.v_ref, ...), custom_call_target="tpu_custom_call", output_to_operand_aliasing={{0}: (4, {}), {1}: (5, {})} | custom-call | flops 536870912 | bytes 524288 | tf_op jit(solution)/shard_map/attend/pallas_call | solution.py:212
  92.7 2.9 collective-permute-start.10
  99.1 9.9 %all-gather.2.cloned.1.call-done = bf16[6912,768]{1,0:T(8,128)(2,1)} async-done(((bf16[216,768]{1,0:T(8,128)(2,1)}), bf16[6912,768]{1,0:T(8,128)(2,1)}) %all-gather.2.cloned.1.call-update) | async-done | bytes 10616848 | tf_op jit(solution)/shard_map/all_gather | solution.py:634
  115.3 3.3 copy.176
  121.4 21.0 %feed.1 = (f32[512,768]{1,0:T(8,128)S(1)}, f32[512,768]{1,0:T(8,128)S(1)}, bf16[2,768,1536]{2,1,0:T(8,128)(2,1)}, bf16[2,3072,384]{2,1,0:T(8,128)(2,1)}, f32[1,3072]{1,0:T(1,128)S(1)}) custom-call(s32[1]{0:T(128)} %bitcast.31.core_ref, bf16[512,768]{1,0:T(8,128)(2,1)S(1)} %get-tuple-element.169.n_ref, bf16[512,768]{1,0:T(8,128)(2,1)S(1)} %get-tuple-element.165.g_ref, ...), custom_call_target="tpu_custom_call" | custom-call | flops 536870912 | bytes 524288 | tf_op jit(solution)/shard_map/feed/pallas_call | solution.py:423
  142.4 6.1 %fusion.64 = (bf16[1,3072,384]{2,1,0:T(8,128)(2,1)}, bf16[1,3072,384]{2,1,0:T(8,128)(2,1)}) fusion(bf16[2,3072,384]{2,1,0:T(8,128)(2,1)} %get-tuple-element.102), kind=kLoop, calls=%fused_computation.225 | loop fusion | bytes 9437184 | tf_op jit(solution)/shard_map/slice | solution.py:762
  151.5 4.6 %turn.1 = (f32[512,768]{1,0:T(8,128)}, bf16[512,384]{1,0:T(8,128)(2,1)S(1)}, bf16[512,384]{1,0:T(8,128)(2,1)}, bf16[768,384]{1,0:T(8,128)(2,1)S(1)}, bf16[768,38...) custom-call(s32[1]{0:T(128)} %bitcast.31.core_ref, ...), custom_call_target="tpu_custom_call" | custom-call | flops 536870912 | bytes 524288 | tf_op jit(solution)/shard_map/turn/pallas_call | solution.py:486
  160.5 6.2 %collective-permute-done.12 = bf16[768,1536]{1,0:T(8,128)(2,1)S(1)} collective-permute-done((bf16[768,1536]{1,0:T(8,128)(2,1)S(1)}, bf16[768,1536]{1,0:T(8,128)(2,1)S(1)}, u32[]{:S(2)}, u32[]{:S(2)}) %collective-permute-start.12) | collective-permute-done | bytes 2359328 | tf_op jit(solution)/shard_map/ppermute | solution.py:32
  168.4 4.8 %collective-permute-start.13 = (bf16[8,48,1536]{2,1,0:T(8,128)(2,1)}, bf16[8,48,1536]{2,1,0:T(8,128)(2,1)}, u32[]{:S(2)}, u32[]{:S(2)}) collective-permute-start(bf16[8,48,1536]{2,1,0:T(8,128)(2,1)} %bitcast.43), channel_id=1, source_target_pairs={{0,2},{1,3},{2,0},{3,1},{4,6},{5,7},{6,4},{7,5},{8,10},{9,11},{10,... | collective-permute-start | bytes 3538952 | tf_op jit(solution)/shard_map/ppermute | solution.py:32
  183.3 6.6 %attend_back.3 = (bf16[1024,384]{1,0:T(8,128)(2,1)S(1)}, bf16[2048,384]{1,0:T(8,128)(2,1)S(1)}, bf16[2048,384]{1,0:T(8,128)(2,1)}) custom-call(s32[1]{0:T(128)} %bitcast.15.far_ref, bf16[1024,384]{1,0:T(8,128)(2,1)S(1)} %copy-done.2, bf16[2048,768]{1,0:T(8,128)(2,1)} %copy-done, bf16[2048,768]{1,0:T(8,128)(2,1)} %copy-done, bf16[1024,384]{1,0:T(8,128)(2,1)S(1)} %bitcast.299, ...), custom_call_target="tpu_custom_call" | custom-call | flops 536870912 | bytes 524288 | tf_op jit(solution)/shard_map/attend_back/pallas_call | solution.py:304
  189.9 6.4 %attend_back.4 = (bf16[1024,384]{1,0:T(8,128)(2,1)S(1)}, bf16[2048,384]{1,0:T(8,128)(2,1)S(1)}, bf16[2048,384]{1,0:T(8,128)(2,1)}) custom-call(s32[1]{0:T(128)} %bitcast.15.far_ref, bf16[1024,384]{1,0:T(8,128)(2,1)S(1)} %copy-done.2, bf16[2048,768]{1,0:T(8,128)(2,1)} %copy-done, ...), custom_call_target="tpu_custom_call", output_to_operand_aliasing={{0}: (7, {}), {1}: (8, {}), {2}: (9, {})} | custom-call | flops 536870912 | bytes 524288 | tf_op jit(solution)/shard_map/attend_back/pallas_call | solution.py:304
  196.3 3.3 collective-permute-done.13
  203.9 7.2 %collective-permute-done.15 = bf16[8,240,384]{2,1,0:T(8,128)(2,1)S(1)} collective-permute-done((bf16[8,240,384]{2,1,0:T(8,128)(2,1)S(1)}, bf16[8,240,384]{2,1,0:T(8,128)(2,1)S(1)}, u32[]{:S(2)}, u32[]{:S(2)}) %collective-permute-start.15) | collective-permute-done | bytes 1474592 | tf_op jit(solution)/shard_map/ppermute | solution.py:32
  218.5 3.1 fusion.12
  221.6 6.8 %attend_back.5 = (bf16[1024,384]{1,0:T(8,128)(2,1)S(1)}, bf16[2048,384]{1,0:T(8,128)(2,1)S(1)}, bf16[2048,384]{1,0:T(8,128)(2,1)}) custom-call(s32[1]{0:T(128)} %bitcast.15.far_ref, bf16[1024,384]{1,0:T(8,128)(2,1)S(1)} %copy-done.2, bf16[2048,768]{1,0:T(8,128)(2,1)} %copy-done, ...), custom_call_target="tpu_custom_call", output_to_operand_aliasing={{0}: (7, {}), {1}: (8, {}), {2}: (9, {})} | custom-call | flops 536870912 | bytes 524288 | tf_op jit(solution)/shard_map/attend_back/pallas_call | solution.py:304
  234.3 6.1 %qkv_grads.1 = (bf16[768,640]{1,0:T(8,128)(2,1)S(1)}, bf16[768,512]{1,0:T(8,128)(2,1)S(1)}) custom-call(bf16[2048,768]{1,0:T(8,128)(2,1)} %copy-done.33, bf16[1024,384]{1,0:T(8,128)(2,1)S(1)} %get-tuple-element.126.dq_ref, bf16[2048,384]{1,0:T(8,128)(2,1)S(1)} %get-tuple-element.122.dk_ref, bf16[2048,384]{1,0:T(8,128)(2,1)S(1)} %copy-done.5), custom_call_target="tpu_custom_call" | custom-call | flops 536870912 | bytes 524288 | tf_op jit(solution)/shard_map/qkv_grads/pallas_call | solution.py:353
  243.6 7.0 %collective-permute-start.19 = (bf16[8,48,640]{2,1,0:T(8,128)(2,1)}, bf16[8,48,640]{2,1,0:T(8,128)(2,1)}, u32[]{:S(2)}, u32[]{:S(2)}) collective-permute-start(bf16[8,48,640]{2,1,0:T(8,128)(2,1)} %bitcast.64), channel_id=1, source_target_pairs={{0,2},{1,3},{2,0},{3,1},{4,6},{5,7},{6,4},{7,5},{8,10},{9,11},{10,... | collective-permute-start | bytes 1474568 | tf_op jit(solution)/shard_map/ppermute | solution.py:32
  250.6 9.9 %norm_back.1 = (f32[2,512,768]{2,1,0:T(8,128)}, bf16[2,512,768]{2,1,0:T(8,128)(2,1)S(1)}, f32[1,768]{1,0:T(1,128)S(1)}, f32[1,768]{1,0:T(1,128)S(1)}, f32[1,384]{1,0:T(1,128)S(1)}, /*index=5*/f32[1,384]{1,0:T(1,128)S(1)}) custom-call(s32[1]{0:T(128)} %bitcast.31.core_ref, bf16[1024,384]{1,0:T(8,128)(2,1)S(1)} %get-tuple-element.126.dq_ref, ...), custom_call_target="tpu_custom_call" | custom-call | flops 536870912 | bytes 524288 | tf_op jit(solution)/shard_map/norm_back/pallas_call | solution.py:551
  263.8 13.1 %all-to-all-start = ((f32[32,1,288]{2,1,0:T(1,128)}), f32[32,1,288]{2,1,0:T(1,128)S(1)}, u32[]{:S(2)}, u32[]{:S(2)}) async-start(f32[32,1,288]{2,1,0:T(1,128)} %all_to_all.6), calls=%async_computation | async-start | bytes 98304 | tf_op jit(solution)/shard_map/all_to_all | solution.py:828
  291.1 7.3 %collective-permute-done.32 = bf16[1,240,384]{2,1,0:T(8,128)(2,1)S(1)} collective-permute-done((bf16[1,240,384]{2,1,0:T(8,128)(2,1)S(1)}, bf16[1,240,384]{2,1,0:T(8,128)(2,1)S(1)}, u32[]{:S(2)}, u32[]{:S(2)}) %collective-permute-start.32) | collective-permute-done | bytes 184352 | tf_op jit(solution)/shard_map/ppermute | solution.py:32
  322.8 3.2 collective-permute-start.24
  (360 shorter events, 128.8 us)
Async XLA Ops:
  7.3 101.7 %all-gather.2.cloned.1.call-start = ((), (), s32[]{:S(2)}) async-start(), calls=%async_computation.1 | async-start | bytes 10948608 | tf_op jit(solution)/shard_map/all_gather | solution.py:634
  16.2 9.6 %collective-permute-start.2 = (bf16[1,48,1280]{2,1,0:T(8,128)(2,1)S(1)}, bf16[1,48,1280]{2,1,0:T(8,128)(2,1)S(1)}, u32[]{:S(2)}, u32[]{:S(2)}) collective-permute-start(bf16[1,48,1280]{2,1,0:T(8,128)(2,1)S(1)} %bitcast.364), channel_id=1, source_target_pairs={{0,16},{1,17},{2,18},{3,19},{4,20},{5,21},{6,22},{7,23},{8,24},{9,... | collective-permute-start | bytes 368648 | tf_op jit(solution)/shard_map/ppermute | solution.py:32
  25.8 12.5 %collective-permute-start.3 = (bf16[2,48,1280]{2,1,0:T(8,128)(2,1)S(1)}, bf16[2,48,1280]{2,1,0:T(8,128)(2,1)S(1)}, u32[]{:S(2)}, u32[]{:S(2)}) collective-permute-start(bf16[2,48,1280]{2,1,0:T(8,128)(2,1)S(1)} %constant_dynamic-update-slice_fusion.3), channel_id=1, source_target_pairs={{0,8},{1,9},{2,10},{3,11},{4,12},{5,13},{6,14},{7,15},{8,0},{9,1},... | collective-permute-start | bytes 737288 | tf_op jit(solution)/shard_map/ppermute | solution.py:32
  26.9 17.8 %collective-permute-start = (bf16[512,768]{1,0:T(8,128)(2,1)S(1)}, bf16[512,768]{1,0:T(8,128)(2,1)}, u32[]{:S(2)}, u32[]{:S(2)}) collective-permute-start(bf16[512,768]{1,0:T(8,128)(2,1)S(1)} %bitcast.360), channel_id=1, source_target_pairs={{0,2},{1,3},{4,6},{5,7},{8,10},{9,11},{12,14},{13,15},{16,18},{17,... | collective-permute-start | bytes 2359304 | tf_op jit(solution)/shard_map/ppermute | solution.py:640
  30.6 27.6 %collective-permute-start.5 = (bf16[512,768]{1,0:T(8,128)(2,1)S(1)}, bf16[512,768]{1,0:T(8,128)(2,1)S(1)}, u32[]{:S(2)}, u32[]{:S(2)}) collective-permute-start(bf16[512,768]{1,0:T(8,128)(2,1)S(1)} %bitcast.361), channel_id=1, source_target_pairs={{0,1},{1,0},{2,3},{3,2},{4,5},{5,4},{6,7},{7,6},{8,9},{9,8},{10,11... | collective-permute-start | bytes 2359304 | tf_op jit(solution)/shard_map/ppermute | solution.py:32
  38.5 16.0 %collective-permute-start.6 = (bf16[4,48,512]{2,1,0:T(8,128)(2,1)S(1)}, bf16[4,48,512]{2,1,0:T(8,128)(2,1)S(1)}, u32[]{:S(2)}, u32[]{:S(2)}) collective-permute-start(bf16[4,48,512]{2,1,0:T(8,128)(2,1)S(1)} %pad_maximum_fusion.5), channel_id=1, source_target_pairs={{0,4},{1,5},{2,6},{3,7},{4,0},{5,1},{6,2},{7,3},{8,12},{9,13},{10,... | collective-permute-start | bytes 589832 | tf_op jit(solution)/shard_map/ppermute | solution.py:32
  39.7 17.2 %collective-permute-start.8 = (bf16[4,48,768]{2,1,0:T(8,128)(2,1)S(1)}, bf16[4,48,768]{2,1,0:T(8,128)(2,1)S(1)}, u32[]{:S(2)}, u32[]{:S(2)}) collective-permute-start(bf16[4,48,768]{2,1,0:T(8,128)(2,1)S(1)} %slice.251), channel_id=1, source_target_pairs={{0,2},{1,3},{2,0},{3,1},{4,6},{5,7},{6,4},{7,5},{8,10},{9,11},{10,... | collective-permute-start | bytes 884744 | tf_op jit(solution)/shard_map/ppermute | solution.py:32
  44.8 13.6 %collective-permute-start.4 = (bf16[512,768]{1,0:T(8,128)(2,1)}, bf16[512,768]{1,0:T(8,128)(2,1)S(1)}, u32[]{:S(2)}, u32[]{:S(2)}) collective-permute-start(bf16[512,768]{1,0:T(8,128)(2,1)} %collective-permute-done), channel_id=1, source_target_pairs={{0,1},{1,0},{2,3},{3,2},{4,5},{5,4},{6,7},{7,6},{8,9},{9,8},{10,11... | collective-permute-start | bytes 2359304 | tf_op jit(solution)/shard_map/ppermute | solution.py:32
  54.5 15.1 %collective-permute-start.7 = (bf16[8,48,512]{2,1,0:T(8,128)(2,1)S(1)}, bf16[8,48,512]{2,1,0:T(8,128)(2,1)S(1)}, u32[]{:S(2)}, u32[]{:S(2)}) collective-permute-start(bf16[8,48,512]{2,1,0:T(8,128)(2,1)S(1)} %bitcast.353), channel_id=1, source_target_pairs={{0,2},{1,3},{2,0},{3,1},{4,6},{5,7},{6,4},{7,5},{8,10},{9,11},{10,... | collective-permute-start | bytes 1179656 | tf_op jit(solution)/shard_map/ppermute | solution.py:32
  57.0 12.6 %collective-permute-start.9 = (bf16[8,48,768]{2,1,0:T(8,128)(2,1)S(1)}, bf16[8,48,768]{2,1,0:T(8,128)(2,1)S(1)}, u32[]{:S(2)}, u32[]{:S(2)}) collective-permute-start(bf16[8,48,768]{2,1,0:T(8,128)(2,1)S(1)} %bitcast.343), channel_id=1, source_target_pairs={{0,4},{1,5},{2,6},{3,7},{4,0},{5,1},{6,2},{7,3},{8,12},{9,13},{10,... | collective-permute-start | bytes 1769480 | tf_op jit(solution)/shard_map/ppermute | solution.py:32
  157.9 16.0 %collective-permute-start.14 = (bf16[16,240,384]{2,1,0:T(8,128)(2,1)}, bf16[16,240,384]{2,1,0:T(8,128)(2,1)}, u32[]{:S(2)}, u32[]{:S(2)}) collective-permute-start(bf16[16,240,384]{2,1,0:T(8,128)(2,1)} %pad_maximum_fusion.1), channel_id=1, source_target_pairs={{0,1},{1,0},{2,3},{3,2},{4,5},{5,4},{6,7},{7,6},{8,9},{9,8},{10,11... | collective-permute-start | bytes 8847368 | tf_op jit(solution)/shard_map/ppermute | solution.py:32
  160.1 6.6 %collective-permute-start.12 = (bf16[768,1536]{1,0:T(8,128)(2,1)S(1)}, bf16[768,1536]{1,0:T(8,128)(2,1)S(1)}, u32[]{:S(2)}, u32[]{:S(2)}) collective-permute-start(bf16[768,1536]{1,0:T(8,128)(2,1)S(1)} %get-tuple-element.174), channel_id=1, source_target_pairs={{0,1},{1,0},{2,3},{3,2},{4,5},{5,4},{6,7},{7,6},{8,9},{9,8},{10,11... | collective-permute-start | bytes 7077896 | tf_op jit(solution)/shard_map/ppermute | solution.py:32
  168.4 31.2 %collective-permute-start.13 = (bf16[8,48,1536]{2,1,0:T(8,128)(2,1)}, bf16[8,48,1536]{2,1,0:T(8,128)(2,1)}, u32[]{:S(2)}, u32[]{:S(2)}) collective-permute-start(bf16[8,48,1536]{2,1,0:T(8,128)(2,1)} %bitcast.43), channel_id=1, source_target_pairs={{0,2},{1,3},{2,0},{3,1},{4,6},{5,7},{6,4},{7,5},{8,10},{9,11},{10,... | collective-permute-start | bytes 3538952 | tf_op jit(solution)/shard_map/ppermute | solution.py:32
  173.3 5.2 %collective-permute-start.11 = (bf16[512,384]{1,0:T(8,128)(2,1)}, bf16[512,384]{1,0:T(8,128)(2,1)S(1)}, u32[]{:S(2)}, u32[]{:S(2)}) collective-permute-start(bf16[512,384]{1,0:T(8,128)(2,1)} %get-tuple-element.100), channel_id=1, source_target_pairs={{0,1},{1,0},{2,3},{3,2},{4,5},{5,4},{6,7},{7,6},{8,9},{9,8},{10,11... | collective-permute-start | bytes 1179656 | tf_op jit(solution)/shard_map/ppermute | solution.py:32
  176.2 34.9 %collective-permute-start.15 = (bf16[8,240,384]{2,1,0:T(8,128)(2,1)S(1)}, bf16[8,240,384]{2,1,0:T(8,128)(2,1)S(1)}, u32[]{:S(2)}, u32[]{:S(2)}) collective-permute-start(bf16[8,240,384]{2,1,0:T(8,128)(2,1)S(1)} %bitcast.355), channel_id=1, source_target_pairs={{0,4},{1,5},{2,6},{3,7},{4,0},{5,1},{6,2},{7,3},{8,12},{9,13},{10,... | collective-permute-start | bytes 4423688 | tf_op jit(solution)/shard_map/ppermute | solution.py:32
  201.7 26.7 %collective-permute-start.16 = (bf16[4,48,1536]{2,1,0:T(8,128)(2,1)}, bf16[4,48,1536]{2,1,0:T(8,128)(2,1)}, u32[]{:S(2)}, u32[]{:S(2)}) collective-permute-start(bf16[4,48,1536]{2,1,0:T(8,128)(2,1)} %fusion.11), channel_id=1, source_target_pairs={{0,4},{1,5},{2,6},{3,7},{4,0},{5,1},{6,2},{7,3},{8,12},{9,13},{10,... | collective-permute-start | bytes 1769480 | tf_op jit(solution)/shard_map/ppermute | solution.py:32
  212.6 18.6 %collective-permute-start.17 = (bf16[4,240,384]{2,1,0:T(8,128)(2,1)}, bf16[4,240,384]{2,1,0:T(8,128)(2,1)}, u32[]{:S(2)}, u32[]{:S(2)}) collective-permute-start(bf16[4,240,384]{2,1,0:T(8,128)(2,1)} %fusion.10), channel_id=1, source_target_pairs={{0,2},{1,3},{2,0},{3,1},{4,6},{5,7},{6,4},{7,5},{8,10},{9,11},{10,... | collective-permute-start | bytes 2211848 | tf_op jit(solution)/shard_map/ppermute | solution.py:32
  230.6 46.7 %collective-permute-start.21 = (bf16[2,48,1536]{2,1,0:T(8,128)(2,1)}, bf16[2,48,1536]{2,1,0:T(8,128)(2,1)}, u32[]{:S(2)}, u32[]{:S(2)}) collective-permute-start(bf16[2,48,1536]{2,1,0:T(8,128)(2,1)} %fusion.16), channel_id=1, source_target_pairs={{0,8},{1,9},{2,10},{3,11},{4,12},{5,13},{6,14},{7,15},{8,0},{9,1},... | collective-permute-start | bytes 884744 | tf_op jit(solution)/shard_map/ppermute | solution.py:32
  233.5 52.5 %collective-permute-start.22 = (bf16[2,240,384]{2,1,0:T(8,128)(2,1)}, bf16[2,240,384]{2,1,0:T(8,128)(2,1)}, u32[]{:S(2)}, u32[]{:S(2)}) collective-permute-start(bf16[2,240,384]{2,1,0:T(8,128)(2,1)} %fusion.15), channel_id=1, source_target_pairs={{0,8},{1,9},{2,10},{3,11},{4,12},{5,13},{6,14},{7,15},{8,0},{9,1},... | collective-permute-start | bytes 1105928 | tf_op jit(solution)/shard_map/ppermute | solution.py:32
  242.4 45.2 %collective-permute-start.20 = (bf16[8,48,512]{2,1,0:T(8,128)(2,1)}, bf16[8,48,512]{2,1,0:T(8,128)(2,1)S(1)}, u32[]{:S(2)}, u32[]{:S(2)}) collective-permute-start(bf16[8,48,512]{2,1,0:T(8,128)(2,1)} %bitcast.66), channel_id=1, source_target_pairs={{0,4},{1,5},{2,6},{3,7},{4,0},{5,1},{6,2},{7,3},{8,12},{9,13},{10,... | collective-permute-start | bytes 1179656 | tf_op jit(solution)/shard_map/ppermute | solution.py:32
  243.6 44.6 %collective-permute-start.19 = (bf16[8,48,640]{2,1,0:T(8,128)(2,1)}, bf16[8,48,640]{2,1,0:T(8,128)(2,1)}, u32[]{:S(2)}, u32[]{:S(2)}) collective-permute-start(bf16[8,48,640]{2,1,0:T(8,128)(2,1)} %bitcast.64), channel_id=1, source_target_pairs={{0,2},{1,3},{2,0},{3,1},{4,6},{5,7},{6,4},{7,5},{8,10},{9,11},{10,... | collective-permute-start | bytes 1474568 | tf_op jit(solution)/shard_map/ppermute | solution.py:32
  263.8 20.4 %all-to-all-start = ((f32[32,1,288]{2,1,0:T(1,128)}), f32[32,1,288]{2,1,0:T(1,128)S(1)}, u32[]{:S(2)}, u32[]{:S(2)}) async-start(f32[32,1,288]{2,1,0:T(1,128)} %all_to_all.6), calls=%async_computation | async-start | bytes 98304 | tf_op jit(solution)/shard_map/all_to_all | solution.py:828
  277.0 12.7 %collective-permute-start.18 = (bf16[2,512,768]{2,1,0:T(8,128)(2,1)}, bf16[2,512,768]{2,1,0:T(8,128)(2,1)}, u32[]{:S(2)}, u32[]{:S(2)}) collective-permute-start(bf16[2,512,768]{2,1,0:T(8,128)(2,1)} %copy-done.26), channel_id=1, source_target_pairs={{0,1},{1,0},{2,3},{3,2},{4,5},{5,4},{6,7},{7,6},{8,9},{9,8},{10,11... | collective-permute-start | bytes 4718600 | tf_op jit(solution)/shard_map/ppermute | solution.py:32
  279.3 23.0 %collective-permute-start.34 = (bf16[1,48,1536]{2,1,0:T(8,128)(2,1)}, bf16[1,48,1536]{2,1,0:T(8,128)(2,1)}, u32[]{:S(2)}, u32[]{:S(2)}) collective-permute-start(bf16[1,48,1536]{2,1,0:T(8,128)(2,1)} %fusion.28), channel_id=1, source_target_pairs={{0,16},{1,17},{2,18},{3,19},{4,20},{5,21},{6,22},{7,23},{8,24},{9,... | collective-permute-start | bytes 442376 | tf_op jit(solution)/shard_map/ppermute | solution.py:32
  287.5 11.0 %collective-permute-start.32 = (bf16[1,240,384]{2,1,0:T(8,128)(2,1)S(1)}, bf16[1,240,384]{2,1,0:T(8,128)(2,1)S(1)}, u32[]{:S(2)}, u32[]{:S(2)}) collective-permute-start(bf16[1,240,384]{2,1,0:T(8,128)(2,1)S(1)} %fusion.24), channel_id=1, source_target_pairs={{0,16},{1,17},{2,18},{3,19},{4,20},{5,21},{6,22},{7,23},{8,24},{9,... | collective-permute-start | bytes 552968 | tf_op jit(solution)/shard_map/ppermute | solution.py:32
  287.7 14.7 %collective-permute-start.28 = (bf16[4,48,512]{2,1,0:T(8,128)(2,1)S(1)}, bf16[4,48,512]{2,1,0:T(8,128)(2,1)S(1)}, u32[]{:S(2)}, u32[]{:S(2)}) collective-permute-start(bf16[4,48,512]{2,1,0:T(8,128)(2,1)S(1)} %fusion.18), channel_id=1, source_target_pairs={{0,2},{1,3},{2,0},{3,1},{4,6},{5,7},{6,4},{7,5},{8,10},{9,11},{10,... | collective-permute-start | bytes 589832 | tf_op jit(solution)/shard_map/ppermute | solution.py:32
  289.3 14.6 %collective-permute-start.25 = (bf16[4,48,640]{2,1,0:T(8,128)(2,1)S(1)}, bf16[4,48,640]{2,1,0:T(8,128)(2,1)S(1)}, u32[]{:S(2)}, u32[]{:S(2)}) collective-permute-start(bf16[4,48,640]{2,1,0:T(8,128)(2,1)S(1)} %fusion.17), channel_id=1, source_target_pairs={{0,4},{1,5},{2,6},{3,7},{4,0},{5,1},{6,2},{7,3},{8,12},{9,13},{10,... | collective-permute-start | bytes 737288 | tf_op jit(solution)/shard_map/ppermute | solution.py:32
  300.0 20.7 %collective-permute-start.23 = (bf16[512,768]{1,0:T(8,128)(2,1)S(1)}, bf16[512,768]{1,0:T(8,128)(2,1)S(1)}, u32[]{:S(2)}, u32[]{:S(2)}) collective-permute-start(bf16[512,768]{1,0:T(8,128)(2,1)S(1)} %fusion.13), channel_id=1, source_target_pairs={{2,0},{3,1},{6,4},{7,5},{10,8},{11,9},{14,12},{15,13},{18,16},{19,... | collective-permute-start | bytes 2359304 | tf_op jit(solution)/shard_map/ppermute | solution.py:802
  301.8 16.1 %collective-permute-start.33 = (f32[120,384]{1,0:T(8,128)S(1)}, f32[120,384]{1,0:T(8,128)S(1)}, u32[]{:S(2)}, u32[]{:S(2)}) collective-permute-start(f32[120,384]{1,0:T(8,128)S(1)} %pad_maximum_fusion.7), channel_id=1, source_target_pairs={{0,1},{1,0},{2,3},{3,2},{4,5},{5,4},{6,7},{7,6},{8,9},{9,8},{10,11... | collective-permute-start | bytes 552968 | tf_op jit(solution)/shard_map/ppermute | solution.py:32
  304.9 5.0 %collective-permute-start.26 = (bf16[2,48,640]{2,1,0:T(8,128)(2,1)S(1)}, bf16[2,48,640]{2,1,0:T(8,128)(2,1)S(1)}, u32[]{:S(2)}, u32[]{:S(2)}) collective-permute-start(bf16[2,48,640]{2,1,0:T(8,128)(2,1)S(1)} %fusion.29), channel_id=1, source_target_pairs={{0,8},{1,9},{2,10},{3,11},{4,12},{5,13},{6,14},{7,15},{8,0},{9,1},... | collective-permute-start | bytes 368648 | tf_op jit(solution)/shard_map/ppermute | solution.py:32
  306.3 6.5 %collective-permute-start.35 = (f32[24,1536]{1,0:T(8,128)S(1)}, f32[24,1536]{1,0:T(8,128)S(1)}, u32[]{:S(2)}, u32[]{:S(2)}) collective-permute-start(f32[24,1536]{1,0:T(8,128)S(1)} %dynamic-slice_bitcast_fusion), channel_id=1, source_target_pairs={{0,1},{1,0},{2,3},{3,2},{4,5},{5,4},{6,7},{7,6},{8,9},{9,8},{10,11... | collective-permute-start | bytes 442376 | tf_op jit(solution)/shard_map/ppermute | solution.py:32
  307.0 6.5 %collective-permute-start.30 = (bf16[1,48,512]{2,1,0:T(8,128)(2,1)S(1)}, bf16[1,48,512]{2,1,0:T(8,128)(2,1)S(1)}, u32[]{:S(2)}, u32[]{:S(2)}) collective-permute-start(bf16[1,48,512]{2,1,0:T(8,128)(2,1)S(1)} %fusion.43), channel_id=1, source_target_pairs={{0,16},{1,17},{2,18},{3,19},{4,20},{5,21},{6,22},{7,23},{8,24},{9,... | collective-permute-start | bytes 147464 | tf_op jit(solution)/shard_map/ppermute | solution.py:32
  (71 other events, 411.5 us)
Sparse Core Ops, SparseCore 0:
  13.1 95.8 all-gather.1

commit v3 on v2

--- a/solution.py
+++ b/solution.py
@@ -1,3 +1,5 @@
+import functools
+
 import jax
 import jax.numpy as jnp
 from jax import lax
@@ -63,10 +65,10 @@
     return whole.reshape(high * 2 * low, rows, cols)
 
 
-def gather_common(block):
+def gather_common(block, wait):
     block, done = block[None], []
     for bit in reversed(range(3, flat_bits())):
-        block = grow(block, done, bit)
+        block = grow(block, done, bit, wait if bit == 3 else ())
         done.append(bit)
     return block
 
@@ -330,7 +332,7 @@
     )(far, query, keyval, keyval, grad, out, lse, *earlier)
 
 
-def grads_kernel(n_ref, dq_ref, dk_ref, dv_ref, a_ref, b_ref):
+def grads_kernel(n_ref, dq_ref, dk_ref, dv_ref, mine_ref, other_ref, a_ref, b_ref):
     near, width = dq_ref.shape
     turned = jnp.transpose(n_ref[...])
     low = jnp.concatenate(
@@ -338,6 +340,7 @@
             dot(turned[:, :near], dq_ref[...]).astype(LOW),
             dot(turned, dk_ref[...]).astype(LOW),
             dot(turned, dv_ref[...]).astype(LOW),
+            (mine_ref[...].astype(FULL) + other_ref[...].astype(FULL)).astype(LOW),
         ],
         1,
     )
@@ -346,20 +349,19 @@
     b_ref[...] = low[:, cut:]
 
 
-def qkv_grads(normed, dq, dk, dv):
+def qkv_grads(normed, dq, dk, dv, mine, other):
     width = normed.shape[1]
-    cols = 3 * dq.shape[1]
-    cut = (cols // LANES + 1) // 2 * LANES
+    cut = 2 * dq.shape[1]
     return pl.pallas_call(
         grads_kernel,
         out_shape=(
             jax.ShapeDtypeStruct((width, cut), LOW),
-            jax.ShapeDtypeStruct((width, cols - cut), LOW),
+            jax.ShapeDtypeStruct((width, cut), LOW),
         ),
         compiler_params=pltpu.CompilerParams(vmem_limit_bytes=VMEM),
         cost_estimate=SHORT,
         name="qkv_grads",
-    )(normed, dq, dk, dv)
+    )(normed, dq, dk, dv, mine, other)
 
 
 CURVE = 0.7978845608028654
@@ -367,9 +369,12 @@
 
 
 def feed_kernel(
-    core_ref, n_ref, g_ref, fc_ref, fb_ref, pr_ref,
-    out_ref, back_ref, fc_grad_ref, pr_grad_ref, fb_grad_ref, turned_ref,
+    shard_rows, core_ref, n_ref, g_ref, fc_ref, fb_ref, *refs
 ):
+    pieces, refs = refs[:-8], refs[-8:]
+    out_ref, back_ref, fc_send_ref, fc_keep_ref, pr_send_ref, pr_keep_ref = refs[:6]
+    fb_grad_ref, turned_ref = refs[6:]
+
     step = pl.program_id(0)
     half = g_ref.shape[1] // 2
 
@@ -377,7 +382,19 @@
     def _():
         turned_ref[...] = jnp.transpose(n_ref[...])
 
-    proj = pr_ref[...].reshape(fc_ref.shape[1], n_ref.shape[1])
+    if len(pieces) == 1:
+        proj = pieces[0][...]
+    else:
+        size = shard_rows
+        wide = [piece[...].astype(FULL) for piece in pieces]
+        proj = jnp.concatenate(
+            [
+                piece[at : at + size]
+                for at in range(0, wide[0].shape[0], size)
+                for piece in wide
+            ],
+            0,
+        ).astype(LOW)
     grad = g_ref[...]
     hidden = dot(n_ref[...], fc_ref[...]) + fb_ref[...]
     square = hidden * hidden
@@ -401,51 +418,73 @@
         back_ref[...] += back
 
     fb_grad_ref[...] = jnp.sum(grad_hidden.astype(FULL), 0, keepdims=True)
-    fc_grad_ref[0] = dot(turned_ref[...], grad_hidden).astype(LOW)
+    fc_grad = dot(turned_ref[...], grad_hidden).astype(LOW)
+    others = pl.num_programs(0) // 2
+
+    @pl.when(step < others)
+    def _():
+        fc_send_ref[...] = fc_grad
+
+    @pl.when(step >= others)
+    def _():
+        fc_keep_ref[...] = fc_grad
+
     pr_grad = dot_tn(active, grad)
     low, high = pr_grad[:, :half].astype(LOW), pr_grad[:, half:].astype(LOW)
     first = core_ref[0] == 0
-    pr_grad_ref[0] = jnp.where(first, high, low)
-    pr_grad_ref[1] = jnp.where(first, low, high)
-
-
-def feed(core, normed, grad, fc, fc_bias, proj, proj_rows):
+    pr_send_ref[...] = jnp.where(first, high, low)
+    pr_keep_ref[...] = jnp.where(first, low, high)
+
+
+def feed(core, normed, grad, late, fc_bias, proj, shard_rows):
     rows, width = normed.shape
-    hidden = fc.shape[1]
-    chunk = hidden // 4
-    group = chunk // proj_rows
-    steps = hidden // (2 * chunk)
+    hidden = fc_bias.shape[1]
+    chunk = width
+    blocks = hidden // chunk
+    steps = blocks // 2
 
     def block(i, s):
         return jnp.where(i < steps, (1 - s[0]) * steps + i, s[0] * steps + i - steps)
 
     whole = pl.BlockSpec((rows, width), lambda i, s: (0, 0))
+    if proj is None:
+        pieces = [late] * blocks
+        piece_specs = [
+            pl.BlockSpec((width // blocks, width), lambda i, s, at=at: (block(i, s), at))
+            for at in range(blocks + 1, 2 * blocks + 1)
+        ]
+    else:
+        pieces = [proj]
+        piece_specs = [pl.BlockSpec((chunk, width), lambda i, s: (block(i, s), 0))]
+    half = pl.BlockSpec((chunk, width // 2), lambda i, s: (block(i, s), 0))
     return pl.pallas_call(
-        feed_kernel,
+        functools.partial(feed_kernel, shard_rows),
         out_shape=(
             jax.ShapeDtypeStruct((rows, width), FULL),
             jax.ShapeDtypeStruct((rows, width), FULL),
-            jax.ShapeDtypeStruct((2, width, hidden // 2), LOW),
-            jax.ShapeDtypeStruct((2, hidden, width // 2), LOW),
+            jax.ShapeDtypeStruct((width, hidden // 2), LOW),
+            jax.ShapeDtypeStruct((width, hidden // 2), LOW),
+            jax.ShapeDtypeStruct((hidden, width // 2), LOW),
+            jax.ShapeDtypeStruct((hidden, width // 2), LOW),
             jax.ShapeDtypeStruct((1, hidden), FULL),
         ),
         grid_spec=pltpu.PrefetchScalarGridSpec(
             num_scalar_prefetch=1,
-            grid=(2 * steps,),
+            grid=(blocks,),
             in_specs=[
                 whole,
                 whole,
                 pl.BlockSpec((width, chunk), lambda i, s: (0, block(i, s))),
                 pl.BlockSpec((1, chunk), lambda i, s: (0, block(i, s))),
-                pl.BlockSpec((group, proj_rows, width), lambda i, s: (block(i, s), 0, 0)),
+                *piece_specs,
             ],
             out_specs=(
                 whole,
                 whole,
-                pl.BlockSpec(
-                    (1, width, chunk), lambda i, s: (jnp.where(i < steps, 0, 1), 0, lax.rem(i, steps))
-                ),
-                pl.BlockSpec((2, chunk, width // 2), lambda i, s: (0, block(i, s), 0)),
+                pl.BlockSpec((width, chunk), lambda i, s: (0, jnp.minimum(i, steps - 1))),
+                pl.BlockSpec((width, chunk), lambda i, s: (0, jnp.maximum(i - steps, 0))),
+                half,
+                half,
                 pl.BlockSpec((1, chunk), lambda i, s: (0, block(i, s))),
             ),
             scratch_shapes=[pltpu.VMEM((width, rows), LOW)],
@@ -453,7 +492,7 @@
         compiler_params=pltpu.CompilerParams(vmem_limit_bytes=VMEM),
         cost_estimate=SHORT,
         name="feed",
-    )(core, normed, grad, fc, fc_bias, proj)
+    )(core, normed, grad, late, fc_bias, *pieces)
 
 
 def turn_kernel(
@@ -479,13 +518,39 @@
         sent[...] = jnp.where(first, two, one)
 
 
-def turn(core, grad, hat, root, gain, grad_valid, attended, weight):
+def turn(core, grad, hat, root, gain, grad_valid, attended, late, at):
     rows, width = grad.shape
-    vmem = pl.BlockSpec(memory_space=pltpu.VMEM)
     shape = jax.ShapeDtypeStruct
+
+    def spec(*dims):
+        return pl.BlockSpec(dims, lambda i, s: (0, 0))
+
+    whole = spec(rows, width)
     return pl.pallas_call(
         turn_kernel,
-        in_specs=[pl.BlockSpec(memory_space=pltpu.SMEM)] + [vmem] * 7,
+        grid_spec=pltpu.PrefetchScalarGridSpec(
+            num_scalar_prefetch=1,
+            grid=(1,),
+            in_specs=[
+                whole,
+                whole,
+                spec(rows, 1),
+                spec(1, width),
+                whole,
+                whole,
+                pl.BlockSpec((width, width), lambda i, s: (0, at)),
+            ],
+            out_specs=(
+                whole,
+                spec(rows, width // 2),
+                spec(rows, width // 2),
+                spec(width, width // 2),
+                spec(width, width // 2),
+                spec(1, width),
+                spec(1, width),
+                spec(1, width),
+            ),
+        ),
         out_shape=(
             shape((rows, width), FULL),
             shape((rows, width // 2), LOW),
@@ -499,7 +564,7 @@
         compiler_params=pltpu.CompilerParams(vmem_limit_bytes=VMEM),
         cost_estimate=SHORT,
         name="turn",
-    )(core, grad, hat, root, gain, grad_valid, attended, weight)
+    )(core, grad, hat, root, gain, grad_valid, attended, late)
 
 
 def norm_back_kernel(
@@ -630,10 +695,10 @@
 
     high, hidden_width = proj_weight.shape[0], fc_weight.shape[1]
     blocks = hidden_width // width
-    fc_rows = [fc_weight[:, i * width : (i + 1) * width] for i in range(blocks)]
+    proj_rows = [proj_weight[i * slice_rows : (i + 1) * slice_rows] for i in range(blocks)]
     late = lax.all_gather(
-        jnp.concatenate([proj_weight, *fc_rows, out_weight], 0), ALL, axis=0, tiled=True
-    ).reshape(count, high + (blocks + 1) * slice_rows, width)
+        jnp.concatenate([fc_weight, out_weight, *proj_rows], 1), ALL, axis=0, tiled=True
+    )
 
     mine = tokens[0]
     flips = [(i, i ^ 2) for i in range(count) if not i & 2]
@@ -655,14 +720,7 @@
     )
     keep, send = jnp.concatenate([keep, small], 1), jnp.concatenate([send, small], 1)
     chip = pair(keep, swap(send, 0), core, 0).reshape(2 * slice_rows, 3 * half + LANES)
-    block = gather_common(chip)
-    parts = [
-        jnp.concatenate([block[:, :, :half], block[:, :, 3 * half :]], 2),
-        block[:, :, half : 3 * half],
-    ]
-    first_parts = gather_step(parts, plans, 0)
-
-    before = after(before, block)
+    block = gather_common(chip, (before,))
     far_tokens = pair(before, swap(before, 0), core, 0).reshape(near, width)
     slots = jnp.arange(near, dtype=jnp.int32)
     thoughts = thought_pos[0]
@@ -681,6 +739,12 @@
     own = core * quarter
     inputs = lax.dynamic_slice_in_dim(inputs_near, own, quarter, 0).astype(FULL)
 
+    parts = [
+        jnp.concatenate([block[:, :, :half], block[:, :, 3 * half :]], 2),
+        block[:, :, half : 3 * half],
+    ]
+    first_parts = gather_step(parts, plans, 0)
+
     parts = gather_step(first_parts, plans, 1, (hat_all, root_all))
     q_weight = parts[0][:, :, :half].reshape(width, half)
     keyval_weight = parts[1].reshape(width, 2 * half)
@@ -719,10 +783,7 @@
     keep, send = rows_to_core(heads)
     attended = beside(keep, swap(send, 0), core)
     late = after(late, attended)
-    fc_full = late[:, high : high + blocks * slice_rows]
-    fc_full = fc_full.reshape(count, blocks, slice_rows, width).transpose(0, 2, 1, 3)
-    fc_full = fc_full.reshape(width, hidden_width)
-    out_full = late[:, high + blocks * slice_rows :].reshape(width, width)
+    out_full = late[:, hidden_width : hidden_width + width]
 
     middle = inputs + dot(attended, out_full) + out_bias_full
     hat_two, root_two = normalize(middle)
@@ -730,13 +791,13 @@
     my_slots = (2 * second + core) * quarter + jnp.arange(quarter, dtype=jnp.int32)
     valid = (my_slots < lengths[0])[:, None]
     grad_valid = jnp.where(valid, cotangent[0], jnp.zeros_like(cotangent[0]))
-    proj_full, proj_rows = late, high
-    if high % 16:
-        proj_full, proj_rows = late[:, :high].reshape(1, hidden_width, width), hidden_width // 4
-        proj_full = proj_full.reshape(4, proj_rows, width)
     core_at = core.astype(jnp.int32).reshape(1)
-    fed, grad_normed_two, fc_grads, proj_grads, fc_bias_grad = feed(
-        core_at, normed_two, grad_valid, fc_full, fc_bias_full, proj_full, proj_rows
+    proj_full = None
+    if slice_rows % 8:
+        proj_full = late[:, hidden_width + width :].reshape(count, slice_rows, blocks, width)
+        proj_full = proj_full.transpose(0, 2, 1, 3).reshape(hidden_width, width)
+    fed, grad_normed_two, fc_send, fc_keep, proj_send, proj_keep, fc_bias_grad = feed(
+        core_at, normed_two, grad_valid, late, fc_bias_full, proj_full, slice_rows
     )
     fc_bias_grad = fc_bias_grad[0]
     output = middle + fed + proj_bias_full
@@ -745,42 +806,36 @@
 
     chips = count // 2
     fc_shape = (chips, 2 * slice_rows, hidden_width // 2)
-    fc_pair = [fc_grads[1].reshape(fc_shape), swap(fc_grads[0], 0).reshape(fc_shape)]
+    proj_shape = (chips, 2 * high, half)
+    fc_pair = [fc_keep.reshape(fc_shape), swap(fc_send, 0).reshape(fc_shape)]
+    proj_pair = [proj_keep.reshape(proj_shape), swap(proj_send, 0).reshape(proj_shape)]
 
     turned = turn(
-        core_at, grad_normed_two, hat_two, root_two, gain_two, grad_valid, attended, out_full
+        core_at, grad_normed_two, hat_two, root_two, gain_two, grad_valid, attended, late, blocks
     )
     grad_middle, keep, send, out_kept, out_send = turned[:5]
     second_gain_grad, second_shift_grad, out_bias_grad = (value[0] for value in turned[5:])
     grad_heads = pair(keep, swap(send, 0), core, 0).reshape(near, half)
-    out_shape = (chips, 2 * slice_rows, half)
-    proj_shape = (chips, 2 * high, half)
-    proj_kept, proj_send = (
-        jnp.concatenate(
-            [grad.reshape(proj_shape), other.reshape(out_shape)], 1
-        )
-        for grad, other in ((proj_grads[1], out_kept), (proj_grads[0], out_send))
-    )
-    proj_pair = [proj_kept, swap(proj_send, 0)]
     early = [start_sum(fc_pair, 0, hidden_width // 2), start_sum(proj_pair, 0, half)]
-    early_plans = plans
-    ready = prepare(early, early_plans, 0)
+    ready = prepare(early, plans, 0)
+    out_got = swap(after(out_send, *sends(ready)), 0)
 
     grads = ()
     now = after(grad_heads, *sends(ready))
     for which in range(pairs):
         if which == 2:
-            ready = prepare(exchange(ready, grads), early_plans, 1)
+            ready = prepare(exchange(ready, grads), plans, 1)
             now = after(grad_heads, *sends(ready))
         grads = attend_back(
             far, query, keyval, now, heads, logsums, which, grads
         )
-    ready = prepare(exchange(ready, grads), early_plans, 2)
+    out_got = after(out_got, *grads)
+    ready = prepare(exchange(ready, grads), plans, 2)
     grad_query, grad_key, grad_value = after(grads, *sends(ready))
 
     last = [
         start_sum([value.reshape(chips, 2 * slice_rows, -1)], 0, value.shape[1])
-        for value in qkv_grads(normed, grad_query, grad_key, grad_value)
+        for value in qkv_grads(normed, grad_query, grad_key, grad_value, out_kept, out_got)
     ]
     last_ready = prepare(last, plans, 0)
 
@@ -794,9 +849,9 @@
         hat_all,
     )
     got = swap(part_send, 0)
-    ready = prepare(exchange(ready, (part_send,)), early_plans, 3)
     last = exchange(last_ready, (part_send,))
     last_ready = prepare(last, plans, 1)
+    ready = prepare(exchange(ready, sends(last_ready)), plans, 3)
     got = after(got, *sends(last_ready), *sends(ready))
     far_sum = (part[0] + got[0].astype(FULL)).astype(LOW)
     back = lax.ppermute(far_sum, ALL, [(b, a) for a, b in flips])
@@ -831,33 +886,17 @@
         last_ready = prepare(last, plans, step)
     last = exchange(last_ready)
     for step in range(4, flat_bits() - 1):
-        ready = prepare(exchange(ready), early_plans, step)
-    early = exchange(ready, (far_sum,))
-    fc_total, proj_total = (value.total()[0] for value in early)
+        ready = prepare(exchange(ready), plans, step)
+    fc_total, proj_total = (value.total()[0] for value in exchange(ready, (far_sum,)))
     fc_weight_grad = jnp.concatenate(finish(fc_total, slice_rows), 1)
 
-    def by_core(total):
-        mine = lax.dynamic_slice_in_dim(total, core * (total.shape[0] // 2), total.shape[0] // 2, 0)
-        return mine
-
-    def by_other(total):
-        size = total.shape[0] // 2
-        return lax.dynamic_slice_in_dim(total, (1 - core) * size, size, 0)
-
-    proj_part, out_part = proj_total[: 2 * high], proj_total[2 * high :]
-    mine = jnp.concatenate([by_core(proj_part), by_core(out_part)], 0)
-    other = swap(jnp.concatenate([by_other(proj_part), by_other(out_part)], 0), 0)
-    both = beside(mine, other, core)
-    proj_weight_grad, out_weight_grad = both[:high], both[high:]
+    proj_weight_grad = jnp.concatenate(finish(proj_total, high), 1)
     sides = finish(jnp.concatenate([value.total()[0] for value in last], 1), slice_rows)
-    qkv_weight_grad = jnp.concatenate(
-        [
-            side[:, kind * half : (kind + 1) * half]
-            for kind in range(3)
-            for side in sides
-        ],
-        1,
-    )
+    kinds = [
+        jnp.concatenate([side[:, i * half : (i + 1) * half] for side in sides], 1)
+        for i in range(4)
+    ]
+    qkv_weight_grad, out_weight_grad = jnp.concatenate(kinds[:3], 1), kinds[3]
 
     grad_normed = part[1] + got[1].astype(FULL) + back.astype(FULL)
     hat = lax.dynamic_slice_in_dim(hat_all, own, quarter, 0)

time: 342 us -> 322 us (0.942)
  starting transfers between devices: 78.6 us -> 55.2 us
  local copies, waits for them, and re-layouts: 53.5 us -> 39.3 us
  waiting for transfers between devices: 60.2 us -> 70.1 us
  Pallas kernels: 72.6 us -> 77.1 us
    ppermute x33 -> x34, starting transfers between devices: 56.8 us -> 43.7 us  [swap(): return lax.ppermute(value, ALL, [(i, i ^ 1 << bit) for i in range(count)])]
    slice x6 -> x2, local copies, waits for them, and re-layouts: 10.5 us -> 0.02 us  [shards(): side[:, i * half:(i + 1) * half]]
    unnamed x143 -> x115, local copies, waits for them, and re-layouts: 18.9 us -> 8.78 us
    all_to_all x1, starting transfers between devices: 13.1 us -> 3.01 us  [shards(): lax.all_to_all(packed, ALL, 0, 0, tiled=True)]
    all_gather x1, waiting for transfers between devices: 9.86 us -> 17.4 us  [shards(): lax.all_gather(jnp.concatenate([fc_weight, out_weight, *proj_rows], 1), A...]
    pallas_call x2, Pallas kernels: 25.6 us -> 29.7 us  [the longest x1 24.4 us: feed(): pl.pallas_call(functools.partial(feed_kernel, shard_rows), out_shape=(jax...]
    all_to_all x1, waiting for transfers between devices: 2.45 us -> 6.45 us  [shards(): lax.all_to_all(packed, ALL, 0, 0, tiled=True)]
    ppermute x1, waiting for transfers between devices: 3.5 us -> 0.01 us  [shards(): before = lax.ppermute(mine, ALL, flips)]
  transfers between devices with their start and end apart: 38 -> 39, of which waited for: 16 -> 19; matrix products, arithmetic and copies ran while one was open for 20% -> 23% of each run, Pallas kernels for 14% -> 15%
where the time goes in v3:
time: 322 us; the launch traced here: 316 us
  Pallas kernels  77.1 us (24%)
  waiting for transfers between devices  70.1 us (22%)
  starting transfers between devices  55.2 us (17%)
  other arithmetic  52 us (16%)
  local copies, waits for them, and re-layouts  39.3 us (12%)
  between operations  16.3 us (5%)
  matrix products  6.2 us (2%)
    ppermute x34, waiting for transfers between devices, swap(): return lax.ppermute(value, ALL, [(i, i ^ 1 << bit) for i in range(count)])  44.4 us
    ppermute x34, starting transfers between devices, swap(): return lax.ppermute(value, ALL, [(i, i ^ 1 << bit) for i in range(count)])  43.7 us
    pallas_call x1, Pallas kernels, feed(): pl.pallas_call(functools.partial(feed_kernel, shard_rows), out_shape=(jax...  24.4 us
    pallas_call x3, Pallas kernels, attend_back(): pl.pallas_call(attend_back_kernel, out_shape=(jax.ShapeDtypeStruct((near,...  19.6 us
    convert_element_type x14, other arithmetic, prepare(): send = self.total(bit, 1 - bit_of(bit)).astype(self.kind)  18.3 us
    all_gather x1, waiting for transfers between devices, shards(): lax.all_gather(jnp.concatenate([fc_weight, out_weight, *proj_rows], 1), A...  17.4 us
    pallas_call x3, Pallas kernels, attend(): pl.pallas_call(attend_kernel, out_shape=(jax.ShapeDtypeStruct((near, widt...  11 us
    pallas_call x1, Pallas kernels, norm_back(): pl.pallas_call(norm_back_kernel, out_shape=(shape((2, quarter, width), FU...  10.2 us
  transfers between devices with their start and end apart: 39, of which 19 were waited for; matrix products, arithmetic and copies ran while one was open for 23% of the time, Pallas kernels for 15%

profile of v3, /device:TPU:1, one launch (start us, length us, event | category | flops | bytes accessed | tf_op | source)
XLA Modules:
  0.0 316.3 jit_solution(7058197169247269603)
XLA Ops:
  15.0 4.6 %collective-permute-start = (bf16[512,768]{1,0:T(8,128)(2,1)S(1)}, bf16[512,768]{1,0:T(8,128)(2,1)S(1)}, u32[]{:S(2)}, u32[]{:S(2)}) collective-permute-start(bf16[512,768]{1,0:T(8,128)(2,1)S(1)} %bitcast.312), channel_id=1, source_target_pairs={{0,2},{1,3},{4,6},{5,7},{8,10},{9,11},{12,14},{13,15},{16,18},{17,... | collective-permute-start | bytes 2359304 | tf_op jit(solution)/shard_map/ppermute | solution.py:705
  22.0 5.8 %collective-permute-done.4 = bf16[1,48,1280]{2,1,0:T(8,128)(2,1)S(1)} collective-permute-done((bf16[1,48,1280]{2,1,0:T(8,128)(2,1)S(1)}, bf16[1,48,1280]{2,1,0:T(8,128)(2,1)S(1)}, u32[]{:S(2)}, u32[]{:S(2)}) %collective-permute-start.4) | collective-permute-done | bytes 122912 | tf_op jit(solution)/shard_map/ppermute | solution.py:34
  27.9 4.1 %collective-permute-start.5 = (bf16[2,48,1280]{2,1,0:T(8,128)(2,1)S(1)}, bf16[2,48,1280]{2,1,0:T(8,128)(2,1)S(1)}, u32[]{:S(2)}, u32[]{:S(2)}) collective-permute-start(bf16[2,48,1280]{2,1,0:T(8,128)(2,1)S(1)} %constant_dynamic-update-slice_fusion.3), channel_id=1, source_target_pairs={{0,8},{1,9},{2,10},{3,11},{4,12},{5,13},{6,14},{7,15},{8,0},{9,1},... | collective-permute-start | bytes 737288 | tf_op jit(solution)/shard_map/ppermute | solution.py:34
  34.6 5.9 %collective-permute-done.5 = bf16[2,48,1280]{2,1,0:T(8,128)(2,1)S(1)} collective-permute-done((bf16[2,48,1280]{2,1,0:T(8,128)(2,1)S(1)}, bf16[2,48,1280]{2,1,0:T(8,128)(2,1)S(1)}, u32[]{:S(2)}, u32[]{:S(2)}) %collective-permute-start.5) | collective-permute-done | bytes 245792 | tf_op jit(solution)/shard_map/ppermute | solution.py:34
  43.6 6.0 %collective-permute-done.6 = bf16[4,48,512]{2,1,0:T(8,128)(2,1)S(1)} collective-permute-done((bf16[4,48,512]{2,1,0:T(8,128)(2,1)S(1)}, bf16[4,48,512]{2,1,0:T(8,128)(2,1)S(1)}, u32[]{:S(2)}, u32[]{:S(2)}) %collective-permute-start.6) | collective-permute-done | bytes 196640 | tf_op jit(solution)/shard_map/ppermute | solution.py:34
  49.7 5.9 %collective-permute-done.8 = bf16[4,48,768]{2,1,0:T(8,128)(2,1)S(1)} collective-permute-done((bf16[4,48,768]{2,1,0:T(8,128)(2,1)S(1)}, bf16[4,48,768]{2,1,0:T(8,128)(2,1)S(1)}, u32[]{:S(2)}, u32[]{:S(2)}) %collective-permute-start.8) | collective-permute-done | bytes 294944 | tf_op jit(solution)/shard_map/ppermute | solution.py:34
  57.9 3.1 fusion.2
  61.0 3.6 %fusion.hat_ref = f32[2048,768]{1,0:T(8,128)} fusion(f32[2048]{0:T(1024)S(1)} %add_rsqrt_fusion, f32[2048]{0:T(1024)S(1)} %broadcast_multiply_fusion, bf16[1024,768]{1,0:T(8,128)(2,1)S(1)} %maximum_select_fusion.1, bf16[1024,768]{1,0:T(8,128)(2,1)S(1)} %maximum_select_fusion), kind=kLoop, calls=%fused_computation.2 | loop fusion | flops 9437184 | bytes 9453568 | tf_op jit(solution)/shard_map/mul | solution.py:657
  66.4 2.5 add_convert_fusion.1.n_ref
  70.5 2.8 add_convert_fusion.k_ref.v_ref
  73.4 3.6 %attend.3 = (bf16[1024,384]{1,0:T(8,128)(2,1)S(1)}, f32[3,8,1024]{2,1,0:T(8,128)S(1)}) custom-call(s32[1]{0:T(128)} %bitcast.7.far_ref, bf16[1024,384]{1,0:T(8,128)(2,1)S(1)} %add_convert_fusion.6.q_ref, bf16[2048,768]{1,0:T(8,128)(2,1)S(1)} %add_convert_fusion.k_ref.v_ref, bf16[2048,768]{1,0:T(8,128)(2,1)S(1)} %add_convert_fusion.k_ref.v_ref), custom_call_target="tpu_custom_call" | custom-call | flops 536870912 | bytes 524288 | tf_op jit(solution)/shard_map/attend/pallas_call | solution.py:214
  77.0 3.6 %attend.4 = (bf16[1024,384]{1,0:T(8,128)(2,1)S(1)}, f32[3,8,1024]{2,1,0:T(8,128)S(1)}) custom-call(s32[1]{0:T(128)} %bitcast.7.far_ref, bf16[1024,384]{1,0:T(8,128)(2,1)S(1)} %add_convert_fusion.6.q_ref, bf16[2048,768]{1,0:T(8,128)(2,1)S(1)} %add_convert_fusion.k_ref.v_ref, ...), custom_call_target="tpu_custom_call", output_to_operand_aliasing={{0}: (4, {}), {1}: (5, {})} | custom-call | flops 536870912 | bytes 524288 | tf_op jit(solution)/shard_map/attend/pallas_call | solution.py:214
  80.6 3.8 %attend.5 = (bf16[1024,384]{1,0:T(8,128)(2,1)S(1)}, f32[3,8,1024]{2,1,0:T(8,128)S(1)}) custom-call(s32[1]{0:T(128)} %bitcast.7.far_ref, bf16[1024,384]{1,0:T(8,128)(2,1)S(1)} %add_convert_fusion.6.q_ref, bf16[2048,768]{1,0:T(8,128)(2,1)S(1)} %add_convert_fusion.k_ref.v_ref, ...), custom_call_target="tpu_custom_call", output_to_operand_aliasing={{0}: (4, {}), {1}: (5, {})} | custom-call | flops 536870912 | bytes 524288 | tf_op jit(solution)/shard_map/attend/pallas_call | solution.py:214
  85.3 3.7 %collective-permute-start.10 = (bf16[512,384]{1,0:T(8,128)(2,1)S(1)}, bf16[512,384]{1,0:T(8,128)(2,1)S(1)}, u32[]{:S(2)}, u32[]{:S(2)}) collective-permute-start(bf16[512,384]{1,0:T(8,128)(2,1)S(1)} %constant_dynamic-slice_fusion.8), channel_id=1, source_target_pairs={{0,1},{1,0},{2,3},{3,2},{4,5},{5,4},{6,7},{7,6},{8,9},{9,8},{10,11... | collective-permute-start | bytes 1179656 | tf_op jit(solution)/shard_map/ppermute | solution.py:34
  90.7 17.4 %all-gather.2.cloned.1.call-done.fc_ref.refs_0_.refs_1_.refs_2_.refs_3_.w_ref = bf16[768,6912]{1,0:T(8,128)(2,1)} async-done(((bf16[24,6912]{1,0:T(8,128)(2,1)}), bf16[768,6912]{1,0:T(8,128)(2,1)}) %all-gather.2.cloned.1.call-update) | async-done | bytes 10616848 | tf_op jit(solution)/shard_map/all_gather | solution.py:699
  108.1 2.4 fusion.61
  112.3 24.4 %feed.1 = (f32[512,768]{1,0:T(8,128)S(1)}, f32[512,768]{1,0:T(8,128)S(1)}, bf16[768,1536]{1,0:T(8,128)(2,1)}, bf16[768,1536]{1,0:T(8,128)(2,1)}, bf16[3072,384]{...) custom-call(s32[1]{0:T(128)} %bitcast.29.core_ref, bf16[512,768]{1,0:T(8,128)(2,1)S(1)} %get-tuple-element.177.n_ref, ...), custom_call_target="tpu_custom_call" | custom-call | flops 536870912 | bytes 524288 | tf_op jit(solution)/shard_map/feed/pallas_call | solution.py:460
  139.8 4.1 %collective-permute-done.12 = bf16[768,1536]{1,0:T(8,128)(2,1)} collective-permute-done((bf16[768,1536]{1,0:T(8,128)(2,1)}, bf16[768,1536]{1,0:T(8,128)(2,1)}, u32[]{:S(2)}, u32[]{:S(2)}) %collective-permute-start.12) | collective-permute-done | bytes 2359328 | tf_op jit(solution)/shard_map/ppermute | solution.py:34
  143.9 3.0 add_convert_fusion.3
  148.1 5.3 %turn.1 = (f32[512,768]{1,0:T(8,128)S(1)}, bf16[512,384]{1,0:T(8,128)(2,1)S(1)}, bf16[512,384]{1,0:T(8,128)(2,1)}, bf16[768,384]{1,0:T(8,128)(2,1)S(1)}, bf16[76...) custom-call(s32[1]{0:T(128)} %bitcast.29.core_ref, ...), custom_call_target="tpu_custom_call" | custom-call | flops 536870912 | bytes 524288 | tf_op jit(solution)/shard_map/turn/pallas_call | solution.py:529
  154.0 2.9 add_convert_fusion.2
  166.0 6.6 %attend_back.3 = (bf16[1024,384]{1,0:T(8,128)(2,1)S(1)}, bf16[2048,384]{1,0:T(8,128)(2,1)S(1)}, bf16[2048,384]{1,0:T(8,128)(2,1)}) custom-call(s32[1]{0:T(128)} %bitcast.7.far_ref, bf16[1024,384]{1,0:T(8,128)(2,1)S(1)} %copy-done.2, bf16[2048,768]{1,0:T(8,128)(2,1)} %copy-done, bf16[2048,768]{1,0:T(8,128)(2,1)} %copy-done, bf16[1024,384]{1,0:T(8,128)(2,1)S(1)} %bitcast.267, ...), custom_call_target="tpu_custom_call" | custom-call | flops 536870912 | bytes 524288 | tf_op jit(solution)/shard_map/attend_back/pallas_call | solution.py:306
  172.6 6.4 %attend_back.4 = (bf16[1024,384]{1,0:T(8,128)(2,1)S(1)}, bf16[2048,384]{1,0:T(8,128)(2,1)S(1)}, bf16[2048,384]{1,0:T(8,128)(2,1)}) custom-call(s32[1]{0:T(128)} %bitcast.7.far_ref, bf16[1024,384]{1,0:T(8,128)(2,1)S(1)} %copy-done.2, bf16[2048,768]{1,0:T(8,128)(2,1)} %copy-done, ...), custom_call_target="tpu_custom_call", output_to_operand_aliasing={{0}: (7, {}), {1}: (8, {}), {2}: (9, {})} | custom-call | flops 536870912 | bytes 524288 | tf_op jit(solution)/shard_map/attend_back/pallas_call | solution.py:306
  185.0 11.0 %collective-permute-start.17 = (bf16[4,192,384]{2,1,0:T(8,128)(2,1)S(1)}, bf16[4,192,384]{2,1,0:T(8,128)(2,1)S(1)}, u32[]{:S(2)}, u32[]{:S(2)}) collective-permute-start(bf16[4,192,384]{2,1,0:T(8,128)(2,1)S(1)} %fusion.9), channel_id=1, source_target_pairs={{0,2},{1,3},{2,0},{3,1},{4,6},{5,7},{6,4},{7,5},{8,10},{9,11},{10,... | collective-permute-start | bytes 1769480 | tf_op jit(solution)/shard_map/ppermute | solution.py:34
  197.0 6.6 %attend_back.5 = (bf16[1024,384]{1,0:T(8,128)(2,1)S(1)}, bf16[2048,384]{1,0:T(8,128)(2,1)S(1)}, bf16[2048,384]{1,0:T(8,128)(2,1)}) custom-call(s32[1]{0:T(128)} %bitcast.7.far_ref, bf16[1024,384]{1,0:T(8,128)(2,1)S(1)} %copy-done.2, bf16[2048,768]{1,0:T(8,128)(2,1)} %copy-done, ...), custom_call_target="tpu_custom_call", output_to_operand_aliasing={{0}: (7, {}), {1}: (8, {}), {2}: (9, {})} | custom-call | flops 536870912 | bytes 524288 | tf_op jit(solution)/shard_map/attend_back/pallas_call | solution.py:306
  206.0 3.5 %collective-permute-done.17 = bf16[4,192,384]{2,1,0:T(8,128)(2,1)S(1)} collective-permute-done((bf16[4,192,384]{2,1,0:T(8,128)(2,1)S(1)}, bf16[4,192,384]{2,1,0:T(8,128)(2,1)S(1)}, u32[]{:S(2)}, u32[]{:S(2)}) %collective-permute-start.17) | collective-permute-done | bytes 589856 | tf_op jit(solution)/shard_map/ppermute | solution.py:34
  211.6 6.6 %qkv_grads.1 = (bf16[768,768]{1,0:T(8,128)(2,1)S(1)}, bf16[768,768]{1,0:T(8,128)(2,1)S(1)}) custom-call(bf16[2048,768]{1,0:T(8,128)(2,1)} %copy-done.20, bf16[1024,384]{1,0:T(8,128)(2,1)S(1)} %get-tuple-element.134.dq_ref, bf16[2048,384]{1,0:T(8,128)(2,1)S(1)} %get-tuple-element.126.dk_ref, bf16[2048,384]{1,0:T(8,128)(2,1)} %get-tuple-element.127.dv_ref, ...), custom_call_target="tpu_custom_call" | custom-call | flops 536870912 | bytes 524288 | tf_op jit(solution)/shard_map/qkv_grads/pallas_call | solution.py:355
  220.7 3.1 collective-permute-start.20
  225.6 10.2 %norm_back.1 = (f32[2,512,768]{2,1,0:T(8,128)}, bf16[2,512,768]{2,1,0:T(8,128)(2,1)}, f32[1,768]{1,0:T(1,128)S(1)}, f32[1,768]{1,0:T(1,128)S(1)}, f32[1,384]{1,0:T(1,128)S(1)}, /*index=5*/f32[1,384]{1,0:T(1,128)S(1)}) custom-call(s32[1]{0:T(128)} %bitcast.29.core_ref, bf16[1024,384]{1,0:T(8,128)(2,1)S(1)} %get-tuple-element.134.dq_ref, ...), custom_call_target="tpu_custom_call" | custom-call | flops 536870912 | bytes 524288 | tf_op jit(solution)/shard_map/norm_back/pallas_call | solution.py:616
  250.1 3.0 all-to-all-start
  253.9 6.4 %all-to-all-done = f32[32,1,288]{2,1,0:T(1,128)} async-done(((f32[32,1,288]{2,1,0:T(1,128)}), f32[32,1,288]{2,1,0:T(1,128)}, u32[]{:S(2)}, u32[]{:S(2)}) %all-to-all-start) | async-done | bytes 36896 | tf_op jit(solution)/shard_map/all_to_all | solution.py:883
  278.6 2.9 collective-permute-done.33
  (323 shorter events, 115.0 us)
Async XLA Ops:
  7.3 100.8 %all-gather.2.cloned.1.call-start = ((), (), s32[]{:S(2)}) async-start(), calls=%async_computation.1 | async-start | bytes 10948608 | tf_op jit(solution)/shard_map/all_gather | solution.py:699
  15.0 25.5 %collective-permute-start = (bf16[512,768]{1,0:T(8,128)(2,1)S(1)}, bf16[512,768]{1,0:T(8,128)(2,1)S(1)}, u32[]{:S(2)}, u32[]{:S(2)}) collective-permute-start(bf16[512,768]{1,0:T(8,128)(2,1)S(1)} %bitcast.312), channel_id=1, source_target_pairs={{0,2},{1,3},{4,6},{5,7},{8,10},{9,11},{12,14},{13,15},{16,18},{17,... | collective-permute-start | bytes 2359304 | tf_op jit(solution)/shard_map/ppermute | solution.py:705
  19.7 8.2 %collective-permute-start.4 = (bf16[1,48,1280]{2,1,0:T(8,128)(2,1)S(1)}, bf16[1,48,1280]{2,1,0:T(8,128)(2,1)S(1)}, u32[]{:S(2)}, u32[]{:S(2)}) collective-permute-start(bf16[1,48,1280]{2,1,0:T(8,128)(2,1)S(1)} %bitcast.322), channel_id=1, source_target_pairs={{0,16},{1,17},{2,18},{3,19},{4,20},{5,21},{6,22},{7,23},{8,24},{9,... | collective-permute-start | bytes 368648 | tf_op jit(solution)/shard_map/ppermute | solution.py:34
  27.9 12.6 %collective-permute-start.5 = (bf16[2,48,1280]{2,1,0:T(8,128)(2,1)S(1)}, bf16[2,48,1280]{2,1,0:T(8,128)(2,1)S(1)}, u32[]{:S(2)}, u32[]{:S(2)}) collective-permute-start(bf16[2,48,1280]{2,1,0:T(8,128)(2,1)S(1)} %constant_dynamic-update-slice_fusion.3), channel_id=1, source_target_pairs={{0,8},{1,9},{2,10},{3,11},{4,12},{5,13},{6,14},{7,15},{8,0},{9,1},... | collective-permute-start | bytes 737288 | tf_op jit(solution)/shard_map/ppermute | solution.py:34
  32.0 11.4 %collective-permute-start.2 = (bf16[512,768]{1,0:T(8,128)(2,1)S(1)}, bf16[512,768]{1,0:T(8,128)(2,1)S(1)}, u32[]{:S(2)}, u32[]{:S(2)}) collective-permute-start(bf16[512,768]{1,0:T(8,128)(2,1)S(1)} %bitcast.313), channel_id=1, source_target_pairs={{0,1},{1,0},{2,3},{3,2},{4,5},{5,4},{6,7},{7,6},{8,9},{9,8},{10,11... | collective-permute-start | bytes 2359304 | tf_op jit(solution)/shard_map/ppermute | solution.py:34
  40.6 15.2 %collective-permute-start.1 = (bf16[512,768]{1,0:T(8,128)(2,1)S(1)}, bf16[512,768]{1,0:T(8,128)(2,1)S(1)}, u32[]{:S(2)}, u32[]{:S(2)}) collective-permute-start(bf16[512,768]{1,0:T(8,128)(2,1)S(1)} %collective-permute-done), channel_id=1, source_target_pairs={{0,1},{1,0},{2,3},{3,2},{4,5},{5,4},{6,7},{7,6},{8,9},{9,8},{10,11... | collective-permute-start | bytes 2359304 | tf_op jit(solution)/shard_map/ppermute | solution.py:34
  42.0 7.6 %collective-permute-start.6 = (bf16[4,48,512]{2,1,0:T(8,128)(2,1)S(1)}, bf16[4,48,512]{2,1,0:T(8,128)(2,1)S(1)}, u32[]{:S(2)}, u32[]{:S(2)}) collective-permute-start(bf16[4,48,512]{2,1,0:T(8,128)(2,1)S(1)} %pad_maximum_fusion.4), channel_id=1, source_target_pairs={{0,4},{1,5},{2,6},{3,7},{4,0},{5,1},{6,2},{7,3},{8,12},{9,13},{10,... | collective-permute-start | bytes 589832 | tf_op jit(solution)/shard_map/ppermute | solution.py:34
  43.2 12.4 %collective-permute-start.8 = (bf16[4,48,768]{2,1,0:T(8,128)(2,1)S(1)}, bf16[4,48,768]{2,1,0:T(8,128)(2,1)S(1)}, u32[]{:S(2)}, u32[]{:S(2)}) collective-permute-start(bf16[4,48,768]{2,1,0:T(8,128)(2,1)S(1)} %slice.221), channel_id=1, source_target_pairs={{0,2},{1,3},{2,0},{3,1},{4,6},{5,7},{6,4},{7,5},{8,10},{9,11},{10,... | collective-permute-start | bytes 884744 | tf_op jit(solution)/shard_map/ppermute | solution.py:34
  49.6 15.2 %collective-permute-start.7 = (bf16[8,48,512]{2,1,0:T(8,128)(2,1)S(1)}, bf16[8,48,512]{2,1,0:T(8,128)(2,1)S(1)}, u32[]{:S(2)}, u32[]{:S(2)}) collective-permute-start(bf16[8,48,512]{2,1,0:T(8,128)(2,1)S(1)} %bitcast.306), channel_id=1, source_target_pairs={{0,2},{1,3},{2,0},{3,1},{4,6},{5,7},{6,4},{7,5},{8,10},{9,11},{10,... | collective-permute-start | bytes 1179656 | tf_op jit(solution)/shard_map/ppermute | solution.py:34
  55.7 14.2 %collective-permute-start.9 = (bf16[8,48,768]{2,1,0:T(8,128)(2,1)S(1)}, bf16[8,48,768]{2,1,0:T(8,128)(2,1)S(1)}, u32[]{:S(2)}, u32[]{:S(2)}) collective-permute-start(bf16[8,48,768]{2,1,0:T(8,128)(2,1)S(1)} %bitcast.291), channel_id=1, source_target_pairs={{0,4},{1,5},{2,6},{3,7},{4,0},{5,1},{6,2},{7,3},{8,12},{9,13},{10,... | collective-permute-start | bytes 1769480 | tf_op jit(solution)/shard_map/ppermute | solution.py:34
  139.3 14.7 %collective-permute-start.14 = (bf16[3072,384]{1,0:T(8,128)(2,1)}, bf16[3072,384]{1,0:T(8,128)(2,1)}, u32[]{:S(2)}, u32[]{:S(2)}) collective-permute-start(bf16[3072,384]{1,0:T(8,128)(2,1)} %get-tuple-element.108), channel_id=1, source_target_pairs={{0,1},{1,0},{2,3},{3,2},{4,5},{5,4},{6,7},{7,6},{8,9},{9,8},{10,11... | collective-permute-start | bytes 7077896 | tf_op jit(solution)/shard_map/ppermute | solution.py:34
  147.0 34.8 %collective-permute-start.13 = (bf16[8,48,1536]{2,1,0:T(8,128)(2,1)}, bf16[8,48,1536]{2,1,0:T(8,128)(2,1)}, u32[]{:S(2)}, u32[]{:S(2)}) collective-permute-start(bf16[8,48,1536]{2,1,0:T(8,128)(2,1)} %bitcast.38), channel_id=1, source_target_pairs={{0,2},{1,3},{2,0},{3,1},{4,6},{5,7},{6,4},{7,5},{8,10},{9,11},{10,... | collective-permute-start | bytes 3538952 | tf_op jit(solution)/shard_map/ppermute | solution.py:34
  153.5 10.5 %collective-permute-start.11 = (bf16[512,384]{1,0:T(8,128)(2,1)}, bf16[512,384]{1,0:T(8,128)(2,1)}, u32[]{:S(2)}, u32[]{:S(2)}) collective-permute-start(bf16[512,384]{1,0:T(8,128)(2,1)} %get-tuple-element.104), channel_id=1, source_target_pairs={{0,1},{1,0},{2,3},{3,2},{4,5},{5,4},{6,7},{7,6},{8,9},{9,8},{10,11... | collective-permute-start | bytes 1179656 | tf_op jit(solution)/shard_map/ppermute | solution.py:34
  156.9 27.3 %collective-permute-start.15 = (bf16[8,192,384]{2,1,0:T(8,128)(2,1)}, bf16[8,192,384]{2,1,0:T(8,128)(2,1)S(1)}, u32[]{:S(2)}, u32[]{:S(2)}) collective-permute-start(bf16[8,192,384]{2,1,0:T(8,128)(2,1)} %bitcast.41), channel_id=1, source_target_pairs={{0,4},{1,5},{2,6},{3,7},{4,0},{5,1},{6,2},{7,3},{8,12},{9,13},{10,... | collective-permute-start | bytes 3538952 | tf_op jit(solution)/shard_map/ppermute | solution.py:34
  165.1 38.6 %collective-permute-start.18 = (bf16[768,384]{1,0:T(8,128)(2,1)}, bf16[768,384]{1,0:T(8,128)(2,1)S(1)}, u32[]{:S(2)}, u32[]{:S(2)}) collective-permute-start(bf16[768,384]{1,0:T(8,128)(2,1)} %get-tuple-element.130), channel_id=1, source_target_pairs={{0,1},{1,0},{2,3},{3,2},{4,5},{5,4},{6,7},{7,6},{8,9},{9,8},{10,11... | collective-permute-start | bytes 1769480 | tf_op jit(solution)/shard_map/ppermute | solution.py:34
  184.4 19.3 %collective-permute-start.16 = (bf16[4,48,1536]{2,1,0:T(8,128)(2,1)S(1)}, bf16[4,48,1536]{2,1,0:T(8,128)(2,1)S(1)}, u32[]{:S(2)}, u32[]{:S(2)}) collective-permute-start(bf16[4,48,1536]{2,1,0:T(8,128)(2,1)S(1)} %fusion.10), channel_id=1, source_target_pairs={{0,4},{1,5},{2,6},{3,7},{4,0},{5,1},{6,2},{7,3},{8,12},{9,13},{10,... | collective-permute-start | bytes 1769480 | tf_op jit(solution)/shard_map/ppermute | solution.py:34
  185.0 24.4 %collective-permute-start.17 = (bf16[4,192,384]{2,1,0:T(8,128)(2,1)S(1)}, bf16[4,192,384]{2,1,0:T(8,128)(2,1)S(1)}, u32[]{:S(2)}, u32[]{:S(2)}) collective-permute-start(bf16[4,192,384]{2,1,0:T(8,128)(2,1)S(1)} %fusion.9), channel_id=1, source_target_pairs={{0,2},{1,3},{2,0},{3,1},{4,6},{5,7},{6,4},{7,5},{8,10},{9,11},{10,... | collective-permute-start | bytes 1769480 | tf_op jit(solution)/shard_map/ppermute | solution.py:34
  220.7 42.2 %collective-permute-start.20 = (bf16[8,48,768]{2,1,0:T(8,128)(2,1)}, bf16[8,48,768]{2,1,0:T(8,128)(2,1)}, u32[]{:S(2)}, u32[]{:S(2)}) collective-permute-start(bf16[8,48,768]{2,1,0:T(8,128)(2,1)} %bitcast.56), channel_id=1, source_target_pairs={{0,2},{1,3},{2,0},{3,1},{4,6},{5,7},{6,4},{7,5},{8,10},{9,11},{10,... | collective-permute-start | bytes 1769480 | tf_op jit(solution)/shard_map/ppermute | solution.py:34
  223.8 39.1 %collective-permute-start.21 = (bf16[8,48,768]{2,1,0:T(8,128)(2,1)}, bf16[8,48,768]{2,1,0:T(8,128)(2,1)}, u32[]{:S(2)}, u32[]{:S(2)}) collective-permute-start(bf16[8,48,768]{2,1,0:T(8,128)(2,1)} %bitcast.58), channel_id=1, source_target_pairs={{0,4},{1,5},{2,6},{3,7},{4,0},{5,1},{6,2},{7,3},{8,12},{9,13},{10,... | collective-permute-start | bytes 1769480 | tf_op jit(solution)/shard_map/ppermute | solution.py:34
  224.1 42.8 %collective-permute-start.22 = (bf16[2,48,1536]{2,1,0:T(8,128)(2,1)}, bf16[2,48,1536]{2,1,0:T(8,128)(2,1)}, u32[]{:S(2)}, u32[]{:S(2)}) collective-permute-start(bf16[2,48,1536]{2,1,0:T(8,128)(2,1)} %fusion.17), channel_id=1, source_target_pairs={{0,8},{1,9},{2,10},{3,11},{4,12},{5,13},{6,14},{7,15},{8,0},{9,1},... | collective-permute-start | bytes 884744 | tf_op jit(solution)/shard_map/ppermute | solution.py:34
  225.1 41.8 %collective-permute-start.23 = (bf16[2,192,384]{2,1,0:T(8,128)(2,1)}, bf16[2,192,384]{2,1,0:T(8,128)(2,1)}, u32[]{:S(2)}, u32[]{:S(2)}) collective-permute-start(bf16[2,192,384]{2,1,0:T(8,128)(2,1)} %fusion.16), channel_id=1, source_target_pairs={{0,8},{1,9},{2,10},{3,11},{4,12},{5,13},{6,14},{7,15},{8,0},{9,1},... | collective-permute-start | bytes 884744 | tf_op jit(solution)/shard_map/ppermute | solution.py:34
  235.8 36.3 %collective-permute-start.19 = (bf16[2,512,768]{2,1,0:T(8,128)(2,1)}, bf16[2,512,768]{2,1,0:T(8,128)(2,1)}, u32[]{:S(2)}, u32[]{:S(2)}) collective-permute-start(bf16[2,512,768]{2,1,0:T(8,128)(2,1)} %get-tuple-element.136), channel_id=1, source_target_pairs={{0,1},{1,0},{2,3},{3,2},{4,5},{5,4},{6,7},{7,6},{8,9},{9,8},{10,11... | collective-permute-start | bytes 4718600 | tf_op jit(solution)/shard_map/ppermute | solution.py:34
  250.1 10.2 %all-to-all-start = ((f32[32,1,288]{2,1,0:T(1,128)}), f32[32,1,288]{2,1,0:T(1,128)}, u32[]{:S(2)}, u32[]{:S(2)}) async-start(f32[32,1,288]{2,1,0:T(1,128)} %all_to_all.6), calls=%async_computation | async-start | bytes 98304 | tf_op jit(solution)/shard_map/all_to_all | solution.py:883
  266.2 8.9 %collective-permute-start.26 = (bf16[4,48,768]{2,1,0:T(8,128)(2,1)S(1)}, bf16[4,48,768]{2,1,0:T(8,128)(2,1)S(1)}, u32[]{:S(2)}, u32[]{:S(2)}) collective-permute-start(bf16[4,48,768]{2,1,0:T(8,128)(2,1)S(1)} %fusion.15), channel_id=1, source_target_pairs={{0,4},{1,5},{2,6},{3,7},{4,0},{5,1},{6,2},{7,3},{8,12},{9,13},{10,... | collective-permute-start | bytes 884744 | tf_op jit(solution)/shard_map/ppermute | solution.py:34
  266.5 9.9 %collective-permute-start.29 = (bf16[4,48,768]{2,1,0:T(8,128)(2,1)S(1)}, bf16[4,48,768]{2,1,0:T(8,128)(2,1)S(1)}, u32[]{:S(2)}, u32[]{:S(2)}) collective-permute-start(bf16[4,48,768]{2,1,0:T(8,128)(2,1)S(1)} %fusion.14), channel_id=1, source_target_pairs={{0,2},{1,3},{2,0},{3,1},{4,6},{5,7},{6,4},{7,5},{8,10},{9,11},{10,... | collective-permute-start | bytes 884744 | tf_op jit(solution)/shard_map/ppermute | solution.py:34
  268.5 13.0 %collective-permute-start.33 = (bf16[1,48,1536]{2,1,0:T(8,128)(2,1)S(1)}, bf16[1,48,1536]{2,1,0:T(8,128)(2,1)S(1)}, u32[]{:S(2)}, u32[]{:S(2)}) collective-permute-start(bf16[1,48,1536]{2,1,0:T(8,128)(2,1)S(1)} %fusion.27), channel_id=1, source_target_pairs={{0,16},{1,17},{2,18},{3,19},{4,20},{5,21},{6,22},{7,23},{8,24},{9,... | collective-permute-start | bytes 442376 | tf_op jit(solution)/shard_map/ppermute | solution.py:34
  269.9 14.8 %collective-permute-start.35 = (bf16[1,192,384]{2,1,0:T(8,128)(2,1)S(1)}, bf16[1,192,384]{2,1,0:T(8,128)(2,1)S(1)}, u32[]{:S(2)}, u32[]{:S(2)}) collective-permute-start(bf16[1,192,384]{2,1,0:T(8,128)(2,1)S(1)} %fusion.25), channel_id=1, source_target_pairs={{0,16},{1,17},{2,18},{3,19},{4,20},{5,21},{6,22},{7,23},{8,24},{9,... | collective-permute-start | bytes 442376 | tf_op jit(solution)/shard_map/ppermute | solution.py:34
  273.5 27.1 %collective-permute-start.24 = (bf16[512,768]{1,0:T(8,128)(2,1)S(1)}, bf16[512,768]{1,0:T(8,128)(2,1)S(1)}, u32[]{:S(2)}, u32[]{:S(2)}) collective-permute-start(bf16[512,768]{1,0:T(8,128)(2,1)S(1)} %fusion.13), channel_id=1, source_target_pairs={{2,0},{3,1},{6,4},{7,5},{10,8},{11,9},{14,12},{15,13},{18,16},{19,... | collective-permute-start | bytes 2359304 | tf_op jit(solution)/shard_map/ppermute | solution.py:857
  276.0 11.8 %collective-permute-start.27 = (bf16[2,48,768]{2,1,0:T(8,128)(2,1)S(1)}, bf16[2,48,768]{2,1,0:T(8,128)(2,1)S(1)}, u32[]{:S(2)}, u32[]{:S(2)}) collective-permute-start(bf16[2,48,768]{2,1,0:T(8,128)(2,1)S(1)} %fusion.23), channel_id=1, source_target_pairs={{0,8},{1,9},{2,10},{3,11},{4,12},{5,13},{6,14},{7,15},{8,0},{9,1},... | collective-permute-start | bytes 442376 | tf_op jit(solution)/shard_map/ppermute | solution.py:34
  277.4 13.6 %collective-permute-start.30 = (bf16[2,48,768]{2,1,0:T(8,128)(2,1)S(1)}, bf16[2,48,768]{2,1,0:T(8,128)(2,1)S(1)}, u32[]{:S(2)}, u32[]{:S(2)}) collective-permute-start(bf16[2,48,768]{2,1,0:T(8,128)(2,1)S(1)} %fusion.22), channel_id=1, source_target_pairs={{0,8},{1,9},{2,10},{3,11},{4,12},{5,13},{6,14},{7,15},{8,0},{9,1},... | collective-permute-start | bytes 442376 | tf_op jit(solution)/shard_map/ppermute | solution.py:34
  282.8 9.4 %collective-permute-start.34 = (f32[24,1536]{1,0:T(8,128)S(1)}, f32[24,1536]{1,0:T(8,128)S(1)}, u32[]{:S(2)}, u32[]{:S(2)}) collective-permute-start(f32[24,1536]{1,0:T(8,128)S(1)} %dynamic-slice_bitcast_fusion.1), channel_id=1, source_target_pairs={{0,1},{1,0},{2,3},{3,2},{4,5},{5,4},{6,7},{7,6},{8,9},{9,8},{10,11... | collective-permute-start | bytes 442376 | tf_op jit(solution)/shard_map/ppermute | solution.py:34
  285.9 13.5 %collective-permute-start.36 = (f32[96,384]{1,0:T(8,128)S(1)}, f32[96,384]{1,0:T(8,128)S(1)}, u32[]{:S(2)}, u32[]{:S(2)}) collective-permute-start(f32[96,384]{1,0:T(8,128)S(1)} %dynamic-slice_bitcast_fusion), channel_id=1, source_target_pairs={{0,1},{1,0},{2,3},{3,2},{4,5},{5,4},{6,7},{7,6},{8,9},{9,8},{10,11... | collective-permute-start | bytes 442376 | tf_op jit(solution)/shard_map/ppermute | solution.py:34
  (59 other events, 412.0 us)
Sparse Core Ops, SparseCore 0:
  13.1 94.9 all-gather.1

commit v4 on v3

--- a/solution.py
+++ b/solution.py
@@ -65,10 +65,10 @@
     return whole.reshape(high * 2 * low, rows, cols)
 
 
-def gather_common(block, wait):
+def gather_common(block):
     block, done = block[None], []
     for bit in reversed(range(3, flat_bits())):
-        block = grow(block, done, bit, wait if bit == 3 else ())
+        block = grow(block, done, bit)
         done.append(bit)
     return block
 
@@ -124,11 +124,12 @@
 
 
 def exchange(prepared, wait=()):
-    out = []
-    for send, keep, bit in prepared:
-        got = after(swap(send, bit), *wait)
-        out.append(Sum(keep.addends + [(got, keep.left, (0, got.shape[2]))], keep.left, keep.kind))
-    return out
+    gots = [swap(send, bit) for send, _, bit in prepared]
+    gots = after(gots, *wait) if wait else gots
+    return [
+        Sum(keep.addends + [(got, keep.left, (0, got.shape[2]))], keep.left, keep.kind)
+        for got, (_, keep, _) in zip(gots, prepared)
+    ]
 
 
 def start_sum(arrays, start, size, kind=LOW):
@@ -160,43 +161,43 @@
     return jnp.where(lane // HEAD == head, value, jnp.zeros_like(value))
 
 
-def causal(size):
-    shape = (size, size)
+def causal(rows, cols):
+    shape = (rows, cols)
     return lax.broadcasted_iota(jnp.int32, shape, 0) <= lax.broadcasted_iota(jnp.int32, shape, 1)
 
 
-def attend_kernel(far_ref, q_ref, k_ref, v_ref, *refs):
-    out_ref, lse_ref, top_ref, acc_ref = refs[-4:]
-    size = q_ref.shape[0]
-    mine = pl.program_id(0)
+def attend_kernel(far_ref, q_ref, k_ref, v_ref, out_ref, lse_ref, top_ref, acc_ref):
+    near = q_ref.shape[0]
+    size = near // 2
     query = q_ref[...] * jnp.asarray(SCALE, LOW)
 
-    def step(block, first):
-        at = pl.ds(pl.multiple_of(block * size, size), size)
-        key = k_ref[at, :]
-        value = jnp.transpose(v_ref[at, :])
+    def step(keys, queries, masked, first):
+        key = k_ref[keys, :]
+        value = jnp.transpose(v_ref[keys, :])
         for head in range(2):
-            ones = jnp.ones((16, size), LOW)
+            ones = jnp.ones((16, key.shape[0]), LOW)
             wide = jnp.concatenate([value[head * HEAD : (head + 1) * HEAD], ones], 0)
-            scores = dot_nt(key, head_lanes(query, head))
+            scores = dot_nt(key, head_lanes(query[queries], head))
+            if masked:
+                scores = jnp.where(causal(*scores.shape), scores, -1e9)
             row = slice(head, head + 1)
+            top = jnp.max(scores, 0, keepdims=True)
             if first:
-                scores = jnp.where(causal(size), scores, -1e9)
-                top = jnp.max(scores, 0, keepdims=True)
-                acc_ref[head] = dot(wide, jnp.exp(scores - top).astype(LOW))
+                acc_ref[head, :, queries] = dot(wide, jnp.exp(scores - top).astype(LOW))
             else:
-                old = top_ref[row, :]
-                top = jnp.maximum(old, jnp.max(scores, 0, keepdims=True))
-                acc_ref[head] = acc_ref[head] * jnp.exp(old - top) + dot(
+                old = top_ref[row, queries]
+                top = jnp.maximum(old, top)
+                acc_ref[head, :, queries] = acc_ref[head, :, queries] * jnp.exp(old - top) + dot(
                     wide, jnp.exp(scores - top).astype(LOW)
                 )
-            top_ref[row, :] = top
-
-    step(mine, True)
-
-    @pl.loop(0, mine + far_ref[0])
-    def _(i):
-        step(jnp.where(i < mine, 0, 2 + i - mine), False)
+            top_ref[row, queries] = top
+
+    step(slice(0, size), slice(0, near), True, True)
+    step(slice(size, near), slice(size, near), True, False)
+
+    @pl.when(far_ref[0] > 0)
+    def _():
+        step(slice(near, 2 * near), slice(0, near), False, False)
 
     outs = []
     for head in range(2):
@@ -206,11 +207,11 @@
     out_ref[...] = jnp.transpose(jnp.concatenate(outs, 0)).astype(LOW)
 
 
-def attend(far, query, keyval, quarter, which, earlier):
+def attend(far, query, keyval):
     near, width = query.shape
     total = keyval.shape[0]
     pairs = width // LANES
-    rows = pl.BlockSpec((quarter, LANES), lambda i, s: (i, which))
+    rows = pl.BlockSpec((near, LANES), lambda p, s: (0, p))
     return pl.pallas_call(
         attend_kernel,
         out_shape=(
@@ -219,24 +220,22 @@
         ),
         grid_spec=pltpu.PrefetchScalarGridSpec(
             num_scalar_prefetch=1,
-            grid=(near // quarter,),
+            grid=(pairs,),
             in_specs=[
                 rows,
-                pl.BlockSpec((total, LANES), lambda i, s: (0, which)),
-                pl.BlockSpec((total, LANES), lambda i, s: (0, which + pairs)),
-            ]
-            + [pl.BlockSpec(memory_space=pl.ANY)] * len(earlier),
-            out_specs=(rows, pl.BlockSpec((1, 8, quarter), lambda i, s: (which, 0, i))),
+                pl.BlockSpec((total, LANES), lambda p, s: (0, p)),
+                pl.BlockSpec((total, LANES), lambda p, s: (0, p + pairs)),
+            ],
+            out_specs=(rows, pl.BlockSpec((1, 8, near), lambda p, s: (p, 0, 0))),
             scratch_shapes=[
-                pltpu.VMEM((8, quarter), FULL),
-                pltpu.VMEM((2, HEAD + 16, quarter), FULL),
+                pltpu.VMEM((8, near), FULL),
+                pltpu.VMEM((2, HEAD + 16, near), FULL),
             ],
         ),
-        input_output_aliases={4 + i: i for i in range(len(earlier))},
         compiler_params=pltpu.CompilerParams(vmem_limit_bytes=VMEM),
         cost_estimate=SHORT,
         name="attend",
-    )(far, query, keyval, keyval, *earlier)
+    )(far, query, keyval, keyval)
 
 
 def attend_back_kernel(
@@ -265,7 +264,7 @@
                 g_head = head_lanes(grad[span], head)
                 probs = jnp.exp(dot_nt(key, q_head) - lse_ref[0, head : head + 1, span])
                 if masked:
-                    probs = jnp.where(causal(size), probs, 0.0)
+                    probs = jnp.where(causal(size, size), probs, 0.0)
                 moved = probs * (dot_nt(value, g_head) - delta[head][:, span])
                 moved, probs = moved.astype(LOW), probs.astype(LOW)
                 new_k, new_v = dot(moved, q_head), dot(probs, g_head)
@@ -436,6 +435,34 @@
     pr_keep_ref[...] = jnp.where(first, low, high)
 
 
+def beside_kernel(fc_ref, proj_ref, last_ref, out_ref):
+    rows, at = fc_ref.shape
+    width = proj_ref.shape[1]
+    out_ref[:, :at] = fc_ref[...]
+    out_ref[:, 2 * at :] = last_ref[...]
+    wide = proj_ref[...].astype(FULL)
+    for i in range(wide.shape[0] // rows):
+        out_ref[:, at + i * width : at + (i + 1) * width] = wide[i * rows : (i + 1) * rows].astype(
+            LOW
+        )
+
+
+def beside_rows(fc, proj, last):
+    rows = fc.shape[0]
+    if rows % 8:
+        return jnp.concatenate(
+            [fc] + [proj[i : i + rows] for i in range(0, proj.shape[0], rows)] + [last], 1
+        )
+    vmem = pl.BlockSpec(memory_space=pltpu.VMEM)
+    return pl.pallas_call(
+        beside_kernel,
+        in_specs=[vmem, vmem, vmem],
+        out_shape=jax.ShapeDtypeStruct((rows, 2 * fc.shape[1] + last.shape[1]), LOW),
+        cost_estimate=SHORT,
+        name="beside",
+    )(fc, proj, last)
+
+
 def feed(core, normed, grad, late, fc_bias, proj, shard_rows):
     rows, width = normed.shape
     hidden = fc_bias.shape[1]
@@ -451,7 +478,7 @@
         pieces = [late] * blocks
         piece_specs = [
             pl.BlockSpec((width // blocks, width), lambda i, s, at=at: (block(i, s), at))
-            for at in range(blocks + 1, 2 * blocks + 1)
+            for at in range(blocks, 2 * blocks)
         ]
     else:
         pieces = [proj]
@@ -497,7 +524,7 @@
 
 def turn_kernel(
     core_ref, n_ref, hat_ref, root_ref, gain_ref, g_ref, att_ref, w_ref,
-    middle_ref, keep_ref, send_ref, w_keep_ref, w_send_ref, gain_grad_ref, shift_ref, bias_ref,
+    middle_ref, keep_ref, send_ref, w_keep_ref, w_send_ref, gain_grad_ref, shift_ref, bias_ref, last_ref,
 ):
     half = keep_ref.shape[1]
     grad, hat = n_ref[...], hat_ref[...]
@@ -505,6 +532,7 @@
     shift_ref[...] = jnp.sum(grad, 0, keepdims=True)
     middle = g_ref[...].astype(FULL) + normalize_back(grad, gain_ref[...], hat, root_ref[...])
     middle_ref[...] = middle
+    last_ref[...] = jnp.sum(g_ref[...].astype(FULL), 0, keepdims=True)
     low = middle.astype(LOW)
     bias_ref[...] = jnp.sum(low.astype(FULL), 0, keepdims=True)
     first = core_ref[0] == 0
@@ -549,6 +577,7 @@
                 spec(1, width),
                 spec(1, width),
                 spec(1, width),
+                spec(1, width),
             ),
         ),
         out_shape=(
@@ -557,6 +586,7 @@
             shape((rows, width // 2), LOW),
             shape((width, width // 2), LOW),
             shape((width, width // 2), LOW),
+            shape((1, width), FULL),
             shape((1, width), FULL),
             shape((1, width), FULL),
             shape((1, width), FULL),
@@ -648,6 +678,52 @@
         cost_estimate=SHORT,
         name="norm_back",
     )(core, dq, dk, dv, q_weight, keyval_weight, hat)
+
+
+def pack_kernel(slots, core_ref, *refs):
+    out_ref = refs[-1]
+    count = out_ref.shape[0]
+    spreads = {}
+    for slot, parts in enumerate(slots):
+        total = None
+        for ref_at, size, shift, by_core in parts:
+            line = refs[ref_at][...]
+            length = line.shape[1]
+            shape = (count, length)
+            device = lax.broadcasted_iota(jnp.int32, shape, 0) - (shift + by_core * core_ref[0])
+            lane = lax.broadcasted_iota(jnp.int32, shape, 1) - device * size
+            piece = jnp.where((lane >= 0) & (lane < size), line, 0.0)
+            if (length, size) not in spreads:
+                shape = (length, LANES)
+                at = lax.broadcasted_iota(jnp.int32, shape, 0).astype(FULL)
+                at = at - size * jnp.floor((at + 0.5) * (1.0 / size))
+                lane = lax.broadcasted_iota(jnp.int32, shape, 1).astype(FULL)
+                spreads[length, size] = jnp.where(at == lane, 1.0, 0.0)
+            piece = lax.dot_general(
+                piece,
+                spreads[length, size],
+                (((1,), (0,)), ((), ())),
+                precision=lax.Precision.HIGHEST,
+                preferred_element_type=FULL,
+            )
+            total = piece if total is None else total + piece
+        out_ref[:, slot * LANES : (slot + 1) * LANES] = total
+
+
+def pack(core, count, q_sum, v_sum, lines):
+    size = 4 * q_sum.shape[1] // count
+    slots = [[(0, size, 0, count // 4), (1, size, count // 2, count // 4)]]
+    slots += [[(2 + i, line.shape[1] // count, 0, 0)] for i, line in enumerate(lines)]
+    vmem = pl.BlockSpec(memory_space=pltpu.VMEM)
+    packed = pl.pallas_call(
+        functools.partial(pack_kernel, slots),
+        in_specs=[pl.BlockSpec(memory_space=pltpu.SMEM)] + [vmem] * (2 + len(lines)),
+        out_shape=jax.ShapeDtypeStruct((count, len(slots) * LANES), FULL),
+        compiler_params=pltpu.CompilerParams(vmem_limit_bytes=VMEM),
+        cost_estimate=SHORT,
+        name="pack",
+    )(core, q_sum, v_sum, *lines)
+    return packed, [slot[0][1] for slot in slots]
 
 
 def normalize(values):
@@ -695,9 +771,8 @@
 
     high, hidden_width = proj_weight.shape[0], fc_weight.shape[1]
     blocks = hidden_width // width
-    proj_rows = [proj_weight[i * slice_rows : (i + 1) * slice_rows] for i in range(blocks)]
     late = lax.all_gather(
-        jnp.concatenate([fc_weight, out_weight, *proj_rows], 1), ALL, axis=0, tiled=True
+        beside_rows(fc_weight, proj_weight, out_weight), ALL, axis=0, tiled=True
     )
 
     mine = tokens[0]
@@ -720,7 +795,7 @@
     )
     keep, send = jnp.concatenate([keep, small], 1), jnp.concatenate([send, small], 1)
     chip = pair(keep, swap(send, 0), core, 0).reshape(2 * slice_rows, 3 * half + LANES)
-    block = gather_common(chip, (before,))
+    block = gather_common(chip)
     far_tokens = pair(before, swap(before, 0), core, 0).reshape(near, width)
     slots = jnp.arange(near, dtype=jnp.int32)
     thoughts = thought_pos[0]
@@ -743,7 +818,7 @@
         jnp.concatenate([block[:, :, :half], block[:, :, 3 * half :]], 2),
         block[:, :, half : 3 * half],
     ]
-    first_parts = gather_step(parts, plans, 0)
+    first_parts = gather_step(parts, plans, 0, (before,))
 
     parts = gather_step(first_parts, plans, 1, (hat_all, root_all))
     q_weight = parts[0][:, :, :half].reshape(width, half)
@@ -776,15 +851,11 @@
         )
 
     pairs = half // LANES
-    heads = ()
-    for which in range(pairs):
-        heads = attend(far, query, keyval, quarter, which, heads)
-    heads, logsums = heads
+    heads, logsums = attend(far, query, keyval)
     keep, send = rows_to_core(heads)
     attended = beside(keep, swap(send, 0), core)
     late = after(late, attended)
-    out_full = late[:, hidden_width : hidden_width + width]
-
+    out_full = late[:, 2 * hidden_width :]
     middle = inputs + dot(attended, out_full) + out_bias_full
     hat_two, root_two = normalize(middle)
     normed_two = (hat_two * gain_two + shift_two).astype(LOW)
@@ -794,28 +865,28 @@
     core_at = core.astype(jnp.int32).reshape(1)
     proj_full = None
     if slice_rows % 8:
-        proj_full = late[:, hidden_width + width :].reshape(count, slice_rows, blocks, width)
+        proj_full = late[:, hidden_width : 2 * hidden_width].reshape(count, slice_rows, blocks, width)
         proj_full = proj_full.transpose(0, 2, 1, 3).reshape(hidden_width, width)
     fed, grad_normed_two, fc_send, fc_keep, proj_send, proj_keep, fc_bias_grad = feed(
         core_at, normed_two, grad_valid, late, fc_bias_full, proj_full, slice_rows
     )
-    fc_bias_grad = fc_bias_grad[0]
     output = middle + fed + proj_bias_full
     mixed = jnp.where(valid, output, 0.0).astype(LOW)[None]
-    proj_bias_grad = jnp.sum(grad_valid.astype(FULL), 0)
 
     chips = count // 2
     fc_shape = (chips, 2 * slice_rows, hidden_width // 2)
     proj_shape = (chips, 2 * high, half)
-    fc_pair = [fc_keep.reshape(fc_shape), swap(fc_send, 0).reshape(fc_shape)]
-    proj_pair = [proj_keep.reshape(proj_shape), swap(proj_send, 0).reshape(proj_shape)]
+    fc_got, proj_got = swap(fc_send, 0), swap(proj_send, 0)
 
     turned = turn(
-        core_at, grad_normed_two, hat_two, root_two, gain_two, grad_valid, attended, late, blocks
+        core_at, grad_normed_two, hat_two, root_two, gain_two, grad_valid, attended, late, 2 * blocks
     )
     grad_middle, keep, send, out_kept, out_send = turned[:5]
-    second_gain_grad, second_shift_grad, out_bias_grad = (value[0] for value in turned[5:])
+    second_gain_grad, second_shift_grad, out_bias_grad, proj_bias_grad = turned[5:]
     grad_heads = pair(keep, swap(send, 0), core, 0).reshape(near, half)
+    fc_got, proj_got = after((fc_got, proj_got), grad_middle)
+    fc_pair = [fc_keep.reshape(fc_shape), fc_got.reshape(fc_shape)]
+    proj_pair = [proj_keep.reshape(proj_shape), proj_got.reshape(proj_shape)]
     early = [start_sum(fc_pair, 0, hidden_width // 2), start_sum(proj_pair, 0, half)]
     ready = prepare(early, plans, 0)
     out_got = swap(after(out_send, *sends(ready)), 0)
@@ -849,37 +920,28 @@
         hat_all,
     )
     got = swap(part_send, 0)
-    last = exchange(last_ready, (part_send,))
-    last_ready = prepare(last, plans, 1)
-    ready = prepare(exchange(ready, sends(last_ready)), plans, 3)
+    both = exchange(last_ready + ready, (part_send,))
+    last_ready = prepare(both[:2], plans, 1)
+    ready = prepare(both[2:], plans, 3)
     got = after(got, *sends(last_ready), *sends(ready))
     far_sum = (part[0] + got[0].astype(FULL)).astype(LOW)
     back = lax.ppermute(far_sum, ALL, [(b, a) for a, b in flips])
-    first_gain_grad, first_shift_grad, q_sum, v_sum = (
-        value[0] for value in (first_gain_grad, first_shift_grad, q_sum, v_sum)
-    )
-    zero = jnp.zeros((half,), FULL)
-    low_core = core == 0
-    qv_bias_grad = jnp.concatenate(
-        [
-            jnp.where(low_core, q_sum, zero),
-            jnp.where(low_core, zero, q_sum),
-            jnp.where(low_core, v_sum, zero),
-            jnp.where(low_core, zero, v_sum),
-        ]
-    )
-    grads = (
-        qv_bias_grad,
-        out_bias_grad,
-        fc_bias_grad,
-        proj_bias_grad,
-        first_gain_grad,
-        first_shift_grad,
-        second_gain_grad,
-        second_shift_grad,
-    )
-    sizes = [grad.shape[0] // count for grad in grads]
-    packed = jnp.concatenate([g.reshape(count, s) for g, s in zip(grads, sizes)], 1)
+    packed, sizes = pack(
+        core_at,
+        count,
+        q_sum,
+        v_sum,
+        (
+            out_bias_grad,
+            fc_bias_grad,
+            proj_bias_grad,
+            first_gain_grad,
+            first_shift_grad,
+            second_gain_grad,
+            second_shift_grad,
+        ),
+    )
+    packed = after(packed, far_sum)
     share = jnp.sum(lax.all_to_all(packed, ALL, 0, 0, tiled=True), 0, keepdims=True)
     for step in range(2, flat_bits() - 1):
         last = exchange(last_ready, (far_sum,))
@@ -909,10 +971,7 @@
     following = lax.ppermute(moved[:1], "ctx", [(i, i - 1) for i in range(1, ctx)])
     tokens_grad = (kept + jnp.concatenate([moved[1:], following], 0))[None]
 
-    shares, at = [], 0
-    for size in sizes:
-        shares.append(share[0, at : at + size])
-        at += size
+    shares = [share[0, i * LANES : i * LANES + size] for i, size in enumerate(sizes)]
     return (
         mixed,
         tokens_grad,

time: 322 us -> 299 us (0.929)
  local copies, waits for them, and re-layouts: 39.3 us -> 21.3 us
  waiting for transfers between devices: 70.1 us -> 64.2 us
    all_to_all x1, waiting for transfers between devices: 6.45 us -> 0.01 us  [shards(): lax.all_to_all(packed, ALL, 0, 0, tiled=True)]
    ppermute x1, waiting for transfers between devices: 0.01 us -> 6.35 us  [shards(): before = lax.ppermute(mine, ALL, flips)]
    another operation x8 -> x2, local copies, waits for them, and re-layouts: 6.11 us -> 0.16 us  [the longest x6 4.11 us: shards(): g.reshape(count, s)]
    select_n x4 -> x0, local copies, waits for them, and re-layouts: 5.41 us -> none  [the longest x1 1.36 us: shards(): jnp.where(low_core, v_sum, zero)]
    ppermute x34, waiting for transfers between devices: 44.4 us -> 39.6 us  [swap(): return lax.ppermute(value, ALL, [(i, i ^ 1 << bit) for i in range(count)])]
    pallas_call x0 -> x2, Pallas kernels: none -> 4.29 us  [the longest x1 2.47 us: pack(): pl.pallas_call(functools.partial(pack_kernel, slots), in_specs=[pl.BlockS...]
    dynamic_slice x8, local copies, waits for them, and re-layouts: 6.52 us -> 2.44 us  [total(): piece = lax.dynamic_slice(view, (*begin, 0, start), (*width, rows, size))]
    pallas_call x3 -> x1, Pallas kernels: 11 us -> 8.62 us  [attend(): pl.pallas_call(attend_kernel, out_shape=(jax.ShapeDtypeStruct((near, widt...]
  transfers between devices with their start and end apart: 39 -> 39, of which waited for: 19 -> 18; matrix products, arithmetic and copies ran while one was open for 23% -> 18% of each run, Pallas kernels for 15% -> 16%
where the time goes in v4:
time: 299 us; the launch traced here: 294 us
  Pallas kernels  79.1 us (26%)
  waiting for transfers between devices  64.2 us (21%)
  starting transfers between devices  55.9 us (19%)
  other arithmetic  51 us (17%)
  local copies, waits for them, and re-layouts  21.3 us (7%)
  between operations  16.2 us (5%)
  matrix products  6.19 us (2%)
    ppermute x34, starting transfers between devices, swap(): return lax.ppermute(value, ALL, [(i, i ^ 1 << bit) for i in range(count)])  44.1 us
    ppermute x34, waiting for transfers between devices, swap(): return lax.ppermute(value, ALL, [(i, i ^ 1 << bit) for i in range(count)])  39.6 us
    pallas_call x1, Pallas kernels, feed(): pl.pallas_call(functools.partial(feed_kernel, shard_rows), out_shape=(jax...  24.4 us
    pallas_call x3, Pallas kernels, attend_back(): pl.pallas_call(attend_back_kernel, out_shape=(jax.ShapeDtypeStruct((near,...  19.6 us
    convert_element_type x14, other arithmetic, prepare(): send = self.total(bit, 1 - bit_of(bit)).astype(self.kind)  16.7 us
    all_gather x1, waiting for transfers between devices, shards(): lax.all_gather(beside_rows(fc_weight, proj_weight, out_weight), ALL, axis...  16.1 us
    pallas_call x1, Pallas kernels, norm_back(): pl.pallas_call(norm_back_kernel, out_shape=(shape((2, quarter, width), FU...  9.96 us
    pallas_call x1, Pallas kernels, attend(): pl.pallas_call(attend_kernel, out_shape=(jax.ShapeDtypeStruct((near, widt...  8.62 us
  transfers between devices with their start and end apart: 39, of which 18 were waited for; matrix products, arithmetic and copies ran while one was open for 18% of the time, Pallas kernels for 16%

profile of v4, /device:TPU:1, one launch (start us, length us, event | category | flops | bytes accessed | tf_op | source)
XLA Modules:
  0.0 293.9 jit_solution(5219672553543730039)
XLA Ops:
  11.5 3.5 %collective-permute-start.4 = (bf16[1,48,1280]{2,1,0:T(8,128)(2,1)S(1)}, bf16[1,48,1280]{2,1,0:T(8,128)(2,1)S(1)}, u32[]{:S(2)}, u32[]{:S(2)}) collective-permute-start(bf16[1,48,1280]{2,1,0:T(8,128)(2,1)S(1)} %bitcast.321), channel_id=1, source_target_pairs={{0,16},{1,17},{2,18},{3,19},{4,20},{5,21},{6,22},{7,23},{8,24},{9,... | collective-permute-start | bytes 368648 | tf_op jit(solution)/shard_map/ppermute | solution.py:34
  15.0 6.0 %collective-permute-done.4 = bf16[1,48,1280]{2,1,0:T(8,128)(2,1)S(1)} collective-permute-done((bf16[1,48,1280]{2,1,0:T(8,128)(2,1)S(1)}, bf16[1,48,1280]{2,1,0:T(8,128)(2,1)S(1)}, u32[]{:S(2)}, u32[]{:S(2)}) %collective-permute-start.4) | collective-permute-done | bytes 122912 | tf_op jit(solution)/shard_map/ppermute | solution.py:34
  22.0 4.0 %collective-permute-start = (bf16[512,768]{1,0:T(8,128)(2,1)S(1)}, bf16[512,768]{1,0:T(8,128)(2,1)}, u32[]{:S(2)}, u32[]{:S(2)}) collective-permute-start(bf16[512,768]{1,0:T(8,128)(2,1)S(1)} %bitcast.308), channel_id=1, source_target_pairs={{0,2},{1,3},{4,6},{5,7},{8,10},{9,11},{12,14},{13,15},{16,18},{17,... | collective-permute-start | bytes 2359304 | tf_op jit(solution)/shard_map/ppermute | solution.py:780
  27.1 5.3 %collective-permute-done.5 = bf16[2,48,1280]{2,1,0:T(8,128)(2,1)S(1)} collective-permute-done((bf16[2,48,1280]{2,1,0:T(8,128)(2,1)S(1)}, bf16[2,48,1280]{2,1,0:T(8,128)(2,1)S(1)}, u32[]{:S(2)}, u32[]{:S(2)}) %collective-permute-start.5) | collective-permute-done | bytes 245792 | tf_op jit(solution)/shard_map/ppermute | solution.py:34
  34.9 6.3 %collective-permute-done = bf16[512,768]{1,0:T(8,128)(2,1)} collective-permute-done((bf16[512,768]{1,0:T(8,128)(2,1)S(1)}, bf16[512,768]{1,0:T(8,128)(2,1)}, u32[]{:S(2)}, u32[]{:S(2)}) %collective-permute-start) | collective-permute-done | bytes 786464 | tf_op jit(solution)/shard_map/ppermute | solution.py:780
  41.3 2.9 collective-permute-start.1
  47.4 3.9 %collective-permute-done.8 = bf16[4,48,768]{2,1,0:T(8,128)(2,1)} collective-permute-done((bf16[4,48,768]{2,1,0:T(8,128)(2,1)S(1)}, bf16[4,48,768]{2,1,0:T(8,128)(2,1)}, u32[]{:S(2)}, u32[]{:S(2)}) %collective-permute-start.8) | collective-permute-done | bytes 294944 | tf_op jit(solution)/shard_map/ppermute | solution.py:34
  56.7 3.1 %fusion.2 = f32[2048]{0:T(1024)S(1)} fusion(f32[2048]{0:T(1024)S(1)} %broadcast_multiply_fusion, bf16[1024,768]{1,0:T(8,128)(2,1)S(1)} %maximum_select_fusion.1, bf16[1024,768]{1,0:T(8,128)(2,1)S(1)} %maximum_select_fusion), kind=kLoop, calls=%fused_computation.4 | loop fusion | flops 11008000 | bytes 3162112 | tf_op jit(solution)/shard_map/reduce_sum | solution.py:731
  59.9 3.6 %fusion.hat_ref = f32[2048,768]{1,0:T(8,128)} fusion(f32[2048]{0:T(1024)S(1)} %add_rsqrt_fusion, f32[2048]{0:T(1024)S(1)} %broadcast_multiply_fusion, bf16[1024,768]{1,0:T(8,128)(2,1)S(1)} %maximum_select_fusion.1, bf16[1024,768]{1,0:T(8,128)(2,1)S(1)} %maximum_select_fusion), kind=kLoop, calls=%fused_computation.2 | loop fusion | flops 9437184 | bytes 9453568 | tf_op jit(solution)/shard_map/mul | solution.py:733
  69.9 2.8 add_convert_fusion.k_ref.v_ref
  72.7 8.6 %attend.1 = (bf16[1024,384]{1,0:T(8,128)(2,1)S(1)}, f32[3,8,1024]{2,1,0:T(8,128)S(1)}) custom-call(s32[1]{0:T(128)} %bitcast.7.far_ref, bf16[1024,384]{1,0:T(8,128)(2,1)S(1)} %add_convert_fusion.6.q_ref, bf16[2048,768]{1,0:T(8,128)(2,1)S(1)} %add_convert_fusion.k_ref.v_ref, bf16[2048,768]{1,0:T(8,128)(2,1)S(1)} %add_convert_fusion.k_ref.v_ref), custom_call_target="tpu_custom_call" | custom-call | flops 536870912 | bytes 524288 | tf_op jit(solution)/shard_map/attend/pallas_call | solution.py:215
  82.3 5.1 %collective-permute-start.10 = (bf16[512,384]{1,0:T(8,128)(2,1)S(1)}, bf16[512,384]{1,0:T(8,128)(2,1)S(1)}, u32[]{:S(2)}, u32[]{:S(2)}) collective-permute-start(bf16[512,384]{1,0:T(8,128)(2,1)S(1)} %constant_dynamic-slice_fusion.8), channel_id=1, source_target_pairs={{0,1},{1,0},{2,3},{3,2},{4,5},{5,4},{6,7},{7,6},{8,9},{9,8},{10,11... | collective-permute-start | bytes 1179656 | tf_op jit(solution)/shard_map/ppermute | solution.py:34
  89.4 16.1 %all-gather.2.cloned.1.call-done.fc_ref.refs_0_.refs_1_.refs_2_.refs_3_.w_ref = bf16[768,6912]{1,0:T(8,128)(2,1)} async-done(((bf16[24,6912]{1,0:T(8,128)(2,1)}), bf16[768,6912]{1,0:T(8,128)(2,1)}) %all-gather.2.cloned.1.call-update) | async-done | bytes 10616848 | tf_op jit(solution)/shard_map/all_gather | solution.py:774
  105.5 2.4 fusion.57
  109.7 24.4 %feed.1 = (f32[512,768]{1,0:T(8,128)S(1)}, f32[512,768]{1,0:T(8,128)S(1)}, bf16[768,1536]{1,0:T(8,128)(2,1)}, bf16[768,1536]{1,0:T(8,128)(2,1)}, bf16[3072,384]{...) custom-call(s32[1]{0:T(128)} %bitcast.29.core_ref, bf16[512,768]{1,0:T(8,128)(2,1)S(1)} %get-tuple-element.173.n_ref, ...), custom_call_target="tpu_custom_call" | custom-call | flops 536870912 | bytes 524288 | tf_op jit(solution)/shard_map/feed/pallas_call | solution.py:487
  137.2 5.5 %turn.1 = (f32[512,768]{1,0:T(8,128)S(1)}, bf16[512,384]{1,0:T(8,128)(2,1)S(1)}, bf16[512,384]{1,0:T(8,128)(2,1)S(1)}, bf16[768,384]{1,0:T(8,128)(2,1)S(1)}, bf1...) custom-call(s32[1]{0:T(128)} %bitcast.29.core_ref, ...), custom_call_target="tpu_custom_call" | custom-call | flops 536870912 | bytes 524288 | tf_op jit(solution)/shard_map/turn/pallas_call | solution.py:557
  144.7 2.8 add_convert_fusion.3
  148.8 2.7 add_convert_fusion.2
  156.2 6.6 %attend_back.3 = (bf16[1024,384]{1,0:T(8,128)(2,1)S(1)}, bf16[2048,384]{1,0:T(8,128)(2,1)S(1)}, bf16[2048,384]{1,0:T(8,128)(2,1)}) custom-call(s32[1]{0:T(128)} %bitcast.7.far_ref, bf16[1024,384]{1,0:T(8,128)(2,1)S(1)} %copy-done.2, bf16[2048,768]{1,0:T(8,128)(2,1)} %copy-done, bf16[2048,768]{1,0:T(8,128)(2,1)} %copy-done, bf16[1024,384]{1,0:T(8,128)(2,1)S(1)} %bitcast.268, ...), custom_call_target="tpu_custom_call" | custom-call | flops 536870912 | bytes 524288 | tf_op jit(solution)/shard_map/attend_back/pallas_call | solution.py:305
  162.8 6.4 %attend_back.4 = (bf16[1024,384]{1,0:T(8,128)(2,1)S(1)}, bf16[2048,384]{1,0:T(8,128)(2,1)S(1)}, bf16[2048,384]{1,0:T(8,128)(2,1)}) custom-call(s32[1]{0:T(128)} %bitcast.7.far_ref, bf16[1024,384]{1,0:T(8,128)(2,1)S(1)} %copy-done.2, bf16[2048,768]{1,0:T(8,128)(2,1)} %copy-done, ...), custom_call_target="tpu_custom_call", output_to_operand_aliasing={{0}: (7, {}), {1}: (8, {}), {2}: (9, {})} | custom-call | flops 536870912 | bytes 524288 | tf_op jit(solution)/shard_map/attend_back/pallas_call | solution.py:305
  172.2 3.0 %collective-permute-done.14 = bf16[8,48,1536]{2,1,0:T(8,128)(2,1)} collective-permute-done((bf16[8,48,1536]{2,1,0:T(8,128)(2,1)}, bf16[8,48,1536]{2,1,0:T(8,128)(2,1)}, u32[]{:S(2)}, u32[]{:S(2)}) %collective-permute-start.14) | collective-permute-done | bytes 1179680 | tf_op jit(solution)/shard_map/ppermute | solution.py:34
  175.3 3.5 %collective-permute-done.15 = bf16[8,192,384]{2,1,0:T(8,128)(2,1)} collective-permute-done((bf16[8,192,384]{2,1,0:T(8,128)(2,1)}, bf16[8,192,384]{2,1,0:T(8,128)(2,1)}, u32[]{:S(2)}, u32[]{:S(2)}) %collective-permute-start.15) | collective-permute-done | bytes 1179680 | tf_op jit(solution)/shard_map/ppermute | solution.py:34
  183.9 4.6 %collective-permute-start.17 = (bf16[4,192,384]{2,1,0:T(8,128)(2,1)}, bf16[4,192,384]{2,1,0:T(8,128)(2,1)}, u32[]{:S(2)}, u32[]{:S(2)}) collective-permute-start(bf16[4,192,384]{2,1,0:T(8,128)(2,1)} %fusion.9), channel_id=1, source_target_pairs={{0,2},{1,3},{2,0},{3,1},{4,6},{5,7},{6,4},{7,5},{8,10},{9,11},{10,... | collective-permute-start | bytes 1769480 | tf_op jit(solution)/shard_map/ppermute | solution.py:34
  191.0 6.6 %attend_back.5 = (bf16[1024,384]{1,0:T(8,128)(2,1)S(1)}, bf16[2048,384]{1,0:T(8,128)(2,1)S(1)}, bf16[2048,384]{1,0:T(8,128)(2,1)}) custom-call(s32[1]{0:T(128)} %bitcast.7.far_ref, bf16[1024,384]{1,0:T(8,128)(2,1)S(1)} %copy-done.2, bf16[2048,768]{1,0:T(8,128)(2,1)} %copy-done, ...), custom_call_target="tpu_custom_call", output_to_operand_aliasing={{0}: (7, {}), {1}: (8, {}), {2}: (9, {})} | custom-call | flops 536870912 | bytes 524288 | tf_op jit(solution)/shard_map/attend_back/pallas_call | solution.py:305
  198.5 3.6 %collective-permute-done.17 = bf16[4,192,384]{2,1,0:T(8,128)(2,1)} collective-permute-done((bf16[4,192,384]{2,1,0:T(8,128)(2,1)}, bf16[4,192,384]{2,1,0:T(8,128)(2,1)}, u32[]{:S(2)}, u32[]{:S(2)}) %collective-permute-start.17) | collective-permute-done | bytes 589856 | tf_op jit(solution)/shard_map/ppermute | solution.py:34
  204.9 6.7 %qkv_grads.1 = (bf16[768,768]{1,0:T(8,128)(2,1)S(1)}, bf16[768,768]{1,0:T(8,128)(2,1)S(1)}) custom-call(bf16[2048,768]{1,0:T(8,128)(2,1)} %copy-done.30, bf16[1024,384]{1,0:T(8,128)(2,1)S(1)} %copy-done.10, bf16[2048,384]{1,0:T(8,128)(2,1)S(1)} %get-tuple-element.126.dk_ref, bf16[2048,384]{1,0:T(8,128)(2,1)} %get-tuple-element.127.dv_ref, ...), custom_call_target="tpu_custom_call" | custom-call | flops 536870912 | bytes 524288 | tf_op jit(solution)/shard_map/qkv_grads/pallas_call | solution.py:354
  216.5 10.0 %norm_back.1 = (f32[2,512,768]{2,1,0:T(8,128)}, bf16[2,512,768]{2,1,0:T(8,128)(2,1)S(1)}, f32[1,768]{1,0:T(1,128)S(1)}, f32[1,768]{1,0:T(1,128)S(1)}, f32[1,384]{1,0:T(1,128)S(1)}, /*index=5*/f32[1,384]{1,0:T(1,128)S(1)}) custom-call(s32[1]{0:T(128)} %bitcast.29.core_ref, bf16[1024,384]{1,0:T(8,128)(2,1)S(1)} %copy-done.10, ...), custom_call_target="tpu_custom_call" | custom-call | flops 536870912 | bytes 524288 | tf_op jit(solution)/shard_map/norm_back/pallas_call | solution.py:646
  229.2 2.5 pack.1
  243.8 2.4 collective-permute-done.33
  246.2 3.2 %collective-permute-done.34 = bf16[1,192,384]{2,1,0:T(8,128)(2,1)S(1)} collective-permute-done((bf16[1,192,384]{2,1,0:T(8,128)(2,1)S(1)}, bf16[1,192,384]{2,1,0:T(8,128)(2,1)S(1)}, u32[]{:S(2)}, u32[]{:S(2)}) %collective-permute-start.34) | collective-permute-done | bytes 147488 | tf_op jit(solution)/shard_map/ppermute | solution.py:34
  255.4 4.3 %all-to-all-start = ((f32[32,1,1024]{2,1,0:T(1,128)}), f32[32,1,1024]{2,1,0:T(1,128)S(1)}, u32[]{:S(2)}, u32[]{:S(2)}) async-start(f32[32,1,1024]{2,1,0:T(1,128)} %copy.106), calls=%async_computation | async-start | bytes 262144 | tf_op jit(solution)/shard_map/all_to_all | solution.py:945
  275.8 2.8 fusion.51
  (289 shorter events, 102.4 us)
Async XLA Ops:
  7.3 98.2 %all-gather.2.cloned.1.call-start = ((), (), s32[]{:S(2)}) async-start(), calls=%async_computation.1 | async-start | bytes 10948608 | tf_op jit(solution)/shard_map/all_gather | solution.py:774
  11.5 9.6 %collective-permute-start.4 = (bf16[1,48,1280]{2,1,0:T(8,128)(2,1)S(1)}, bf16[1,48,1280]{2,1,0:T(8,128)(2,1)S(1)}, u32[]{:S(2)}, u32[]{:S(2)}) collective-permute-start(bf16[1,48,1280]{2,1,0:T(8,128)(2,1)S(1)} %bitcast.321), channel_id=1, source_target_pairs={{0,16},{1,17},{2,18},{3,19},{4,20},{5,21},{6,22},{7,23},{8,24},{9,... | collective-permute-start | bytes 368648 | tf_op jit(solution)/shard_map/ppermute | solution.py:34
  21.1 11.2 %collective-permute-start.5 = (bf16[2,48,1280]{2,1,0:T(8,128)(2,1)S(1)}, bf16[2,48,1280]{2,1,0:T(8,128)(2,1)S(1)}, u32[]{:S(2)}, u32[]{:S(2)}) collective-permute-start(bf16[2,48,1280]{2,1,0:T(8,128)(2,1)S(1)} %constant_dynamic-update-slice_fusion.1), channel_id=1, source_target_pairs={{0,8},{1,9},{2,10},{3,11},{4,12},{5,13},{6,14},{7,15},{8,0},{9,1},... | collective-permute-start | bytes 737288 | tf_op jit(solution)/shard_map/ppermute | solution.py:34
  22.0 19.2 %collective-permute-start = (bf16[512,768]{1,0:T(8,128)(2,1)S(1)}, bf16[512,768]{1,0:T(8,128)(2,1)}, u32[]{:S(2)}, u32[]{:S(2)}) collective-permute-start(bf16[512,768]{1,0:T(8,128)(2,1)S(1)} %bitcast.308), channel_id=1, source_target_pairs={{0,2},{1,3},{4,6},{5,7},{8,10},{9,11},{12,14},{13,15},{16,18},{17,... | collective-permute-start | bytes 2359304 | tf_op jit(solution)/shard_map/ppermute | solution.py:780
  26.1 27.3 %collective-permute-start.2 = (bf16[512,768]{1,0:T(8,128)(2,1)S(1)}, bf16[512,768]{1,0:T(8,128)(2,1)S(1)}, u32[]{:S(2)}, u32[]{:S(2)}) collective-permute-start(bf16[512,768]{1,0:T(8,128)(2,1)S(1)} %bitcast.309), channel_id=1, source_target_pairs={{0,1},{1,0},{2,3},{3,2},{4,5},{5,4},{6,7},{7,6},{8,9},{9,8},{10,11... | collective-permute-start | bytes 2359304 | tf_op jit(solution)/shard_map/ppermute | solution.py:34
  32.5 12.4 %collective-permute-start.6 = (bf16[4,48,512]{2,1,0:T(8,128)(2,1)S(1)}, bf16[4,48,512]{2,1,0:T(8,128)(2,1)S(1)}, u32[]{:S(2)}, u32[]{:S(2)}) collective-permute-start(bf16[4,48,512]{2,1,0:T(8,128)(2,1)S(1)} %pad_maximum_fusion.4), channel_id=1, source_target_pairs={{0,4},{1,5},{2,6},{3,7},{4,0},{5,1},{6,2},{7,3},{8,12},{9,13},{10,... | collective-permute-start | bytes 589832 | tf_op jit(solution)/shard_map/ppermute | solution.py:34
  33.5 17.8 %collective-permute-start.8 = (bf16[4,48,768]{2,1,0:T(8,128)(2,1)S(1)}, bf16[4,48,768]{2,1,0:T(8,128)(2,1)}, u32[]{:S(2)}, u32[]{:S(2)}) collective-permute-start(bf16[4,48,768]{2,1,0:T(8,128)(2,1)S(1)} %slice.205), channel_id=1, source_target_pairs={{0,2},{1,3},{2,0},{3,1},{4,6},{5,7},{6,4},{7,5},{8,10},{9,11},{10,... | collective-permute-start | bytes 884744 | tf_op jit(solution)/shard_map/ppermute | solution.py:34
  41.3 12.3 %collective-permute-start.1 = (bf16[512,768]{1,0:T(8,128)(2,1)}, bf16[512,768]{1,0:T(8,128)(2,1)S(1)}, u32[]{:S(2)}, u32[]{:S(2)}) collective-permute-start(bf16[512,768]{1,0:T(8,128)(2,1)} %collective-permute-done), channel_id=1, source_target_pairs={{0,1},{1,0},{2,3},{3,2},{4,5},{5,4},{6,7},{7,6},{8,9},{9,8},{10,11... | collective-permute-start | bytes 2359304 | tf_op jit(solution)/shard_map/ppermute | solution.py:34
  45.0 18.5 %collective-permute-start.7 = (bf16[8,48,512]{2,1,0:T(8,128)(2,1)S(1)}, bf16[8,48,512]{2,1,0:T(8,128)(2,1)S(1)}, u32[]{:S(2)}, u32[]{:S(2)}) collective-permute-start(bf16[8,48,512]{2,1,0:T(8,128)(2,1)S(1)} %bitcast.306), channel_id=1, source_target_pairs={{0,2},{1,3},{2,0},{3,1},{4,6},{5,7},{6,4},{7,5},{8,10},{9,11},{10,... | collective-permute-start | bytes 1179656 | tf_op jit(solution)/shard_map/ppermute | solution.py:34
  52.3 12.1 %collective-permute-start.9 = (bf16[8,48,768]{2,1,0:T(8,128)(2,1)S(1)}, bf16[8,48,768]{2,1,0:T(8,128)(2,1)}, u32[]{:S(2)}, u32[]{:S(2)}) collective-permute-start(bf16[8,48,768]{2,1,0:T(8,128)(2,1)S(1)} %bitcast.291), channel_id=1, source_target_pairs={{0,4},{1,5},{2,6},{3,7},{4,0},{5,1},{6,2},{7,3},{8,12},{9,13},{10,... | collective-permute-start | bytes 1769480 | tf_op jit(solution)/shard_map/ppermute | solution.py:34
  136.7 8.0 %collective-permute-start.13 = (bf16[3072,384]{1,0:T(8,128)(2,1)}, bf16[3072,384]{1,0:T(8,128)(2,1)}, u32[]{:S(2)}, u32[]{:S(2)}) collective-permute-start(bf16[3072,384]{1,0:T(8,128)(2,1)} %get-tuple-element.105), channel_id=1, source_target_pairs={{0,1},{1,0},{2,3},{3,2},{4,5},{5,4},{6,7},{7,6},{8,9},{9,8},{10,11... | collective-permute-start | bytes 7077896 | tf_op jit(solution)/shard_map/ppermute | solution.py:34
  147.6 27.7 %collective-permute-start.14 = (bf16[8,48,1536]{2,1,0:T(8,128)(2,1)}, bf16[8,48,1536]{2,1,0:T(8,128)(2,1)}, u32[]{:S(2)}, u32[]{:S(2)}) collective-permute-start(bf16[8,48,1536]{2,1,0:T(8,128)(2,1)} %bitcast.38), channel_id=1, source_target_pairs={{0,2},{1,3},{2,0},{3,1},{4,6},{5,7},{6,4},{7,5},{8,10},{9,11},{10,... | collective-permute-start | bytes 3538952 | tf_op jit(solution)/shard_map/ppermute | solution.py:34
  151.5 27.3 %collective-permute-start.15 = (bf16[8,192,384]{2,1,0:T(8,128)(2,1)}, bf16[8,192,384]{2,1,0:T(8,128)(2,1)}, u32[]{:S(2)}, u32[]{:S(2)}) collective-permute-start(bf16[8,192,384]{2,1,0:T(8,128)(2,1)} %bitcast.41), channel_id=1, source_target_pairs={{0,4},{1,5},{2,6},{3,7},{4,0},{5,1},{6,2},{7,3},{8,12},{9,13},{10,... | collective-permute-start | bytes 3538952 | tf_op jit(solution)/shard_map/ppermute | solution.py:34
  154.6 43.9 %collective-permute-start.18 = (bf16[768,384]{1,0:T(8,128)(2,1)}, bf16[768,384]{1,0:T(8,128)(2,1)}, u32[]{:S(2)}, u32[]{:S(2)}) collective-permute-start(bf16[768,384]{1,0:T(8,128)(2,1)} %get-tuple-element.130), channel_id=1, source_target_pairs={{0,1},{1,0},{2,3},{3,2},{4,5},{5,4},{6,7},{7,6},{8,9},{9,8},{10,11... | collective-permute-start | bytes 1769480 | tf_op jit(solution)/shard_map/ppermute | solution.py:34
  182.0 16.5 %collective-permute-start.16 = (bf16[4,48,1536]{2,1,0:T(8,128)(2,1)}, bf16[4,48,1536]{2,1,0:T(8,128)(2,1)}, u32[]{:S(2)}, u32[]{:S(2)}) collective-permute-start(bf16[4,48,1536]{2,1,0:T(8,128)(2,1)} %fusion.10), channel_id=1, source_target_pairs={{0,4},{1,5},{2,6},{3,7},{4,0},{5,1},{6,2},{7,3},{8,12},{9,13},{10,... | collective-permute-start | bytes 1769480 | tf_op jit(solution)/shard_map/ppermute | solution.py:34
  183.9 18.2 %collective-permute-start.17 = (bf16[4,192,384]{2,1,0:T(8,128)(2,1)}, bf16[4,192,384]{2,1,0:T(8,128)(2,1)}, u32[]{:S(2)}, u32[]{:S(2)}) collective-permute-start(bf16[4,192,384]{2,1,0:T(8,128)(2,1)} %fusion.9), channel_id=1, source_target_pairs={{0,2},{1,3},{2,0},{3,1},{4,6},{5,7},{6,4},{7,5},{8,10},{9,11},{10,... | collective-permute-start | bytes 1769480 | tf_op jit(solution)/shard_map/ppermute | solution.py:34
  211.8 20.0 %collective-permute-start.20 = (bf16[8,48,768]{2,1,0:T(8,128)(2,1)S(1)}, bf16[8,48,768]{2,1,0:T(8,128)(2,1)S(1)}, u32[]{:S(2)}, u32[]{:S(2)}) collective-permute-start(bf16[8,48,768]{2,1,0:T(8,128)(2,1)S(1)} %bitcast.312), channel_id=1, source_target_pairs={{0,2},{1,3},{2,0},{3,1},{4,6},{5,7},{6,4},{7,5},{8,10},{9,11},{10,... | collective-permute-start | bytes 1769480 | tf_op jit(solution)/shard_map/ppermute | solution.py:34
  213.9 17.9 %collective-permute-start.21 = (bf16[8,48,768]{2,1,0:T(8,128)(2,1)S(1)}, bf16[8,48,768]{2,1,0:T(8,128)(2,1)S(1)}, u32[]{:S(2)}, u32[]{:S(2)}) collective-permute-start(bf16[8,48,768]{2,1,0:T(8,128)(2,1)S(1)} %bitcast.311), channel_id=1, source_target_pairs={{0,4},{1,5},{2,6},{3,7},{4,0},{5,1},{6,2},{7,3},{8,12},{9,13},{10,... | collective-permute-start | bytes 1769480 | tf_op jit(solution)/shard_map/ppermute | solution.py:34
  215.0 16.7 %collective-permute-start.22 = (bf16[2,48,1536]{2,1,0:T(8,128)(2,1)S(1)}, bf16[2,48,1536]{2,1,0:T(8,128)(2,1)S(1)}, u32[]{:S(2)}, u32[]{:S(2)}) collective-permute-start(bf16[2,48,1536]{2,1,0:T(8,128)(2,1)S(1)} %fusion.17), channel_id=1, source_target_pairs={{0,8},{1,9},{2,10},{3,11},{4,12},{5,13},{6,14},{7,15},{8,0},{9,1},... | collective-permute-start | bytes 884744 | tf_op jit(solution)/shard_map/ppermute | solution.py:34
  216.1 15.7 %collective-permute-start.23 = (bf16[2,192,384]{2,1,0:T(8,128)(2,1)S(1)}, bf16[2,192,384]{2,1,0:T(8,128)(2,1)S(1)}, u32[]{:S(2)}, u32[]{:S(2)}) collective-permute-start(bf16[2,192,384]{2,1,0:T(8,128)(2,1)S(1)} %fusion.16), channel_id=1, source_target_pairs={{0,8},{1,9},{2,10},{3,11},{4,12},{5,13},{6,14},{7,15},{8,0},{9,1},... | collective-permute-start | bytes 884744 | tf_op jit(solution)/shard_map/ppermute | solution.py:34
  226.5 11.2 %collective-permute-start.19 = (bf16[2,512,768]{2,1,0:T(8,128)(2,1)S(1)}, bf16[2,512,768]{2,1,0:T(8,128)(2,1)S(1)}, u32[]{:S(2)}, u32[]{:S(2)}) collective-permute-start(bf16[2,512,768]{2,1,0:T(8,128)(2,1)S(1)} %get-tuple-element.136), channel_id=1, source_target_pairs={{0,1},{1,0},{2,3},{3,2},{4,5},{5,4},{6,7},{7,6},{8,9},{9,8},{10,11... | collective-permute-start | bytes 4718600 | tf_op jit(solution)/shard_map/ppermute | solution.py:34
  232.0 8.7 %collective-permute-start.26 = (bf16[4,48,768]{2,1,0:T(8,128)(2,1)S(1)}, bf16[4,48,768]{2,1,0:T(8,128)(2,1)S(1)}, u32[]{:S(2)}, u32[]{:S(2)}) collective-permute-start(bf16[4,48,768]{2,1,0:T(8,128)(2,1)S(1)} %fusion.15), channel_id=1, source_target_pairs={{0,4},{1,5},{2,6},{3,7},{4,0},{5,1},{6,2},{7,3},{8,12},{9,13},{10,... | collective-permute-start | bytes 884744 | tf_op jit(solution)/shard_map/ppermute | solution.py:34
  232.5 8.4 %collective-permute-start.27 = (bf16[4,48,768]{2,1,0:T(8,128)(2,1)S(1)}, bf16[4,48,768]{2,1,0:T(8,128)(2,1)S(1)}, u32[]{:S(2)}, u32[]{:S(2)}) collective-permute-start(bf16[4,48,768]{2,1,0:T(8,128)(2,1)S(1)} %fusion.14), channel_id=1, source_target_pairs={{0,2},{1,3},{2,0},{3,1},{4,6},{5,7},{6,4},{7,5},{8,10},{9,11},{10,... | collective-permute-start | bytes 884744 | tf_op jit(solution)/shard_map/ppermute | solution.py:34
  233.9 12.3 %collective-permute-start.33 = (bf16[1,48,1536]{2,1,0:T(8,128)(2,1)S(1)}, bf16[1,48,1536]{2,1,0:T(8,128)(2,1)S(1)}, u32[]{:S(2)}, u32[]{:S(2)}) collective-permute-start(bf16[1,48,1536]{2,1,0:T(8,128)(2,1)S(1)} %fusion.27), channel_id=1, source_target_pairs={{0,16},{1,17},{2,18},{3,19},{4,20},{5,21},{6,22},{7,23},{8,24},{9,... | collective-permute-start | bytes 442376 | tf_op jit(solution)/shard_map/ppermute | solution.py:34
  236.8 12.6 %collective-permute-start.34 = (bf16[1,192,384]{2,1,0:T(8,128)(2,1)S(1)}, bf16[1,192,384]{2,1,0:T(8,128)(2,1)S(1)}, u32[]{:S(2)}, u32[]{:S(2)}) collective-permute-start(bf16[1,192,384]{2,1,0:T(8,128)(2,1)S(1)} %fusion.25), channel_id=1, source_target_pairs={{0,16},{1,17},{2,18},{3,19},{4,20},{5,21},{6,22},{7,23},{8,24},{9,... | collective-permute-start | bytes 442376 | tf_op jit(solution)/shard_map/ppermute | solution.py:34
  238.7 37.0 %collective-permute-start.24 = (bf16[512,768]{1,0:T(8,128)(2,1)}, bf16[512,768]{1,0:T(8,128)(2,1)}, u32[]{:S(2)}, u32[]{:S(2)}) collective-permute-start(bf16[512,768]{1,0:T(8,128)(2,1)} %fusion.13), channel_id=1, source_target_pairs={{2,0},{3,1},{6,4},{7,5},{10,8},{11,9},{14,12},{15,13},{18,16},{19,... | collective-permute-start | bytes 2359304 | tf_op jit(solution)/shard_map/ppermute | solution.py:928
  241.6 18.1 %collective-permute-start.28 = (bf16[2,48,768]{2,1,0:T(8,128)(2,1)}, bf16[2,48,768]{2,1,0:T(8,128)(2,1)}, u32[]{:S(2)}, u32[]{:S(2)}) collective-permute-start(bf16[2,48,768]{2,1,0:T(8,128)(2,1)} %fusion.23), channel_id=1, source_target_pairs={{0,8},{1,9},{2,10},{3,11},{4,12},{5,13},{6,14},{7,15},{8,0},{9,1},... | collective-permute-start | bytes 442376 | tf_op jit(solution)/shard_map/ppermute | solution.py:34
  243.4 16.3 %collective-permute-start.29 = (bf16[2,48,768]{2,1,0:T(8,128)(2,1)}, bf16[2,48,768]{2,1,0:T(8,128)(2,1)}, u32[]{:S(2)}, u32[]{:S(2)}) collective-permute-start(bf16[2,48,768]{2,1,0:T(8,128)(2,1)} %fusion.22), channel_id=1, source_target_pairs={{0,8},{1,9},{2,10},{3,11},{4,12},{5,13},{6,14},{7,15},{8,0},{9,1},... | collective-permute-start | bytes 442376 | tf_op jit(solution)/shard_map/ppermute | solution.py:34
  251.3 12.9 %collective-permute-start.35 = (f32[24,1536]{1,0:T(8,128)}, f32[24,1536]{1,0:T(8,128)}, u32[]{:S(2)}, u32[]{:S(2)}) collective-permute-start(f32[24,1536]{1,0:T(8,128)} %dynamic-slice_bitcast_fusion.1), channel_id=1, source_target_pairs={{0,1},{1,0},{2,3},{3,2},{4,5},{5,4},{6,7},{7,6},{8,9},{9,8},{10,11... | collective-permute-start | bytes 442376 | tf_op jit(solution)/shard_map/ppermute | solution.py:34
  254.6 11.3 %collective-permute-start.36 = (f32[96,384]{1,0:T(8,128)}, f32[96,384]{1,0:T(8,128)}, u32[]{:S(2)}, u32[]{:S(2)}) collective-permute-start(f32[96,384]{1,0:T(8,128)} %dynamic-slice_bitcast_fusion), channel_id=1, source_target_pairs={{0,1},{1,0},{2,3},{3,2},{4,5},{5,4},{6,7},{7,6},{8,9},{9,8},{10,11... | collective-permute-start | bytes 442376 | tf_op jit(solution)/shard_map/ppermute | solution.py:34
  255.4 18.6 %all-to-all-start = ((f32[32,1,1024]{2,1,0:T(1,128)}), f32[32,1,1024]{2,1,0:T(1,128)S(1)}, u32[]{:S(2)}, u32[]{:S(2)}) async-start(f32[32,1,1024]{2,1,0:T(1,128)} %copy.106), calls=%async_computation | async-start | bytes 262144 | tf_op jit(solution)/shard_map/all_to_all | solution.py:945
  260.8 8.9 %collective-permute-start.30 = (bf16[1,48,768]{2,1,0:T(8,128)(2,1)S(1)}, bf16[1,48,768]{2,1,0:T(8,128)(2,1)S(1)}, u32[]{:S(2)}, u32[]{:S(2)}) collective-permute-start(bf16[1,48,768]{2,1,0:T(8,128)(2,1)S(1)} %fusion.36), channel_id=1, source_target_pairs={{0,16},{1,17},{2,18},{3,19},{4,20},{5,21},{6,22},{7,23},{8,24},{9,... | collective-permute-start | bytes 221192 | tf_op jit(solution)/shard_map/ppermute | solution.py:34
  (57 other events, 321.3 us)
Sparse Core Ops, SparseCore 0:
  11.0 94.4 all-gather.1

commit v5 on v4

--- a/solution.py
+++ b/solution.py
@@ -14,7 +14,8 @@
 LANES = 128
 SCALE = 0.125
 VMEM = 48 << 20
-SHORT = pl.CostEstimate(flops=1 << 29, bytes_accessed=1 << 19, transcendentals=0)
+SHORT = pl.CostEstimate(flops=1 << 20, bytes_accessed=1 << 12, transcendentals=0)
+LONG = pl.CostEstimate(flops=12 << 30, bytes_accessed=1 << 12, transcendentals=0)
 
 
 def flat_bits():
@@ -65,10 +66,10 @@
     return whole.reshape(high * 2 * low, rows, cols)
 
 
-def gather_common(block):
+def gather_common(block, wait=()):
     block, done = block[None], []
     for bit in reversed(range(3, flat_bits())):
-        block = grow(block, done, bit)
+        block = grow(block, done, bit, () if done else wait)
         done.append(bit)
     return block
 
@@ -83,40 +84,74 @@
 
 
 class Sum:
-    def __init__(self, addends, left, kind=LOW):
+    def __init__(self, addends, left):
         self.addends = addends
         self.left = left
-        self.kind = kind
-
-    def total(self, bit=None, place=None):
-        result = None
-        for value, bits, (start, size) in self.addends:
-            rows = value.shape[1]
-            dims, begin, width = [], [], []
-            for b in sorted(bits, reverse=True):
-                dims.append(2)
-                if b == bit:
-                    begin.append(place)
-                    width.append(1)
-                elif b in self.left:
-                    begin.append(0)
-                    width.append(2)
-                else:
-                    begin.append(bit_of(b))
-                    width.append(1)
-            view = value.reshape(*dims, rows, value.shape[2])
-            piece = lax.dynamic_slice(view, (*begin, 0, start), (*width, rows, size))
-            piece = piece.reshape(-1, rows, size).astype(FULL)
-            result = piece if result is None else result + piece
-        return result
-
-    def prepare(self, bit):
-        send = self.total(bit, 1 - bit_of(bit)).astype(self.kind)
-        return send, Sum(self.addends, [b for b in self.left if b != bit], self.kind), bit
+
+
+def group_of(bits, left, bit):
+    order, rest = sorted(bits, reverse=True), sorted(left, reverse=True)
+
+    def index(i, s):
+        group = 0
+        for b in order:
+            here = (s[0] >> b) & 1
+            if b == bit:
+                here = 1 - here
+            elif b in rest:
+                here = (i >> (len(rest) - 1 - rest.index(b))) & 1
+            group = 2 * group + here
+        return (group, 0, 0)
+
+    return index
+
+
+def total_of(refs):
+    total = refs[0][0].astype(FULL)
+    for ref in refs[1:]:
+        total = total + ref[0].astype(FULL)
+    return total
+
+
+def send_kernel(counts, at_ref, *refs):
+    outs = refs[len(refs) - len(counts) :]
+    for count, out_ref in zip(counts, outs):
+        out_ref[0] = total_of(refs[:count]).astype(LOW)
+        refs = refs[count:]
+
+
+def specs_of(sums, bits):
+    arrays, specs = [], []
+    for value, bit in zip(sums, bits):
+        left = [b for b in value.left if b != bit]
+        for array, own in value.addends:
+            arrays.append(array)
+            specs.append(pl.BlockSpec((1, *array.shape[1:]), group_of(own, left, bit)))
+    return arrays, specs
 
 
 def prepare(sums, plans, step):
-    return [value.prepare(plan[step]) for value, plan in zip(sums, plans)]
+    bits = [plan[step] for plan in plans]
+    arrays, specs = specs_of(sums, bits)
+    groups = 1 << (len(sums[0].left) - 1)
+    shapes = [value.addends[0][0].shape[1:] for value in sums]
+    sent = pl.pallas_call(
+        functools.partial(send_kernel, [len(value.addends) for value in sums]),
+        out_shape=tuple(jax.ShapeDtypeStruct((groups, *shape), LOW) for shape in shapes),
+        grid_spec=pltpu.PrefetchScalarGridSpec(
+            num_scalar_prefetch=1,
+            grid=(groups,),
+            in_specs=specs,
+            out_specs=tuple(pl.BlockSpec((1, *shape), lambda i, s: (i, 0, 0)) for shape in shapes),
+        ),
+        compiler_params=pltpu.CompilerParams(vmem_limit_bytes=VMEM),
+        cost_estimate=LONG,
+        name="send",
+    )(flat_index().astype(jnp.int32).reshape(1), *arrays)
+    return [
+        (send, Sum(value.addends, [b for b in value.left if b != bit]), bit)
+        for send, value, bit in zip(sent, sums, bits)
+    ]
 
 
 def sends(prepared):
@@ -127,21 +162,88 @@
     gots = [swap(send, bit) for send, _, bit in prepared]
     gots = after(gots, *wait) if wait else gots
     return [
-        Sum(keep.addends + [(got, keep.left, (0, got.shape[2]))], keep.left, keep.kind)
+        Sum(keep.addends + [(got, keep.left)], keep.left)
         for got, (_, keep, _) in zip(gots, prepared)
     ]
 
 
-def start_sum(arrays, start, size, kind=LOW):
+def start_sum(arrays):
     links = list(range(1, flat_bits()))
-    return Sum([(value, links, (start, size)) for value in arrays], links, kind)
-
-
-def finish(total, rows):
-    core = bit_of(0)
-    mine = lax.dynamic_slice_in_dim(total, core * rows, rows, 0)
-    other = swap(lax.dynamic_slice_in_dim(total, (1 - core) * rows, rows, 0), 0)
-    return jnp.where(core == 0, mine, other), jnp.where(core == 0, other, mine)
+    return Sum([(value, links) for value in arrays], links)
+
+
+def finish_kernel(counts, at_ref, *refs):
+    mine_ref, send_ref = refs[-2:]
+    rows = mine_ref.shape[0]
+    first = (at_ref[0] & 1) == 0
+    column = 0
+    for count in counts:
+        total = total_of(refs[:count])
+        refs = refs[count:]
+        half, cols = total.shape[0] // 2, total.shape[1]
+        one, two = total[:half], total[half:]
+        mine, other = jnp.where(first, one, two), jnp.where(first, two, one)
+        for at in range(0, half, rows):
+            mine_ref[:, column : column + cols] = mine[at : at + rows]
+            send_ref[:, column : column + cols] = other[at : at + rows]
+            column += cols
+
+
+def settle_kernel(at_ref, mine_ref, other_ref, fc_ref, proj_ref, qkv_ref, out_ref):
+    first = (at_ref[0] & 1) == 0
+    rows = mine_ref.shape[0]
+    half = out_ref.shape[1] // 2
+    start = 0
+
+    def both(size):
+        mine, other = mine_ref[:, start : start + size], other_ref[:, start : start + size]
+        return jnp.where(first, mine, other), jnp.where(first, other, mine)
+
+    size = fc_ref.shape[1] // 2
+    fc_ref[:, :size], fc_ref[:, size:] = both(size)
+    start += size
+    for at in range(0, proj_ref.shape[0], rows):
+        proj_ref[at : at + rows, :half], proj_ref[at : at + rows, half:] = both(half)
+        start += half
+    for kind in range(3):
+        at = 2 * kind * half
+        qkv_ref[:, at : at + half], qkv_ref[:, at + half : at + 2 * half] = both(half)
+        start += half
+    out_ref[:, :half], out_ref[:, half:] = both(half)
+
+
+def finish(sums, rows, widths):
+    at = flat_index().astype(jnp.int32).reshape(1)
+    arrays, specs = specs_of(sums, [None] * len(sums))
+    total = sum(
+        value.addends[0][0].shape[1] // (2 * rows) * value.addends[0][0].shape[2]
+        for value in sums
+    )
+    shape = jax.ShapeDtypeStruct
+    whole = pl.BlockSpec((rows, total), lambda i, s: (0, 0))
+    mine, send = pl.pallas_call(
+        functools.partial(finish_kernel, [len(value.addends) for value in sums]),
+        out_shape=(shape((rows, total), FULL),) * 2,
+        grid_spec=pltpu.PrefetchScalarGridSpec(
+            num_scalar_prefetch=1, grid=(1,), in_specs=specs, out_specs=(whole, whole)
+        ),
+        compiler_params=pltpu.CompilerParams(vmem_limit_bytes=VMEM),
+        cost_estimate=SHORT,
+        name="finish",
+    )(at, *arrays)
+    return pl.pallas_call(
+        settle_kernel,
+        out_shape=tuple(shape(size, FULL) for size in widths),
+        grid_spec=pltpu.PrefetchScalarGridSpec(
+            num_scalar_prefetch=1,
+            grid=(1,),
+            in_specs=[whole, whole],
+            out_specs=tuple(pl.BlockSpec(size, lambda i, s: (0, 0)) for size in widths),
+        ),
+        compiler_params=pltpu.CompilerParams(vmem_limit_bytes=VMEM),
+        cost_estimate=SHORT,
+        name="settle",
+    )(at, mine, swap(send, 0))
 
 
 def dot(a, b):
@@ -714,15 +816,21 @@
     size = 4 * q_sum.shape[1] // count
     slots = [[(0, size, 0, count // 4), (1, size, count // 2, count // 4)]]
     slots += [[(2 + i, line.shape[1] // count, 0, 0)] for i, line in enumerate(lines)]
-    vmem = pl.BlockSpec(memory_space=pltpu.VMEM)
+    lines = (q_sum, v_sum, *lines)
+    whole = lambda i, s: (0, 0)
     packed = pl.pallas_call(
         functools.partial(pack_kernel, slots),
-        in_specs=[pl.BlockSpec(memory_space=pltpu.SMEM)] + [vmem] * (2 + len(lines)),
         out_shape=jax.ShapeDtypeStruct((count, len(slots) * LANES), FULL),
+        grid_spec=pltpu.PrefetchScalarGridSpec(
+            num_scalar_prefetch=1,
+            grid=(1,),
+            in_specs=[pl.BlockSpec(line.shape, whole) for line in lines],
+            out_specs=pl.BlockSpec((count, len(slots) * LANES), whole),
+        ),
         compiler_params=pltpu.CompilerParams(vmem_limit_bytes=VMEM),
         cost_estimate=SHORT,
         name="pack",
-    )(core, q_sum, v_sum, *lines)
+    )(core, *lines)
     return packed, [slot[0][1] for slot in slots]
 
 
@@ -795,7 +903,7 @@
     )
     keep, send = jnp.concatenate([keep, small], 1), jnp.concatenate([send, small], 1)
     chip = pair(keep, swap(send, 0), core, 0).reshape(2 * slice_rows, 3 * half + LANES)
-    block = gather_common(chip)
+    block = gather_common(chip, (before,))
     far_tokens = pair(before, swap(before, 0), core, 0).reshape(near, width)
     slots = jnp.arange(near, dtype=jnp.int32)
     thoughts = thought_pos[0]
@@ -818,7 +926,7 @@
         jnp.concatenate([block[:, :, :half], block[:, :, 3 * half :]], 2),
         block[:, :, half : 3 * half],
     ]
-    first_parts = gather_step(parts, plans, 0, (before,))
+    first_parts = gather_step(parts, plans, 0)
 
     parts = gather_step(first_parts, plans, 1, (hat_all, root_all))
     q_weight = parts[0][:, :, :half].reshape(width, half)
@@ -887,7 +995,7 @@
     fc_got, proj_got = after((fc_got, proj_got), grad_middle)
     fc_pair = [fc_keep.reshape(fc_shape), fc_got.reshape(fc_shape)]
     proj_pair = [proj_keep.reshape(proj_shape), proj_got.reshape(proj_shape)]
-    early = [start_sum(fc_pair, 0, hidden_width // 2), start_sum(proj_pair, 0, half)]
+    early = [start_sum(fc_pair), start_sum(proj_pair)]
     ready = prepare(early, plans, 0)
     out_got = swap(after(out_send, *sends(ready)), 0)
 
@@ -905,7 +1013,7 @@
     grad_query, grad_key, grad_value = after(grads, *sends(ready))
 
     last = [
-        start_sum([value.reshape(chips, 2 * slice_rows, -1)], 0, value.shape[1])
+        start_sum([value.reshape(chips, 2 * slice_rows, -1)])
         for value in qkv_grads(normed, grad_query, grad_key, grad_value, out_kept, out_got)
     ]
     last_ready = prepare(last, plans, 0)
@@ -949,16 +1057,17 @@
     last = exchange(last_ready)
     for step in range(4, flat_bits() - 1):
         ready = prepare(exchange(ready), plans, step)
-    fc_total, proj_total = (value.total()[0] for value in exchange(ready, (far_sum,)))
-    fc_weight_grad = jnp.concatenate(finish(fc_total, slice_rows), 1)
-
-    proj_weight_grad = jnp.concatenate(finish(proj_total, high), 1)
-    sides = finish(jnp.concatenate([value.total()[0] for value in last], 1), slice_rows)
-    kinds = [
-        jnp.concatenate([side[:, i * half : (i + 1) * half] for side in sides], 1)
-        for i in range(4)
-    ]
-    qkv_weight_grad, out_weight_grad = jnp.concatenate(kinds[:3], 1), kinds[3]
+    early = exchange(ready, (far_sum,))
+    fc_weight_grad, proj_weight_grad, qkv_weight_grad, out_weight_grad = finish(
+        early + last,
+        slice_rows,
+        (
+            (slice_rows, hidden_width),
+            (high, width),
+            (slice_rows, 3 * width),
+            (slice_rows, width),
+        ),
+    )
 
     grad_normed = part[1] + got[1].astype(FULL) + back.astype(FULL)
     hat = lax.dynamic_slice_in_dim(hat_all, own, quarter, 0)

time: 299 us -> 291 us (0.973)
  other arithmetic: 51 us -> 25.8 us
  Pallas kernels: 79.1 us -> 93.8 us
  waiting for transfers between devices: 64.2 us -> 69.8 us
    convert_element_type x14 -> x0, other arithmetic: 16.7 us -> none  [prepare(): send = self.total(bit, 1 - bit_of(bit)).astype(self.kind)]
    pallas_call x1 -> x11, Pallas kernels: 2.47 us -> 17 us  [the longest x8 11.9 us: prepare(): pl.pallas_call(functools.partial(send_kernel, [len(value.addends) for val...]
    ppermute x34 -> x32, starting transfers between devices: 44.1 us -> 38.3 us  [swap(): return lax.ppermute(value, ALL, [(i, i ^ 1 << bit) for i in range(count)])]
    add x4 -> x0, other arithmetic: 5.52 us -> none  [total(): result = piece if result is None else result + piece]
    all_to_all x1, starting transfers between devices: 4.29 us -> 8.72 us  [shards(): lax.all_to_all(packed, ALL, 0, 0, tiled=True)]
    ppermute x34 -> x32, waiting for transfers between devices: 39.6 us -> 43.4 us  [swap(): return lax.ppermute(value, ALL, [(i, i ^ 1 << bit) for i in range(count)])]
    dynamic_slice x10 -> x0, local copies, waits for them, and re-layouts: 3.79 us -> none  [the longest x8 2.44 us: total(): piece = lax.dynamic_slice(view, (*begin, 0, start), (*width, rows, size))]
    unnamed x106 -> x118, local copies, waits for them, and re-layouts: 8.5 us -> 11.6 us
  transfers between devices with their start and end apart: 39 -> 37, of which waited for: 18 -> 18; matrix products, arithmetic and copies ran while one was open for 18% -> 12% of each run, Pallas kernels for 16% -> 17%
where the time goes in v5:
time: 291 us; the launch traced here: 286 us
  Pallas kernels  93.8 us (32%)
  waiting for transfers between devices  69.8 us (24%)
  starting transfers between devices  54.3 us (19%)
  other arithmetic  25.8 us (9%)
  local copies, waits for them, and re-layouts  19.6 us (7%)
  between operations  16.3 us (6%)
  matrix products  6.2 us (2%)
    ppermute x32, waiting for transfers between devices, swap(): return lax.ppermute(value, ALL, [(i, i ^ 1 << bit) for i in range(count)])  43.4 us
    ppermute x32, starting transfers between devices, swap(): return lax.ppermute(value, ALL, [(i, i ^ 1 << bit) for i in range(count)])  38.3 us
    pallas_call x1, Pallas kernels, feed(): pl.pallas_call(functools.partial(feed_kernel, shard_rows), out_shape=(jax...  24.1 us
    pallas_call x3, Pallas kernels, attend_back(): pl.pallas_call(attend_back_kernel, out_shape=(jax.ShapeDtypeStruct((near,...  19.6 us
    all_gather x1, waiting for transfers between devices, shards(): lax.all_gather(beside_rows(fc_weight, proj_weight, out_weight), ALL, axis...  18.2 us
    pallas_call x8, Pallas kernels, prepare(): pl.pallas_call(functools.partial(send_kernel, [len(value.addends) for val...  11.9 us
    unnamed x118, local copies, waits for them, and re-layouts  11.6 us
    pallas_call x1, Pallas kernels, norm_back(): pl.pallas_call(norm_back_kernel, out_shape=(shape((2, quarter, width), FU...  10.3 us
  transfers between devices with their start and end apart: 37, of which 18 were waited for; matrix products, arithmetic and copies ran while one was open for 12% of the time, Pallas kernels for 17%

profile of v5, /device:TPU:1, one launch (start us, length us, event | category | flops | bytes accessed | tf_op | source)
XLA Modules:
  0.0 285.8 jit_solution(2602766246221422200)
XLA Ops:
  9.3 4.0 %collective-permute-start = (bf16[512,768]{1,0:T(8,128)(2,1)}, bf16[512,768]{1,0:T(8,128)(2,1)S(1)}, u32[]{:S(2)}, u32[]{:S(2)}) collective-permute-start(bf16[512,768]{1,0:T(8,128)(2,1)} %bitcast.135), channel_id=1, source_target_pairs={{0,2},{1,3},{4,6},{5,7},{8,10},{9,11},{12,14},{13,15},{16,18},{17,... | collective-permute-start | bytes 2359304 | tf_op jit(solution)/shard_map/ppermute | solution.py:888
  19.5 5.8 %collective-permute-done.4 = bf16[1,48,1280]{2,1,0:T(8,128)(2,1)S(1)} collective-permute-done((bf16[1,48,1280]{2,1,0:T(8,128)(2,1)S(1)}, bf16[1,48,1280]{2,1,0:T(8,128)(2,1)S(1)}, u32[]{:S(2)}, u32[]{:S(2)}) %collective-permute-start.4) | collective-permute-done | bytes 122912 | tf_op jit(solution)/shard_map/ppermute | solution.py:35
  25.3 6.8 %collective-permute-done = bf16[512,768]{1,0:T(8,128)(2,1)S(1)} collective-permute-done((bf16[512,768]{1,0:T(8,128)(2,1)}, bf16[512,768]{1,0:T(8,128)(2,1)S(1)}, u32[]{:S(2)}, u32[]{:S(2)}) %collective-permute-start) | collective-permute-done | bytes 786464 | tf_op jit(solution)/shard_map/ppermute | solution.py:888
  36.2 2.6 collective-permute-done.5
  44.9 3.6 %collective-permute-start.7 = (bf16[8,48,512]{2,1,0:T(8,128)(2,1)S(1)}, bf16[8,48,512]{2,1,0:T(8,128)(2,1)S(1)}, u32[]{:S(2)}, u32[]{:S(2)}) collective-permute-start(bf16[8,48,512]{2,1,0:T(8,128)(2,1)S(1)} %bitcast.133), channel_id=1, source_target_pairs={{0,2},{1,3},{2,0},{3,1},{4,6},{5,7},{6,4},{7,5},{8,10},{9,11},{10,... | collective-permute-start | bytes 1179656 | tf_op jit(solution)/shard_map/ppermute | solution.py:35
  48.5 5.0 %collective-permute-done.8 = bf16[4,48,768]{2,1,0:T(8,128)(2,1)S(1)} collective-permute-done((bf16[4,48,768]{2,1,0:T(8,128)(2,1)S(1)}, bf16[4,48,768]{2,1,0:T(8,128)(2,1)S(1)}, u32[]{:S(2)}, u32[]{:S(2)}) %collective-permute-start.8) | collective-permute-done | bytes 294944 | tf_op jit(solution)/shard_map/ppermute | solution.py:35
  55.8 3.2 %fusion.2 = f32[2048]{0:T(1024)S(1)} fusion(f32[2048]{0:T(1024)S(1)} %broadcast_multiply_fusion, bf16[1024,768]{1,0:T(8,128)(2,1)S(1)} %maximum_select_fusion.1, bf16[1024,768]{1,0:T(8,128)(2,1)S(1)} %maximum_select_fusion), kind=kLoop, calls=%fused_computation.4 | loop fusion | flops 11008000 | bytes 3162112 | tf_op jit(solution)/shard_map/reduce_sum | solution.py:839
  59.0 3.6 %fusion.hat_ref = f32[2048,768]{1,0:T(8,128)} fusion(f32[2048]{0:T(1024)S(1)} %add_rsqrt_fusion, f32[2048]{0:T(1024)S(1)} %broadcast_multiply_fusion, bf16[1024,768]{1,0:T(8,128)(2,1)S(1)} %maximum_select_fusion.1, bf16[1024,768]{1,0:T(8,128)(2,1)S(1)} %maximum_select_fusion), kind=kLoop, calls=%fused_computation.2 | loop fusion | flops 9437184 | bytes 9453568 | tf_op jit(solution)/shard_map/mul | solution.py:841
  63.6 2.5 add_convert_fusion.1.n_ref
  68.6 2.8 add_convert_fusion.k_ref.v_ref
  71.5 8.8 %attend.1 = (bf16[1024,384]{1,0:T(8,128)(2,1)S(1)}, f32[3,8,1024]{2,1,0:T(8,128)S(1)}) custom-call(s32[1]{0:T(128)} %bitcast.7.far_ref, bf16[1024,384]{1,0:T(8,128)(2,1)S(1)} %add_convert_fusion.4.q_ref, bf16[2048,768]{1,0:T(8,128)(2,1)S(1)} %add_convert_fusion.k_ref.v_ref, bf16[2048,768]{1,0:T(8,128)(2,1)S(1)} %add_convert_fusion.k_ref.v_ref), custom_call_target="tpu_custom_call" | custom-call | flops 1048576 | bytes 4096 | tf_op jit(solution)/shard_map/attend/pallas_call | solution.py:317
  81.2 4.2 %collective-permute-start.10 = (bf16[512,384]{1,0:T(8,128)(2,1)S(1)}, bf16[512,384]{1,0:T(8,128)(2,1)}, u32[]{:S(2)}, u32[]{:S(2)}) collective-permute-start(bf16[512,384]{1,0:T(8,128)(2,1)S(1)} %constant_dynamic-slice_fusion), channel_id=1, source_target_pairs={{0,1},{1,0},{2,3},{3,2},{4,5},{5,4},{6,7},{7,6},{8,9},{9,8},{10,11... | collective-permute-start | bytes 1179656 | tf_op jit(solution)/shard_map/ppermute | solution.py:35
  88.1 18.2 %all-gather.2.cloned.1.call-done.fc_ref.refs_0_.refs_1_.refs_2_.refs_3_.w_ref = bf16[768,6912]{1,0:T(8,128)(2,1)} async-done(((bf16[24,6912]{1,0:T(8,128)(2,1)}), bf16[768,6912]{1,0:T(8,128)(2,1)}) %all-gather.2.cloned.1.call-update) | async-done | bytes 10616848 | tf_op jit(solution)/shard_map/all_gather | solution.py:882
  106.3 2.4 fusion.27
  110.5 24.1 %feed.1 = (f32[512,768]{1,0:T(8,128)S(1)}, f32[512,768]{1,0:T(8,128)S(1)}, bf16[768,1536]{1,0:T(8,128)(2,1)}, bf16[768,1536]{1,0:T(8,128)(2,1)}, bf16[3072,384]{...) custom-call(s32[1]{0:T(128)} %bitcast.29.core_ref, bf16[512,768]{1,0:T(8,128)(2,1)S(1)} %get-tuple-element.215.n_ref, ...), custom_call_target="tpu_custom_call" | custom-call | flops 1048576 | bytes 4096 | tf_op jit(solution)/shard_map/feed/pallas_call | solution.py:589
  137.6 5.5 %turn.1 = (f32[512,768]{1,0:T(8,128)S(1)}, bf16[512,384]{1,0:T(8,128)(2,1)S(1)}, bf16[512,384]{1,0:T(8,128)(2,1)S(1)}, bf16[768,384]{1,0:T(8,128)(2,1)S(1)}, bf1...) custom-call(s32[1]{0:T(128)} %bitcast.29.core_ref, ...), custom_call_target="tpu_custom_call" | custom-call | flops 1048576 | bytes 4096 | tf_op jit(solution)/shard_map/turn/pallas_call | solution.py:659
  145.2 5.0 %send.8 = (bf16[8,48,1536]{2,1,0:T(8,128)(2,1)S(1)}, bf16[8,192,384]{2,1,0:T(8,128)(2,1)S(1)}) custom-call(s32[1]{0:T(128)} %bitcast.35.at_ref, bf16[16,48,1536]{2,1,0:T(8,128)(2,1)S(1)} %bitcast.103, bf16[16,48,1536]{2,1,0:T(8,128)(2,1)} %bitcast.37.refs_1_, bf16[16,192,384]{2,1,0:T(8,128)(2,1)} %bitcast.123, ...), custom_call_target="tpu_custom_call" | custom-call | flops 12884901888 | bytes 4096 | tf_op jit(solution)/shard_map/send/pallas_call | solution.py:138
  154.5 6.4 %attend_back.3 = (bf16[1024,384]{1,0:T(8,128)(2,1)S(1)}, bf16[2048,384]{1,0:T(8,128)(2,1)S(1)}, bf16[2048,384]{1,0:T(8,128)(2,1)}) custom-call(s32[1]{0:T(128)} %bitcast.7.far_ref, bf16[1024,384]{1,0:T(8,128)(2,1)S(1)} %copy-done.2, bf16[2048,768]{1,0:T(8,128)(2,1)} %copy-done, bf16[2048,768]{1,0:T(8,128)(2,1)} %copy-done, bf16[1024,384]{1,0:T(8,128)(2,1)S(1)} %bitcast.95, ...), custom_call_target="tpu_custom_call" | custom-call | flops 1048576 | bytes 4096 | tf_op jit(solution)/shard_map/attend_back/pallas_call | solution.py:407
  160.9 6.6 %attend_back.4 = (bf16[1024,384]{1,0:T(8,128)(2,1)S(1)}, bf16[2048,384]{1,0:T(8,128)(2,1)S(1)}, bf16[2048,384]{1,0:T(8,128)(2,1)}) custom-call(s32[1]{0:T(128)} %bitcast.7.far_ref, bf16[1024,384]{1,0:T(8,128)(2,1)S(1)} %copy-done.2, bf16[2048,768]{1,0:T(8,128)(2,1)} %copy-done, ...), custom_call_target="tpu_custom_call", output_to_operand_aliasing={{0}: (7, {}), {1}: (8, {}), {2}: (9, {})} | custom-call | flops 1048576 | bytes 4096 | tf_op jit(solution)/shard_map/attend_back/pallas_call | solution.py:407
  167.5 10.1 %collective-permute-done.14.refs_2_ = bf16[8,48,1536]{2,1,0:T(8,128)(2,1)S(1)} collective-permute-done((bf16[8,48,1536]{2,1,0:T(8,128)(2,1)S(1)}, bf16[8,48,1536]{2,1,0:T(8,128)(2,1)S(1)}, u32[]{:S(2)}, u32[]{:S(2)}) %collective-permute-start.14) | collective-permute-done | bytes 1179680 | tf_op jit(solution)/shard_map/ppermute | solution.py:35
  178.4 3.0 %send.9 = (bf16[4,48,1536]{2,1,0:T(8,128)(2,1)S(1)}, bf16[4,192,384]{2,1,0:T(8,128)(2,1)S(1)}) custom-call(s32[1]{0:T(128)} %bitcast.35.at_ref, bf16[16,48,1536]{2,1,0:T(8,128)(2,1)S(1)} %bitcast.104, bf16[16,48,1536]{2,1,0:T(8,128)(2,1)} %bitcast.37.refs_1_, bf16[8,48,1536]{2,1,0:T(8,128)(2,1)S(1)} %collective-permute-done.14.refs_2_, ...), custom_call_target="tpu_custom_call" | custom-call | flops 12884901888 | bytes 4096 | tf_op jit(solution)/shard_map/send/pallas_call | solution.py:138
  183.5 6.6 %attend_back.5 = (bf16[1024,384]{1,0:T(8,128)(2,1)S(1)}, bf16[2048,384]{1,0:T(8,128)(2,1)S(1)}, bf16[2048,384]{1,0:T(8,128)(2,1)}) custom-call(s32[1]{0:T(128)} %bitcast.7.far_ref, bf16[1024,384]{1,0:T(8,128)(2,1)S(1)} %copy-done.2, bf16[2048,768]{1,0:T(8,128)(2,1)} %copy-done, ...), custom_call_target="tpu_custom_call", output_to_operand_aliasing={{0}: (7, {}), {1}: (8, {}), {2}: (9, {})} | custom-call | flops 1048576 | bytes 4096 | tf_op jit(solution)/shard_map/attend_back/pallas_call | solution.py:407
  190.1 4.9 %collective-permute-done.16.refs_3_ = bf16[4,48,1536]{2,1,0:T(8,128)(2,1)S(1)} collective-permute-done((bf16[4,48,1536]{2,1,0:T(8,128)(2,1)S(1)}, bf16[4,48,1536]{2,1,0:T(8,128)(2,1)S(1)}, u32[]{:S(2)}, u32[]{:S(2)}) %collective-permute-start.16) | collective-permute-done | bytes 589856 | tf_op jit(solution)/shard_map/ppermute | solution.py:35
  197.5 6.6 %qkv_grads.1 = (bf16[768,768]{1,0:T(8,128)(2,1)S(1)}, bf16[768,768]{1,0:T(8,128)(2,1)S(1)}) custom-call(bf16[2048,768]{1,0:T(8,128)(2,1)} %copy-done.41, bf16[1024,384]{1,0:T(8,128)(2,1)S(1)} %get-tuple-element.162.dq_ref, bf16[2048,384]{1,0:T(8,128)(2,1)S(1)} %get-tuple-element.152.dk_ref, bf16[2048,384]{1,0:T(8,128)(2,1)} %get-tuple-element.153.dv_ref, ...), custom_call_target="tpu_custom_call" | custom-call | flops 1048576 | bytes 4096 | tf_op jit(solution)/shard_map/qkv_grads/pallas_call | solution.py:456
  204.4 2.4 collective-permute-start.20
  209.2 10.3 %norm_back.1 = (f32[2,512,768]{2,1,0:T(8,128)}, bf16[2,512,768]{2,1,0:T(8,128)(2,1)}, f32[1,768]{1,0:T(1,128)S(1)}, f32[1,768]{1,0:T(1,128)S(1)}, f32[1,384]{1,0:T(1,128)S(1)}, /*index=5*/f32[1,384]{1,0:T(1,128)S(1)}) custom-call(s32[1]{0:T(128)} %bitcast.29.core_ref, bf16[1024,384]{1,0:T(8,128)(2,1)S(1)} %get-tuple-element.162.dq_ref, ...), custom_call_target="tpu_custom_call" | custom-call | flops 1048576 | bytes 4096 | tf_op jit(solution)/shard_map/norm_back/pallas_call | solution.py:748
  219.5 2.5 collective-permute-start.19
  225.2 3.1 %fusion.11 = bf16[512,768]{1,0:T(8,128)(2,1)} fusion(f32[2,512,768]{2,1,0:T(8,128)} %get-tuple-element.163, bf16[2,512,768]{2,1,0:T(8,128)(2,1)S(1)} %collective-permute-done.19), kind=kLoop, calls=%fused_computation.27 | loop fusion | flops 1179648 | bytes 3145728 | tf_op jit(solution)/shard_map/convert_element_type | solution.py:1035
  231.8 2.5 pack.1
  238.8 8.7 %all-to-all-start = ((f32[32,1,1024]{2,1,0:T(1,128)}), f32[32,1,1024]{2,1,0:T(1,128)}, u32[]{:S(2)}, u32[]{:S(2)}) async-start(f32[32,1,1024]{2,1,0:T(1,128)} %copy.50), calls=%async_computation | async-start | bytes 262144 | tf_op jit(solution)/shard_map/all_to_all | solution.py:1053
  257.5 5.5 %collective-permute-done.33.refs_21_ = bf16[1,48,768]{2,1,0:T(8,128)(2,1)S(1)} collective-permute-done((bf16[1,48,768]{2,1,0:T(8,128)(2,1)S(1)}, bf16[1,48,768]{2,1,0:T(8,128)(2,1)S(1)}, u32[]{:S(2)}, u32[]{:S(2)}) %collective-permute-start.33) | collective-permute-done | bytes 73760 | tf_op jit(solution)/shard_map/ppermute | solution.py:35
  267.5 2.8 fusion.23
  (268 shorter events, 79.4 us)
Async XLA Ops:
  7.3 99.0 %all-gather.2.cloned.1.call-start = ((), (), s32[]{:S(2)}) async-start(), calls=%async_computation.1 | async-start | bytes 10948608 | tf_op jit(solution)/shard_map/all_gather | solution.py:882
  9.3 22.9 %collective-permute-start = (bf16[512,768]{1,0:T(8,128)(2,1)}, bf16[512,768]{1,0:T(8,128)(2,1)S(1)}, u32[]{:S(2)}, u32[]{:S(2)}) collective-permute-start(bf16[512,768]{1,0:T(8,128)(2,1)} %bitcast.135), channel_id=1, source_target_pairs={{0,2},{1,3},{4,6},{5,7},{8,10},{9,11},{12,14},{13,15},{16,18},{17,... | collective-permute-start | bytes 2359304 | tf_op jit(solution)/shard_map/ppermute | solution.py:888
  17.1 8.2 %collective-permute-start.4 = (bf16[1,48,1280]{2,1,0:T(8,128)(2,1)S(1)}, bf16[1,48,1280]{2,1,0:T(8,128)(2,1)S(1)}, u32[]{:S(2)}, u32[]{:S(2)}) collective-permute-start(bf16[1,48,1280]{2,1,0:T(8,128)(2,1)S(1)} %bitcast.138), channel_id=1, source_target_pairs={{0,16},{1,17},{2,18},{3,19},{4,20},{5,21},{6,22},{7,23},{8,24},{9,... | collective-permute-start | bytes 368648 | tf_op jit(solution)/shard_map/ppermute | solution.py:35
  32.2 6.7 %collective-permute-start.5 = (bf16[2,48,1280]{2,1,0:T(8,128)(2,1)S(1)}, bf16[2,48,1280]{2,1,0:T(8,128)(2,1)S(1)}, u32[]{:S(2)}, u32[]{:S(2)}) collective-permute-start(bf16[2,48,1280]{2,1,0:T(8,128)(2,1)S(1)} %constant_dynamic-update-slice_fusion.1), channel_id=1, source_target_pairs={{0,8},{1,9},{2,10},{3,11},{4,12},{5,13},{6,14},{7,15},{8,0},{9,1},... | collective-permute-start | bytes 737288 | tf_op jit(solution)/shard_map/ppermute | solution.py:35
  33.5 9.0 %collective-permute-start.2 = (bf16[512,768]{1,0:T(8,128)(2,1)S(1)}, bf16[512,768]{1,0:T(8,128)(2,1)S(1)}, u32[]{:S(2)}, u32[]{:S(2)}) collective-permute-start(bf16[512,768]{1,0:T(8,128)(2,1)S(1)} %bitcast.136), channel_id=1, source_target_pairs={{0,1},{1,0},{2,3},{3,2},{4,5},{5,4},{6,7},{7,6},{8,9},{9,8},{10,11... | collective-permute-start | bytes 2359304 | tf_op jit(solution)/shard_map/ppermute | solution.py:35
  36.1 17.6 %collective-permute-start.1 = (bf16[512,768]{1,0:T(8,128)(2,1)S(1)}, bf16[512,768]{1,0:T(8,128)(2,1)S(1)}, u32[]{:S(2)}, u32[]{:S(2)}) collective-permute-start(bf16[512,768]{1,0:T(8,128)(2,1)S(1)} %collective-permute-done), channel_id=1, source_target_pairs={{0,1},{1,0},{2,3},{3,2},{4,5},{5,4},{6,7},{7,6},{8,9},{9,8},{10,11... | collective-permute-start | bytes 2359304 | tf_op jit(solution)/shard_map/ppermute | solution.py:35
  39.0 5.8 %collective-permute-start.6 = (bf16[4,48,512]{2,1,0:T(8,128)(2,1)S(1)}, bf16[4,48,512]{2,1,0:T(8,128)(2,1)S(1)}, u32[]{:S(2)}, u32[]{:S(2)}) collective-permute-start(bf16[4,48,512]{2,1,0:T(8,128)(2,1)S(1)} %pad_maximum_fusion.2), channel_id=1, source_target_pairs={{0,4},{1,5},{2,6},{3,7},{4,0},{5,1},{6,2},{7,3},{8,12},{9,13},{10,... | collective-permute-start | bytes 589832 | tf_op jit(solution)/shard_map/ppermute | solution.py:35
  40.6 13.0 %collective-permute-start.8 = (bf16[4,48,768]{2,1,0:T(8,128)(2,1)S(1)}, bf16[4,48,768]{2,1,0:T(8,128)(2,1)S(1)}, u32[]{:S(2)}, u32[]{:S(2)}) collective-permute-start(bf16[4,48,768]{2,1,0:T(8,128)(2,1)S(1)} %slice.173), channel_id=1, source_target_pairs={{0,2},{1,3},{2,0},{3,1},{4,6},{5,7},{6,4},{7,5},{8,10},{9,11},{10,... | collective-permute-start | bytes 884744 | tf_op jit(solution)/shard_map/ppermute | solution.py:35
  44.9 17.7 %collective-permute-start.7 = (bf16[8,48,512]{2,1,0:T(8,128)(2,1)S(1)}, bf16[8,48,512]{2,1,0:T(8,128)(2,1)S(1)}, u32[]{:S(2)}, u32[]{:S(2)}) collective-permute-start(bf16[8,48,512]{2,1,0:T(8,128)(2,1)S(1)} %bitcast.133), channel_id=1, source_target_pairs={{0,2},{1,3},{2,0},{3,1},{4,6},{5,7},{6,4},{7,5},{8,10},{9,11},{10,... | collective-permute-start | bytes 1179656 | tf_op jit(solution)/shard_map/ppermute | solution.py:35
  53.6 13.5 %collective-permute-start.9 = (bf16[8,48,768]{2,1,0:T(8,128)(2,1)S(1)}, bf16[8,48,768]{2,1,0:T(8,128)(2,1)}, u32[]{:S(2)}, u32[]{:S(2)}) collective-permute-start(bf16[8,48,768]{2,1,0:T(8,128)(2,1)S(1)} %bitcast.128), channel_id=1, source_target_pairs={{0,4},{1,5},{2,6},{3,7},{4,0},{5,1},{6,2},{7,3},{8,12},{9,13},{10,... | collective-permute-start | bytes 1769480 | tf_op jit(solution)/shard_map/ppermute | solution.py:35
  136.9 8.3 %collective-permute-start.12 = (bf16[768,1536]{1,0:T(8,128)(2,1)}, bf16[768,1536]{1,0:T(8,128)(2,1)}, u32[]{:S(2)}, u32[]{:S(2)}) collective-permute-start(bf16[768,1536]{1,0:T(8,128)(2,1)} %get-tuple-element.124), channel_id=1, source_target_pairs={{0,1},{1,0},{2,3},{3,2},{4,5},{5,4},{6,7},{7,6},{8,9},{9,8},{10,11... | collective-permute-start | bytes 7077896 | tf_op jit(solution)/shard_map/ppermute | solution.py:35
  137.1 8.0 %collective-permute-start.13 = (bf16[3072,384]{1,0:T(8,128)(2,1)}, bf16[3072,384]{1,0:T(8,128)(2,1)}, u32[]{:S(2)}, u32[]{:S(2)}) collective-permute-start(bf16[3072,384]{1,0:T(8,128)(2,1)} %get-tuple-element.125), channel_id=1, source_target_pairs={{0,1},{1,0},{2,3},{3,2},{4,5},{5,4},{6,7},{7,6},{8,9},{9,8},{10,11... | collective-permute-start | bytes 7077896 | tf_op jit(solution)/shard_map/ppermute | solution.py:35
  150.2 27.4 %collective-permute-start.14 = (bf16[8,48,1536]{2,1,0:T(8,128)(2,1)S(1)}, bf16[8,48,1536]{2,1,0:T(8,128)(2,1)S(1)}, u32[]{:S(2)}, u32[]{:S(2)}) collective-permute-start(bf16[8,48,1536]{2,1,0:T(8,128)(2,1)S(1)} %get-tuple-element.129), channel_id=1, source_target_pairs={{0,2},{1,3},{2,0},{3,1},{4,6},{5,7},{6,4},{7,5},{8,10},{9,11},{10,... | collective-permute-start | bytes 3538952 | tf_op jit(solution)/shard_map/ppermute | solution.py:35
  151.5 27.0 %collective-permute-start.15 = (bf16[8,192,384]{2,1,0:T(8,128)(2,1)S(1)}, bf16[8,192,384]{2,1,0:T(8,128)(2,1)S(1)}, u32[]{:S(2)}, u32[]{:S(2)}) collective-permute-start(bf16[8,192,384]{2,1,0:T(8,128)(2,1)S(1)} %get-tuple-element.130), channel_id=1, source_target_pairs={{0,4},{1,5},{2,6},{3,7},{4,0},{5,1},{6,2},{7,3},{8,12},{9,13},{10,... | collective-permute-start | bytes 3538952 | tf_op jit(solution)/shard_map/ppermute | solution.py:35
  154.1 36.0 %collective-permute-start.18 = (bf16[768,384]{1,0:T(8,128)(2,1)}, bf16[768,384]{1,0:T(8,128)(2,1)S(1)}, u32[]{:S(2)}, u32[]{:S(2)}) collective-permute-start(bf16[768,384]{1,0:T(8,128)(2,1)} %get-tuple-element.156), channel_id=1, source_target_pairs={{0,1},{1,0},{2,3},{3,2},{4,5},{5,4},{6,7},{7,6},{8,9},{9,8},{10,11... | collective-permute-start | bytes 1769480 | tf_op jit(solution)/shard_map/ppermute | solution.py:35
  181.5 13.5 %collective-permute-start.16 = (bf16[4,48,1536]{2,1,0:T(8,128)(2,1)S(1)}, bf16[4,48,1536]{2,1,0:T(8,128)(2,1)S(1)}, u32[]{:S(2)}, u32[]{:S(2)}) collective-permute-start(bf16[4,48,1536]{2,1,0:T(8,128)(2,1)S(1)} %get-tuple-element.141), channel_id=1, source_target_pairs={{0,4},{1,5},{2,6},{3,7},{4,0},{5,1},{6,2},{7,3},{8,12},{9,13},{10,... | collective-permute-start | bytes 1769480 | tf_op jit(solution)/shard_map/ppermute | solution.py:35
  182.3 13.5 %collective-permute-start.17 = (bf16[4,192,384]{2,1,0:T(8,128)(2,1)S(1)}, bf16[4,192,384]{2,1,0:T(8,128)(2,1)S(1)}, u32[]{:S(2)}, u32[]{:S(2)}) collective-permute-start(bf16[4,192,384]{2,1,0:T(8,128)(2,1)S(1)} %get-tuple-element.142), channel_id=1, source_target_pairs={{0,2},{1,3},{2,0},{3,1},{4,6},{5,7},{6,4},{7,5},{8,10},{9,11},{10,... | collective-permute-start | bytes 1769480 | tf_op jit(solution)/shard_map/ppermute | solution.py:35
  204.4 17.5 %collective-permute-start.20 = (bf16[8,48,768]{2,1,0:T(8,128)(2,1)S(1)}, bf16[8,48,768]{2,1,0:T(8,128)(2,1)S(1)}, u32[]{:S(2)}, u32[]{:S(2)}) collective-permute-start(bf16[8,48,768]{2,1,0:T(8,128)(2,1)S(1)} %get-tuple-element.160), channel_id=1, source_target_pairs={{0,2},{1,3},{2,0},{3,1},{4,6},{5,7},{6,4},{7,5},{8,10},{9,11},{10,... | collective-permute-start | bytes 1769480 | tf_op jit(solution)/shard_map/ppermute | solution.py:35
  206.8 15.2 %collective-permute-start.21 = (bf16[8,48,768]{2,1,0:T(8,128)(2,1)S(1)}, bf16[8,48,768]{2,1,0:T(8,128)(2,1)S(1)}, u32[]{:S(2)}, u32[]{:S(2)}) collective-permute-start(bf16[8,48,768]{2,1,0:T(8,128)(2,1)S(1)} %get-tuple-element.161), channel_id=1, source_target_pairs={{0,4},{1,5},{2,6},{3,7},{4,0},{5,1},{6,2},{7,3},{8,12},{9,13},{10,... | collective-permute-start | bytes 1769480 | tf_op jit(solution)/shard_map/ppermute | solution.py:35
  207.7 14.2 %collective-permute-start.22 = (bf16[2,48,1536]{2,1,0:T(8,128)(2,1)S(1)}, bf16[2,48,1536]{2,1,0:T(8,128)(2,1)S(1)}, u32[]{:S(2)}, u32[]{:S(2)}) collective-permute-start(bf16[2,48,1536]{2,1,0:T(8,128)(2,1)S(1)} %get-tuple-element.149), channel_id=1, source_target_pairs={{0,8},{1,9},{2,10},{3,11},{4,12},{5,13},{6,14},{7,15},{8,0},{9,1},... | collective-permute-start | bytes 884744 | tf_op jit(solution)/shard_map/ppermute | solution.py:35
  208.7 13.3 %collective-permute-start.23 = (bf16[2,192,384]{2,1,0:T(8,128)(2,1)S(1)}, bf16[2,192,384]{2,1,0:T(8,128)(2,1)S(1)}, u32[]{:S(2)}, u32[]{:S(2)}) collective-permute-start(bf16[2,192,384]{2,1,0:T(8,128)(2,1)S(1)} %get-tuple-element.150), channel_id=1, source_target_pairs={{0,8},{1,9},{2,10},{3,11},{4,12},{5,13},{6,14},{7,15},{8,0},{9,1},... | collective-permute-start | bytes 884744 | tf_op jit(solution)/shard_map/ppermute | solution.py:35
  219.5 5.7 %collective-permute-start.19 = (bf16[2,512,768]{2,1,0:T(8,128)(2,1)}, bf16[2,512,768]{2,1,0:T(8,128)(2,1)S(1)}, u32[]{:S(2)}, u32[]{:S(2)}) collective-permute-start(bf16[2,512,768]{2,1,0:T(8,128)(2,1)} %get-tuple-element.164), channel_id=1, source_target_pairs={{0,1},{1,0},{2,3},{3,2},{4,5},{5,4},{6,7},{7,6},{8,9},{9,8},{10,11... | collective-permute-start | bytes 4718600 | tf_op jit(solution)/shard_map/ppermute | solution.py:35
  222.3 7.1 %collective-permute-start.28 = (bf16[4,48,768]{2,1,0:T(8,128)(2,1)S(1)}, bf16[4,48,768]{2,1,0:T(8,128)(2,1)S(1)}, u32[]{:S(2)}, u32[]{:S(2)}) collective-permute-start(bf16[4,48,768]{2,1,0:T(8,128)(2,1)S(1)} %get-tuple-element.167), channel_id=1, source_target_pairs={{0,4},{1,5},{2,6},{3,7},{4,0},{5,1},{6,2},{7,3},{8,12},{9,13},{10,... | collective-permute-start | bytes 884744 | tf_op jit(solution)/shard_map/ppermute | solution.py:35
  222.7 6.7 %collective-permute-start.29 = (bf16[4,48,768]{2,1,0:T(8,128)(2,1)S(1)}, bf16[4,48,768]{2,1,0:T(8,128)(2,1)S(1)}, u32[]{:S(2)}, u32[]{:S(2)}) collective-permute-start(bf16[4,48,768]{2,1,0:T(8,128)(2,1)S(1)} %get-tuple-element.168), channel_id=1, source_target_pairs={{0,2},{1,3},{2,0},{3,1},{4,6},{5,7},{6,4},{7,5},{8,10},{9,11},{10,... | collective-permute-start | bytes 884744 | tf_op jit(solution)/shard_map/ppermute | solution.py:35
  230.1 17.4 %collective-permute-start.30 = (bf16[2,48,768]{2,1,0:T(8,128)(2,1)S(1)}, bf16[2,48,768]{2,1,0:T(8,128)(2,1)S(1)}, u32[]{:S(2)}, u32[]{:S(2)}) collective-permute-start(bf16[2,48,768]{2,1,0:T(8,128)(2,1)S(1)} %get-tuple-element.178), channel_id=1, source_target_pairs={{0,8},{1,9},{2,10},{3,11},{4,12},{5,13},{6,14},{7,15},{8,0},{9,1},... | collective-permute-start | bytes 442376 | tf_op jit(solution)/shard_map/ppermute | solution.py:35
  231.2 16.4 %collective-permute-start.31 = (bf16[2,48,768]{2,1,0:T(8,128)(2,1)S(1)}, bf16[2,48,768]{2,1,0:T(8,128)(2,1)S(1)}, u32[]{:S(2)}, u32[]{:S(2)}) collective-permute-start(bf16[2,48,768]{2,1,0:T(8,128)(2,1)S(1)} %get-tuple-element.179), channel_id=1, source_target_pairs={{0,8},{1,9},{2,10},{3,11},{4,12},{5,13},{6,14},{7,15},{8,0},{9,1},... | collective-permute-start | bytes 442376 | tf_op jit(solution)/shard_map/ppermute | solution.py:35
  234.3 22.6 %collective-permute-start.26 = (bf16[1,48,1536]{2,1,0:T(8,128)(2,1)S(1)}, bf16[1,48,1536]{2,1,0:T(8,128)(2,1)S(1)}, u32[]{:S(2)}, u32[]{:S(2)}) collective-permute-start(bf16[1,48,1536]{2,1,0:T(8,128)(2,1)S(1)} %copy-done.36), channel_id=1, source_target_pairs={{0,16},{1,17},{2,18},{3,19},{4,20},{5,21},{6,22},{7,23},{8,24},{9,... | collective-permute-start | bytes 442376 | tf_op jit(solution)/shard_map/ppermute | solution.py:35
  235.9 21.0 %collective-permute-start.27 = (bf16[1,192,384]{2,1,0:T(8,128)(2,1)S(1)}, bf16[1,192,384]{2,1,0:T(8,128)(2,1)S(1)}, u32[]{:S(2)}, u32[]{:S(2)}) collective-permute-start(bf16[1,192,384]{2,1,0:T(8,128)(2,1)S(1)} %get-tuple-element.172), channel_id=1, source_target_pairs={{0,16},{1,17},{2,18},{3,19},{4,20},{5,21},{6,22},{7,23},{8,24},{9,... | collective-permute-start | bytes 442376 | tf_op jit(solution)/shard_map/ppermute | solution.py:35
  236.8 30.7 %collective-permute-start.24 = (bf16[512,768]{1,0:T(8,128)(2,1)}, bf16[512,768]{1,0:T(8,128)(2,1)S(1)}, u32[]{:S(2)}, u32[]{:S(2)}) collective-permute-start(bf16[512,768]{1,0:T(8,128)(2,1)} %fusion.11), channel_id=1, source_target_pairs={{2,0},{3,1},{6,4},{7,5},{10,8},{11,9},{14,12},{15,13},{18,16},{19,... | collective-permute-start | bytes 2359304 | tf_op jit(solution)/shard_map/ppermute | solution.py:1036
  238.8 26.6 %all-to-all-start = ((f32[32,1,1024]{2,1,0:T(1,128)}), f32[32,1,1024]{2,1,0:T(1,128)}, u32[]{:S(2)}, u32[]{:S(2)}) async-start(f32[32,1,1024]{2,1,0:T(1,128)} %copy.50), calls=%async_computation | async-start | bytes 262144 | tf_op jit(solution)/shard_map/all_to_all | solution.py:1053
  255.7 7.3 %collective-permute-start.33 = (bf16[1,48,768]{2,1,0:T(8,128)(2,1)S(1)}, bf16[1,48,768]{2,1,0:T(8,128)(2,1)S(1)}, u32[]{:S(2)}, u32[]{:S(2)}) collective-permute-start(bf16[1,48,768]{2,1,0:T(8,128)(2,1)S(1)} %get-tuple-element.183), channel_id=1, source_target_pairs={{0,16},{1,17},{2,18},{3,19},{4,20},{5,21},{6,22},{7,23},{8,24},{9,... | collective-permute-start | bytes 221192 | tf_op jit(solution)/shard_map/ppermute | solution.py:35
  264.7 10.0 %collective-permute-start.34 = (f32[24,4608]{1,0:T(8,128)S(1)}, f32[24,4608]{1,0:T(8,128)S(1)}, u32[]{:S(2)}, u32[]{:S(2)}) collective-permute-start(f32[24,4608]{1,0:T(8,128)S(1)} %get-tuple-element.185), channel_id=1, source_target_pairs={{0,1},{1,0},{2,3},{3,2},{4,5},{5,4},{6,7},{7,6},{8,9},{9,8},{10,11... | collective-permute-start | bytes 1327112 | tf_op jit(solution)/shard_map/ppermute | solution.py:35
  (63 other events, 520.0 us)
Sparse Core Ops, SparseCore 0:
  11.0 95.2 all-gather.1

commit v6 on v5

--- a/solution.py
+++ b/solution.py
@@ -14,6 +14,7 @@
 LANES = 128
 SCALE = 0.125
 VMEM = 48 << 20
+MOST = 60 << 20
 SHORT = pl.CostEstimate(flops=1 << 20, bytes_accessed=1 << 12, transcendentals=0)
 LONG = pl.CostEstimate(flops=12 << 30, bytes_accessed=1 << 12, transcendentals=0)
 
@@ -89,7 +90,7 @@
         self.left = left
 
 
-def group_of(bits, left, bit):
+def group_of(bits, left, bit, part):
     order, rest = sorted(bits, reverse=True), sorted(left, reverse=True)
 
     def index(i, s):
@@ -101,7 +102,7 @@
             elif b in rest:
                 here = (i >> (len(rest) - 1 - rest.index(b))) & 1
             group = 2 * group + here
-        return (group, 0, 0)
+        return (group, 0, part)
 
     return index
 
@@ -109,24 +110,38 @@
 def total_of(refs):
     total = refs[0][0].astype(FULL)
     for ref in refs[1:]:
-        total = total + ref[0].astype(FULL)
+        value = ref[0].astype(FULL)
+        rows, cols = value.shape
+        if cols != total.shape[1]:
+            size = total.shape[1]
+            value = jnp.concatenate([value[:, i : i + size] for i in range(0, cols, size)], 0)
+        total = total + value
     return total
 
 
-def send_kernel(counts, at_ref, *refs):
-    outs = refs[len(refs) - len(counts) :]
-    for count, out_ref in zip(counts, outs):
-        out_ref[0] = total_of(refs[:count]).astype(LOW)
+def send_kernel(counts, joined, at_ref, *refs):
+    outs = refs[len(refs) - (1 if joined else len(counts)) :]
+    column = 0
+    for which, count in enumerate(counts):
+        total = total_of(refs[:count]).astype(LOW)
         refs = refs[count:]
+        if not joined:
+            outs[which][0] = total
+            continue
+        rows = outs[0].shape[1]
+        for at in range(0, total.shape[0], rows):
+            outs[0][0, :, column : column + total.shape[1]] = total[at : at + rows]
+            column += total.shape[1]
 
 
 def specs_of(sums, bits):
     arrays, specs = [], []
     for value, bit in zip(sums, bits):
         left = [b for b in value.left if b != bit]
-        for array, own in value.addends:
+        for array, own, part, parts in value.addends:
+            rows, cols = array.shape[1:]
             arrays.append(array)
-            specs.append(pl.BlockSpec((1, *array.shape[1:]), group_of(own, left, bit)))
+            specs.append(pl.BlockSpec((1, rows, cols // parts), group_of(own, left, bit, part)))
     return arrays, specs
 
 
@@ -135,8 +150,13 @@
     arrays, specs = specs_of(sums, bits)
     groups = 1 << (len(sums[0].left) - 1)
     shapes = [value.addends[0][0].shape[1:] for value in sums]
+    sizes = {rows * cols for rows, cols in shapes}
+    joined = len(set(bits)) == 1 and len(sizes) == 1 and len(sums) > 1
+    if joined:
+        low = min(rows for rows, _ in shapes)
+        shapes = [(low, len(sums) * sizes.pop() // low)]
     sent = pl.pallas_call(
-        functools.partial(send_kernel, [len(value.addends) for value in sums]),
+        functools.partial(send_kernel, [len(value.addends) for value in sums], joined),
         out_shape=tuple(jax.ShapeDtypeStruct((groups, *shape), LOW) for shape in shapes),
         grid_spec=pltpu.PrefetchScalarGridSpec(
             num_scalar_prefetch=1,
@@ -144,14 +164,14 @@
             in_specs=specs,
             out_specs=tuple(pl.BlockSpec((1, *shape), lambda i, s: (i, 0, 0)) for shape in shapes),
         ),
-        compiler_params=pltpu.CompilerParams(vmem_limit_bytes=VMEM),
+        compiler_params=pltpu.CompilerParams(vmem_limit_bytes=VMEM if groups > 2 else MOST),
         cost_estimate=LONG,
         name="send",
     )(flat_index().astype(jnp.int32).reshape(1), *arrays)
-    return [
-        (send, Sum(value.addends, [b for b in value.left if b != bit]), bit)
-        for send, value, bit in zip(sent, sums, bits)
-    ]
+    kept = [Sum(value.addends, [b for b in value.left if b != bit]) for value, bit in zip(sums, bits)]
+    if joined:
+        return [(sent[0], kept, bits[0])]
+    return [(send, [keep], bit) for send, keep, bit in zip(sent, kept, bits)]
 
 
 def sends(prepared):
@@ -162,14 +182,15 @@
     gots = [swap(send, bit) for send, _, bit in prepared]
     gots = after(gots, *wait) if wait else gots
     return [
-        Sum(keep.addends + [(got, keep.left)], keep.left)
-        for got, (_, keep, _) in zip(gots, prepared)
+        Sum(keep.addends + [(got, keep.left, part, len(kept))], keep.left)
+        for got, (_, kept, _) in zip(gots, prepared)
+        for part, keep in enumerate(kept)
     ]
 
 
 def start_sum(arrays):
     links = list(range(1, flat_bits()))
-    return Sum([(value, links) for value in arrays], links)
+    return Sum([(value, links, 0, 1) for value in arrays], links)
 
 
 def finish_kernel(counts, at_ref, *refs):
@@ -568,9 +589,9 @@
 def feed(core, normed, grad, late, fc_bias, proj, shard_rows):
     rows, width = normed.shape
     hidden = fc_bias.shape[1]
-    chunk = width
-    blocks = hidden // chunk
-    steps = blocks // 2
+    chunk = 2 * width
+    blocks = hidden // width
+    steps = hidden // (2 * chunk)
 
     def block(i, s):
         return jnp.where(i < steps, (1 - s[0]) * steps + i, s[0] * steps + i - steps)
@@ -579,7 +600,7 @@
     if proj is None:
         pieces = [late] * blocks
         piece_specs = [
-            pl.BlockSpec((width // blocks, width), lambda i, s, at=at: (block(i, s), at))
+            pl.BlockSpec((chunk * width // hidden, width), lambda i, s, at=at: (block(i, s), at))
             for at in range(blocks, 2 * blocks)
         ]
     else:
@@ -599,7 +620,7 @@
         ),
         grid_spec=pltpu.PrefetchScalarGridSpec(
             num_scalar_prefetch=1,
-            grid=(blocks,),
+            grid=(2 * steps,),
             in_specs=[
                 whole,
                 whole,
@@ -1049,11 +1070,11 @@
             second_shift_grad,
         ),
     )
-    packed = after(packed, far_sum)
-    share = jnp.sum(lax.all_to_all(packed, ALL, 0, 0, tiled=True), 0, keepdims=True)
     for step in range(2, flat_bits() - 1):
         last = exchange(last_ready, (far_sum,))
         last_ready = prepare(last, plans, step)
+    packed = after(packed, *sends(last_ready))
+    share = jnp.sum(lax.all_to_all(packed, ALL, 0, 0, tiled=True), 0, keepdims=True)
     last = exchange(last_ready)
     for step in range(4, flat_bits() - 1):
         ready = prepare(exchange(ready), plans, step)

time: 291 us -> 288 us (0.990)
  waiting for transfers between devices: 69.8 us -> 66.3 us
  Pallas kernels: 93.8 us -> 97 us
    ppermute x32 -> x28, waiting for transfers between devices: 43.4 us -> 38 us  [swap(): return lax.ppermute(value, ALL, [(i, i ^ 1 << bit) for i in range(count)])]
    pallas_call x8, Pallas kernels: 11.9 us -> 17.3 us  [prepare(): pl.pallas_call(functools.partial(send_kernel, [len(value.addends) for val...]
    ppermute x32 -> x28, starting transfers between devices: 38.3 us -> 34.8 us  [swap(): return lax.ppermute(value, ALL, [(i, i ^ 1 << bit) for i in range(count)])]
    unnamed x118 -> x112, local copies, waits for them, and re-layouts: 11.6 us -> 10.1 us
  transfers between devices with their start and end apart: 37 -> 33, of which waited for: 18 -> 15; matrix products, arithmetic and copies ran while one was open for 12% -> 13% of each run, Pallas kernels for 17% -> 17%
where the time goes in v6:
time: 288 us; the launch traced here: 284 us
  Pallas kernels  97 us (34%)
  waiting for transfers between devices  66.3 us (23%)
  starting transfers between devices  52.7 us (18%)
  other arithmetic  26.1 us (9%)
  local copies, waits for them, and re-layouts  19 us (7%)
  between operations  16.2 us (6%)
  matrix products  6.3 us (2%)
    ppermute x28, waiting for transfers between devices, swap(): return lax.ppermute(value, ALL, [(i, i ^ 1 << bit) for i in range(count)])  38 us
    ppermute x28, starting transfers between devices, swap(): return lax.ppermute(value, ALL, [(i, i ^ 1 << bit) for i in range(count)])  34.8 us
    pallas_call x1, Pallas kernels, feed(): pl.pallas_call(functools.partial(feed_kernel, shard_rows), out_shape=(jax...  22.9 us
    pallas_call x3, Pallas kernels, attend_back(): pl.pallas_call(attend_back_kernel, out_shape=(jax.ShapeDtypeStruct((near,...  19.6 us
    all_gather x1, waiting for transfers between devices, shards(): lax.all_gather(beside_rows(fc_weight, proj_weight, out_weight), ALL, axis...  19 us
    pallas_call x8, Pallas kernels, prepare(): pl.pallas_call(functools.partial(send_kernel, [len(value.addends) for val...  17.3 us
    all_to_all x1, starting transfers between devices, shards(): lax.all_to_all(packed, ALL, 0, 0, tiled=True)  10.7 us
    pallas_call x1, Pallas kernels, norm_back(): pl.pallas_call(norm_back_kernel, out_shape=(shape((2, quarter, width), FU...  10.2 us
  transfers between devices with their start and end apart: 33, of which 15 were waited for; matrix products, arithmetic and copies ran while one was open for 13% of the time, Pallas kernels for 17%

profile of v6, /device:TPU:1, one launch (start us, length us, event | category | flops | bytes accessed | tf_op | source)
XLA Modules:
  0.0 283.6 jit_solution(14616392708382392434)
XLA Ops:
  9.3 4.0 %collective-permute-start = (bf16[512,768]{1,0:T(8,128)(2,1)}, bf16[512,768]{1,0:T(8,128)(2,1)S(1)}, u32[]{:S(2)}, u32[]{:S(2)}) collective-permute-start(bf16[512,768]{1,0:T(8,128)(2,1)} %bitcast.135), channel_id=1, source_target_pairs={{0,2},{1,3},{4,6},{5,7},{8,10},{9,11},{12,14},{13,15},{16,18},{17,... | collective-permute-start | bytes 2359304 | tf_op jit(solution)/shard_map/ppermute | solution.py:909
  19.6 5.8 %collective-permute-done.4 = bf16[1,48,1280]{2,1,0:T(8,128)(2,1)S(1)} collective-permute-done((bf16[1,48,1280]{2,1,0:T(8,128)(2,1)S(1)}, bf16[1,48,1280]{2,1,0:T(8,128)(2,1)S(1)}, u32[]{:S(2)}, u32[]{:S(2)}) %collective-permute-start.4) | collective-permute-done | bytes 122912 | tf_op jit(solution)/shard_map/ppermute | solution.py:36
  25.3 6.8 %collective-permute-done = bf16[512,768]{1,0:T(8,128)(2,1)S(1)} collective-permute-done((bf16[512,768]{1,0:T(8,128)(2,1)}, bf16[512,768]{1,0:T(8,128)(2,1)S(1)}, u32[]{:S(2)}, u32[]{:S(2)}) %collective-permute-start) | collective-permute-done | bytes 786464 | tf_op jit(solution)/shard_map/ppermute | solution.py:909
  36.3 2.9 %collective-permute-done.5 = bf16[2,48,1280]{2,1,0:T(8,128)(2,1)} collective-permute-done((bf16[2,48,1280]{2,1,0:T(8,128)(2,1)S(1)}, bf16[2,48,1280]{2,1,0:T(8,128)(2,1)}, u32[]{:S(2)}, u32[]{:S(2)}) %collective-permute-start.5) | collective-permute-done | bytes 245792 | tf_op jit(solution)/shard_map/ppermute | solution.py:36
  43.8 6.1 %collective-permute-done.6 = bf16[4,48,512]{2,1,0:T(8,128)(2,1)S(1)} collective-permute-done((bf16[4,48,512]{2,1,0:T(8,128)(2,1)S(1)}, bf16[4,48,512]{2,1,0:T(8,128)(2,1)S(1)}, u32[]{:S(2)}, u32[]{:S(2)}) %collective-permute-start.6) | collective-permute-done | bytes 196640 | tf_op jit(solution)/shard_map/ppermute | solution.py:36
  51.5 3.3 %collective-permute-done.8 = bf16[4,48,768]{2,1,0:T(8,128)(2,1)S(1)} collective-permute-done((bf16[4,48,768]{2,1,0:T(8,128)(2,1)S(1)}, bf16[4,48,768]{2,1,0:T(8,128)(2,1)S(1)}, u32[]{:S(2)}, u32[]{:S(2)}) %collective-permute-start.8) | collective-permute-done | bytes 294944 | tf_op jit(solution)/shard_map/ppermute | solution.py:36
  57.2 3.1 %fusion.2 = f32[2048]{0:T(1024)S(1)} fusion(f32[2048]{0:T(1024)S(1)} %broadcast_multiply_fusion, bf16[1024,768]{1,0:T(8,128)(2,1)S(1)} %maximum_select_fusion.1, bf16[1024,768]{1,0:T(8,128)(2,1)S(1)} %maximum_select_fusion), kind=kLoop, calls=%fused_computation.4 | loop fusion | flops 11008000 | bytes 3162112 | tf_op jit(solution)/shard_map/reduce_sum | solution.py:860
  60.4 3.6 %fusion.hat_ref = f32[2048,768]{1,0:T(8,128)} fusion(f32[2048]{0:T(1024)S(1)} %add_rsqrt_fusion, f32[2048]{0:T(1024)S(1)} %broadcast_multiply_fusion, bf16[1024,768]{1,0:T(8,128)(2,1)S(1)} %maximum_select_fusion.1, bf16[1024,768]{1,0:T(8,128)(2,1)S(1)} %maximum_select_fusion), kind=kLoop, calls=%fused_computation.2 | loop fusion | flops 9437184 | bytes 9453568 | tf_op jit(solution)/shard_map/mul | solution.py:862
  65.0 2.5 add_convert_fusion.1.n_ref
  70.0 2.8 add_convert_fusion.k_ref.v_ref
  72.8 8.6 %attend.1 = (bf16[1024,384]{1,0:T(8,128)(2,1)S(1)}, f32[3,8,1024]{2,1,0:T(8,128)S(1)}) custom-call(s32[1]{0:T(128)} %bitcast.7.far_ref, bf16[1024,384]{1,0:T(8,128)(2,1)S(1)} %add_convert_fusion.4.q_ref, bf16[2048,768]{1,0:T(8,128)(2,1)S(1)} %add_convert_fusion.k_ref.v_ref, bf16[2048,768]{1,0:T(8,128)(2,1)S(1)} %add_convert_fusion.k_ref.v_ref), custom_call_target="tpu_custom_call" | custom-call | flops 1048576 | bytes 4096 | tf_op jit(solution)/shard_map/attend/pallas_call | solution.py:338
  82.4 3.2 %collective-permute-start.10 = (bf16[512,384]{1,0:T(8,128)(2,1)S(1)}, bf16[512,384]{1,0:T(8,128)(2,1)S(1)}, u32[]{:S(2)}, u32[]{:S(2)}) collective-permute-start(bf16[512,384]{1,0:T(8,128)(2,1)S(1)} %constant_dynamic-slice_fusion), channel_id=1, source_target_pairs={{0,1},{1,0},{2,3},{3,2},{4,5},{5,4},{6,7},{7,6},{8,9},{9,8},{10,11... | collective-permute-start | bytes 1179656 | tf_op jit(solution)/shard_map/ppermute | solution.py:36
  88.4 19.0 %all-gather.2.cloned.1.call-done.fc_ref.refs_0_.refs_1_.refs_2_.refs_3_.w_ref = bf16[768,6912]{1,0:T(8,128)(2,1)} async-done(((bf16[24,6912]{1,0:T(8,128)(2,1)}), bf16[768,6912]{1,0:T(8,128)(2,1)}) %all-gather.2.cloned.1.call-update) | async-done | bytes 10616848 | tf_op jit(solution)/shard_map/all_gather | solution.py:903
  107.4 2.5 fusion.27
  111.7 22.9 %feed.1 = (f32[512,768]{1,0:T(8,128)S(1)}, f32[512,768]{1,0:T(8,128)S(1)}, bf16[768,1536]{1,0:T(8,128)(2,1)}, bf16[768,1536]{1,0:T(8,128)(2,1)}, bf16[3072,384]{...) custom-call(s32[1]{0:T(128)} %bitcast.29.core_ref, bf16[512,768]{1,0:T(8,128)(2,1)S(1)} %get-tuple-element.193.n_ref, ...), custom_call_target="tpu_custom_call" | custom-call | flops 1048576 | bytes 4096 | tf_op jit(solution)/shard_map/feed/pallas_call | solution.py:610
  137.7 4.6 %turn.1 = (f32[512,768]{1,0:T(8,128)S(1)}, bf16[512,384]{1,0:T(8,128)(2,1)S(1)}, bf16[512,384]{1,0:T(8,128)(2,1)S(1)}, bf16[768,384]{1,0:T(8,128)(2,1)S(1)}, bf1...) custom-call(s32[1]{0:T(128)} %bitcast.29.core_ref, ...), custom_call_target="tpu_custom_call" | custom-call | flops 1048576 | bytes 4096 | tf_op jit(solution)/shard_map/turn/pallas_call | solution.py:680
  145.2 4.8 %send.8 = (bf16[8,48,1536]{2,1,0:T(8,128)(2,1)S(1)}, bf16[8,192,384]{2,1,0:T(8,128)(2,1)S(1)}) custom-call(s32[1]{0:T(128)} %bitcast.35.at_ref, bf16[16,48,1536]{2,1,0:T(8,128)(2,1)S(1)} %bitcast.105, bf16[16,48,1536]{2,1,0:T(8,128)(2,1)} %bitcast.37.refs_1_, bf16[16,192,384]{2,1,0:T(8,128)(2,1)} %bitcast.125, ...), custom_call_target="tpu_custom_call" | custom-call | flops 12884901888 | bytes 4096 | tf_op jit(solution)/shard_map/send/pallas_call | solution.py:158
  154.3 6.6 %attend_back.3 = (bf16[1024,384]{1,0:T(8,128)(2,1)S(1)}, bf16[2048,384]{1,0:T(8,128)(2,1)S(1)}, bf16[2048,384]{1,0:T(8,128)(2,1)}) custom-call(s32[1]{0:T(128)} %bitcast.7.far_ref, bf16[1024,384]{1,0:T(8,128)(2,1)S(1)} %copy-done.2, bf16[2048,768]{1,0:T(8,128)(2,1)} %copy-done, bf16[2048,768]{1,0:T(8,128)(2,1)} %copy-done, bf16[1024,384]{1,0:T(8,128)(2,1)S(1)} %bitcast.95, ...), custom_call_target="tpu_custom_call" | custom-call | flops 1048576 | bytes 4096 | tf_op jit(solution)/shard_map/attend_back/pallas_call | solution.py:428
  160.9 6.4 %attend_back.4 = (bf16[1024,384]{1,0:T(8,128)(2,1)S(1)}, bf16[2048,384]{1,0:T(8,128)(2,1)S(1)}, bf16[2048,384]{1,0:T(8,128)(2,1)}) custom-call(s32[1]{0:T(128)} %bitcast.7.far_ref, bf16[1024,384]{1,0:T(8,128)(2,1)S(1)} %copy-done.2, bf16[2048,768]{1,0:T(8,128)(2,1)} %copy-done, ...), custom_call_target="tpu_custom_call", output_to_operand_aliasing={{0}: (7, {}), {1}: (8, {}), {2}: (9, {})} | custom-call | flops 1048576 | bytes 4096 | tf_op jit(solution)/shard_map/attend_back/pallas_call | solution.py:428
  167.3 10.1 %collective-permute-done.14.refs_2_ = bf16[8,48,1536]{2,1,0:T(8,128)(2,1)S(1)} collective-permute-done((bf16[8,48,1536]{2,1,0:T(8,128)(2,1)S(1)}, bf16[8,48,1536]{2,1,0:T(8,128)(2,1)S(1)}, u32[]{:S(2)}, u32[]{:S(2)}) %collective-permute-start.14) | collective-permute-done | bytes 1179680 | tf_op jit(solution)/shard_map/ppermute | solution.py:36
  178.3 3.1 %send.9 = (bf16[4,48,1536]{2,1,0:T(8,128)(2,1)S(1)}, bf16[4,192,384]{2,1,0:T(8,128)(2,1)S(1)}) custom-call(s32[1]{0:T(128)} %bitcast.35.at_ref, bf16[16,48,1536]{2,1,0:T(8,128)(2,1)S(1)} %bitcast.106, bf16[16,48,1536]{2,1,0:T(8,128)(2,1)} %bitcast.37.refs_1_, bf16[8,48,1536]{2,1,0:T(8,128)(2,1)S(1)} %collective-permute-done.14.refs_2_, ...), custom_call_target="tpu_custom_call" | custom-call | flops 12884901888 | bytes 4096 | tf_op jit(solution)/shard_map/send/pallas_call | solution.py:158
  183.3 6.6 %attend_back.5 = (bf16[1024,384]{1,0:T(8,128)(2,1)S(1)}, bf16[2048,384]{1,0:T(8,128)(2,1)S(1)}, bf16[2048,384]{1,0:T(8,128)(2,1)}) custom-call(s32[1]{0:T(128)} %bitcast.7.far_ref, bf16[1024,384]{1,0:T(8,128)(2,1)S(1)} %copy-done.2, bf16[2048,768]{1,0:T(8,128)(2,1)} %copy-done, ...), custom_call_target="tpu_custom_call", output_to_operand_aliasing={{0}: (7, {}), {1}: (8, {}), {2}: (9, {})} | custom-call | flops 1048576 | bytes 4096 | tf_op jit(solution)/shard_map/attend_back/pallas_call | solution.py:428
  190.8 4.2 %collective-permute-done.16.refs_3_ = bf16[4,48,1536]{2,1,0:T(8,128)(2,1)} collective-permute-done((bf16[4,48,1536]{2,1,0:T(8,128)(2,1)S(1)}, bf16[4,48,1536]{2,1,0:T(8,128)(2,1)}, u32[]{:S(2)}, u32[]{:S(2)}) %collective-permute-start.16) | collective-permute-done | bytes 589856 | tf_op jit(solution)/shard_map/ppermute | solution.py:36
  195.7 2.6 send.10
  198.3 6.6 %qkv_grads.1 = (bf16[768,768]{1,0:T(8,128)(2,1)S(1)}, bf16[768,768]{1,0:T(8,128)(2,1)S(1)}) custom-call(bf16[2048,768]{1,0:T(8,128)(2,1)} %copy-done.38, bf16[1024,384]{1,0:T(8,128)(2,1)S(1)} %get-tuple-element.149.dq_ref, bf16[2048,384]{1,0:T(8,128)(2,1)S(1)} %get-tuple-element.139.dk_ref, bf16[2048,384]{1,0:T(8,128)(2,1)} %get-tuple-element.140.dv_ref, ...), custom_call_target="tpu_custom_call" | custom-call | flops 1048576 | bytes 4096 | tf_op jit(solution)/shard_map/qkv_grads/pallas_call | solution.py:477
  209.6 10.2 %norm_back.1 = (f32[2,512,768]{2,1,0:T(8,128)}, bf16[2,512,768]{2,1,0:T(8,128)(2,1)}, f32[1,768]{1,0:T(1,128)S(1)}, f32[1,768]{1,0:T(1,128)S(1)}, f32[1,384]{1,0:T(1,128)S(1)}, /*index=5*/f32[1,384]{1,0:T(1,128)S(1)}) custom-call(s32[1]{0:T(128)} %bitcast.29.core_ref, bf16[1024,384]{1,0:T(8,128)(2,1)S(1)} %get-tuple-element.149.dq_ref, ...), custom_call_target="tpu_custom_call" | custom-call | flops 1048576 | bytes 4096 | tf_op jit(solution)/shard_map/norm_back/pallas_call | solution.py:769
  226.3 2.6 fusion.11
  233.6 2.5 pack.1
  243.4 10.7 %all-to-all-start = ((f32[32,1,1024]{2,1,0:T(1,128)}), f32[32,1,1024]{2,1,0:T(1,128)S(1)}, u32[]{:S(2)}, u32[]{:S(2)}) async-start(f32[32,1,1024]{2,1,0:T(1,128)} %copy.50), calls=%async_computation | async-start | bytes 262144 | tf_op jit(solution)/shard_map/all_to_all | solution.py:1077
  254.1 2.7 fusion.10
  258.6 4.8 %collective-permute-start.30 = (f32[24,4608]{1,0:T(8,128)S(1)}, f32[24,4608]{1,0:T(8,128)S(1)}, u32[]{:S(2)}, u32[]{:S(2)}) collective-permute-start(f32[24,4608]{1,0:T(8,128)S(1)} %get-tuple-element.163), channel_id=1, source_target_pairs={{0,1},{1,0},{2,3},{3,2},{4,5},{5,4},{6,7},{7,6},{8,9},{9,8},{10,11... | collective-permute-start | bytes 1327112 | tf_op jit(solution)/shard_map/ppermute | solution.py:36
  264.5 2.8 fusion.23
  (254 shorter events, 78.3 us)
Async XLA Ops:
  7.3 100.1 %all-gather.2.cloned.1.call-start = ((), (), s32[]{:S(2)}) async-start(), calls=%async_computation.1 | async-start | bytes 10948608 | tf_op jit(solution)/shard_map/all_gather | solution.py:903
  9.3 22.9 %collective-permute-start = (bf16[512,768]{1,0:T(8,128)(2,1)}, bf16[512,768]{1,0:T(8,128)(2,1)S(1)}, u32[]{:S(2)}, u32[]{:S(2)}) collective-permute-start(bf16[512,768]{1,0:T(8,128)(2,1)} %bitcast.135), channel_id=1, source_target_pairs={{0,2},{1,3},{4,6},{5,7},{8,10},{9,11},{12,14},{13,15},{16,18},{17,... | collective-permute-start | bytes 2359304 | tf_op jit(solution)/shard_map/ppermute | solution.py:909
  17.2 8.2 %collective-permute-start.4 = (bf16[1,48,1280]{2,1,0:T(8,128)(2,1)S(1)}, bf16[1,48,1280]{2,1,0:T(8,128)(2,1)S(1)}, u32[]{:S(2)}, u32[]{:S(2)}) collective-permute-start(bf16[1,48,1280]{2,1,0:T(8,128)(2,1)S(1)} %bitcast.138), channel_id=1, source_target_pairs={{0,16},{1,17},{2,18},{3,19},{4,20},{5,21},{6,22},{7,23},{8,24},{9,... | collective-permute-start | bytes 368648 | tf_op jit(solution)/shard_map/ppermute | solution.py:36
  32.2 7.0 %collective-permute-start.5 = (bf16[2,48,1280]{2,1,0:T(8,128)(2,1)S(1)}, bf16[2,48,1280]{2,1,0:T(8,128)(2,1)}, u32[]{:S(2)}, u32[]{:S(2)}) collective-permute-start(bf16[2,48,1280]{2,1,0:T(8,128)(2,1)S(1)} %constant_dynamic-update-slice_fusion.1), channel_id=1, source_target_pairs={{0,8},{1,9},{2,10},{3,11},{4,12},{5,13},{6,14},{7,15},{8,0},{9,1},... | collective-permute-start | bytes 737288 | tf_op jit(solution)/shard_map/ppermute | solution.py:36
  33.6 10.0 %collective-permute-start.2 = (bf16[512,768]{1,0:T(8,128)(2,1)S(1)}, bf16[512,768]{1,0:T(8,128)(2,1)S(1)}, u32[]{:S(2)}, u32[]{:S(2)}) collective-permute-start(bf16[512,768]{1,0:T(8,128)(2,1)S(1)} %bitcast.136), channel_id=1, source_target_pairs={{0,1},{1,0},{2,3},{3,2},{4,5},{5,4},{6,7},{7,6},{8,9},{9,8},{10,11... | collective-permute-start | bytes 2359304 | tf_op jit(solution)/shard_map/ppermute | solution.py:36
  36.2 18.9 %collective-permute-start.1 = (bf16[512,768]{1,0:T(8,128)(2,1)S(1)}, bf16[512,768]{1,0:T(8,128)(2,1)S(1)}, u32[]{:S(2)}, u32[]{:S(2)}) collective-permute-start(bf16[512,768]{1,0:T(8,128)(2,1)S(1)} %collective-permute-done), channel_id=1, source_target_pairs={{0,1},{1,0},{2,3},{3,2},{4,5},{5,4},{6,7},{7,6},{8,9},{9,8},{10,11... | collective-permute-start | bytes 2359304 | tf_op jit(solution)/shard_map/ppermute | solution.py:36
  40.3 9.6 %collective-permute-start.6 = (bf16[4,48,512]{2,1,0:T(8,128)(2,1)S(1)}, bf16[4,48,512]{2,1,0:T(8,128)(2,1)S(1)}, u32[]{:S(2)}, u32[]{:S(2)}) collective-permute-start(bf16[4,48,512]{2,1,0:T(8,128)(2,1)S(1)} %pad_maximum_fusion.2), channel_id=1, source_target_pairs={{0,4},{1,5},{2,6},{3,7},{4,0},{5,1},{6,2},{7,3},{8,12},{9,13},{10,... | collective-permute-start | bytes 589832 | tf_op jit(solution)/shard_map/ppermute | solution.py:36
  41.9 13.0 %collective-permute-start.8 = (bf16[4,48,768]{2,1,0:T(8,128)(2,1)S(1)}, bf16[4,48,768]{2,1,0:T(8,128)(2,1)S(1)}, u32[]{:S(2)}, u32[]{:S(2)}) collective-permute-start(bf16[4,48,768]{2,1,0:T(8,128)(2,1)S(1)} %slice.173), channel_id=1, source_target_pairs={{0,2},{1,3},{2,0},{3,1},{4,6},{5,7},{6,4},{7,5},{8,10},{9,11},{10,... | collective-permute-start | bytes 884744 | tf_op jit(solution)/shard_map/ppermute | solution.py:36
  49.9 14.1 %collective-permute-start.7 = (bf16[8,48,512]{2,1,0:T(8,128)(2,1)S(1)}, bf16[8,48,512]{2,1,0:T(8,128)(2,1)S(1)}, u32[]{:S(2)}, u32[]{:S(2)}) collective-permute-start(bf16[8,48,512]{2,1,0:T(8,128)(2,1)S(1)} %bitcast.133), channel_id=1, source_target_pairs={{0,2},{1,3},{2,0},{3,1},{4,6},{5,7},{6,4},{7,5},{8,10},{9,11},{10,... | collective-permute-start | bytes 1179656 | tf_op jit(solution)/shard_map/ppermute | solution.py:36
  54.9 13.6 %collective-permute-start.9 = (bf16[8,48,768]{2,1,0:T(8,128)(2,1)S(1)}, bf16[8,48,768]{2,1,0:T(8,128)(2,1)}, u32[]{:S(2)}, u32[]{:S(2)}) collective-permute-start(bf16[8,48,768]{2,1,0:T(8,128)(2,1)S(1)} %bitcast.123), channel_id=1, source_target_pairs={{0,4},{1,5},{2,6},{3,7},{4,0},{5,1},{6,2},{7,3},{8,12},{9,13},{10,... | collective-permute-start | bytes 1769480 | tf_op jit(solution)/shard_map/ppermute | solution.py:36
  82.4 4.9 %collective-permute-start.10 = (bf16[512,384]{1,0:T(8,128)(2,1)S(1)}, bf16[512,384]{1,0:T(8,128)(2,1)S(1)}, u32[]{:S(2)}, u32[]{:S(2)}) collective-permute-start(bf16[512,384]{1,0:T(8,128)(2,1)S(1)} %constant_dynamic-slice_fusion), channel_id=1, source_target_pairs={{0,1},{1,0},{2,3},{3,2},{4,5},{5,4},{6,7},{7,6},{8,9},{9,8},{10,11... | collective-permute-start | bytes 1179656 | tf_op jit(solution)/shard_map/ppermute | solution.py:36
  136.9 7.4 %collective-permute-start.12 = (bf16[768,1536]{1,0:T(8,128)(2,1)}, bf16[768,1536]{1,0:T(8,128)(2,1)}, u32[]{:S(2)}, u32[]{:S(2)}) collective-permute-start(bf16[768,1536]{1,0:T(8,128)(2,1)} %get-tuple-element.113), channel_id=1, source_target_pairs={{0,1},{1,0},{2,3},{3,2},{4,5},{5,4},{6,7},{7,6},{8,9},{9,8},{10,11... | collective-permute-start | bytes 7077896 | tf_op jit(solution)/shard_map/ppermute | solution.py:36
  137.2 8.0 %collective-permute-start.13 = (bf16[3072,384]{1,0:T(8,128)(2,1)}, bf16[3072,384]{1,0:T(8,128)(2,1)}, u32[]{:S(2)}, u32[]{:S(2)}) collective-permute-start(bf16[3072,384]{1,0:T(8,128)(2,1)} %get-tuple-element.114), channel_id=1, source_target_pairs={{0,1},{1,0},{2,3},{3,2},{4,5},{5,4},{6,7},{7,6},{8,9},{9,8},{10,11... | collective-permute-start | bytes 7077896 | tf_op jit(solution)/shard_map/ppermute | solution.py:36
  150.0 27.4 %collective-permute-start.14 = (bf16[8,48,1536]{2,1,0:T(8,128)(2,1)S(1)}, bf16[8,48,1536]{2,1,0:T(8,128)(2,1)S(1)}, u32[]{:S(2)}, u32[]{:S(2)}) collective-permute-start(bf16[8,48,1536]{2,1,0:T(8,128)(2,1)S(1)} %get-tuple-element.118), channel_id=1, source_target_pairs={{0,2},{1,3},{2,0},{3,1},{4,6},{5,7},{6,4},{7,5},{8,10},{9,11},{10,... | collective-permute-start | bytes 3538952 | tf_op jit(solution)/shard_map/ppermute | solution.py:36
  151.3 27.0 %collective-permute-start.15 = (bf16[8,192,384]{2,1,0:T(8,128)(2,1)S(1)}, bf16[8,192,384]{2,1,0:T(8,128)(2,1)S(1)}, u32[]{:S(2)}, u32[]{:S(2)}) collective-permute-start(bf16[8,192,384]{2,1,0:T(8,128)(2,1)S(1)} %get-tuple-element.119), channel_id=1, source_target_pairs={{0,4},{1,5},{2,6},{3,7},{4,0},{5,1},{6,2},{7,3},{8,12},{9,13},{10,... | collective-permute-start | bytes 3538952 | tf_op jit(solution)/shard_map/ppermute | solution.py:36
  151.6 2.2 collective-permute-start.11
  153.9 36.0 %collective-permute-start.18 = (bf16[768,384]{1,0:T(8,128)(2,1)S(1)}, bf16[768,384]{1,0:T(8,128)(2,1)S(1)}, u32[]{:S(2)}, u32[]{:S(2)}) collective-permute-start(bf16[768,384]{1,0:T(8,128)(2,1)S(1)} %get-tuple-element.143), channel_id=1, source_target_pairs={{0,1},{1,0},{2,3},{3,2},{4,5},{5,4},{6,7},{7,6},{8,9},{9,8},{10,11... | collective-permute-start | bytes 1769480 | tf_op jit(solution)/shard_map/ppermute | solution.py:36
  181.4 13.6 %collective-permute-start.16 = (bf16[4,48,1536]{2,1,0:T(8,128)(2,1)S(1)}, bf16[4,48,1536]{2,1,0:T(8,128)(2,1)}, u32[]{:S(2)}, u32[]{:S(2)}) collective-permute-start(bf16[4,48,1536]{2,1,0:T(8,128)(2,1)S(1)} %get-tuple-element.130), channel_id=1, source_target_pairs={{0,4},{1,5},{2,6},{3,7},{4,0},{5,1},{6,2},{7,3},{8,12},{9,13},{10,... | collective-permute-start | bytes 1769480 | tf_op jit(solution)/shard_map/ppermute | solution.py:36
  182.1 13.6 %collective-permute-start.17 = (bf16[4,192,384]{2,1,0:T(8,128)(2,1)S(1)}, bf16[4,192,384]{2,1,0:T(8,128)(2,1)}, u32[]{:S(2)}, u32[]{:S(2)}) collective-permute-start(bf16[4,192,384]{2,1,0:T(8,128)(2,1)S(1)} %get-tuple-element.131), channel_id=1, source_target_pairs={{0,2},{1,3},{2,0},{3,1},{4,6},{5,7},{6,4},{7,5},{8,10},{9,11},{10,... | collective-permute-start | bytes 1769480 | tf_op jit(solution)/shard_map/ppermute | solution.py:36
  205.2 16.8 %collective-permute-start.20 = (bf16[8,48,768]{2,1,0:T(8,128)(2,1)S(1)}, bf16[8,48,768]{2,1,0:T(8,128)(2,1)S(1)}, u32[]{:S(2)}, u32[]{:S(2)}) collective-permute-start(bf16[8,48,768]{2,1,0:T(8,128)(2,1)S(1)} %get-tuple-element.147), channel_id=1, source_target_pairs={{0,2},{1,3},{2,0},{3,1},{4,6},{5,7},{6,4},{7,5},{8,10},{9,11},{10,... | collective-permute-start | bytes 1769480 | tf_op jit(solution)/shard_map/ppermute | solution.py:36
  207.5 14.5 %collective-permute-start.21 = (bf16[8,48,768]{2,1,0:T(8,128)(2,1)S(1)}, bf16[8,48,768]{2,1,0:T(8,128)(2,1)S(1)}, u32[]{:S(2)}, u32[]{:S(2)}) collective-permute-start(bf16[8,48,768]{2,1,0:T(8,128)(2,1)S(1)} %get-tuple-element.148), channel_id=1, source_target_pairs={{0,4},{1,5},{2,6},{3,7},{4,0},{5,1},{6,2},{7,3},{8,12},{9,13},{10,... | collective-permute-start | bytes 1769480 | tf_op jit(solution)/shard_map/ppermute | solution.py:36
  208.5 13.5 %collective-permute-start.22 = (bf16[2,48,3072]{2,1,0:T(8,128)(2,1)S(1)}, bf16[2,48,3072]{2,1,0:T(8,128)(2,1)S(1)}, u32[]{:S(2)}, u32[]{:S(2)}) collective-permute-start(bf16[2,48,3072]{2,1,0:T(8,128)(2,1)S(1)} %copy-done.54), channel_id=1, source_target_pairs={{0,8},{1,9},{2,10},{3,11},{4,12},{5,13},{6,14},{7,15},{8,0},{9,1},... | collective-permute-start | bytes 1769480 | tf_op jit(solution)/shard_map/ppermute | solution.py:36
  219.8 6.5 %collective-permute-start.19 = (bf16[2,512,768]{2,1,0:T(8,128)(2,1)}, bf16[2,512,768]{2,1,0:T(8,128)(2,1)}, u32[]{:S(2)}, u32[]{:S(2)}) collective-permute-start(bf16[2,512,768]{2,1,0:T(8,128)(2,1)} %get-tuple-element.151), channel_id=1, source_target_pairs={{0,1},{1,0},{2,3},{3,2},{4,5},{5,4},{6,7},{7,6},{8,9},{9,8},{10,11... | collective-permute-start | bytes 4718600 | tf_op jit(solution)/shard_map/ppermute | solution.py:36
  223.3 6.6 %collective-permute-start.26 = (bf16[4,48,768]{2,1,0:T(8,128)(2,1)S(1)}, bf16[4,48,768]{2,1,0:T(8,128)(2,1)S(1)}, u32[]{:S(2)}, u32[]{:S(2)}) collective-permute-start(bf16[4,48,768]{2,1,0:T(8,128)(2,1)S(1)} %get-tuple-element.154), channel_id=1, source_target_pairs={{0,4},{1,5},{2,6},{3,7},{4,0},{5,1},{6,2},{7,3},{8,12},{9,13},{10,... | collective-permute-start | bytes 884744 | tf_op jit(solution)/shard_map/ppermute | solution.py:36
  223.6 6.3 %collective-permute-start.27 = (bf16[4,48,768]{2,1,0:T(8,128)(2,1)S(1)}, bf16[4,48,768]{2,1,0:T(8,128)(2,1)S(1)}, u32[]{:S(2)}, u32[]{:S(2)}) collective-permute-start(bf16[4,48,768]{2,1,0:T(8,128)(2,1)S(1)} %get-tuple-element.155), channel_id=1, source_target_pairs={{0,2},{1,3},{2,0},{3,1},{4,6},{5,7},{6,4},{7,5},{8,10},{9,11},{10,... | collective-permute-start | bytes 884744 | tf_op jit(solution)/shard_map/ppermute | solution.py:36
  233.3 6.2 %collective-permute-start.28 = (bf16[2,48,1536]{2,1,0:T(8,128)(2,1)}, bf16[2,48,1536]{2,1,0:T(8,128)(2,1)S(1)}, u32[]{:S(2)}, u32[]{:S(2)}) collective-permute-start(bf16[2,48,1536]{2,1,0:T(8,128)(2,1)} %send.14), channel_id=1, source_target_pairs={{0,8},{1,9},{2,10},{3,11},{4,12},{5,13},{6,14},{7,15},{8,0},{9,1},... | collective-permute-start | bytes 884744 | tf_op jit(solution)/shard_map/ppermute | solution.py:36
  236.1 20.7 %collective-permute-start.25 = (bf16[1,48,3072]{2,1,0:T(8,128)(2,1)}, bf16[1,48,3072]{2,1,0:T(8,128)(2,1)S(1)}, u32[]{:S(2)}, u32[]{:S(2)}) collective-permute-start(bf16[1,48,3072]{2,1,0:T(8,128)(2,1)} %send.13), channel_id=1, source_target_pairs={{0,16},{1,17},{2,18},{3,19},{4,20},{5,21},{6,22},{7,23},{8,24},{9,... | collective-permute-start | bytes 884744 | tf_op jit(solution)/shard_map/ppermute | solution.py:36
  238.2 26.3 %collective-permute-start.23 = (bf16[512,768]{1,0:T(8,128)(2,1)}, bf16[512,768]{1,0:T(8,128)(2,1)S(1)}, u32[]{:S(2)}, u32[]{:S(2)}) collective-permute-start(bf16[512,768]{1,0:T(8,128)(2,1)} %fusion.11), channel_id=1, source_target_pairs={{2,0},{3,1},{6,4},{7,5},{10,8},{11,9},{14,12},{15,13},{18,16},{19,... | collective-permute-start | bytes 2359304 | tf_op jit(solution)/shard_map/ppermute | solution.py:1057
  242.3 14.5 %collective-permute-start.29 = (bf16[1,48,1536]{2,1,0:T(8,128)(2,1)}, bf16[1,48,1536]{2,1,0:T(8,128)(2,1)S(1)}, u32[]{:S(2)}, u32[]{:S(2)}) collective-permute-start(bf16[1,48,1536]{2,1,0:T(8,128)(2,1)} %send.15), channel_id=1, source_target_pairs={{0,16},{1,17},{2,18},{3,19},{4,20},{5,21},{6,22},{7,23},{8,24},{9,... | collective-permute-start | bytes 442376 | tf_op jit(solution)/shard_map/ppermute | solution.py:36
  243.4 20.0 %all-to-all-start = ((f32[32,1,1024]{2,1,0:T(1,128)}), f32[32,1,1024]{2,1,0:T(1,128)S(1)}, u32[]{:S(2)}, u32[]{:S(2)}) async-start(f32[32,1,1024]{2,1,0:T(1,128)} %copy.50), calls=%async_computation | async-start | bytes 262144 | tf_op jit(solution)/shard_map/all_to_all | solution.py:1077
  258.6 16.9 %collective-permute-start.30 = (f32[24,4608]{1,0:T(8,128)S(1)}, f32[24,4608]{1,0:T(8,128)S(1)}, u32[]{:S(2)}, u32[]{:S(2)}) collective-permute-start(f32[24,4608]{1,0:T(8,128)S(1)} %get-tuple-element.163), channel_id=1, source_target_pairs={{0,1},{1,0},{2,3},{3,2},{4,5},{5,4},{6,7},{7,6},{8,9},{9,8},{10,11... | collective-permute-start | bytes 1327112 | tf_op jit(solution)/shard_map/ppermute | solution.py:36
  269.2 4.9 %collective-permute-start.24 = (f32[1,768]{1,0:T(1,128)S(1)}, f32[1,768]{1,0:T(1,128)S(1)}, u32[]{:S(2)}, u32[]{:S(2)}) collective-permute-start(f32[1,768]{1,0:T(1,128)S(1)} %slice.181), channel_id=1, source_target_pairs={{1,0},{2,1},{3,2},{5,4},{6,5},{7,6},{9,8},{10,9},{11,10},{13,12},{... | collective-permute-start | bytes 9224 | tf_op jit(solution)/shard_map/ppermute | solution.py:1101
  (56 other events, 321.6 us)
Sparse Core Ops, SparseCore 0:
  11.0 96.3 all-gather.1

commit v7 on v6

--- a/solution.py
+++ b/solution.py
@@ -714,7 +714,7 @@
             shape((1, width), FULL),
             shape((1, width), FULL),
         ),
-        compiler_params=pltpu.CompilerParams(vmem_limit_bytes=VMEM),
+        compiler_params=pltpu.CompilerParams(vmem_limit_bytes=56 << 20),
         cost_estimate=SHORT,
         name="turn",
     )(core, grad, hat, root, gain, grad_valid, attended, late)
@@ -1075,7 +1075,7 @@
         last_ready = prepare(last, plans, step)
     packed = after(packed, *sends(last_ready))
     share = jnp.sum(lax.all_to_all(packed, ALL, 0, 0, tiled=True), 0, keepdims=True)
-    last = exchange(last_ready)
+    last = exchange(last_ready, (back,))
     for step in range(4, flat_bits() - 1):
         ready = prepare(exchange(ready), plans, step)
     early = exchange(ready, (far_sum,))

time: 288 us -> 287 us (level)
    all_to_all x1, waiting for transfers between devices: 0.01 us -> 3.38 us  [shards(): lax.all_to_all(packed, ALL, 0, 0, tiled=True)]
    unnamed x112 -> x124, local copies, waits for them, and re-layouts: 10.1 us -> 7.31 us
  transfers between devices with their start and end apart: 33 -> 33, of which waited for: 15 -> 16; matrix products, arithmetic and copies ran while one was open for 13% -> 14% of each run, Pallas kernels for 17% -> 17%
where the time goes in v7:
time: 287 us; the launch traced here: 282 us
  Pallas kernels  98.5 us (34%)
  waiting for transfers between devices  66 us (23%)
  starting transfers between devices  50.2 us (17%)
  other arithmetic  27 us (9%)
  local copies, waits for them, and re-layouts  17.5 us (6%)
  between operations  16.2 us (6%)
  matrix products  6.18 us (2%)
    ppermute x28, waiting for transfers between devices, swap(): return lax.ppermute(value, ALL, [(i, i ^ 1 << bit) for i in range(count)])  36.8 us
    ppermute x28, starting transfers between devices, swap(): return lax.ppermute(value, ALL, [(i, i ^ 1 << bit) for i in range(count)])  32.6 us
    pallas_call x1, Pallas kernels, feed(): pl.pallas_call(functools.partial(feed_kernel, shard_rows), out_shape=(jax...  22.9 us
    pallas_call x3, Pallas kernels, attend_back(): pl.pallas_call(attend_back_kernel, out_shape=(jax.ShapeDtypeStruct((near,...  19.6 us
    all_gather x1, waiting for transfers between devices, shards(): lax.all_gather(beside_rows(fc_weight, proj_weight, out_weight), ALL, axis...  18.9 us
    pallas_call x8, Pallas kernels, prepare(): pl.pallas_call(functools.partial(send_kernel, [len(value.addends) for val...  17.3 us
    pallas_call x1, Pallas kernels, norm_back(): pl.pallas_call(norm_back_kernel, out_shape=(shape((2, quarter, width), FU...  10.3 us
    all_to_all x1, starting transfers between devices, shards(): lax.all_to_all(packed, ALL, 0, 0, tiled=True)  9.95 us
  transfers between devices with their start and end apart: 33, of which 16 were waited for; matrix products, arithmetic and copies ran while one was open for 14% of the time, Pallas kernels for 17%

profile of v7, /device:TPU:1, one launch (start us, length us, event | category | flops | bytes accessed | tf_op | source)
XLA Modules:
  0.0 281.6 jit_solution(2703850061633567440)
XLA Ops:
  9.3 4.0 %collective-permute-start = (bf16[512,768]{1,0:T(8,128)(2,1)}, bf16[512,768]{1,0:T(8,128)(2,1)S(1)}, u32[]{:S(2)}, u32[]{:S(2)}) collective-permute-start(bf16[512,768]{1,0:T(8,128)(2,1)} %bitcast.135), channel_id=1, source_target_pairs={{0,2},{1,3},{4,6},{5,7},{8,10},{9,11},{12,14},{13,15},{16,18},{17,... | collective-permute-start | bytes 2359304 | tf_op jit(solution)/shard_map/ppermute | solution.py:909
  19.5 5.8 %collective-permute-done.4 = bf16[1,48,1280]{2,1,0:T(8,128)(2,1)S(1)} collective-permute-done((bf16[1,48,1280]{2,1,0:T(8,128)(2,1)S(1)}, bf16[1,48,1280]{2,1,0:T(8,128)(2,1)S(1)}, u32[]{:S(2)}, u32[]{:S(2)}) %collective-permute-start.4) | collective-permute-done | bytes 122912 | tf_op jit(solution)/shard_map/ppermute | solution.py:36
  25.3 6.8 %collective-permute-done = bf16[512,768]{1,0:T(8,128)(2,1)S(1)} collective-permute-done((bf16[512,768]{1,0:T(8,128)(2,1)}, bf16[512,768]{1,0:T(8,128)(2,1)S(1)}, u32[]{:S(2)}, u32[]{:S(2)}) %collective-permute-start) | collective-permute-done | bytes 786464 | tf_op jit(solution)/shard_map/ppermute | solution.py:909
  36.3 2.9 %collective-permute-done.5 = bf16[2,48,1280]{2,1,0:T(8,128)(2,1)} collective-permute-done((bf16[2,48,1280]{2,1,0:T(8,128)(2,1)S(1)}, bf16[2,48,1280]{2,1,0:T(8,128)(2,1)}, u32[]{:S(2)}, u32[]{:S(2)}) %collective-permute-start.5) | collective-permute-done | bytes 245792 | tf_op jit(solution)/shard_map/ppermute | solution.py:36
  43.7 6.1 %collective-permute-done.6 = bf16[4,48,512]{2,1,0:T(8,128)(2,1)S(1)} collective-permute-done((bf16[4,48,512]{2,1,0:T(8,128)(2,1)S(1)}, bf16[4,48,512]{2,1,0:T(8,128)(2,1)S(1)}, u32[]{:S(2)}, u32[]{:S(2)}) %collective-permute-start.6) | collective-permute-done | bytes 196640 | tf_op jit(solution)/shard_map/ppermute | solution.py:36
  51.5 3.3 %collective-permute-done.8 = bf16[4,48,768]{2,1,0:T(8,128)(2,1)S(1)} collective-permute-done((bf16[4,48,768]{2,1,0:T(8,128)(2,1)S(1)}, bf16[4,48,768]{2,1,0:T(8,128)(2,1)S(1)}, u32[]{:S(2)}, u32[]{:S(2)}) %collective-permute-start.8) | collective-permute-done | bytes 294944 | tf_op jit(solution)/shard_map/ppermute | solution.py:36
  57.2 3.1 %fusion.2 = f32[2048]{0:T(1024)S(1)} fusion(f32[2048]{0:T(1024)S(1)} %broadcast_multiply_fusion, bf16[1024,768]{1,0:T(8,128)(2,1)S(1)} %maximum_select_fusion.1, bf16[1024,768]{1,0:T(8,128)(2,1)S(1)} %maximum_select_fusion), kind=kLoop, calls=%fused_computation.4 | loop fusion | flops 11008000 | bytes 3162112 | tf_op jit(solution)/shard_map/reduce_sum | solution.py:860
  60.4 3.6 %fusion.hat_ref = f32[2048,768]{1,0:T(8,128)} fusion(f32[2048]{0:T(1024)S(1)} %add_rsqrt_fusion, f32[2048]{0:T(1024)S(1)} %broadcast_multiply_fusion, bf16[1024,768]{1,0:T(8,128)(2,1)S(1)} %maximum_select_fusion.1, bf16[1024,768]{1,0:T(8,128)(2,1)S(1)} %maximum_select_fusion), kind=kLoop, calls=%fused_computation.2 | loop fusion | flops 9437184 | bytes 9453568 | tf_op jit(solution)/shard_map/mul | solution.py:862
  64.9 2.5 add_convert_fusion.1.n_ref
  69.9 2.8 %add_convert_fusion.k_ref.v_ref = bf16[2048,768]{1,0:T(8,128)(2,1)S(1)} fusion(bf16[2048,768]{1,0:T(8,128)(2,1)S(1)} %add_convert_fusion.1.n_ref, bf16[768,768]{1,0:T(8,128)(2,1)S(1)} %bitcast.98, f32[768]{0:T(1024)S(1)} %pad_reduce_fusion), kind=kOutput, calls=%fused_computation.5 | convolution fusion | flops 2419064832 | bytes 7474176 | tf_op jit(solution)/shard_map/dot_general | solution.py:271
  72.8 8.6 %attend.1 = (bf16[1024,384]{1,0:T(8,128)(2,1)S(1)}, f32[3,8,1024]{2,1,0:T(8,128)S(1)}) custom-call(s32[1]{0:T(128)} %bitcast.7.far_ref, bf16[1024,384]{1,0:T(8,128)(2,1)S(1)} %add_convert_fusion.4.q_ref, bf16[2048,768]{1,0:T(8,128)(2,1)S(1)} %add_convert_fusion.k_ref.v_ref, bf16[2048,768]{1,0:T(8,128)(2,1)S(1)} %add_convert_fusion.k_ref.v_ref), custom_call_target="tpu_custom_call" | custom-call | flops 1048576 | bytes 4096 | tf_op jit(solution)/shard_map/attend/pallas_call | solution.py:338
  82.4 3.2 %collective-permute-start.10 = (bf16[512,384]{1,0:T(8,128)(2,1)S(1)}, bf16[512,384]{1,0:T(8,128)(2,1)S(1)}, u32[]{:S(2)}, u32[]{:S(2)}) collective-permute-start(bf16[512,384]{1,0:T(8,128)(2,1)S(1)} %constant_dynamic-slice_fusion), channel_id=1, source_target_pairs={{0,1},{1,0},{2,3},{3,2},{4,5},{5,4},{6,7},{7,6},{8,9},{9,8},{10,11... | collective-permute-start | bytes 1179656 | tf_op jit(solution)/shard_map/ppermute | solution.py:36
  88.5 18.9 %all-gather.2.cloned.1.call-done.fc_ref.refs_0_.refs_1_.refs_2_.refs_3_.w_ref = bf16[768,6912]{1,0:T(8,128)(2,1)} async-done(((bf16[24,6912]{1,0:T(8,128)(2,1)}), bf16[768,6912]{1,0:T(8,128)(2,1)}) %all-gather.2.cloned.1.call-update) | async-done | bytes 10616848 | tf_op jit(solution)/shard_map/all_gather | solution.py:903
  111.6 22.9 %feed.1 = (f32[512,768]{1,0:T(8,128)S(1)}, f32[512,768]{1,0:T(8,128)S(1)}, bf16[768,1536]{1,0:T(8,128)(2,1)}, bf16[768,1536]{1,0:T(8,128)(2,1)}, bf16[3072,384]{...) custom-call(s32[1]{0:T(128)} %bitcast.29.core_ref, bf16[512,768]{1,0:T(8,128)(2,1)S(1)} %get-tuple-element.195.n_ref, ...), custom_call_target="tpu_custom_call" | custom-call | flops 1048576 | bytes 4096 | tf_op jit(solution)/shard_map/feed/pallas_call | solution.py:610
  138.9 6.1 %turn.1 = (f32[512,768]{1,0:T(8,128)}, bf16[512,384]{1,0:T(8,128)(2,1)}, bf16[512,384]{1,0:T(8,128)(2,1)}, bf16[768,384]{1,0:T(8,128)(2,1)}, bf16[768,384]{1,0:T...) custom-call(s32[1]{0:T(128)} %bitcast.29.core_ref, ...), custom_call_target="tpu_custom_call" | custom-call | flops 1048576 | bytes 4096 | tf_op jit(solution)/shard_map/turn/pallas_call | solution.py:680
  145.1 4.9 %send.8 = (bf16[8,48,1536]{2,1,0:T(8,128)(2,1)S(1)}, bf16[8,192,384]{2,1,0:T(8,128)(2,1)S(1)}) custom-call(s32[1]{0:T(128)} %bitcast.35.at_ref, bf16[16,48,1536]{2,1,0:T(8,128)(2,1)S(1)} %bitcast.105, bf16[16,48,1536]{2,1,0:T(8,128)(2,1)} %bitcast.37.refs_1_, bf16[16,192,384]{2,1,0:T(8,128)(2,1)} %bitcast.125, ...), custom_call_target="tpu_custom_call" | custom-call | flops 12884901888 | bytes 4096 | tf_op jit(solution)/shard_map/send/pallas_call | solution.py:158
  154.3 6.6 %attend_back.3 = (bf16[1024,384]{1,0:T(8,128)(2,1)S(1)}, bf16[2048,384]{1,0:T(8,128)(2,1)S(1)}, bf16[2048,384]{1,0:T(8,128)(2,1)}) custom-call(s32[1]{0:T(128)} %bitcast.7.far_ref, bf16[1024,384]{1,0:T(8,128)(2,1)S(1)} %copy-done.2, bf16[2048,768]{1,0:T(8,128)(2,1)} %copy-done, bf16[2048,768]{1,0:T(8,128)(2,1)} %copy-done, bf16[1024,384]{1,0:T(8,128)(2,1)S(1)} %bitcast.95, ...), custom_call_target="tpu_custom_call" | custom-call | flops 1048576 | bytes 4096 | tf_op jit(solution)/shard_map/attend_back/pallas_call | solution.py:428
  160.9 6.4 %attend_back.4 = (bf16[1024,384]{1,0:T(8,128)(2,1)S(1)}, bf16[2048,384]{1,0:T(8,128)(2,1)S(1)}, bf16[2048,384]{1,0:T(8,128)(2,1)}) custom-call(s32[1]{0:T(128)} %bitcast.7.far_ref, bf16[1024,384]{1,0:T(8,128)(2,1)S(1)} %copy-done.2, bf16[2048,768]{1,0:T(8,128)(2,1)} %copy-done, ...), custom_call_target="tpu_custom_call", output_to_operand_aliasing={{0}: (7, {}), {1}: (8, {}), {2}: (9, {})} | custom-call | flops 1048576 | bytes 4096 | tf_op jit(solution)/shard_map/attend_back/pallas_call | solution.py:428
  167.3 10.0 %collective-permute-done.14.refs_2_ = bf16[8,48,1536]{2,1,0:T(8,128)(2,1)S(1)} collective-permute-done((bf16[8,48,1536]{2,1,0:T(8,128)(2,1)S(1)}, bf16[8,48,1536]{2,1,0:T(8,128)(2,1)S(1)}, u32[]{:S(2)}, u32[]{:S(2)}) %collective-permute-start.14) | collective-permute-done | bytes 1179680 | tf_op jit(solution)/shard_map/ppermute | solution.py:36
  178.2 3.1 %send.9 = (bf16[4,48,1536]{2,1,0:T(8,128)(2,1)S(1)}, bf16[4,192,384]{2,1,0:T(8,128)(2,1)S(1)}) custom-call(s32[1]{0:T(128)} %bitcast.35.at_ref, bf16[16,48,1536]{2,1,0:T(8,128)(2,1)S(1)} %bitcast.106, bf16[16,48,1536]{2,1,0:T(8,128)(2,1)} %bitcast.37.refs_1_, bf16[8,48,1536]{2,1,0:T(8,128)(2,1)S(1)} %collective-permute-done.14.refs_2_, ...), custom_call_target="tpu_custom_call" | custom-call | flops 12884901888 | bytes 4096 | tf_op jit(solution)/shard_map/send/pallas_call | solution.py:158
  183.4 6.6 %attend_back.5 = (bf16[1024,384]{1,0:T(8,128)(2,1)S(1)}, bf16[2048,384]{1,0:T(8,128)(2,1)S(1)}, bf16[2048,384]{1,0:T(8,128)(2,1)}) custom-call(s32[1]{0:T(128)} %bitcast.7.far_ref, bf16[1024,384]{1,0:T(8,128)(2,1)S(1)} %copy-done.2, bf16[2048,768]{1,0:T(8,128)(2,1)} %copy-done, ...), custom_call_target="tpu_custom_call", output_to_operand_aliasing={{0}: (7, {}), {1}: (8, {}), {2}: (9, {})} | custom-call | flops 1048576 | bytes 4096 | tf_op jit(solution)/shard_map/attend_back/pallas_call | solution.py:428
  190.8 4.1 %collective-permute-done.16.refs_3_ = bf16[4,48,1536]{2,1,0:T(8,128)(2,1)} collective-permute-done((bf16[4,48,1536]{2,1,0:T(8,128)(2,1)S(1)}, bf16[4,48,1536]{2,1,0:T(8,128)(2,1)}, u32[]{:S(2)}, u32[]{:S(2)}) %collective-permute-start.16) | collective-permute-done | bytes 589856 | tf_op jit(solution)/shard_map/ppermute | solution.py:36
  195.6 2.6 send.10
  198.2 6.6 %qkv_grads.1 = (bf16[768,768]{1,0:T(8,128)(2,1)S(1)}, bf16[768,768]{1,0:T(8,128)(2,1)S(1)}) custom-call(bf16[2048,768]{1,0:T(8,128)(2,1)} %copy-done.40, bf16[1024,384]{1,0:T(8,128)(2,1)S(1)} %get-tuple-element.150.dq_ref, bf16[2048,384]{1,0:T(8,128)(2,1)S(1)} %get-tuple-element.140.dk_ref, bf16[2048,384]{1,0:T(8,128)(2,1)} %get-tuple-element.141.dv_ref, ...), custom_call_target="tpu_custom_call" | custom-call | flops 1048576 | bytes 4096 | tf_op jit(solution)/shard_map/qkv_grads/pallas_call | solution.py:477
  205.1 2.4 collective-permute-start.20
  209.6 10.3 %norm_back.1 = (f32[2,512,768]{2,1,0:T(8,128)}, bf16[2,512,768]{2,1,0:T(8,128)(2,1)}, f32[1,768]{1,0:T(1,128)S(1)}, f32[1,768]{1,0:T(1,128)S(1)}, f32[1,384]{1,0:T(1,128)S(1)}, /*index=5*/f32[1,384]{1,0:T(1,128)S(1)}) custom-call(s32[1]{0:T(128)} %bitcast.29.core_ref, bf16[1024,384]{1,0:T(8,128)(2,1)S(1)} %get-tuple-element.150.dq_ref, ...), custom_call_target="tpu_custom_call" | custom-call | flops 1048576 | bytes 4096 | tf_op jit(solution)/shard_map/norm_back/pallas_call | solution.py:769
  226.5 2.6 fusion.11
  233.9 2.5 pack.1
  243.0 9.9 %all-to-all-start = ((f32[32,1,1024]{2,1,0:T(1,128)}), f32[32,1,1024]{2,1,0:T(1,128)S(1)}, u32[]{:S(2)}, u32[]{:S(2)}) async-start(f32[32,1,1024]{2,1,0:T(1,128)} %copy.50), calls=%async_computation | async-start | bytes 262144 | tf_op jit(solution)/shard_map/all_to_all | solution.py:1077
  253.0 2.5 fusion.10
  257.8 3.4 %all-to-all-done = f32[32,1,1024]{2,1,0:T(1,128)S(1)} async-done(((f32[32,1,1024]{2,1,0:T(1,128)}), f32[32,1,1024]{2,1,0:T(1,128)S(1)}, u32[]{:S(2)}, u32[]{:S(2)}) %all-to-all-start) | async-done | bytes 131104 | tf_op jit(solution)/shard_map/all_to_all | solution.py:1077
  262.4 2.8 fusion.23
  (266 shorter events, 77.3 us)
Async XLA Ops:
  7.3 100.1 %all-gather.2.cloned.1.call-start = ((), (), s32[]{:S(2)}) async-start(), calls=%async_computation.1 | async-start | bytes 10948608 | tf_op jit(solution)/shard_map/all_gather | solution.py:903
  9.3 22.9 %collective-permute-start = (bf16[512,768]{1,0:T(8,128)(2,1)}, bf16[512,768]{1,0:T(8,128)(2,1)S(1)}, u32[]{:S(2)}, u32[]{:S(2)}) collective-permute-start(bf16[512,768]{1,0:T(8,128)(2,1)} %bitcast.135), channel_id=1, source_target_pairs={{0,2},{1,3},{4,6},{5,7},{8,10},{9,11},{12,14},{13,15},{16,18},{17,... | collective-permute-start | bytes 2359304 | tf_op jit(solution)/shard_map/ppermute | solution.py:909
  17.2 8.2 %collective-permute-start.4 = (bf16[1,48,1280]{2,1,0:T(8,128)(2,1)S(1)}, bf16[1,48,1280]{2,1,0:T(8,128)(2,1)S(1)}, u32[]{:S(2)}, u32[]{:S(2)}) collective-permute-start(bf16[1,48,1280]{2,1,0:T(8,128)(2,1)S(1)} %bitcast.138), channel_id=1, source_target_pairs={{0,16},{1,17},{2,18},{3,19},{4,20},{5,21},{6,22},{7,23},{8,24},{9,... | collective-permute-start | bytes 368648 | tf_op jit(solution)/shard_map/ppermute | solution.py:36
  32.2 7.0 %collective-permute-start.5 = (bf16[2,48,1280]{2,1,0:T(8,128)(2,1)S(1)}, bf16[2,48,1280]{2,1,0:T(8,128)(2,1)}, u32[]{:S(2)}, u32[]{:S(2)}) collective-permute-start(bf16[2,48,1280]{2,1,0:T(8,128)(2,1)S(1)} %constant_dynamic-update-slice_fusion.1), channel_id=1, source_target_pairs={{0,8},{1,9},{2,10},{3,11},{4,12},{5,13},{6,14},{7,15},{8,0},{9,1},... | collective-permute-start | bytes 737288 | tf_op jit(solution)/shard_map/ppermute | solution.py:36
  33.6 10.0 %collective-permute-start.2 = (bf16[512,768]{1,0:T(8,128)(2,1)S(1)}, bf16[512,768]{1,0:T(8,128)(2,1)S(1)}, u32[]{:S(2)}, u32[]{:S(2)}) collective-permute-start(bf16[512,768]{1,0:T(8,128)(2,1)S(1)} %bitcast.136), channel_id=1, source_target_pairs={{0,1},{1,0},{2,3},{3,2},{4,5},{5,4},{6,7},{7,6},{8,9},{9,8},{10,11... | collective-permute-start | bytes 2359304 | tf_op jit(solution)/shard_map/ppermute | solution.py:36
  36.2 18.9 %collective-permute-start.1 = (bf16[512,768]{1,0:T(8,128)(2,1)S(1)}, bf16[512,768]{1,0:T(8,128)(2,1)S(1)}, u32[]{:S(2)}, u32[]{:S(2)}) collective-permute-start(bf16[512,768]{1,0:T(8,128)(2,1)S(1)} %collective-permute-done), channel_id=1, source_target_pairs={{0,1},{1,0},{2,3},{3,2},{4,5},{5,4},{6,7},{7,6},{8,9},{9,8},{10,11... | collective-permute-start | bytes 2359304 | tf_op jit(solution)/shard_map/ppermute | solution.py:36
  40.3 9.5 %collective-permute-start.6 = (bf16[4,48,512]{2,1,0:T(8,128)(2,1)S(1)}, bf16[4,48,512]{2,1,0:T(8,128)(2,1)S(1)}, u32[]{:S(2)}, u32[]{:S(2)}) collective-permute-start(bf16[4,48,512]{2,1,0:T(8,128)(2,1)S(1)} %pad_maximum_fusion.2), channel_id=1, source_target_pairs={{0,4},{1,5},{2,6},{3,7},{4,0},{5,1},{6,2},{7,3},{8,12},{9,13},{10,... | collective-permute-start | bytes 589832 | tf_op jit(solution)/shard_map/ppermute | solution.py:36
  41.9 13.0 %collective-permute-start.8 = (bf16[4,48,768]{2,1,0:T(8,128)(2,1)S(1)}, bf16[4,48,768]{2,1,0:T(8,128)(2,1)S(1)}, u32[]{:S(2)}, u32[]{:S(2)}) collective-permute-start(bf16[4,48,768]{2,1,0:T(8,128)(2,1)S(1)} %slice.173), channel_id=1, source_target_pairs={{0,2},{1,3},{2,0},{3,1},{4,6},{5,7},{6,4},{7,5},{8,10},{9,11},{10,... | collective-permute-start | bytes 884744 | tf_op jit(solution)/shard_map/ppermute | solution.py:36
  49.9 14.1 %collective-permute-start.7 = (bf16[8,48,512]{2,1,0:T(8,128)(2,1)S(1)}, bf16[8,48,512]{2,1,0:T(8,128)(2,1)S(1)}, u32[]{:S(2)}, u32[]{:S(2)}) collective-permute-start(bf16[8,48,512]{2,1,0:T(8,128)(2,1)S(1)} %bitcast.133), channel_id=1, source_target_pairs={{0,2},{1,3},{2,0},{3,1},{4,6},{5,7},{6,4},{7,5},{8,10},{9,11},{10,... | collective-permute-start | bytes 1179656 | tf_op jit(solution)/shard_map/ppermute | solution.py:36
  54.9 13.6 %collective-permute-start.9 = (bf16[8,48,768]{2,1,0:T(8,128)(2,1)S(1)}, bf16[8,48,768]{2,1,0:T(8,128)(2,1)}, u32[]{:S(2)}, u32[]{:S(2)}) collective-permute-start(bf16[8,48,768]{2,1,0:T(8,128)(2,1)S(1)} %bitcast.123), channel_id=1, source_target_pairs={{0,4},{1,5},{2,6},{3,7},{4,0},{5,1},{6,2},{7,3},{8,12},{9,13},{10,... | collective-permute-start | bytes 1769480 | tf_op jit(solution)/shard_map/ppermute | solution.py:36
  82.4 4.9 %collective-permute-start.10 = (bf16[512,384]{1,0:T(8,128)(2,1)S(1)}, bf16[512,384]{1,0:T(8,128)(2,1)S(1)}, u32[]{:S(2)}, u32[]{:S(2)}) collective-permute-start(bf16[512,384]{1,0:T(8,128)(2,1)S(1)} %constant_dynamic-slice_fusion), channel_id=1, source_target_pairs={{0,1},{1,0},{2,3},{3,2},{4,5},{5,4},{6,7},{7,6},{8,9},{9,8},{10,11... | collective-permute-start | bytes 1179656 | tf_op jit(solution)/shard_map/ppermute | solution.py:36
  136.8 8.1 %collective-permute-start.12 = (bf16[768,1536]{1,0:T(8,128)(2,1)}, bf16[768,1536]{1,0:T(8,128)(2,1)}, u32[]{:S(2)}, u32[]{:S(2)}) collective-permute-start(bf16[768,1536]{1,0:T(8,128)(2,1)} %get-tuple-element.114), channel_id=1, source_target_pairs={{0,1},{1,0},{2,3},{3,2},{4,5},{5,4},{6,7},{7,6},{8,9},{9,8},{10,11... | collective-permute-start | bytes 7077896 | tf_op jit(solution)/shard_map/ppermute | solution.py:36
  137.1 8.0 %collective-permute-start.13 = (bf16[3072,384]{1,0:T(8,128)(2,1)}, bf16[3072,384]{1,0:T(8,128)(2,1)}, u32[]{:S(2)}, u32[]{:S(2)}) collective-permute-start(bf16[3072,384]{1,0:T(8,128)(2,1)} %get-tuple-element.115), channel_id=1, source_target_pairs={{0,1},{1,0},{2,3},{3,2},{4,5},{5,4},{6,7},{7,6},{8,9},{9,8},{10,11... | collective-permute-start | bytes 7077896 | tf_op jit(solution)/shard_map/ppermute | solution.py:36
  150.0 27.3 %collective-permute-start.14 = (bf16[8,48,1536]{2,1,0:T(8,128)(2,1)S(1)}, bf16[8,48,1536]{2,1,0:T(8,128)(2,1)S(1)}, u32[]{:S(2)}, u32[]{:S(2)}) collective-permute-start(bf16[8,48,1536]{2,1,0:T(8,128)(2,1)S(1)} %get-tuple-element.119), channel_id=1, source_target_pairs={{0,2},{1,3},{2,0},{3,1},{4,6},{5,7},{6,4},{7,5},{8,10},{9,11},{10,... | collective-permute-start | bytes 3538952 | tf_op jit(solution)/shard_map/ppermute | solution.py:36
  151.3 27.0 %collective-permute-start.15 = (bf16[8,192,384]{2,1,0:T(8,128)(2,1)S(1)}, bf16[8,192,384]{2,1,0:T(8,128)(2,1)S(1)}, u32[]{:S(2)}, u32[]{:S(2)}) collective-permute-start(bf16[8,192,384]{2,1,0:T(8,128)(2,1)S(1)} %get-tuple-element.120), channel_id=1, source_target_pairs={{0,4},{1,5},{2,6},{3,7},{4,0},{5,1},{6,2},{7,3},{8,12},{9,13},{10,... | collective-permute-start | bytes 3538952 | tf_op jit(solution)/shard_map/ppermute | solution.py:36
  151.6 2.2 collective-permute-start.11
  153.9 36.1 %collective-permute-start.18 = (bf16[768,384]{1,0:T(8,128)(2,1)S(1)}, bf16[768,384]{1,0:T(8,128)(2,1)S(1)}, u32[]{:S(2)}, u32[]{:S(2)}) collective-permute-start(bf16[768,384]{1,0:T(8,128)(2,1)S(1)} %copy-done.57), channel_id=1, source_target_pairs={{0,1},{1,0},{2,3},{3,2},{4,5},{5,4},{6,7},{7,6},{8,9},{9,8},{10,11... | collective-permute-start | bytes 1769480 | tf_op jit(solution)/shard_map/ppermute | solution.py:36
  181.3 13.6 %collective-permute-start.16 = (bf16[4,48,1536]{2,1,0:T(8,128)(2,1)S(1)}, bf16[4,48,1536]{2,1,0:T(8,128)(2,1)}, u32[]{:S(2)}, u32[]{:S(2)}) collective-permute-start(bf16[4,48,1536]{2,1,0:T(8,128)(2,1)S(1)} %get-tuple-element.131), channel_id=1, source_target_pairs={{0,4},{1,5},{2,6},{3,7},{4,0},{5,1},{6,2},{7,3},{8,12},{9,13},{10,... | collective-permute-start | bytes 1769480 | tf_op jit(solution)/shard_map/ppermute | solution.py:36
  182.1 13.5 %collective-permute-start.17 = (bf16[4,192,384]{2,1,0:T(8,128)(2,1)S(1)}, bf16[4,192,384]{2,1,0:T(8,128)(2,1)}, u32[]{:S(2)}, u32[]{:S(2)}) collective-permute-start(bf16[4,192,384]{2,1,0:T(8,128)(2,1)S(1)} %get-tuple-element.132), channel_id=1, source_target_pairs={{0,2},{1,3},{2,0},{3,1},{4,6},{5,7},{6,4},{7,5},{8,10},{9,11},{10,... | collective-permute-start | bytes 1769480 | tf_op jit(solution)/shard_map/ppermute | solution.py:36
  205.1 16.9 %collective-permute-start.20 = (bf16[8,48,768]{2,1,0:T(8,128)(2,1)S(1)}, bf16[8,48,768]{2,1,0:T(8,128)(2,1)S(1)}, u32[]{:S(2)}, u32[]{:S(2)}) collective-permute-start(bf16[8,48,768]{2,1,0:T(8,128)(2,1)S(1)} %get-tuple-element.148), channel_id=1, source_target_pairs={{0,2},{1,3},{2,0},{3,1},{4,6},{5,7},{6,4},{7,5},{8,10},{9,11},{10,... | collective-permute-start | bytes 1769480 | tf_op jit(solution)/shard_map/ppermute | solution.py:36
  207.6 14.5 %collective-permute-start.21 = (bf16[8,48,768]{2,1,0:T(8,128)(2,1)S(1)}, bf16[8,48,768]{2,1,0:T(8,128)(2,1)S(1)}, u32[]{:S(2)}, u32[]{:S(2)}) collective-permute-start(bf16[8,48,768]{2,1,0:T(8,128)(2,1)S(1)} %get-tuple-element.149), channel_id=1, source_target_pairs={{0,4},{1,5},{2,6},{3,7},{4,0},{5,1},{6,2},{7,3},{8,12},{9,13},{10,... | collective-permute-start | bytes 1769480 | tf_op jit(solution)/shard_map/ppermute | solution.py:36
  208.7 13.4 %collective-permute-start.22 = (bf16[2,48,3072]{2,1,0:T(8,128)(2,1)S(1)}, bf16[2,48,3072]{2,1,0:T(8,128)(2,1)S(1)}, u32[]{:S(2)}, u32[]{:S(2)}) collective-permute-start(bf16[2,48,3072]{2,1,0:T(8,128)(2,1)S(1)} %copy-done.58), channel_id=1, source_target_pairs={{0,8},{1,9},{2,10},{3,11},{4,12},{5,13},{6,14},{7,15},{8,0},{9,1},... | collective-permute-start | bytes 1769480 | tf_op jit(solution)/shard_map/ppermute | solution.py:36
  219.9 6.6 %collective-permute-start.19 = (bf16[2,512,768]{2,1,0:T(8,128)(2,1)}, bf16[2,512,768]{2,1,0:T(8,128)(2,1)}, u32[]{:S(2)}, u32[]{:S(2)}) collective-permute-start(bf16[2,512,768]{2,1,0:T(8,128)(2,1)} %get-tuple-element.152), channel_id=1, source_target_pairs={{0,1},{1,0},{2,3},{3,2},{4,5},{5,4},{6,7},{7,6},{8,9},{9,8},{10,11... | collective-permute-start | bytes 4718600 | tf_op jit(solution)/shard_map/ppermute | solution.py:36
  223.2 6.5 %collective-permute-start.26 = (bf16[4,48,768]{2,1,0:T(8,128)(2,1)S(1)}, bf16[4,48,768]{2,1,0:T(8,128)(2,1)S(1)}, u32[]{:S(2)}, u32[]{:S(2)}) collective-permute-start(bf16[4,48,768]{2,1,0:T(8,128)(2,1)S(1)} %get-tuple-element.155), channel_id=1, source_target_pairs={{0,4},{1,5},{2,6},{3,7},{4,0},{5,1},{6,2},{7,3},{8,12},{9,13},{10,... | collective-permute-start | bytes 884744 | tf_op jit(solution)/shard_map/ppermute | solution.py:36
  223.6 6.2 %collective-permute-start.27 = (bf16[4,48,768]{2,1,0:T(8,128)(2,1)S(1)}, bf16[4,48,768]{2,1,0:T(8,128)(2,1)S(1)}, u32[]{:S(2)}, u32[]{:S(2)}) collective-permute-start(bf16[4,48,768]{2,1,0:T(8,128)(2,1)S(1)} %get-tuple-element.156), channel_id=1, source_target_pairs={{0,2},{1,3},{2,0},{3,1},{4,6},{5,7},{6,4},{7,5},{8,10},{9,11},{10,... | collective-permute-start | bytes 884744 | tf_op jit(solution)/shard_map/ppermute | solution.py:36
  233.1 6.3 %collective-permute-start.28 = (bf16[2,48,1536]{2,1,0:T(8,128)(2,1)}, bf16[2,48,1536]{2,1,0:T(8,128)(2,1)S(1)}, u32[]{:S(2)}, u32[]{:S(2)}) collective-permute-start(bf16[2,48,1536]{2,1,0:T(8,128)(2,1)} %send.14), channel_id=1, source_target_pairs={{0,8},{1,9},{2,10},{3,11},{4,12},{5,13},{6,14},{7,15},{8,0},{9,1},... | collective-permute-start | bytes 884744 | tf_op jit(solution)/shard_map/ppermute | solution.py:36
  236.3 19.2 %collective-permute-start.25 = (bf16[1,48,3072]{2,1,0:T(8,128)(2,1)}, bf16[1,48,3072]{2,1,0:T(8,128)(2,1)S(1)}, u32[]{:S(2)}, u32[]{:S(2)}) collective-permute-start(bf16[1,48,3072]{2,1,0:T(8,128)(2,1)} %send.13), channel_id=1, source_target_pairs={{0,16},{1,17},{2,18},{3,19},{4,20},{5,21},{6,22},{7,23},{8,24},{9,... | collective-permute-start | bytes 884744 | tf_op jit(solution)/shard_map/ppermute | solution.py:36
  238.2 24.2 %collective-permute-start.23 = (bf16[512,768]{1,0:T(8,128)(2,1)}, bf16[512,768]{1,0:T(8,128)(2,1)S(1)}, u32[]{:S(2)}, u32[]{:S(2)}) collective-permute-start(bf16[512,768]{1,0:T(8,128)(2,1)} %fusion.11), channel_id=1, source_target_pairs={{2,0},{3,1},{6,4},{7,5},{10,8},{11,9},{14,12},{15,13},{18,16},{19,... | collective-permute-start | bytes 2359304 | tf_op jit(solution)/shard_map/ppermute | solution.py:1057
  243.0 18.2 %all-to-all-start = ((f32[32,1,1024]{2,1,0:T(1,128)}), f32[32,1,1024]{2,1,0:T(1,128)S(1)}, u32[]{:S(2)}, u32[]{:S(2)}) async-start(f32[32,1,1024]{2,1,0:T(1,128)} %copy.50), calls=%async_computation | async-start | bytes 262144 | tf_op jit(solution)/shard_map/all_to_all | solution.py:1077
  255.5 14.0 %collective-permute-start.29 = (bf16[1,48,1536]{2,1,0:T(8,128)(2,1)S(1)}, bf16[1,48,1536]{2,1,0:T(8,128)(2,1)S(1)}, u32[]{:S(2)}, u32[]{:S(2)}) collective-permute-start(bf16[1,48,1536]{2,1,0:T(8,128)(2,1)S(1)} %copy-done.60), channel_id=1, source_target_pairs={{0,16},{1,17},{2,18},{3,19},{4,20},{5,21},{6,22},{7,23},{8,24},{9,... | collective-permute-start | bytes 442376 | tf_op jit(solution)/shard_map/ppermute | solution.py:36
  267.2 4.9 %collective-permute-start.24 = (f32[1,768]{1,0:T(1,128)S(1)}, f32[1,768]{1,0:T(1,128)S(1)}, u32[]{:S(2)}, u32[]{:S(2)}) collective-permute-start(f32[1,768]{1,0:T(1,128)S(1)} %slice.181), channel_id=1, source_target_pairs={{1,0},{2,1},{3,2},{5,4},{6,5},{7,6},{9,8},{10,9},{11,10},{13,12},{... | collective-permute-start | bytes 9224 | tf_op jit(solution)/shard_map/ppermute | solution.py:1101
  271.3 2.2 collective-permute-start.30
  (62 other events, 393.3 us)
Sparse Core Ops, SparseCore 0:
  11.0 96.2 all-gather.1
